TPU v7x, 32 devices: a whole 2x2x4 slice. The times are simulated.
32 devices in a mesh: shard: 8 (over y, x, core), replica: 4 (over z).
Axes of the slice: x: 2, y: 2, z: 4, core: 2. Of those that a mesh axis runs over, the one named last changes fastest.
Arguments:
- tokens: bfloat16 [4096, 768], P(('shard', 'replica')), may hold values from -6 to 6
- positions: int32 [4096], P(('shard', 'replica')), may hold values from 0 to 2047, as said below
- qkv_weight: bfloat16 [768, 2304], P('shard'), may hold values from -0.21875 to 0.21875
- attn_weight: bfloat16 [768, 768], P('shard'), may hold values from -0.875 to 0.875
- glu_weight: bfloat16 [768, 2304], P('shard'), may hold values from -0.21875 to 0.21875
- down_weight: bfloat16 [1152, 768], P('shard'), may hold values from -0.1875 to 0.1875
- attn_gain: bfloat16 [768], P('shard'), may hold values from 0.25 to 1.75
- ffn_gain: bfloat16 [768], P('shard'), may hold values from 0.25 to 1.75
- cotangent: bfloat16 [4096, 768], P(('shard', 'replica')), may hold values from -6 to 6
Outputs:
- mixed: bfloat16 [4096, 768], P(('shard', 'replica'))
- grad_tokens: bfloat16 [4096, 768], P(('shard', 'replica'))
- grad_qkv: float32 [768, 2304], P('shard')
- grad_attn: float32 [768, 768], P('shard')
- grad_glu: float32 [768, 2304], P('shard')
- grad_down: float32 [1152, 768], P('shard')
- grad_attn_gain: float32 [768], P('shard')
- grad_ffn_gain: float32 [768], P('shard')
Inputs may be any that keep to these rules, and one draw needn't show every extreme that they name: `positions`: sequences lie one after another in the stream, each counting 0, 1, 2, ... from its first token; the stream begins with place 0; every sequence holds 1024 to 2048 tokens, except the last, which the stream's end may cut short.
All inputs are finite; a program needn't handle non-finite values.
Results may differ from a plain program's by a relative error of at most 0.02.
Values may be sent and summed in bfloat16 or wider, within the bound.
No kernel may reach another device: no remote copies, remote signals or barrier semaphores. Data moves between devices by JAX's collectives and lax.ppermute only.
A program may use at most 128 MiB of HBM per device.

v0:
```python
import math

import jax
import jax.numpy as jnp
from jax import lax
from jax.sharding import PartitionSpec as P

HEAD = 64
WINDOW = 128


EPSILON = 1e-05
THETA_BASE = 10000.0
NEGATIVE = -1e30


def with_halo(shard, sides, width):
    for axis, dim in sides:
        devices, length = (lax.axis_size(axis), shard.shape[dim])
        up = [(i, (i + 1) % devices) for i in range(devices - 1)]
        down = [(j, i) for i, j in up]
        last = lax.slice_in_dim(shard, length - width, length, axis=dim)
        leading = lax.slice_in_dim(shard, 0, width, axis=dim)
        before = lax.ppermute(last, axis, up)
        after = lax.ppermute(leading, axis, down)
        shard = jnp.concatenate([before, shard, after], axis=dim)
    return shard


def layer_norm(vector, scaling):
    average = jnp.mean(vector, axis=-1, keepdims=True)
    centred = vector - average
    spread = jnp.mean(centred * centred, axis=-1, keepdims=True)
    return centred * lax.rsqrt(spread + EPSILON) * scaling


def rotate(vector, cosine, sine):
    middle = vector.shape[-1] // 2
    turned = jnp.concatenate([-vector[..., middle:], vector[..., :middle]], axis=-1)
    return vector * cosine + turned * sine


def angles(positions, head_size):
    middle = head_size // 2
    inverse = THETA_BASE ** (-(jnp.arange(middle, dtype=jnp.float32) * 2.0 / head_size))
    phases = positions.astype(jnp.float32)[:, None] * inverse[None, :]
    phases = jnp.concatenate([phases, phases], axis=-1)[:, None, :]
    return (jnp.cos(phases), jnp.sin(phases))


def window_mask(near_query, near_key, radius):
    query_at = jnp.arange(near_query.shape[0], dtype=jnp.int32)[:, None]
    key_at = jnp.arange(near_key.shape[0], dtype=jnp.int32)[None, :]
    offset = key_at - radius - query_at
    distance = offset.astype(jnp.float32)
    later_key = near_key[None, :].astype(jnp.float32) >= distance
    later_query = near_query[:, None].astype(jnp.float32) >= -distance
    return (jnp.abs(offset) <= radius) & jnp.where(offset >= 0, later_key, later_query)


def geglu(gate_half, up_half):
    return jax.nn.gelu(gate_half, approximate=False) * up_half


def contract_rows(left, right):
    return lax.dot_general(
        left, right, (((0,), (0,)), ((), ())), preferred_element_type=jnp.float32
    )


def contract_cols(left, right):
    return lax.dot_general(
        left, right, (((1,), (1,)), ((), ())), preferred_element_type=jnp.float32
    )


def on_device(
    tokens,
    positions,
    qkv_weight,
    attn_weight,
    glu_weight,
    down_weight,
    attn_gain,
    ffn_gain,
    cotangent,
):
    row_count, model_width = tokens.shape
    head_count = model_width // HEAD
    radius = WINDOW // 2
    block_rows = min(row_count, 512)
    span_rows = block_rows + 2 * radius
    block_starts = jnp.arange(row_count // block_rows, dtype=jnp.int32) * block_rows
    scale = 1.0 / math.sqrt(HEAD)
    split_dims = (row_count, head_count, HEAD)
    gathered = (
        lax.all_gather(qkv_weight, "shard", axis=0, tiled=True),
        lax.all_gather(attn_weight, "shard", axis=0, tiled=True),
        lax.all_gather(glu_weight, "shard", axis=0, tiled=True),
        lax.all_gather(down_weight, "shard", axis=0, tiled=True),
        lax.all_gather(attn_gain, "shard", axis=0, tiled=True),
        lax.all_gather(ffn_gain, "shard", axis=0, tiled=True),
    )
    qkv_full, attn_full, glu_full, down_full, attn_scale, ffn_scale = gathered
    ffn_width = glu_full.shape[1] // 2
    inputs = tokens.astype(jnp.float32)
    normed = layer_norm(inputs, attn_scale.astype(jnp.float32)).astype(jnp.bfloat16)
    joined = jnp.dot(normed, qkv_full, preferred_element_type=jnp.float32)
    cosine, sine = angles(positions, HEAD)
    queries = rotate(joined[:, :model_width].reshape(split_dims), cosine, sine).astype(jnp.bfloat16)
    key_rows = rotate(joined[:, model_width : 2 * model_width].reshape(split_dims), cosine, sine)
    key_rows = key_rows.astype(jnp.bfloat16).reshape(row_count, model_width)
    value_rows = joined[:, 2 * model_width :].astype(jnp.bfloat16)
    near = jnp.minimum(positions, radius).astype(jnp.bfloat16)
    kv_ext, near_ext = (
        with_halo(
            jnp.concatenate([key_rows, value_rows], axis=1), ((("shard", "replica"), 0),), radius
        ),
        with_halo(near, ((("shard", "replica"), 0),), radius),
    )

    def block_parts():
        keys_blk = kv_ext[:, :model_width].reshape(span_rows, head_count, HEAD)
        values_blk = kv_ext[:, model_width:].reshape(span_rows, head_count, HEAD)
        allowed = window_mask(near, near_ext, radius)
        logits = (
            jnp.einsum("qhd,khd->hqk", queries, keys_blk, preferred_element_type=jnp.float32)
            * scale
        )
        return (queries, keys_blk, values_blk, allowed, logits)

    def attend_block(first_row):
        queries_blk, keys_blk, values_blk, allowed, logits = block_parts()
        scores = jnp.where(allowed[None], logits, NEGATIVE)
        peak = jnp.max(scores, axis=-1, keepdims=True)
        exponent = jnp.exp(scores - peak)
        summed = jnp.sum(exponent, axis=-1, keepdims=True)
        shares = (exponent / summed).astype(jnp.bfloat16)
        result = jnp.einsum("hqk,khd->qhd", shares, values_blk, preferred_element_type=jnp.float32)
        return (result, (peak + jnp.log(summed))[..., 0])

    contexts, log_sums = lax.map(attend_block, block_starts)
    context = contexts.reshape(row_count, model_width).astype(jnp.bfloat16)
    hidden = inputs + jnp.dot(context, attn_full, preferred_element_type=jnp.float32)
    normed_mlp = layer_norm(hidden, ffn_scale.astype(jnp.float32)).astype(jnp.bfloat16)
    gate_up = jnp.dot(normed_mlp, glu_full, preferred_element_type=jnp.float32)
    activated = geglu(gate_up[:, :ffn_width], gate_up[:, ffn_width:]).astype(jnp.bfloat16)
    mixed = (hidden + jnp.dot(activated, down_full, preferred_element_type=jnp.float32)).astype(
        jnp.bfloat16
    )
    regathered = (
        lax.all_gather(qkv_weight, "shard", axis=0, tiled=True),
        lax.all_gather(attn_weight, "shard", axis=0, tiled=True),
        lax.all_gather(glu_weight, "shard", axis=0, tiled=True),
        lax.all_gather(down_weight, "shard", axis=0, tiled=True),
        lax.all_gather(attn_gain, "shard", axis=0, tiled=True),
        lax.all_gather(ffn_gain, "shard", axis=0, tiled=True),
    )
    qkv_back, attn_back, glu_back, down_back, attn_scale_back, ffn_scale_back = regathered
    grad_down = contract_rows(activated, cotangent)
    grad_act = contract_cols(cotangent, down_back)
    ignored, glu_pull = jax.vjp(geglu, gate_up[:, :ffn_width], gate_up[:, ffn_width:])
    grad_gate, grad_up = glu_pull(grad_act)
    grad_gate_up = jnp.concatenate([grad_gate, grad_up], axis=1).astype(jnp.bfloat16)
    grad_glu = contract_rows(normed_mlp, grad_gate_up)
    grad_normed_mlp = contract_cols(grad_gate_up, glu_back)
    ignored, ffn_pull = jax.vjp(layer_norm, hidden, ffn_scale_back.astype(jnp.float32))
    grad_hidden_norm, grad_ffn_gain = ffn_pull(grad_normed_mlp)
    grad_hidden = cotangent.astype(jnp.float32) + grad_hidden_norm
    grad_low = grad_hidden.astype(jnp.bfloat16)
    grad_attn = contract_rows(context, grad_low)
    grad_context = contract_cols(grad_low, attn_back).astype(jnp.bfloat16).reshape(split_dims)

    def revisit_block(running, inputs_blk):
        first_row, log_sum = inputs_blk
        queries_blk, keys_blk, values_blk, allowed, logits = block_parts()
        shares = jnp.where(allowed[None], jnp.exp(logits - log_sum[..., None]), 0.0)
        grad_share = jnp.einsum(
            "qhd,khd->hqk", grad_context, values_blk, preferred_element_type=jnp.float32
        )
        row_dot = jnp.sum(shares * grad_share, axis=-1, keepdims=True)
        grad_logit = (shares * (grad_share - row_dot)).astype(jnp.bfloat16)
        grad_query = (
            jnp.einsum("hqk,khd->qhd", grad_logit, keys_blk, preferred_element_type=jnp.float32)
            * scale
        )
        grad_key = (
            jnp.einsum("hqk,qhd->khd", grad_logit, queries_blk, preferred_element_type=jnp.float32)
            * scale
        )
        grad_value = jnp.einsum(
            "hqk,qhd->khd",
            shares.astype(jnp.bfloat16),
            grad_context,
            preferred_element_type=jnp.float32,
        )
        grad_pair = jnp.concatenate(
            [grad_key.reshape(span_rows, model_width), grad_value.reshape(span_rows, model_width)],
            axis=1,
        )
        current = running
        running = current + grad_pair
        return (running, grad_query)

    start_grads = jnp.zeros((row_count + 2 * radius, 2 * model_width), jnp.float32)
    grad_kv_ext, grad_queries = lax.scan(revisit_block, start_grads, (block_starts, log_sums))
    rims = jnp.concatenate([grad_kv_ext[:radius], grad_kv_ext[row_count + radius :]], axis=0)
    returned = with_halo(rims.astype(jnp.bfloat16), ((("shard", "replica"), 0),), radius).astype(
        rims.dtype
    )
    grad_kv = grad_kv_ext[radius : radius + row_count]
    grad_kv = grad_kv.at[:radius].add(returned[:radius])
    grad_kv = grad_kv.at[row_count - radius :].add(returned[3 * radius :])
    grad_q = rotate(grad_queries.reshape(split_dims), cosine, -sine).reshape(row_count, model_width)
    grad_k = rotate(grad_kv[:, :model_width].reshape(split_dims), cosine, -sine).reshape(
        row_count, model_width
    )
    grad_joined = jnp.concatenate([grad_q, grad_k, grad_kv[:, model_width:]], axis=1).astype(
        jnp.bfloat16
    )
    grad_qkv = contract_rows(normed, grad_joined)
    grad_normed = contract_cols(grad_joined, qkv_back)
    ignored, attn_pull = jax.vjp(layer_norm, inputs, attn_scale_back.astype(jnp.float32))
    grad_in, grad_attn_gain = attn_pull(grad_normed)
    grad_tokens = (grad_hidden + grad_in).astype(jnp.bfloat16)
    owned = (
        lax.psum_scatter(
            grad_qkv.astype(jnp.bfloat16), "shard", scatter_dimension=0, tiled=True
        ).astype(jnp.float32),
        lax.psum_scatter(
            grad_attn.astype(jnp.bfloat16), "shard", scatter_dimension=0, tiled=True
        ).astype(jnp.float32),
        lax.psum_scatter(
            grad_glu.astype(jnp.bfloat16), "shard", scatter_dimension=0, tiled=True
        ).astype(jnp.float32),
        lax.psum_scatter(
            grad_down.astype(jnp.bfloat16), "shard", scatter_dimension=0, tiled=True
        ).astype(jnp.float32),
        lax.psum_scatter(
            grad_attn_gain.astype(jnp.bfloat16), "shard", scatter_dimension=0, tiled=True
        ).astype(jnp.float32),
        lax.psum_scatter(
            grad_ffn_gain.astype(jnp.bfloat16), "shard", scatter_dimension=0, tiled=True
        ).astype(jnp.float32),
    )
    pieces = (
        lax.psum_scatter(
            owned[0].astype(jnp.bfloat16), "replica", scatter_dimension=1, tiled=True
        ).astype(jnp.float32),
        lax.psum_scatter(
            owned[1].astype(jnp.bfloat16), "replica", scatter_dimension=1, tiled=True
        ).astype(jnp.float32),
        lax.psum_scatter(
            owned[2].astype(jnp.bfloat16), "replica", scatter_dimension=1, tiled=True
        ).astype(jnp.float32),
        lax.psum_scatter(
            owned[3].astype(jnp.bfloat16), "replica", scatter_dimension=1, tiled=True
        ).astype(jnp.float32),
    )
    matrices = (
        lax.all_gather(pieces[0].astype(jnp.bfloat16), "replica", axis=1, tiled=True).astype(
            jnp.float32
        ),
        lax.all_gather(pieces[1].astype(jnp.bfloat16), "replica", axis=1, tiled=True).astype(
            jnp.float32
        ),
        lax.all_gather(pieces[2].astype(jnp.bfloat16), "replica", axis=1, tiled=True).astype(
            jnp.float32
        ),
        lax.all_gather(pieces[3].astype(jnp.bfloat16), "replica", axis=1, tiled=True).astype(
            jnp.float32
        ),
    )
    gains = lax.psum((owned[4], owned[5]), "replica")
    results = tuple(matrices) + tuple(gains)
    return (mixed, grad_tokens) + results


def solution(mesh):
    in_specs = (
        P(("shard", "replica"), None),
        P(("shard", "replica")),
        P("shard", None),
        P("shard", None),
        P("shard", None),
        P("shard", None),
        P("shard"),
        P("shard"),
        P(("shard", "replica"), None),
    )
    out_specs = (
        P(("shard", "replica"), None),
        P(("shard", "replica"), None),
        P("shard", None),
        P("shard", None),
        P("shard", None),
        P("shard", None),
        P("shard"),
        P("shard"),
    )
    return jax.shard_map(
        on_device, mesh=mesh, in_specs=in_specs, out_specs=out_specs, check_vma=False
    )
```

profile of v0, /device:TPU:0, one launch (start us, length us, event | category | flops | bytes accessed | tf_op | source)
XLA Modules:
  0.0 448.0 jit_solution(17517074991900671887)
XLA Ops:
  10.3 4.9 %collective-permute-start.2 = (bf16[64]{0:T(256)(128)(2,1)S(1)}, bf16[64]{0:T(256)(128)(2,1)S(1)}, u32[]{:S(2)}, u32[]{:S(2)}) collective-permute-start(bf16[64]{0:T(256)(128)(2,1)S(1)} %get-tuple-element.128), channel_id=1, source_target_pairs={{0,1},{1,2},{2,3},{3,4},{4,5},{5,6},{6,7},{7,8},{8,9},{9,10},{10,1... | collective-permute-start | bytes 392 | tf_op jit(solution)/shard_map/ppermute | solution.py:24
  19.7 16.7 %all-reduce.6 = (bf16[768]{0:T(1024)(128)(2,1)S(1)}, bf16[768]{0:T(1024)(128)(2,1)S(1)}) all-reduce(bf16[768]{0:T(1024)(128)(2,1)S(1)} %dynamic-update-slice.6, bf16[768]{0:T(1024)(128)(2,1)S(1)} %dynamic-update-slice.7), channel_id=1, replica_groups=mesh['shard'=8,'replica'=4] {'shard'}, use_global_device_ids=true, to_apply=%add | all-reduce | flops 1536 | bytes 6144
  37.6 9.1 %all-gather.8.cloned.1.call-done = bf16[768,2304]{1,0:T(8,128)(2,1)} async-done(((bf16[96,2304]{1,0:T(8,128)(2,1)}), bf16[768,2304]{1,0:T(8,128)(2,1)}) %all-gather.8.cloned.1.call-update) | async-done | bytes 3538960 | tf_op jit(solution)/shard_map/all_gather | solution.py:97
  50.2 3.4 collective-permute-start
  55.0 3.1 collective-permute-done
  58.1 7.6 %collective-permute-done.1 = bf16[64,1536]{1,0:T(8,128)(2,1)S(1)} collective-permute-done((bf16[64,1536]{1,0:T(8,128)(2,1)S(1)}, bf16[64,1536]{1,0:T(8,128)(2,1)S(1)}, u32[]{:S(2)}, u32[]{:S(2)}) %collective-permute-start.1) | collective-permute-done | bytes 196640 | tf_op jit(solution)/shard_map/ppermute | solution.py:25
  68.2 4.5 %all-gather.10.cloned.1.call-done = bf16[768,768]{1,0:T(8,128)(2,1)} async-done(((bf16[96,768]{1,0:T(8,128)(2,1)}), bf16[768,768]{1,0:T(8,128)(2,1)}) %all-gather.10.cloned.1.call-update) | async-done | bytes 1179664 | tf_op jit(solution)/shard_map/all_gather | solution.py:98
  75.1 33.4 %all-gather.12.cloned.1.call-done = bf16[768,2304]{1,0:T(8,128)(2,1)} async-done(((bf16[96,2304]{1,0:T(8,128)(2,1)}), bf16[768,2304]{1,0:T(8,128)(2,1)}) %all-gather.12.cloned.1.call-update) | async-done | bytes 3538960 | tf_op jit(solution)/shard_map/all_gather | solution.py:99
  108.5 2.7 fusion.58
  111.3 25.6 %all-gather.14.cloned.1.call-done = bf16[1152,768]{1,0:T(8,128)(2,1)} async-done(((bf16[144,768]{1,0:T(8,128)(2,1)}), bf16[1152,768]{1,0:T(8,128)(2,1)}) %all-gather.14.cloned.1.call-update) | async-done | bytes 1769488 | tf_op jit(solution)/shard_map/all_gather | solution.py:100
  136.8 3.4 add_convert_fusion
  147.9 3.0 convolution_convert_fusion
  159.5 3.5 collective-permute-start.4
  165.7 6.7 %collective-permute-done.4 = bf16[64,1536]{0,1:T(8,128)(2,1)S(1)} collective-permute-done((bf16[64,1536]{0,1:T(8,128)(2,1)S(1)}, bf16[64,1536]{0,1:T(8,128)(2,1)S(1)}, u32[]{:S(2)}, u32[]{:S(2)}) %collective-permute-start.4) | collective-permute-done | bytes 196640 | tf_op jit(solution)/shard_map/ppermute | solution.py:24
  172.4 11.1 %collective-permute-done.5 = bf16[64,1536]{0,1:T(8,128)(2,1)S(1)} collective-permute-done((bf16[64,1536]{0,1:T(8,128)(2,1)S(1)}, bf16[64,1536]{0,1:T(8,128)(2,1)S(1)}, u32[]{:S(2)}, u32[]{:S(2)}) %collective-permute-start.5) | collective-permute-done | bytes 196640 | tf_op jit(solution)/shard_map/ppermute | solution.py:25
  185.1 5.7 %scatter-add.6 = f32[128,1536]{0,1:T(8,128)S(1)} dynamic-update-slice(f32[128,1536]{0,1:T(8,128)S(1)} %fusion.6, f32[64,1536]{0,1:T(8,128)} %fusion.8, s32[]{:T(128)} %constant.152.clone.1, s32[]{:T(128)} %constant.152.clone.1) | dynamic-update-slice | bytes 786436 | tf_op jit(solution)/shard_map/scatter-add | solution.py:212
  192.2 6.6 %scatter-add.9 = f32[128,1536]{0,1:T(8,128)S(1)} dynamic-update-slice(f32[128,1536]{0,1:T(8,128)S(1)} %scatter-add.6, f32[64,1536]{0,1:T(8,128)} %slice_add_fusion, s32[]{:T(128)} %constant.151.clone.1, s32[]{:T(128)} %constant.152.clone.1) | dynamic-update-slice | bytes 786436 | tf_op jit(solution)/shard_map/scatter-add | solution.py:213
  199.8 3.1 convolution_convert_fusion.1
  204.9 22.2 %reduce-scatter.23.cloned.1.call-done = bf16[144,768]{1,0:T(8,128)(2,1)} async-done(((bf16[1152,768]{1,0:T(8,128)(2,1)}), bf16[144,768]{1,0:T(8,128)(2,1)}) %reduce-scatter.23.cloned.1.call-update) | async-done | bytes 221200 | tf_op jit(solution)/shard_map/reduce_scatter | solution.py:236
  229.7 49.3 %reduce-scatter.21.cloned.1.call-done = bf16[96,2304]{1,0:T(8,128)(2,1)} async-done(((bf16[768,2304]{1,0:T(8,128)(2,1)}), bf16[96,2304]{1,0:T(8,128)(2,1)}) %reduce-scatter.21.cloned.1.call-update) | async-done | bytes 442384 | tf_op jit(solution)/shard_map/reduce_scatter | solution.py:233
  282.4 3.4 fusion.29
  286.1 12.7 %all-reduce.5 = (bf16[768]{0:T(1024)(128)(2,1)S(1)}, bf16[768]{0:T(1024)(128)(2,1)S(1)}) all-reduce(bf16[768]{0:T(1024)(128)(2,1)S(1)} %get-tuple-element.90, bf16[768]{0:T(1024)(128)(2,1)S(1)} %copy-done.37), channel_id=10, replica_groups=mesh['shard'=8,'replica'=4] {'shard'}, use_global_device_ids=true, to_apply=%region_20.21.clone | all-reduce | flops 1536 | bytes 6144
  298.9 32.2 %reduce-scatter.17.cloned.1.call-done = bf16[96,2304]{1,0:T(8,128)(2,1)} async-done(((bf16[768,2304]{1,0:T(8,128)(2,1)}), bf16[96,2304]{1,0:T(8,128)(2,1)}) %reduce-scatter.17.cloned.1.call-update) | async-done | bytes 442384 | tf_op jit(solution)/shard_map/reduce_scatter | solution.py:227
  333.2 12.2 %all-reduce.4 = (f32[96]{0:T(128)}, f32[96]{0:T(128)}) all-reduce(f32[96]{0:T(128)S(1)} %dynamic-slice_convert_fusion.1, f32[96]{0:T(128)S(1)} %dynamic-slice_convert_fusion), channel_id=1, replica_groups=mesh['shard'=8,'replica'=4] {'replica'}, use_global_device_ids=true, to_apply=%region_21.22 | all-reduce | flops 192 | bytes 1536 | tf_op jit(solution)/shard_map/psum | solution.py:274
  346.3 6.4 %reduce-scatter.27.cloned.1.call-done = bf16[192,96]{1,0:T(8,128)(2,1)} async-done(((bf16[768,96]{1,0:T(8,128)(2,1)}), bf16[192,96]{1,0:T(8,128)(2,1)}) %reduce-scatter.27.cloned.1.call-update) | async-done | bytes 36880
  352.7 14.6 %all_gather.43 = bf16[96,768]{0,1:T(8,128)(2,1)S(1)} all-gather(bf16[96,192]{0,1:T(8,128)(2,1)} %bitcast.114), channel_id=1, replica_groups=mesh['shard'=8,'replica'=4] {'replica'}, dimensions={1}, use_global_device_ids=true | all-gather | bytes 184320 | tf_op jit(solution)/shard_map/all_gather | solution.py:264
  368.2 5.6 %reduce-scatter.31.cloned.1.call-done = bf16[192,144]{1,0:T(8,128)(2,1)} async-done(((bf16[768,144]{1,0:T(8,128)(2,1)}), bf16[192,144]{1,0:T(8,128)(2,1)}) %reduce-scatter.31.cloned.1.call-update) | async-done | bytes 55312
  374.8 15.5 %all-gather.2 = bf16[4,192,144]{1,2,0:T(8,128)(2,1)S(1)} all-gather(bf16[1,192,144]{1,2,0:T(8,128)(2,1)S(1)} %bitcast.110), channel_id=1, replica_groups=mesh['shard'=8,'replica'=4] {'replica'}, dimensions={0}, use_global_device_ids=true | all-gather | bytes 276480 | tf_op jit(solution)/shard_map/all_gather | solution.py:270
  391.5 5.3 %reduce-scatter.29.cloned.1.call-done = bf16[576,96]{1,0:T(8,128)(2,1)} async-done(((bf16[2304,96]{1,0:T(8,128)(2,1)}), bf16[576,96]{1,0:T(8,128)(2,1)}) %reduce-scatter.29.cloned.1.call-update) | async-done | bytes 110608
  397.9 18.6 %all-gather.1 = bf16[4,576,96]{1,2,0:T(8,128)(2,1)S(1)} all-gather(bf16[1,576,96]{1,2,0:T(8,128)(2,1)S(1)} %bitcast.107), channel_id=1, replica_groups=mesh['shard'=8,'replica'=4] {'replica'}, dimensions={0}, use_global_device_ids=true | all-gather | bytes 552960 | tf_op jit(solution)/shard_map/all_gather | solution.py:267
  418.3 4.3 reduce-scatter.25.cloned.1.call-done
  423.6 15.8 %all-gather = bf16[4,576,96]{1,2,0:T(8,128)(2,1)S(1)} all-gather(bf16[1,576,96]{1,2,0:T(8,128)(2,1)S(1)} %bitcast.108), channel_id=1, replica_groups=mesh['shard'=8,'replica'=4] {'replica'}, dimensions={0}, use_global_device_ids=true | all-gather | bytes 552960 | tf_op jit(solution)/shard_map/all_gather | solution.py:261
  (216 shorter events, 59.4 us)
Async XLA Ops:
  7.2 10.8 %copy-start.40 = (u32[32]{0:T(128)S(1)}, u32[32]{0:T(128)}, u32[]{:S(2)}) copy-start(u32[32]{0:T(128)} %constant.189) | copy-start | bytes 388
  7.2 10.5 %copy-start.1 = (bf16[128,768]{1,0:T(8,128)(2,1)S(1)}, bf16[128,768]{1,0:T(8,128)(2,1)}, u32[]{:S(2)}) copy-start(bf16[128,768]{1,0:T(8,128)(2,1)} %param.13) | copy-start | bytes 589828
  7.2 12.0 %copy-start.45 = (bf16[96]{0:T(256)(128)(2,1)S(1)}, bf16[96]{0:T(256)(128)(2,1)}, u32[]{:S(2)}) copy-start(bf16[96]{0:T(256)(128)(2,1)} %param.19) | copy-start | bytes 580
  7.2 12.3 %copy-start.46 = (bf16[96]{0:T(256)(128)(2,1)S(1)}, bf16[96]{0:T(256)(128)(2,1)}, u32[]{:S(2)}) copy-start(bf16[96]{0:T(256)(128)(2,1)} %param.20) | copy-start | bytes 580
  7.2 39.5 %all-gather.8.cloned.1.call-start = ((), (), s32[]{:S(2)}) async-start(), calls=%async_computation.8 | async-start | bytes 3981312 | tf_op jit(solution)/shard_map/all_gather | solution.py:97
  7.9 64.7 %all-gather.10.cloned.1.call-start = ((), (), s32[]{:S(2)}) async-start(), calls=%async_computation.9 | async-start | bytes 1327104 | tf_op jit(solution)/shard_map/all_gather | solution.py:98
  8.7 99.9 %all-gather.12.cloned.1.call-start = ((), (), s32[]{:S(2)}) async-start(), calls=%async_computation.10 | async-start | bytes 3981312 | tf_op jit(solution)/shard_map/all_gather | solution.py:99
  9.4 127.4 %all-gather.14.cloned.1.call-start = ((), (), s32[]{:S(2)}) async-start(), calls=%async_computation.11 | async-start | bytes 1990656 | tf_op jit(solution)/shard_map/all_gather | solution.py:100
  10.3 27.1 %collective-permute-start.2 = (bf16[64]{0:T(256)(128)(2,1)S(1)}, bf16[64]{0:T(256)(128)(2,1)S(1)}, u32[]{:S(2)}, u32[]{:S(2)}) collective-permute-start(bf16[64]{0:T(256)(128)(2,1)S(1)} %get-tuple-element.128), channel_id=1, source_target_pairs={{0,1},{1,2},{2,3},{3,4},{4,5},{5,6},{6,7},{7,8},{8,9},{9,10},{10,1... | collective-permute-start | bytes 392 | tf_op jit(solution)/shard_map/ppermute | solution.py:24
  15.2 22.2 %collective-permute-start.3 = (bf16[64]{0:T(256)(128)(2,1)S(1)}, bf16[64]{0:T(256)(128)(2,1)S(1)}, u32[]{:S(2)}, u32[]{:S(2)}) collective-permute-start(bf16[64]{0:T(256)(128)(2,1)S(1)} %get-tuple-element.129), channel_id=1, source_target_pairs={{1,0},{2,1},{3,2},{4,3},{5,4},{6,5},{7,6},{8,7},{9,8},{10,9},{11,1... | collective-permute-start | bytes 392 | tf_op jit(solution)/shard_map/ppermute | solution.py:25
  16.5 186.4 %reduce-scatter.19.cloned.1.call-start = ((), (), s32[]{:S(2)}) async-start(), calls=%async_computation.13 | async-start | bytes 1327104 | tf_op jit(solution)/shard_map/reduce_scatter | solution.py:230
  17.7 31.7 %copy-start.28 = (f32[128]{0:T(128)}, f32[128]{0:T(128)S(1)}, u32[]{:S(2)}) copy-start(f32[128]{0:T(128)S(1)} %broadcast_multiply_fusion.4) | copy-start | bytes 1540
  17.9 31.5 %copy-start.30 = (f32[128]{0:T(128)}, f32[128]{0:T(128)S(1)}, u32[]{:S(2)}) copy-start(f32[128]{0:T(128)S(1)} %fusion.45) | copy-start | bytes 1540
  37.2 17.7 %copy-start.23 = (f32[128,64]{0,1:T(8,128)}, f32[128,64]{0,1:T(8,128)S(1)}, u32[]{:S(2)}) copy-start(f32[128,64]{0,1:T(8,128)S(1)} %get-tuple-element.125) | copy-start | bytes 98308
  37.6 29.8 %copy-start.19 = (pred[128,256]{1,0:T(8,128)(4,1)}, pred[128,256]{1,0:T(8,128)(4,1)S(1)}, u32[]{:S(2)}) copy-start(pred[128,256]{1,0:T(8,128)(4,1)S(1)} %fusion.40) | copy-start | bytes 98308
  50.2 7.9 %collective-permute-start = (bf16[64,1536]{1,0:T(8,128)(2,1)S(1)}, bf16[64,1536]{1,0:T(8,128)(2,1)S(1)}, u32[]{:S(2)}, u32[]{:S(2)}) collective-permute-start(bf16[64,1536]{1,0:T(8,128)(2,1)S(1)} %get-tuple-element.116), channel_id=1, source_target_pairs={{0,1},{1,2},{2,3},{3,4},{4,5},{5,6},{6,7},{7,8},{8,9},{9,10},{10,1... | collective-permute-start | bytes 589832 | tf_op jit(solution)/shard_map/ppermute | solution.py:24
  53.6 12.2 %collective-permute-start.1 = (bf16[64,1536]{1,0:T(8,128)(2,1)S(1)}, bf16[64,1536]{1,0:T(8,128)(2,1)S(1)}, u32[]{:S(2)}, u32[]{:S(2)}) collective-permute-start(bf16[64,1536]{1,0:T(8,128)(2,1)S(1)} %get-tuple-element.117), channel_id=1, source_target_pairs={{1,0},{2,1},{3,2},{4,3},{5,4},{6,5},{7,6},{8,7},{9,8},{10,9},{11,1... | collective-permute-start | bytes 589832 | tf_op jit(solution)/shard_map/ppermute | solution.py:25
  68.1 7.0 %copy-start.21 = (bf16[12,64,128]{2,1,0:T(8,128)(2,1)}, bf16[12,64,128]{2,1,0:T(8,128)(2,1)S(1)}, u32[]{:S(2)}) copy-start(bf16[12,64,128]{2,1,0:T(8,128)(2,1)S(1)} %convolution_convert_fusion.5) | copy-start | bytes 589828
  145.8 81.3 %reduce-scatter.23.cloned.1.call-start = ((), (), s32[]{:S(2)}) async-start(), calls=%async_computation.15 | async-start | bytes 1990656 | tf_op jit(solution)/shard_map/reduce_scatter | solution.py:236
  147.8 131.2 %reduce-scatter.21.cloned.1.call-start = ((), (), s32[]{:S(2)}) async-start(), calls=%async_computation.14 | async-start | bytes 3981312 | tf_op jit(solution)/shard_map/reduce_scatter | solution.py:233
  150.9 180.1 %reduce-scatter.17.cloned.1.call-start = ((), (), s32[]{:S(2)}) async-start(), calls=%async_computation.12 | async-start | bytes 3981312 | tf_op jit(solution)/shard_map/reduce_scatter | solution.py:227
  159.5 12.9 %collective-permute-start.4 = (bf16[64,1536]{0,1:T(8,128)(2,1)S(1)}, bf16[64,1536]{0,1:T(8,128)(2,1)S(1)}, u32[]{:S(2)}, u32[]{:S(2)}) collective-permute-start(bf16[64,1536]{0,1:T(8,128)(2,1)S(1)} %get-tuple-element.106), channel_id=1, source_target_pairs={{0,1},{1,2},{2,3},{3,4},{4,5},{5,6},{6,7},{7,8},{8,9},{9,10},{10,1... | collective-permute-start | bytes 589832 | tf_op jit(solution)/shard_map/ppermute | solution.py:24
  163.0 20.5 %collective-permute-start.5 = (bf16[64,1536]{0,1:T(8,128)(2,1)S(1)}, bf16[64,1536]{0,1:T(8,128)(2,1)S(1)}, u32[]{:S(2)}, u32[]{:S(2)}) collective-permute-start(bf16[64,1536]{0,1:T(8,128)(2,1)S(1)} %get-tuple-element.107), channel_id=1, source_target_pairs={{1,0},{2,1},{3,2},{4,3},{5,4},{6,5},{7,6},{8,7},{9,8},{10,9},{11,1... | collective-permute-start | bytes 589832 | tf_op jit(solution)/shard_map/ppermute | solution.py:25
  202.9 78.3 %copy-start.10 = (bf16[128,1152]{1,0:T(8,128)(2,1)S(1)}, bf16[128,1152]{1,0:T(8,128)(2,1)}, u32[]{:S(2)}) copy-start(bf16[128,1152]{1,0:T(8,128)(2,1)} %get-tuple-element.103) | copy-start | bytes 884740
  202.9 78.3 %copy-start.14 = (bf16[1152,768]{1,0:T(8,128)(2,1)S(1)}, bf16[1152,768]{1,0:T(8,128)(2,1)}, u32[]{:S(2)}) copy-start(bf16[1152,768]{1,0:T(8,128)(2,1)} %all-gather.14.cloned.1.call-done) | copy-start | bytes 5308420
  202.9 149.8 %reduce-scatter.27.cloned.1.call-start = ((), (), s32[]{:S(2)}) async-start(), calls=%async_computation.17 | async-start | bytes 245760
  204.9 168.9 %reduce-scatter.31.cloned.1.call-start = ((), (), s32[]{:S(2)}) async-start(), calls=%async_computation.19 | async-start | bytes 491520
  229.0 167.8 %reduce-scatter.29.cloned.1.call-start = ((), (), s32[]{:S(2)}) async-start(), calls=%async_computation.18 | async-start | bytes 737280
  281.2 141.4 %reduce-scatter.25.cloned.1.call-start = ((), (), s32[]{:S(2)}) async-start(), calls=%async_computation.16 | async-start | bytes 737280
  285.7 59.7 %copy-start.4 = (f32[128,768]{1,0:T(8,128)S(1)}, f32[128,768]{1,0:T(8,128)}, u32[]{:S(2)}) copy-start(f32[128,768]{1,0:T(8,128)} %copy-done.3) | copy-start | bytes 1179652
  285.8 59.7 %copy-start.12 = (bf16[128,768]{1,0:T(8,128)(2,1)S(1)}, bf16[128,768]{1,0:T(8,128)(2,1)}, u32[]{:S(2)}) copy-start(bf16[128,768]{1,0:T(8,128)(2,1)} %param.21) | copy-start | bytes 589828
  285.8 59.7 %copy-start.39 = (f32[128]{0:T(128)S(1)}, f32[128]{0:T(128)}, u32[]{:S(2)}) copy-start(f32[128]{0:T(128)} %copy-done.38) | copy-start | bytes 1540
  (33 other events, 63.3 us)
Sparse Core Ops, SparseCore 0:
  9.9 36.7 all-gather.7
  48.6 24.0 all-gather.9
  74.5 33.9 all-gather.11
  110.3 26.5 all-gather.13
  145.9 36.9 reduce-scatter.18
  186.5 40.5 reduce-scatter.22
  231.0 48.0 reduce-scatter.20
  283.0 48.0 reduce-scatter.16
  333.4 19.2 reduce-scatter.26
  354.8 18.8 reduce-scatter.30
  376.7 20.0 reduce-scatter.28
  399.6 22.8 reduce-scatter.24
where the time goes:
time: 449 us; the launch traced here: 448 us
  waiting for transfers between devices  229 us (51%)
  blocking collectives  106 us (24%)
  local copies, waits for them, and re-layouts  35.1 us (8%)
  matrix products  33.4 us (7%)
  between operations  16.5 us (4%)
  starting transfers between devices  16.3 us (4%)
  other arithmetic  12 us (3%)
    reduce_scatter x1, waiting for transfers between devices, on_device(): lax.psum_scatter(grad_glu.astype(jnp.bfloat16), 'shard', scatter_dimensio...  49.3 us
    all_gather x1, waiting for transfers between devices, on_device(): lax.all_gather(glu_weight, 'shard', axis=0, tiled=True)  33.4 us
    reduce_scatter x1, waiting for transfers between devices, on_device(): lax.psum_scatter(grad_qkv.astype(jnp.bfloat16), 'shard', scatter_dimensio...  32.2 us
    unnamed x2, blocking collectives  29.4 us
    all_gather x1, waiting for transfers between devices, on_device(): lax.all_gather(down_weight, 'shard', axis=0, tiled=True)  25.6 us
    unnamed x16, waiting for transfers between devices  23.8 us
    reduce_scatter x1, waiting for transfers between devices, on_device(): lax.psum_scatter(grad_down.astype(jnp.bfloat16), 'shard', scatter_dimensi...  22.2 us
    ppermute x3, waiting for transfers between devices, with_halo(): after = lax.ppermute(leading, axis, down)  18.7 us
  transfers between devices with their start and end apart: 18, of which 15 were waited for; matrix products, arithmetic and copies ran while one was open for 15% of the time, Pallas kernels for 0%

commit v1 on v0

v1 whole, which is shorter than its diff:
```python
import math

import jax
import jax.numpy as jnp
from jax import lax
from jax.experimental import pallas as pl
from jax.experimental.pallas import tpu as pltpu
from jax.sharding import PartitionSpec as P

HEAD = 64
RADIUS = 64
BLOCK = 128
HALF = 384
EPSILON = 1e-05
THETA_BASE = 10000.0
NEGATIVE = -1e30
VMEM_BYTES = 56 * 1024 * 1024
BF = jnp.bfloat16
F32 = jnp.float32


def xor_send(array, axis, bit):
    count = lax.axis_size(axis)
    return lax.ppermute(array, axis, [(i, i ^ bit) for i in range(count)])


def bits_of(count):
    return [1 << i for i in range(count.bit_length() - 1)]


def gather_pieces(first, second, chip_bits):
    streams = ([(0, 0, first)], [(0, 1, second)])
    for stage in range(len(chip_bits)):
        grown = []
        for which, bit in ((0, chip_bits[stage]), (1, chip_bits[-1 - stage])):
            grown.append(
                [(j ^ bit, s, xor_send(a, "shard", bit)) for j, s, a in streams[which]]
            )
        for held, new in zip(streams, grown):
            held.extend(new)
    pieces = streams[0] + streams[1]
    return pieces + [(j ^ 1, s, xor_send(a, "shard", 1)) for j, s, a in pieces]


def add_low(left, right):
    return (left.astype(F32) + right.astype(F32)).astype(BF)


def scatter_sum(send, keep, order):
    for step, bit in enumerate(order):
        total = add_low(keep, xor_send(send, "shard", bit))
        if step + 1 < len(order):
            middle = total.shape[0] // 2
            keep, send = total[:middle], total[middle:]
    return total[0]


def replica_sum(first, second):
    count = lax.axis_size("replica")
    at = lax.axis_index("replica")
    if count == 1:
        return first, second
    bits = bits_of(count)
    odd = (at & 1) != 0
    held = add_low(
        jnp.where(odd, second, first), xor_send(jnp.where(odd, first, second), "replica", 1)
    )
    for bit in bits[1:]:
        high = (at & bit) != 0
        middle = held.shape[0] // 2
        top, bottom = held[:middle], held[middle:]
        held = add_low(
            jnp.where(high, bottom, top), xor_send(jnp.where(high, top, bottom), "replica", bit)
        )
    for bit in reversed(bits[1:]):
        high = (at & bit) != 0
        other = xor_send(held, "replica", bit)
        held = jnp.concatenate([jnp.where(high, other, held), jnp.where(high, held, other)], axis=0)
    other = xor_send(held, "replica", 1)
    return jnp.where(odd, other, held), jnp.where(odd, held, other)


def dot(left, right):
    return jnp.dot(left, right, preferred_element_type=F32)


def dot_cols(left, right):
    return lax.dot_general(left, right, (((1,), (1,)), ((), ())), preferred_element_type=F32)


def dot_rows(left, right):
    return lax.dot_general(left, right, (((0,), (0,)), ((), ())), preferred_element_type=F32)


def standardize(vector):
    average = jnp.mean(vector, axis=-1, keepdims=True)
    centred = vector - average
    spread = jnp.mean(centred * centred, axis=-1, keepdims=True)
    inverse = lax.rsqrt(spread + EPSILON)
    return centred * inverse, inverse


def norm_back(grad, gain, hat, inverse):
    dhat = grad * gain
    mean = jnp.mean(dhat, axis=-1, keepdims=True)
    along = jnp.mean(dhat * hat, axis=-1, keepdims=True)
    return (dhat - mean - hat * along) * inverse


def turned(vector):
    width = vector.shape[-1]
    lane = lax.broadcasted_iota(jnp.int32, vector.shape, 1)
    return jnp.where(
        (lane & 63) < 32, pltpu.roll(vector, width - 32, 1), pltpu.roll(vector, 32, 1)
    )


def place(me, pieces, refs, layout, sems):
    copies = []
    for (j, stream), ref in zip(pieces, refs):
        owner = me ^ j
        for row, rows, col, cols, dst, dst_col in layout[stream]:
            start = owner * rows
            if rows % 16 == 0:
                start = pl.multiple_of(start, 16)
            copy = pltpu.make_async_copy(
                ref.at[pl.ds(row, rows), pl.ds(col, cols)],
                dst.at[pl.ds(start, rows), pl.ds(dst_col, cols)],
                sems.at[len(copies)],
            )
            copy.start()
            copies.append(copy)
    return copies


def call(kernel, out_shape, inputs, in_any, scratch, flops, traffic):
    any_spec = pl.BlockSpec(memory_space=pl.ANY)
    vmem = pl.BlockSpec(memory_space=pltpu.VMEM)
    smem = pl.BlockSpec(memory_space=pltpu.SMEM)
    specs = [smem] + [vmem] * (len(inputs) - 1) + [any_spec] * len(in_any)
    return pl.pallas_call(
        kernel,
        out_shape=out_shape,
        in_specs=specs,
        out_specs=jax.tree.map(lambda _: vmem, out_shape),
        scratch_shapes=scratch,
        compiler_params=pltpu.CompilerParams(vmem_limit_bytes=VMEM_BYTES),
        cost_estimate=pl.CostEstimate(flops=flops, bytes_accessed=traffic, transcendentals=0),
    )(*inputs, *in_any)


def shaped(shape, dtype):
    return jax.ShapeDtypeStruct(shape, dtype)


def qkv_layout(rows, weight, gains):
    wide = 3 * HALF
    return (
        ((0, rows, 0, wide, weight, 0), (0, rows, wide, 128, gains, 0)),
        ((0, rows, 0, wide, weight, wide),),
    )


def project_kernel(pieces, rows, width):
    heads = width // HEAD

    def body(me_ref, before, own, after, cosine, sine, bias, *rest):
        refs, rest = rest[: len(pieces)], rest[len(pieces) :]
        q_out, k_out, v_out, p_out, ctx_out, normed_out, gains_out = rest[:7]
        weight, gain_cols, normed, sems = rest[7:]
        copies = place(me_ref[0], pieces, refs, qkv_layout(rows, weight, gain_cols), sems)
        hats = [standardize(ref[...].astype(F32))[0] for ref in (before, own, after)]
        for copy in copies:
            copy.wait()
        pick = jnp.where(
            lax.broadcasted_iota(jnp.int32, (8, 128), 0)
            == lax.broadcasted_iota(jnp.int32, (8, 128), 1),
            1.0,
            0.0,
        ).astype(BF)
        gains = dot_cols(pick, gain_cols[...])
        gains_out[...] = gains
        for i, hat in enumerate(hats):
            normed[i * BLOCK : (i + 1) * BLOCK, :] = (hat * gains[0:1]).astype(BF)
        normed_out[...] = normed[BLOCK : 2 * BLOCK, :]
        cos2 = jnp.concatenate([cosine[...]] * 2, axis=1)
        sin2 = jnp.concatenate([sine[...]] * 2, axis=1)
        mid = slice(RADIUS, RADIUS + 2 * BLOCK)
        for c in range(0, width, 256):
            joined = dot(normed[mid, :], weight[:, c : c + 256])
            joined = joined * cos2[mid] + turned(joined) * sin2[mid]
            q_out[:, c : c + 256] = joined.astype(BF)
            joined = dot(normed[...], weight[:, width + c : width + c + 256])
            joined = joined * cos2 + turned(joined) * sin2
            k_out[:, c : c + 256] = joined.astype(BF)
            joined = dot(normed[...], weight[:, 2 * width + c : 2 * width + c + 256])
            v_out[:, c : c + 256] = joined.astype(BF)
        lane = lax.broadcasted_iota(jnp.int32, (BLOCK, 128), 1)
        scale = 1.0 / math.sqrt(HEAD)
        for pair in range(heads // 2):
            cols = slice(pair * 128, pair * 128 + 128)
            for b in range(2):
                rows_q = slice(b * BLOCK, (b + 1) * BLOCK)
                rows_k = slice(b * BLOCK, (b + 2) * BLOCK)
                queries, keys, values = q_out[rows_q, cols], k_out[rows_k, cols], v_out[rows_k, cols]
                parts = []
                for h in range(2):
                    mine = (lane < HEAD) if h == 0 else (lane >= HEAD)
                    masked = jnp.where(mine, queries.astype(F32) * scale, 0.0).astype(BF)
                    scores = dot_cols(masked, keys) + bias[rows_q, :]
                    exponent = jnp.exp(scores - jnp.max(scores, axis=1, keepdims=True))
                    total = jnp.sum(exponent, axis=1, keepdims=True)
                    shares = (exponent * (1.0 / total)).astype(BF)
                    p_out[(pair * 2 + h) * 2 + b] = shares
                    parts.append(dot(shares, values))
                ctx_out[rows_q, cols] = jnp.where(lane < HEAD, parts[0], parts[1]).astype(BF)

    return body


def mlp_layout(rows, down_rows, attn, glu, down):
    width, hidden = 2 * HALF, 3 * HALF
    streams = []
    for s in range(2):
        parts = [(0, rows, 0, HALF, attn, s * HALF)]
        for c in range(3):
            parts.append(((1 + c) * rows, rows, 0, HALF, glu, s * hidden + c * HALF))
        if down is not None:
            parts.append((4 * rows, down_rows, 0, HALF, down, s * HALF))
        streams.append(tuple(parts))
    return tuple(streams)


def mlp_kernel(pieces, rows, down_rows, width, hidden, down_given):
    def body(me_ref, before, own, after, ctx, dy_before, dy_own, dy_after, gains, *rest):
        down_ref = None
        if down_given:
            down_ref, rest = rest[0], rest[1:]
        refs, rest = rest[: len(pieces)], rest[len(pieces) :]
        mixed_out, shared_out, ghid_out, gctx_out, fgain_out = rest[:5]
        if down_given:
            attn, glu, x_mid, dy, ggu, sems = rest[5:]
            layout = mlp_layout(rows, down_rows, attn, glu, None)
            down = down_ref
        else:
            attn, glu, x_mid, dy, ggu, down, sems = rest[5:]
            layout = mlp_layout(rows, down_rows, attn, glu, down)
        copies = place(me_ref[0], pieces, refs, layout, sems)
        mine = slice(RADIUS, RADIUS + BLOCK)
        x_mid[0:RADIUS, :] = before[BLOCK - RADIUS :, :].astype(F32)
        x_mid[mine, :] = own[...].astype(F32)
        x_mid[RADIUS + BLOCK :, :] = after[0:RADIUS, :].astype(F32)
        dy[0:RADIUS, :] = dy_before[...]
        dy[mine, :] = dy_own[...]
        dy[RADIUS + BLOCK :, :] = dy_after[...]
        for copy in copies:
            copy.wait()
        x_mid[...] = x_mid[...] + dot(ctx[...], attn[...])
        hat, inverse = standardize(x_mid[...])
        gain = gains[1:2, :]
        normed = (hat * gain).astype(BF)
        low = 0
        shared_out[:, 0:width] = normed[mine]
        mixed = x_mid[mine, :]
        act_at, ggu_at = width, width + hidden
        for c in range(0, hidden, HALF):
            cols = slice(c, c + HALF)
            gate = dot(normed, glu[:, c : c + HALF])
            up = dot(normed, glu[:, hidden + c : hidden + c + HALF])
            grad_act = dot_cols(dy[...], down[c : c + HALF, :])
            share = 0.5 * (1.0 + lax.erf(gate * (1.0 / math.sqrt(2.0))))
            density = jnp.exp(-0.5 * gate * gate) * (1.0 / math.sqrt(2.0 * math.pi))
            gelu = gate * share
            act = (gelu[mine] * up[mine]).astype(BF)
            shared_out[:, act_at + c : act_at + c + HALF] = act
            mixed = mixed + dot(act, down[c : c + HALF, :])
            ggu[:, cols] = (grad_act * up * (share + gate * density)).astype(BF)
            ggu[:, hidden + c : hidden + c + HALF] = (grad_act * gelu).astype(BF)
        mixed_out[...] = mixed.astype(BF)
        shared_out[:, ggu_at : ggu_at + 2 * hidden] = ggu[mine, :]
        grad = dot_cols(ggu[...], glu[...])
        fgain = jnp.sum(grad[mine] * hat[mine], axis=0, keepdims=True)
        fgain_out[...] = jnp.broadcast_to(fgain, fgain_out.shape)
        grad_hidden = dy[...].astype(F32) + norm_back(grad, gain, hat, inverse)
        ghid_out[...] = grad_hidden[mine]
        grad_low = grad_hidden.astype(BF)
        ctx_at = ggu_at + 2 * hidden
        shared_out[:, ctx_at : ctx_at + width] = ctx[mine, :]
        shared_out[:, ctx_at + width : ctx_at + 2 * width] = grad_low[mine]
        gctx_out[...] = dot_cols(grad_low, attn[...]).astype(BF)

    return body


def back_kernel(pieces, rows, width):
    heads = width // HEAD

    def body(me_ref, gctx, q, k, v, p, cosine, sine, own, ghid, gains, fgain, *rest):
        refs, rest = rest[: len(pieces)], rest[len(pieces) :]
        gj_out, gtok_out, weight, gain_cols, sems = rest
        copies = place(me_ref[0], pieces, refs, qkv_layout(rows, weight, gain_cols), sems)
        lane = lax.broadcasted_iota(jnp.int32, (BLOCK, 128), 1)
        scale = 1.0 / math.sqrt(HEAD)
        cos, sin = cosine[BLOCK : 2 * BLOCK, :], sine[BLOCK : 2 * BLOCK, :]
        for pair in range(heads // 2):
            cols = slice(pair * 128, pair * 128 + 128)
            grad_q = jnp.zeros((BLOCK, 128), F32)
            grad_k = jnp.zeros((BLOCK, 128), F32)
            grad_v = jnp.zeros((BLOCK, 128), F32)
            for h in range(2):
                mine = (lane < HEAD) if h == 0 else (lane >= HEAD)
                scores, shares, queries, grads, pieces_q = [], [], [], [], []
                for b in range(2):
                    rows_q = slice(b * BLOCK, (b + 1) * BLOCK)
                    rows_k = slice(b * BLOCK, (b + 2) * BLOCK)
                    keys, values = k[rows_k, cols], v[rows_k, cols]
                    lowered = jnp.where(mine, gctx[rows_q, cols].astype(F32), 0.0).astype(BF)
                    query = jnp.where(mine, q[rows_q, cols].astype(F32) * scale, 0.0).astype(BF)
                    share = p[(pair * 2 + h) * 2 + b]
                    wide = share.astype(F32)
                    grad_share = dot_cols(lowered, values)
                    row = jnp.sum(wide * grad_share, axis=1, keepdims=True)
                    grad_score = (wide * (grad_share - row)).astype(BF)
                    ours = slice(BLOCK, 2 * BLOCK) if b == 0 else slice(0, BLOCK)
                    scores.append(grad_score[:, ours])
                    shares.append(share[:, ours])
                    queries.append(query)
                    grads.append(lowered)
                    mid = slice(RADIUS, BLOCK) if b == 0 else slice(0, RADIUS)
                    pieces_q.append(dot(grad_score[mid], keys))
                part = jnp.concatenate(pieces_q, axis=0) * scale
                grad_q = grad_q + jnp.where(mine, part, 0.0)
                grad_k = grad_k + dot_rows(
                    jnp.concatenate(scores, axis=0), jnp.concatenate(queries, axis=0)
                )
                grad_v = grad_v + dot_rows(
                    jnp.concatenate(shares, axis=0), jnp.concatenate(grads, axis=0)
                )
            at = pair * 128
            gj_out[0:BLOCK, at : at + 128] = (grad_q * cos - turned(grad_q) * sin).astype(BF)
            at += width
            gj_out[0:BLOCK, at : at + 128] = (grad_k * cos - turned(grad_k) * sin).astype(BF)
            at += width
            gj_out[0:BLOCK, at : at + 128] = grad_v.astype(BF)
        for copy in copies:
            copy.wait()
        hat, inverse = standardize(own[...].astype(F32))
        grad = dot_cols(gj_out[0:BLOCK, :], weight[...])
        gain = gains[0:1, :]
        again = jnp.sum(grad * hat, axis=0, keepdims=True)
        gtok_out[...] = (ghid[...] + norm_back(grad, gain, hat, inverse)).astype(BF)
        tail = gj_out.shape[0] - BLOCK
        line = lax.broadcasted_iota(jnp.int32, (tail, width), 0)
        both = jnp.where(line == 0, again, jnp.where(line == 1, fgain[0:1, :], 0.0))
        gj_out[BLOCK:, 0:width] = both.astype(BF)
        gj_out[BLOCK:, width:] = jnp.zeros((tail, 2 * width), BF)

    return body


def slots_of(count, chip_bits):
    streams = []
    for order in (chip_bits, chip_bits[::-1]):
        kept = [0]
        for bit in order[1:][::-1]:
            kept = kept + [j | bit for j in kept]
        table = {j: (1, i) for i, j in enumerate(kept)}
        table.update({j | order[0]: (0, i) for i, j in enumerate(kept)})
        streams.append(table)
    return streams


def weight_grad(me, js, lhs_t, rhs, rows, cols, emit):
    left = jnp.concatenate(
        [
            lhs_t[pl.ds(pl.multiple_of((me ^ j) * rows, 16 if rows % 16 == 0 else 8), rows), :]
            for j in js
        ],
        axis=0,
    ).astype(BF)
    grad = dot(left, rhs[:, cols]).astype(BF)
    for i, j in enumerate(js):
        emit(j, grad[i * rows : (i + 1) * rows])


def mlp_grad_kernel(js, slots, rows, down_rows, width, hidden):
    def body(me_ref, own, other, dy_own, dy_other, *rest):
        outs, (normed_t, act_t, ctx_t, ggu, low, dy) = rest[:4], rest[4:]
        me = me_ref[0]
        act_at, ggu_at = width, width + hidden
        ctx_at = ggu_at + 2 * hidden
        for i, (ref, dref) in enumerate(((own, dy_own), (other, dy_other))):
            tok = slice(i * BLOCK, (i + 1) * BLOCK)
            normed_t[:, tok] = ref[:, 0:width].T.astype(normed_t.dtype)
            act_t[:, tok] = ref[:, act_at : act_at + hidden].T.astype(act_t.dtype)
            ctx_t[:, tok] = ref[:, ctx_at : ctx_at + width].T.astype(ctx_t.dtype)
            ggu[tok, :] = ref[:, ggu_at : ggu_at + 2 * hidden]
            low[tok, :] = ref[:, ctx_at + width : ctx_at + 2 * width]
            dy[tok, :] = dref[...]

        def emit_at(stream, row):
            def emit(j, grad):
                kept, i = slots[stream][j]
                outs[2 * stream + kept][i, row : row + grad.shape[0], :] = grad

            return emit

        for s in range(2):
            half = slice(s * HALF, (s + 1) * HALF)
            weight_grad(me, js, ctx_t, low, rows, half, emit_at(s, 0))
            for c in range(3):
                at = s * hidden + c * HALF
                weight_grad(
                    me, js, normed_t, ggu, rows, slice(at, at + HALF), emit_at(s, (1 + c) * rows)
                )
            weight_grad(me, js, act_t, dy, down_rows, half, emit_at(s, 4 * rows))

    return body


def qkv_grad_kernel(js, slots, rows, width):
    def body(me_ref, normed_own, normed_other, own, other, *rest):
        outs, (normed_t, gj) = rest[:4], rest[4:]
        me = me_ref[0]
        for i, (nref, ref) in enumerate(((normed_own, own), (normed_other, other))):
            tok = slice(i * BLOCK, (i + 1) * BLOCK)
            normed_t[:, tok] = nref[...].T.astype(normed_t.dtype)
            gj[tok, :] = ref[0:BLOCK, :]
        gains = own[BLOCK : BLOCK + 16, 0:width].astype(F32) + other[
            BLOCK : BLOCK + 16, 0:width
        ].astype(F32)
        for s in range(2):

            def emit_at(row):
                def emit(j, grad):
                    kept, i = slots[s][j]
                    outs[2 * s + kept][i, row : row + rows, :] = grad

                return emit

            for c in range(3):
                at = s * 3 * HALF + c * HALF
                weight_grad(me, js, normed_t, gj, rows, slice(at, at + HALF), emit_at(c * rows))
            for j in js:
                kept, i = slots[s][j]
                moved = pltpu.roll(gains, lax.rem(width - (me ^ j) * rows, width), 1)
                outs[2 * s + kept][i, 3 * rows : 3 * rows + 16, :] = moved[:, 0:HALF].astype(BF)

    return body


def on_device(
    tokens,
    positions,
    qkv_weight,
    attn_weight,
    glu_weight,
    down_weight,
    attn_gain,
    ffn_gain,
    cotangent,
):
    block, width = tokens.shape
    rows, down_rows = qkv_weight.shape[0], down_weight.shape[0]
    hidden = glu_weight.shape[1] // 2
    heads = width // HEAD
    count = lax.axis_size("shard")
    everyone = count * lax.axis_size("replica")
    me = lax.axis_index("shard").astype(jnp.int32)
    me_arr = me[None]
    chip_bits = bits_of(count)[1:]

    gain_cols = jnp.pad(jnp.stack([attn_gain, ffn_gain], axis=1), ((0, 0), (0, 126)))
    first = jnp.concatenate([qkv_weight[:, : 3 * HALF], gain_cols], axis=1)
    qkv_parts = gather_pieces(first, qkv_weight[:, 3 * HALF :], chip_bits)

    up = [(i, i + 1) for i in range(everyone - 1)]
    down = [(i + 1, i) for i in range(everyone - 1)]
    both = ("shard", "replica")
    places = jnp.stack([positions >> 8, positions & 255]).astype(BF)
    places = jnp.pad(places, ((0, 14), (0, width - block)))
    before = lax.ppermute(
        jnp.concatenate([tokens, cotangent[block - RADIUS :], places], axis=0), both, up
    )
    after = lax.ppermute(jnp.concatenate([tokens, cotangent[:RADIUS], places], axis=0), both, down)
    dy_other = xor_send(cotangent, "shard", 1)

    def places_of(packed):
        near = packed[block + RADIUS : block + RADIUS + 2, :block].astype(F32)
        return near[0] * 256.0 + near[1]

    where = jnp.concatenate([places_of(before), positions.astype(F32), places_of(after)])
    middle = HEAD // 2
    inverse = THETA_BASE ** (-(jnp.arange(middle, dtype=F32) * 2.0 / HEAD))
    phases = where[:, None] * inverse[None, :]
    cosine, sine = jnp.cos(phases), jnp.sin(phases)
    cosine = jnp.concatenate([cosine] * 4, axis=1)
    sine = jnp.concatenate([-sine, sine, -sine, sine], axis=1)
    offset = (
        jnp.arange(2 * BLOCK, dtype=jnp.int32)[None, :]
        - RADIUS
        - jnp.arange(BLOCK, dtype=jnp.int32)[:, None]
    )
    bias = []
    for b in range(2):
        later_key = where[None, b * BLOCK : (b + 2) * BLOCK] >= offset.astype(F32)
        start = RADIUS + b * BLOCK
        later_query = where[start : start + BLOCK, None] >= -offset.astype(F32)
        allowed = (jnp.abs(offset) <= RADIUS) & jnp.where(offset >= 0, later_key, later_query)
        bias.append(jnp.where(allowed, 0.0, NEGATIVE))
    bias = jnp.concatenate(bias, axis=0).astype(F32)

    packs = []
    for s in range(2):
        half = slice(s * HALF, (s + 1) * HALF)
        parts = [attn_weight[:, half]]
        parts += [
            glu_weight[:, s * hidden + c * HALF : s * hidden + (c + 1) * HALF] for c in range(3)
        ]
        packs.append(jnp.concatenate(parts + [down_weight[:, half]], axis=0))
    mlp_parts = gather_pieces(packs[0], packs[1], chip_bits)

    qkv_names = [(j, s) for j, s, _ in qkv_parts]
    qkv_arrays = [a for _, _, a in qkv_parts]
    mlp_names = [(j, s) for j, s, _ in mlp_parts]
    mlp_arrays = [a for _, _, a in mlp_parts]
    weight_bytes = width * 3 * width * 2

    tok_before, tok_after = before[:block], after[:block]
    q, k, v, p, ctx, normed, gains = call(
        project_kernel(qkv_names, rows, width),
        (
            shaped((2 * BLOCK, width), BF),
            shaped((3 * BLOCK, width), BF),
            shaped((3 * BLOCK, width), BF),
            shaped((2 * heads, BLOCK, 2 * BLOCK), BF),
            shaped((2 * BLOCK, width), BF),
            shaped((BLOCK, width), BF),
            shaped((8, width), F32),
        ),
        (me_arr, tok_before, tokens, tok_after, cosine, sine, bias),
        qkv_arrays,
        [
            pltpu.VMEM((width, 3 * width), BF),
            pltpu.VMEM((width, 128), BF),
            pltpu.VMEM((3 * BLOCK, width), BF),
            pltpu.SemaphoreType.DMA((3 * len(qkv_arrays),)),
        ],
        8_000_000_000,
        2 * weight_bytes,
    )
    normed_other = xor_send(normed, "shard", 1)

    down_full = ()
    extra = [pltpu.VMEM((count * down_rows, width), BF)]
    if down_rows % 16:
        halves = []
        order = me ^ jnp.arange(count, dtype=jnp.int32)
        for s in range(2):
            held = {j: a[4 * rows :] for j, t, a in mlp_parts if t == s}
            halves.append(jnp.stack([held[j] for j in range(count)])[order])
        down_full = (jnp.concatenate(halves, axis=2).reshape(count * down_rows, width),)
        extra = []
    shared_width = 3 * width + 3 * hidden
    mixed, shared, ghid, gctx, fgain = call(
        mlp_kernel(mlp_names, rows, down_rows, width, hidden, bool(down_full)),
        (
            shaped((BLOCK, width), BF),
            shaped((BLOCK, shared_width), BF),
            shaped((BLOCK, width), F32),
            shaped((2 * BLOCK, width), BF),
            shaped((8, width), F32),
        ),
        (
            me_arr,
            tok_before,
            tokens,
            tok_after,
            ctx,
            before[block : block + RADIUS],
            cotangent,
            after[block : block + RADIUS],
            gains,
        )
        + down_full,
        mlp_arrays,
        [
            pltpu.VMEM((width, width), BF),
            pltpu.VMEM((width, 2 * hidden), BF),
            pltpu.VMEM((2 * BLOCK, width), F32),
            pltpu.VMEM((2 * BLOCK, width), BF),
            pltpu.VMEM((2 * BLOCK, 2 * hidden), BF),
        ]
        + extra
        + [pltpu.SemaphoreType.DMA((5 * len(mlp_arrays),))],
        8_000_000_000,
        3 * weight_bytes,
    )
    shared_other = xor_send(shared, "shard", 1)

    gj, grad_tokens = call(
        back_kernel(qkv_names, rows, width),
        (shaped((BLOCK + 16, 3 * width), BF), shaped((BLOCK, width), BF)),
        (me_arr, gctx, q, k, v, p, cosine, sine, tokens, ghid, gains, fgain),
        qkv_arrays,
        [
            pltpu.VMEM((width, 3 * width), BF),
            pltpu.VMEM((width, 128), BF),
            pltpu.SemaphoreType.DMA((3 * len(qkv_arrays),)),
        ],
        8_000_000_000,
        2 * weight_bytes,
    )
    gj_other = xor_send(gj, "shard", 1)

    js = [2 * i for i in range(count // 2)]
    slots = slots_of(count, chip_bits)
    portion = count // 4

    def stack(height):
        return (shaped((portion, height, HALF), BF),) * 4

    act_type = BF if down_rows % 16 == 0 else F32
    height = 4 * rows + down_rows
    sums = call(
        mlp_grad_kernel(js, slots, rows, down_rows, width, hidden),
        stack(height),
        (me_arr, shared, shared_other, cotangent, dy_other),
        [],
        [
            pltpu.VMEM((width, 2 * BLOCK), BF),
            pltpu.VMEM((hidden, 2 * BLOCK), act_type),
            pltpu.VMEM((width, 2 * BLOCK), BF),
            pltpu.VMEM((2 * BLOCK, 2 * hidden), BF),
            pltpu.VMEM((2 * BLOCK, width), BF),
            pltpu.VMEM((2 * BLOCK, width), BF),
        ],
        3_000_000_000,
        2 * weight_bytes,
    )
    mlp_sums = [
        scatter_sum(sums[0], sums[1], chip_bits),
        scatter_sum(sums[2], sums[3], chip_bits[::-1]),
    ]
    mlp_sums = replica_sum(*mlp_sums)

    sums = call(
        qkv_grad_kernel(js, slots, rows, width),
        stack(3 * rows + 16),
        (me_arr, normed, normed_other, gj, gj_other),
        [],
        [pltpu.VMEM((width, 2 * BLOCK), BF), pltpu.VMEM((2 * BLOCK, 3 * width), BF)],
        2_000_000_000,
        weight_bytes,
    )
    qkv_sums = [
        scatter_sum(sums[0], sums[1], chip_bits),
        scatter_sum(sums[2], sums[3], chip_bits[::-1]),
    ]
    qkv_sums = replica_sum(*qkv_sums)

    def columns(sums, first_row):
        return [
            part[first_row + c * rows : first_row + (c + 1) * rows] for part in sums for c in range(3)
        ]

    grad_attn = jnp.concatenate([part[:rows] for part in mlp_sums], axis=1).astype(F32)
    grad_glu = jnp.concatenate(columns(mlp_sums, rows), axis=1).astype(F32)
    grad_down = jnp.concatenate([part[4 * rows :] for part in mlp_sums], axis=1).astype(F32)
    grad_qkv = jnp.concatenate(columns(qkv_sums, 0), axis=1).astype(F32)
    grad_gains = qkv_sums[0][3 * rows :, :rows].astype(F32)
    return (
        mixed,
        grad_tokens,
        grad_qkv,
        grad_attn,
        grad_glu,
        grad_down,
        grad_gains[0],
        grad_gains[1],
    )


def solution(mesh):
    in_specs = (
        P(("shard", "replica"), None),
        P(("shard", "replica")),
        P("shard", None),
        P("shard", None),
        P("shard", None),
        P("shard", None),
        P("shard"),
        P("shard"),
        P(("shard", "replica"), None),
    )
    out_specs = (
        P(("shard", "replica"), None),
        P(("shard", "replica"), None),
        P("shard", None),
        P("shard", None),
        P("shard", None),
        P("shard", None),
        P("shard"),
        P("shard"),
    )
    return jax.shard_map(
        on_device, mesh=mesh, in_specs=in_specs, out_specs=out_specs, check_vma=False
    )
```

time: 449 us -> 223 us (0.50)
  waiting for transfers between devices: 229 us -> 103 us
  blocking collectives: 106 us -> 0 us
  starting transfers between devices: 16.3 us -> 57.7 us
  Pallas kernels: 0 us -> 39.9 us
  matrix products: 33.4 us -> 0 us
  local copies, waits for them, and re-layouts: 35.1 us -> 9.62 us
  between operations: 16.5 us -> 1.41 us
    reduce_scatter x4 -> x0, waiting for transfers between devices: 104 us -> none  [the longest x1 49.3 us: on_device(): lax.psum_scatter(grad_glu.astype(jnp.bfloat16), 'shard', scatter_dimensio...]
    ppermute x6 -> x50, waiting for transfers between devices: 28.5 us -> 103 us  [the longest x48 101 us: xor_send(): return lax.ppermute(array, axis, [(i, i ^ bit) for i in range(count)])]
    all_gather x4 -> x0, waiting for transfers between devices: 72.6 us -> none  [the longest x1 33.4 us: on_device(): lax.all_gather(glu_weight, 'shard', axis=0, tiled=True)]
    all_gather x4 -> x0, blocking collectives: 64.4 us -> none  [the longest x1 18.6 us: on_device(): lax.all_gather(pieces[2].astype(jnp.bfloat16), 'replica', axis=1, tiled=T...]
    ppermute x6 -> x50, starting transfers between devices: 15.6 us -> 57.7 us  [the longest x48 51.9 us: xor_send(): return lax.ppermute(array, axis, [(i, i ^ bit) for i in range(count)])]
    pallas_call x0 -> x5, Pallas kernels: none -> 39.9 us  [call(): pl.pallas_call(kernel, out_shape=out_shape, in_specs=specs, out_specs=jax...]
    dot_general x18 -> x0, matrix products: 33.4 us -> none  [the longest x4 10.9 us: contract_cols(): lax.dot_general(left, right, (((1,), (1,)), ((), ())), preferred_element_...]
    unnamed x2 -> x0, blocking collectives: 29.4 us -> none
  transfers between devices with their start and end apart: 18 -> 50, of which waited for: 15 -> 23; matrix products, arithmetic and copies ran while one was open for 15% -> 6% of each run, Pallas kernels for 0% -> 6%
where the time goes in v1:
time: 223 us
  waiting for transfers between devices  103 us (46%)
  starting transfers between devices  57.7 us (26%)
  Pallas kernels  39.9 us (18%)
  other arithmetic  11.1 us (5%)
  local copies, waits for them, and re-layouts  9.62 us (4%)
    ppermute x48, waiting for transfers between devices, xor_send(): return lax.ppermute(array, axis, [(i, i ^ bit) for i in range(count)])  101 us
    ppermute x48, starting transfers between devices, xor_send(): return lax.ppermute(array, axis, [(i, i ^ bit) for i in range(count)])  51.9 us
    pallas_call x5, Pallas kernels, call(): pl.pallas_call(kernel, out_shape=out_shape, in_specs=specs, out_specs=jax...  39.9 us
    ppermute x1, starting transfers between devices, on_device(): lax.ppermute(jnp.concatenate([tokens, cotangent[block - RADIUS:], places]...  4.57 us
  transfers between devices with their start and end apart: 50, of which 23 were waited for; matrix products, arithmetic and copies ran while one was open for 6% of the time, Pallas kernels for 6%

profile of v1, /device:TPU:0, one launch (start us, length us, event | category | flops | bytes accessed | tf_op | source)
XLA Modules:
  0.0 222.6 jit_solution(16835533913422142525)
XLA Ops:
  1.8 3.0 %collective-permute-start.5 = (bf16[96,1152]{1,0:T(8,128)(2,1)S(1)}, bf16[96,1152]{1,0:T(8,128)(2,1)}, u32[]{:S(2)}, u32[]{:S(2)}) collective-permute-start(bf16[96,1152]{1,0:T(8,128)(2,1)S(1)} %get-tuple-element.62.rest_4_), channel_id=1, source_target_pairs={{0,16},{4,20},{8,24},{12,28},{16,0},{20,4},{24,8},{28,12},{1,17},{... | collective-permute-start | bytes 663560 | tf_op jit(solution)/shard_map/ppermute | solution.py:24
  10.4 4.6 %collective-permute-start = (bf16[208,768]{1,0:T(8,128)(2,1)S(1)}, bf16[208,768]{1,0:T(8,128)(2,1)S(1)}, u32[]{:S(2)}, u32[]{:S(2)}) collective-permute-start(bf16[208,768]{1,0:T(8,128)(2,1)S(1)} %get-tuple-element.75), channel_id=1, source_target_pairs={{0,1},{1,2},{2,3},{3,4},{4,5},{5,6},{6,7},{7,8},{8,9},{9,10},{10,1... | collective-permute-start | bytes 958472 | tf_op jit(solution)/shard_map/ppermute | solution.py:482
  15.2 2.0 collective-permute-start.2
  19.7 3.1 %collective-permute-start.16 = (bf16[528,384]{1,0:T(8,128)(2,1)S(1)}, bf16[528,384]{1,0:T(8,128)(2,1)S(1)}, u32[]{:S(2)}, u32[]{:S(2)}) collective-permute-start(bf16[528,384]{1,0:T(8,128)(2,1)S(1)} %get-tuple-element.73.rest_0_), channel_id=1, source_target_pairs={{0,8},{4,12},{8,0},{12,4},{16,24},{20,28},{24,16},{28,20},{1,9},{5... | collective-permute-start | bytes 1216520 | tf_op jit(solution)/shard_map/ppermute | solution.py:24
  22.8 5.6 %collective-permute-start.12 = (bf16[96,1152]{1,0:T(8,128)(2,1)S(1)}, bf16[96,1152]{1,0:T(8,128)(2,1)S(1)}, u32[]{:S(2)}, u32[]{:S(2)}) collective-permute-start(bf16[96,1152]{1,0:T(8,128)(2,1)S(1)} %get-tuple-element.62.rest_4_), channel_id=1, source_target_pairs={{0,4},{4,0},{8,12},{12,8},{16,20},{20,16},{24,28},{28,24},{1,5},{5... | collective-permute-start | bytes 663560 | tf_op jit(solution)/shard_map/ppermute | solution.py:24
  29.5 2.1 collective-permute-start.17
  33.0 2.6 %collective-permute-done.16.rest_1_ = bf16[528,384]{1,0:T(8,128)(2,1)S(1)} collective-permute-done((bf16[528,384]{1,0:T(8,128)(2,1)S(1)}, bf16[528,384]{1,0:T(8,128)(2,1)S(1)}, u32[]{:S(2)}, u32[]{:S(2)}) %collective-permute-start.16) | collective-permute-done | bytes 405536 | tf_op jit(solution)/shard_map/ppermute | solution.py:24
  37.0 13.0 %collective-permute-done.19.rest_5_ = bf16[528,384]{1,0:T(8,128)(2,1)S(1)} collective-permute-done((bf16[528,384]{1,0:T(8,128)(2,1)S(1)}, bf16[528,384]{1,0:T(8,128)(2,1)S(1)}, u32[]{:S(2)}, u32[]{:S(2)}) %collective-permute-start.19) | collective-permute-done | bytes 405536 | tf_op jit(solution)/shard_map/ppermute | solution.py:24
  53.1 4.0 %collective-permute-done.7.rest_7_ = bf16[96,1152]{1,0:T(8,128)(2,1)S(1)} collective-permute-done((bf16[96,1152]{1,0:T(8,128)(2,1)}, bf16[96,1152]{1,0:T(8,128)(2,1)S(1)}, u32[]{:S(2)}, u32[]{:S(2)}) %collective-permute-start.7) | collective-permute-done | bytes 221216 | tf_op jit(solution)/shard_map/ppermute | solution.py:24
  66.6 2.5 %collective-permute-done.18.rest_3_ = bf16[528,384]{1,0:T(8,128)(2,1)S(1)} collective-permute-done((bf16[528,384]{1,0:T(8,128)(2,1)S(1)}, bf16[528,384]{1,0:T(8,128)(2,1)S(1)}, u32[]{:S(2)}, u32[]{:S(2)}) %collective-permute-start.18) | collective-permute-done | bytes 405536 | tf_op jit(solution)/shard_map/ppermute | solution.py:24
  71.1 8.8 %shard_map.152 = (bf16[256,768]{1,0:T(8,128)(2,1)}, bf16[384,768]{1,0:T(8,128)(2,1)}, bf16[384,768]{1,0:T(8,128)(2,1)}, bf16[24,128,256]{2,1,0:T(8,128)(2,1)}, b...) custom-call(s32[1]{0:T(128)} %bitcast.me_ref, bf16[128,768]{1,0:T(8,128)(2,1)} %slice.234.before, ...), custom_call_target="tpu_custom_call" | custom-call | flops 8000000000 | bytes 7077888 | tf_op jit(solution)/shard_map/pallas_call | solution.py:141
  81.2 11.6 %shard_map.153 = (bf16[128,768]{1,0:T(8,128)(2,1)}, bf16[128,5760]{1,0:T(8,128)(2,1)}, f32[128,768]{1,0:T(8,128)}, bf16[256,768]{1,0:T(8,128)(2,1)}, f32[8,768]{1,0:T(8,128)}) custom-call(s32[1]{0:T(128)} %bitcast.me_ref, bf16[128,768]{1,0:T(8,128)(2,1)} %slice.234.before, bf16[128,768]{1,0:T(8,128)(2,1)} %own.5, bf16[128,768]{1,0:T(8,128)(2,1)} %slice.235.after, ...), custom_call_target="tpu_custom_call" | custom-call | flops 8000000000 | bytes 10616832 | tf_op jit(solution)/shard_map/pallas_call | solution.py:141
  92.8 11.2 %shard_map.154 = (bf16[144,2304]{1,0:T(8,128)(2,1)}, bf16[128,768]{1,0:T(8,128)(2,1)}) custom-call(s32[1]{0:T(128)} %bitcast.me_ref, bf16[256,768]{1,0:T(8,128)(2,1)} %get-tuple-element.33.gctx, bf16[256,768]{1,0:T(8,128)(2,1)} %get-tuple-element.34.q, bf16[384,768]{1,0:T(8,128)(2,1)} %get-tuple-element.35.k, bf16[384,768]{1,0:T(8,128)(2,1)} %get-tuple-element.36.v, ...), custom_call_target="tpu_custom_call" | custom-call | flops 8000000000 | bytes 7077888 | tf_op jit(solution)/shard_map/pallas_call | solution.py:141
  108.0 3.6 %shard_map.155 = (bf16[2,304,384]{2,1,0:T(8,128)(2,1)}, bf16[2,304,384]{2,1,0:T(8,128)(2,1)}, bf16[2,304,384]{2,1,0:T(8,128)(2,1)}, bf16[2,304,384]{2,1,0:T(8,128)(2,1)}) custom-call(s32[1]{0:T(128)} %bitcast.me_ref, bf16[128,768]{1,0:T(8,128)(2,1)} %get-tuple-element.41.normed_own, bf16[128,768]{1,0:T(8,128)(2,1)} %copy-done.40, ...), custom_call_target="tpu_custom_call" | custom-call | flops 2000000000 | bytes 3538944 | tf_op jit(solution)/shard_map/pallas_call | solution.py:141
  114.0 10.5 %collective-permute-done.34 = bf16[2,304,384]{2,1,0:T(8,128)(2,1)S(1)} collective-permute-done((bf16[2,304,384]{2,1,0:T(8,128)(2,1)}, bf16[2,304,384]{2,1,0:T(8,128)(2,1)S(1)}, u32[]{:S(2)}, u32[]{:S(2)}) %collective-permute-start.34) | collective-permute-done | bytes 466976 | tf_op jit(solution)/shard_map/ppermute | solution.py:24
  128.6 4.2 %collective-permute-done.35 = bf16[1,304,384]{2,1,0:T(8,128)(2,1)S(1)} collective-permute-done((bf16[1,304,384]{2,1,0:T(8,128)(2,1)S(1)}, bf16[1,304,384]{2,1,0:T(8,128)(2,1)S(1)}, u32[]{:S(2)}, u32[]{:S(2)}) %collective-permute-start.35) | collective-permute-done | bytes 233504 | tf_op jit(solution)/shard_map/ppermute | solution.py:24
  133.6 2.0 collective-permute-start.36
  135.6 4.1 %collective-permute-done.36 = bf16[304,384]{1,0:T(8,128)(2,1)S(1)} collective-permute-done((bf16[304,384]{1,0:T(8,128)(2,1)S(1)}, bf16[304,384]{1,0:T(8,128)(2,1)S(1)}, u32[]{:S(2)}, u32[]{:S(2)}) %collective-permute-start.36) | collective-permute-done | bytes 233504 | tf_op jit(solution)/shard_map/ppermute | solution.py:24
  141.8 3.9 %collective-permute-done.37 = bf16[152,384]{1,0:T(8,128)(2,1)S(1)} collective-permute-done((bf16[152,384]{1,0:T(8,128)(2,1)S(1)}, bf16[152,384]{1,0:T(8,128)(2,1)S(1)}, u32[]{:S(2)}, u32[]{:S(2)}) %collective-permute-start.37) | collective-permute-done | bytes 116768 | tf_op jit(solution)/shard_map/ppermute | solution.py:24
  145.7 2.2 collective-permute-start.38
  148.6 4.7 %shard_map.156 = (bf16[2,528,384]{2,1,0:T(8,128)(2,1)}, bf16[2,528,384]{2,1,0:T(8,128)(2,1)}, bf16[2,528,384]{2,1,0:T(8,128)(2,1)}, bf16[2,528,384]{2,1,0:T(8,128)(2,1)}) custom-call(s32[1]{0:T(128)} %bitcast.me_ref, bf16[128,5760]{1,0:T(8,128)(2,1)} %get-tuple-element.47.own, bf16[128,5760]{1,0:T(8,128)(2,1)} %collective-permute-done.40.other, ...), custom_call_target="tpu_custom_call" | custom-call | flops 3000000000 | bytes 7077888 | tf_op jit(solution)/shard_map/pallas_call | solution.py:141
  155.2 4.9 %collective-permute-start.39 = (bf16[304,384]{1,0:T(8,128)(2,1)S(1)}, bf16[304,384]{1,0:T(8,128)(2,1)S(1)}, u32[]{:S(2)}, u32[]{:S(2)}) collective-permute-start(bf16[304,384]{1,0:T(8,128)(2,1)S(1)} %pad_maximum_fusion.6), channel_id=1, source_target_pairs={{0,1},{1,0},{2,3},{3,2},{4,5},{5,4},{6,7},{7,6},{8,9},{9,8},{10,11... | collective-permute-start | bytes 700424 | tf_op jit(solution)/shard_map/ppermute | solution.py:24
  160.1 4.0 %collective-permute-done.39 = bf16[304,384]{1,0:T(8,128)(2,1)S(1)} collective-permute-done((bf16[304,384]{1,0:T(8,128)(2,1)S(1)}, bf16[304,384]{1,0:T(8,128)(2,1)S(1)}, u32[]{:S(2)}, u32[]{:S(2)}) %collective-permute-start.39) | collective-permute-done | bytes 233504 | tf_op jit(solution)/shard_map/ppermute | solution.py:24
  164.2 5.6 %collective-permute-done.44 = bf16[2,528,384]{2,1,0:T(8,128)(2,1)S(1)} collective-permute-done((bf16[2,528,384]{2,1,0:T(8,128)(2,1)}, bf16[2,528,384]{2,1,0:T(8,128)(2,1)S(1)}, u32[]{:S(2)}, u32[]{:S(2)}) %collective-permute-start.44) | collective-permute-done | bytes 811040 | tf_op jit(solution)/shard_map/ppermute | solution.py:24
  170.1 2.0 collective-permute-start.45
  174.2 4.8 %collective-permute-done.45 = bf16[1,528,384]{2,1,0:T(8,128)(2,1)S(1)} collective-permute-done((bf16[1,528,384]{2,1,0:T(8,128)(2,1)S(1)}, bf16[1,528,384]{2,1,0:T(8,128)(2,1)S(1)}, u32[]{:S(2)}, u32[]{:S(2)}) %collective-permute-start.45) | collective-permute-done | bytes 405536 | tf_op jit(solution)/shard_map/ppermute | solution.py:24
  179.0 3.0 %collective-permute-done.43 = bf16[1,528,384]{2,1,0:T(8,128)(2,1)S(1)} collective-permute-done((bf16[1,528,384]{2,1,0:T(8,128)(2,1)S(1)}, bf16[1,528,384]{2,1,0:T(8,128)(2,1)S(1)}, u32[]{:S(2)}, u32[]{:S(2)}) %collective-permute-start.43) | collective-permute-done | bytes 405536 | tf_op jit(solution)/shard_map/ppermute | solution.py:24
  182.3 3.3 %collective-permute-start.46 = (bf16[528,384]{1,0:T(8,128)(2,1)S(1)}, bf16[528,384]{1,0:T(8,128)(2,1)S(1)}, u32[]{:S(2)}, u32[]{:S(2)}) collective-permute-start(bf16[528,384]{1,0:T(8,128)(2,1)S(1)} %select_bitcast_fusion), channel_id=1, source_target_pairs={{0,1},{1,0},{2,3},{3,2},{4,5},{5,4},{6,7},{7,6},{8,9},{9,8},{10,11... | collective-permute-start | bytes 1216520 | tf_op jit(solution)/shard_map/ppermute | solution.py:24
  185.7 8.0 %collective-permute-done.46 = bf16[528,384]{1,0:T(8,128)(2,1)S(1)} collective-permute-done((bf16[528,384]{1,0:T(8,128)(2,1)S(1)}, bf16[528,384]{1,0:T(8,128)(2,1)S(1)}, u32[]{:S(2)}, u32[]{:S(2)}) %collective-permute-start.46) | collective-permute-done | bytes 405536 | tf_op jit(solution)/shard_map/ppermute | solution.py:24
  194.3 8.6 %collective-permute-done.47 = bf16[264,384]{1,0:T(8,128)(2,1)S(1)} collective-permute-done((bf16[264,384]{1,0:T(8,128)(2,1)S(1)}, bf16[264,384]{1,0:T(8,128)(2,1)S(1)}, u32[]{:S(2)}, u32[]{:S(2)}) %collective-permute-start.47) | collective-permute-done | bytes 202784 | tf_op jit(solution)/shard_map/ppermute | solution.py:24
  204.1 7.6 %collective-permute-done.48 = bf16[264,384]{1,0:T(8,128)(2,1)S(1)} collective-permute-done((bf16[264,384]{1,0:T(8,128)(2,1)S(1)}, bf16[264,384]{1,0:T(8,128)(2,1)S(1)}, u32[]{:S(2)}, u32[]{:S(2)}) %collective-permute-start.48) | collective-permute-done | bytes 202784 | tf_op jit(solution)/shard_map/ppermute | solution.py:24
  212.8 7.0 %collective-permute-done.49 = bf16[528,384]{1,0:T(8,128)(2,1)S(1)} collective-permute-done((bf16[528,384]{1,0:T(8,128)(2,1)S(1)}, bf16[528,384]{1,0:T(8,128)(2,1)S(1)}, u32[]{:S(2)}, u32[]{:S(2)}) %collective-permute-start.49) | collective-permute-done | bytes 405536 | tf_op jit(solution)/shard_map/ppermute | solution.py:24
  (232 shorter events, 53.0 us)
Async XLA Ops:
  1.8 15.6 %collective-permute-start.5 = (bf16[96,1152]{1,0:T(8,128)(2,1)S(1)}, bf16[96,1152]{1,0:T(8,128)(2,1)}, u32[]{:S(2)}, u32[]{:S(2)}) collective-permute-start(bf16[96,1152]{1,0:T(8,128)(2,1)S(1)} %get-tuple-element.62.rest_4_), channel_id=1, source_target_pairs={{0,16},{4,20},{8,24},{12,28},{16,0},{20,4},{24,8},{28,12},{1,17},{... | collective-permute-start | bytes 663560 | tf_op jit(solution)/shard_map/ppermute | solution.py:24
  4.9 13.1 %collective-permute-start.6 = (bf16[96,1152]{1,0:T(8,128)(2,1)S(1)}, bf16[96,1152]{1,0:T(8,128)(2,1)}, u32[]{:S(2)}, u32[]{:S(2)}) collective-permute-start(bf16[96,1152]{1,0:T(8,128)(2,1)S(1)} %get-tuple-element.62.rest_4_), channel_id=1, source_target_pairs={{0,8},{4,12},{8,0},{12,4},{16,24},{20,28},{24,16},{28,20},{1,9},{5... | collective-permute-start | bytes 663560 | tf_op jit(solution)/shard_map/ppermute | solution.py:24
  9.1 10.6 %collective-permute-start.1 = (bf16[208,768]{1,0:T(8,128)(2,1)S(1)}, bf16[208,768]{1,0:T(8,128)(2,1)S(1)}, u32[]{:S(2)}, u32[]{:S(2)}) collective-permute-start(bf16[208,768]{1,0:T(8,128)(2,1)S(1)} %get-tuple-element.74), channel_id=1, source_target_pairs={{1,0},{2,1},{3,2},{4,3},{5,4},{6,5},{7,6},{8,7},{9,8},{10,9},{11,1... | collective-permute-start | bytes 958472 | tf_op jit(solution)/shard_map/ppermute | solution.py:485
  10.4 12.4 %collective-permute-start = (bf16[208,768]{1,0:T(8,128)(2,1)S(1)}, bf16[208,768]{1,0:T(8,128)(2,1)S(1)}, u32[]{:S(2)}, u32[]{:S(2)}) collective-permute-start(bf16[208,768]{1,0:T(8,128)(2,1)S(1)} %get-tuple-element.75), channel_id=1, source_target_pairs={{0,1},{1,2},{2,3},{3,4},{4,5},{5,6},{6,7},{7,8},{8,9},{9,10},{10,1... | collective-permute-start | bytes 958472 | tf_op jit(solution)/shard_map/ppermute | solution.py:482
  15.2 16.4 %collective-permute-start.2 = (bf16[96,1280]{1,0:T(8,128)(2,1)S(1)}, bf16[96,1280]{1,0:T(8,128)(2,1)}, u32[]{:S(2)}, u32[]{:S(2)}) collective-permute-start(bf16[96,1280]{1,0:T(8,128)(2,1)S(1)} %fusion.3.rest_0_), channel_id=1, source_target_pairs={{0,8},{4,12},{8,0},{12,4},{16,24},{20,28},{24,16},{28,20},{1,9},{5... | collective-permute-start | bytes 737288 | tf_op jit(solution)/shard_map/ppermute | solution.py:24
  17.4 14.3 %collective-permute-start.3 = (bf16[96,1280]{1,0:T(8,128)(2,1)S(1)}, bf16[96,1280]{1,0:T(8,128)(2,1)S(1)}, u32[]{:S(2)}, u32[]{:S(2)}) collective-permute-start(bf16[96,1280]{1,0:T(8,128)(2,1)S(1)} %fusion.3.rest_0_), channel_id=1, source_target_pairs={{0,16},{4,20},{8,24},{12,28},{16,0},{20,4},{24,8},{28,12},{1,17},{... | collective-permute-start | bytes 737288 | tf_op jit(solution)/shard_map/ppermute | solution.py:24
  18.0 15.0 %collective-permute-start.8 = (bf16[96,1280]{1,0:T(8,128)(2,1)S(1)}, bf16[96,1280]{1,0:T(8,128)(2,1)S(1)}, u32[]{:S(2)}, u32[]{:S(2)}) collective-permute-start(bf16[96,1280]{1,0:T(8,128)(2,1)S(1)} %fusion.3.rest_0_), channel_id=1, source_target_pairs={{0,4},{4,0},{8,12},{12,8},{16,20},{20,16},{24,28},{28,24},{1,5},{5... | collective-permute-start | bytes 737288 | tf_op jit(solution)/shard_map/ppermute | solution.py:24
  19.7 15.9 %collective-permute-start.16 = (bf16[528,384]{1,0:T(8,128)(2,1)S(1)}, bf16[528,384]{1,0:T(8,128)(2,1)S(1)}, u32[]{:S(2)}, u32[]{:S(2)}) collective-permute-start(bf16[528,384]{1,0:T(8,128)(2,1)S(1)} %get-tuple-element.73.rest_0_), channel_id=1, source_target_pairs={{0,8},{4,12},{8,0},{12,4},{16,24},{20,28},{24,16},{28,20},{1,9},{5... | collective-permute-start | bytes 1216520 | tf_op jit(solution)/shard_map/ppermute | solution.py:24
  29.5 21.5 %collective-permute-start.17 = (bf16[528,384]{1,0:T(8,128)(2,1)S(1)}, bf16[528,384]{1,0:T(8,128)(2,1)S(1)}, u32[]{:S(2)}, u32[]{:S(2)}) collective-permute-start(bf16[528,384]{1,0:T(8,128)(2,1)S(1)} %get-tuple-element.73.rest_0_), channel_id=1, source_target_pairs={{0,16},{4,20},{8,24},{12,28},{16,0},{20,4},{24,8},{28,12},{1,17},{... | collective-permute-start | bytes 1216520 | tf_op jit(solution)/shard_map/ppermute | solution.py:24
  31.6 18.4 %collective-permute-start.19 = (bf16[528,384]{1,0:T(8,128)(2,1)S(1)}, bf16[528,384]{1,0:T(8,128)(2,1)S(1)}, u32[]{:S(2)}, u32[]{:S(2)}) collective-permute-start(bf16[528,384]{1,0:T(8,128)(2,1)S(1)} %get-tuple-element.72.rest_4_), channel_id=1, source_target_pairs={{0,16},{4,20},{8,24},{12,28},{16,0},{20,4},{24,8},{28,12},{1,17},{... | collective-permute-start | bytes 1216520 | tf_op jit(solution)/shard_map/ppermute | solution.py:24
  31.7 19.4 %collective-permute-start.20 = (bf16[528,384]{1,0:T(8,128)(2,1)S(1)}, bf16[528,384]{1,0:T(8,128)(2,1)S(1)}, u32[]{:S(2)}, u32[]{:S(2)}) collective-permute-start(bf16[528,384]{1,0:T(8,128)(2,1)S(1)} %get-tuple-element.72.rest_4_), channel_id=1, source_target_pairs={{0,8},{4,12},{8,0},{12,4},{16,24},{20,28},{24,16},{28,20},{1,9},{5... | collective-permute-start | bytes 1216520 | tf_op jit(solution)/shard_map/ppermute | solution.py:24
  33.0 18.6 %collective-permute-start.22 = (bf16[528,384]{1,0:T(8,128)(2,1)S(1)}, bf16[528,384]{1,0:T(8,128)(2,1)S(1)}, u32[]{:S(2)}, u32[]{:S(2)}) collective-permute-start(bf16[528,384]{1,0:T(8,128)(2,1)S(1)} %get-tuple-element.73.rest_0_), channel_id=1, source_target_pairs={{0,4},{4,0},{8,12},{12,8},{16,20},{20,16},{24,28},{28,24},{1,5},{5... | collective-permute-start | bytes 1216520 | tf_op jit(solution)/shard_map/ppermute | solution.py:24
  35.5 16.8 %collective-permute-start.26 = (bf16[528,384]{1,0:T(8,128)(2,1)S(1)}, bf16[528,384]{1,0:T(8,128)(2,1)S(1)}, u32[]{:S(2)}, u32[]{:S(2)}) collective-permute-start(bf16[528,384]{1,0:T(8,128)(2,1)S(1)} %get-tuple-element.72.rest_4_), channel_id=1, source_target_pairs={{0,4},{4,0},{8,12},{12,8},{16,20},{20,16},{24,28},{28,24},{1,5},{5... | collective-permute-start | bytes 1216520 | tf_op jit(solution)/shard_map/ppermute | solution.py:24
  57.3 11.8 %collective-permute-start.18 = (bf16[528,384]{1,0:T(8,128)(2,1)S(1)}, bf16[528,384]{1,0:T(8,128)(2,1)S(1)}, u32[]{:S(2)}, u32[]{:S(2)}) collective-permute-start(bf16[528,384]{1,0:T(8,128)(2,1)S(1)} %collective-permute-done.16.rest_1_), channel_id=1, source_target_pairs={{0,16},{4,20},{8,24},{12,28},{16,0},{20,4},{24,8},{28,12},{1,17},{... | collective-permute-start | bytes 1216520 | tf_op jit(solution)/shard_map/ppermute | solution.py:24
  58.7 11.8 %collective-permute-start.23 = (bf16[528,384]{1,0:T(8,128)(2,1)S(1)}, bf16[528,384]{1,0:T(8,128)(2,1)S(1)}, u32[]{:S(2)}, u32[]{:S(2)}) collective-permute-start(bf16[528,384]{1,0:T(8,128)(2,1)S(1)} %collective-permute-done.16.rest_1_), channel_id=1, source_target_pairs={{0,4},{4,0},{8,12},{12,8},{16,20},{20,16},{24,28},{28,24},{1,5},{5... | collective-permute-start | bytes 1216520 | tf_op jit(solution)/shard_map/ppermute | solution.py:24
  59.7 10.8 %collective-permute-start.21 = (bf16[528,384]{1,0:T(8,128)(2,1)S(1)}, bf16[528,384]{1,0:T(8,128)(2,1)S(1)}, u32[]{:S(2)}, u32[]{:S(2)}) collective-permute-start(bf16[528,384]{1,0:T(8,128)(2,1)S(1)} %collective-permute-done.19.rest_5_), channel_id=1, source_target_pairs={{0,8},{4,12},{8,0},{12,4},{16,24},{20,28},{24,16},{28,20},{1,9},{5... | collective-permute-start | bytes 1216520 | tf_op jit(solution)/shard_map/ppermute | solution.py:24
  66.0 14.0 %collective-permute-start.27 = (bf16[528,384]{1,0:T(8,128)(2,1)S(1)}, bf16[528,384]{1,0:T(8,128)(2,1)S(1)}, u32[]{:S(2)}, u32[]{:S(2)}) collective-permute-start(bf16[528,384]{1,0:T(8,128)(2,1)S(1)} %collective-permute-done.19.rest_5_), channel_id=1, source_target_pairs={{0,4},{4,0},{8,12},{12,8},{16,20},{20,16},{24,28},{28,24},{1,5},{5... | collective-permute-start | bytes 1216520 | tf_op jit(solution)/shard_map/ppermute | solution.py:24
  66.1 13.8 %collective-permute-start.24 = (bf16[528,384]{1,0:T(8,128)(2,1)S(1)}, bf16[528,384]{1,0:T(8,128)(2,1)S(1)}, u32[]{:S(2)}, u32[]{:S(2)}) collective-permute-start(bf16[528,384]{1,0:T(8,128)(2,1)S(1)} %collective-permute-done.17.rest_2_), channel_id=1, source_target_pairs={{0,4},{4,0},{8,12},{12,8},{16,20},{20,16},{24,28},{28,24},{1,5},{5... | collective-permute-start | bytes 1216520 | tf_op jit(solution)/shard_map/ppermute | solution.py:24
  69.1 10.9 %collective-permute-start.28 = (bf16[528,384]{1,0:T(8,128)(2,1)S(1)}, bf16[528,384]{1,0:T(8,128)(2,1)S(1)}, u32[]{:S(2)}, u32[]{:S(2)}) collective-permute-start(bf16[528,384]{1,0:T(8,128)(2,1)S(1)} %collective-permute-done.20.rest_6_), channel_id=1, source_target_pairs={{0,4},{4,0},{8,12},{12,8},{16,20},{20,16},{24,28},{28,24},{1,5},{5... | collective-permute-start | bytes 1216520 | tf_op jit(solution)/shard_map/ppermute | solution.py:24
  70.5 9.4 %collective-permute-start.25 = (bf16[528,384]{1,0:T(8,128)(2,1)S(1)}, bf16[528,384]{1,0:T(8,128)(2,1)S(1)}, u32[]{:S(2)}, u32[]{:S(2)}) collective-permute-start(bf16[528,384]{1,0:T(8,128)(2,1)S(1)} %collective-permute-done.18.rest_3_), channel_id=1, source_target_pairs={{0,4},{4,0},{8,12},{12,8},{16,20},{20,16},{24,28},{28,24},{1,5},{5... | collective-permute-start | bytes 1216520 | tf_op jit(solution)/shard_map/ppermute | solution.py:24
  70.6 9.4 %collective-permute-start.29 = (bf16[528,384]{1,0:T(8,128)(2,1)S(1)}, bf16[528,384]{1,0:T(8,128)(2,1)S(1)}, u32[]{:S(2)}, u32[]{:S(2)}) collective-permute-start(bf16[528,384]{1,0:T(8,128)(2,1)S(1)} %collective-permute-done.21.rest_7_), channel_id=1, source_target_pairs={{0,4},{4,0},{8,12},{12,8},{16,20},{20,16},{24,28},{28,24},{1,5},{5... | collective-permute-start | bytes 1216520 | tf_op jit(solution)/shard_map/ppermute | solution.py:24
  111.6 12.9 %collective-permute-start.34 = (bf16[2,304,384]{2,1,0:T(8,128)(2,1)}, bf16[2,304,384]{2,1,0:T(8,128)(2,1)S(1)}, u32[]{:S(2)}, u32[]{:S(2)}) collective-permute-start(bf16[2,304,384]{2,1,0:T(8,128)(2,1)} %get-tuple-element.46), channel_id=1, source_target_pairs={{0,8},{4,12},{8,0},{12,4},{16,24},{20,28},{24,16},{28,20},{1,9},{5... | collective-permute-start | bytes 1400840 | tf_op jit(solution)/shard_map/ppermute | solution.py:24
  112.3 14.3 %collective-permute-start.32 = (bf16[2,304,384]{2,1,0:T(8,128)(2,1)}, bf16[2,304,384]{2,1,0:T(8,128)(2,1)S(1)}, u32[]{:S(2)}, u32[]{:S(2)}) collective-permute-start(bf16[2,304,384]{2,1,0:T(8,128)(2,1)} %get-tuple-element.44), channel_id=1, source_target_pairs={{0,16},{4,20},{8,24},{12,28},{16,0},{20,4},{24,8},{28,12},{1,17},{... | collective-permute-start | bytes 1400840 | tf_op jit(solution)/shard_map/ppermute | solution.py:24
  128.6 19.4 %collective-permute-start.40 = (bf16[128,5760]{1,0:T(8,128)(2,1)S(1)}, bf16[128,5760]{1,0:T(8,128)(2,1)}, u32[]{:S(2)}, u32[]{:S(2)}) collective-permute-start(bf16[128,5760]{1,0:T(8,128)(2,1)S(1)} %copy-done.11), channel_id=1, source_target_pairs={{0,4},{4,0},{8,12},{12,8},{16,20},{20,16},{24,28},{28,24},{1,5},{5... | collective-permute-start | bytes 4423688 | tf_op jit(solution)/shard_map/ppermute | solution.py:24
  145.7 9.4 %collective-permute-start.38 = (bf16[152,384]{1,0:T(8,128)(2,1)S(1)}, bf16[152,384]{1,0:T(8,128)(2,1)S(1)}, u32[]{:S(2)}, u32[]{:S(2)}) collective-permute-start(bf16[152,384]{1,0:T(8,128)(2,1)S(1)} %add_convert_fusion.9), channel_id=1, source_target_pairs={{0,2},{1,3},{2,0},{3,1},{4,6},{5,7},{6,4},{7,5},{8,10},{9,11},{10,... | collective-permute-start | bytes 350216 | tf_op jit(solution)/shard_map/ppermute | solution.py:24
  153.3 16.5 %collective-permute-start.44 = (bf16[2,528,384]{2,1,0:T(8,128)(2,1)}, bf16[2,528,384]{2,1,0:T(8,128)(2,1)S(1)}, u32[]{:S(2)}, u32[]{:S(2)}) collective-permute-start(bf16[2,528,384]{2,1,0:T(8,128)(2,1)} %get-tuple-element.51), channel_id=1, source_target_pairs={{0,8},{4,12},{8,0},{12,4},{16,24},{20,28},{24,16},{28,20},{1,9},{5... | collective-permute-start | bytes 2433032 | tf_op jit(solution)/shard_map/ppermute | solution.py:24
  154.8 19.0 %collective-permute-start.42 = (bf16[2,528,384]{2,1,0:T(8,128)(2,1)}, bf16[2,528,384]{2,1,0:T(8,128)(2,1)S(1)}, u32[]{:S(2)}, u32[]{:S(2)}) collective-permute-start(bf16[2,528,384]{2,1,0:T(8,128)(2,1)} %get-tuple-element.49), channel_id=1, source_target_pairs={{0,16},{4,20},{8,24},{12,28},{16,0},{20,4},{24,8},{28,12},{1,17},{... | collective-permute-start | bytes 2433032 | tf_op jit(solution)/shard_map/ppermute | solution.py:24
  155.2 8.9 %collective-permute-start.39 = (bf16[304,384]{1,0:T(8,128)(2,1)S(1)}, bf16[304,384]{1,0:T(8,128)(2,1)S(1)}, u32[]{:S(2)}, u32[]{:S(2)}) collective-permute-start(bf16[304,384]{1,0:T(8,128)(2,1)S(1)} %pad_maximum_fusion.6), channel_id=1, source_target_pairs={{0,1},{1,0},{2,3},{3,2},{4,5},{5,4},{6,7},{7,6},{8,9},{9,8},{10,11... | collective-permute-start | bytes 700424 | tf_op jit(solution)/shard_map/ppermute | solution.py:24
  170.1 8.9 %collective-permute-start.45 = (bf16[1,528,384]{2,1,0:T(8,128)(2,1)S(1)}, bf16[1,528,384]{2,1,0:T(8,128)(2,1)S(1)}, u32[]{:S(2)}, u32[]{:S(2)}) collective-permute-start(bf16[1,528,384]{2,1,0:T(8,128)(2,1)S(1)} %slice.255), channel_id=1, source_target_pairs={{0,16},{4,20},{8,24},{12,28},{16,0},{20,4},{24,8},{28,12},{1,17},{... | collective-permute-start | bytes 1216520 | tf_op jit(solution)/shard_map/ppermute | solution.py:24
  182.3 11.4 %collective-permute-start.46 = (bf16[528,384]{1,0:T(8,128)(2,1)S(1)}, bf16[528,384]{1,0:T(8,128)(2,1)S(1)}, u32[]{:S(2)}, u32[]{:S(2)}) collective-permute-start(bf16[528,384]{1,0:T(8,128)(2,1)S(1)} %select_bitcast_fusion), channel_id=1, source_target_pairs={{0,1},{1,0},{2,3},{3,2},{4,5},{5,4},{6,7},{7,6},{8,9},{9,8},{10,11... | collective-permute-start | bytes 1216520 | tf_op jit(solution)/shard_map/ppermute | solution.py:24
  194.0 9.0 %collective-permute-start.47 = (bf16[264,384]{1,0:T(8,128)(2,1)S(1)}, bf16[264,384]{1,0:T(8,128)(2,1)S(1)}, u32[]{:S(2)}, u32[]{:S(2)}) collective-permute-start(bf16[264,384]{1,0:T(8,128)(2,1)S(1)} %broadcast_select_fusion.6), channel_id=1, source_target_pairs={{0,2},{1,3},{2,0},{3,1},{4,6},{5,7},{6,4},{7,5},{8,10},{9,11},{10,... | collective-permute-start | bytes 608264 | tf_op jit(solution)/shard_map/ppermute | solution.py:24
  203.0 8.7 %collective-permute-start.48 = (bf16[264,384]{1,0:T(8,128)(2,1)S(1)}, bf16[264,384]{1,0:T(8,128)(2,1)S(1)}, u32[]{:S(2)}, u32[]{:S(2)}) collective-permute-start(bf16[264,384]{1,0:T(8,128)(2,1)S(1)} %add_convert_fusion.8), channel_id=1, source_target_pairs={{0,2},{1,3},{2,0},{3,1},{4,6},{5,7},{6,4},{7,5},{8,10},{9,11},{10,... | collective-permute-start | bytes 608264 | tf_op jit(solution)/shard_map/ppermute | solution.py:24
  (61 other events, 746.0 us)

commit v2 on v1

v2 whole, which is shorter than its diff:
```python
import math

import jax
import jax.numpy as jnp
from jax import lax
from jax.experimental import pallas as pl
from jax.experimental.pallas import tpu as pltpu
from jax.sharding import PartitionSpec as P

HEAD = 64
RADIUS = 64
BLOCK = 128
EPSILON = 1e-05
THETA_BASE = 10000.0
NEGATIVE = -1e30
VMEM_BYTES = 56 * 1024 * 1024
BF = jnp.bfloat16
F32 = jnp.float32


def xor_send(array, axis, bit):
    count = lax.axis_size(axis)
    return lax.ppermute(array, axis, [(i, i ^ bit) for i in range(count)])


def bits_of(count):
    return [1 << i for i in range(count.bit_length() - 1)]


def gather_pieces(own, split, chip_bits):
    if len(chip_bits) == 2:
        x, y = chip_bits
        from_x, from_y = xor_send(own, "shard", x), xor_send(own, "shard", y)
        pieces = [(0, 2, own), (x, 2, from_x), (y, 2, from_y)]
        pieces.append((x | y, 0, xor_send(from_x[:, :split], "shard", y)))
        pieces.append((x | y, 1, xor_send(from_y[:, split:], "shard", x)))
    else:
        streams = ([(0, 0, own[:, :split])], [(0, 1, own[:, split:])])
        for stage in range(len(chip_bits)):
            grown = []
            for which, bit in ((0, chip_bits[stage]), (1, chip_bits[-1 - stage])):
                grown.append(
                    [(j ^ bit, s, xor_send(a, "shard", bit)) for j, s, a in streams[which]]
                )
            for held, more in zip(streams, grown):
                held.extend(more)
        pieces = streams[0] + streams[1]
    return pieces


def with_core(pieces, after=None):
    others = []
    for i, (j, s, a) in enumerate(pieces):
        if after is not None and i >= len(pieces) - 2:
            a, _ = lax.optimization_barrier((a, after))
        others.append((j ^ 1, s, xor_send(a, "shard", 1)))
    return pieces + others


def add_low(left, right):
    return (left.astype(F32) + right.astype(F32)).astype(BF)


def scatter_sum(send, keep, order, after=None):
    for bit in order[:-1]:
        other = xor_send(send, "shard", bit)
        if after is not None:
            other, _ = lax.optimization_barrier((other, after))
        middle = keep.shape[0] // 2
        send = add_low(keep[middle:], other[middle:])
        keep = add_low(keep[:middle], other[:middle])
    return keep, xor_send(send, "shard", order[-1])


def both_sums(sums_0, sums_1):
    return jnp.concatenate([add_low(k[0], o[0]) for k, o in (sums_0, sums_1)], axis=0)


def replica_sum(total):
    for bit in bits_of(lax.axis_size("replica"))[1:]:
        total = add_low(total, xor_send(total, "replica", bit))
    return total, xor_send(total, "replica", 1)


def dot(left, right):
    return jnp.dot(left, right, preferred_element_type=F32)


def dot_cols(left, right):
    return lax.dot_general(left, right, (((1,), (1,)), ((), ())), preferred_element_type=F32)


def dot_rows(left, right):
    return lax.dot_general(left, right, (((0,), (0,)), ((), ())), preferred_element_type=F32)


def standardize(vector):
    average = jnp.mean(vector, axis=-1, keepdims=True)
    centred = vector - average
    spread = jnp.mean(centred * centred, axis=-1, keepdims=True)
    inverse = lax.rsqrt(spread + EPSILON)
    return centred * inverse, inverse


def norm_back(grad, gain, hat, inverse):
    dhat = grad * gain
    mean = jnp.mean(dhat, axis=-1, keepdims=True)
    along = jnp.mean(dhat * hat, axis=-1, keepdims=True)
    return (dhat - mean - hat * along) * inverse


def turned(vector):
    width = vector.shape[-1]
    lane = lax.broadcasted_iota(jnp.int32, vector.shape, 1)
    return jnp.where(
        (lane & 63) < 32, pltpu.roll(vector, width - 32, 1), pltpu.roll(vector, 32, 1)
    )


def place(me, pieces, refs, layout, sems):
    copies = []
    for (j, stream), ref in zip(pieces, refs):
        owner = me ^ j
        for row, rows, col, cols, dst, dst_col in layout[stream]:
            start = owner * rows
            if rows % 16 == 0:
                start = pl.multiple_of(start, 16)
            copy = pltpu.make_async_copy(
                ref.at[pl.ds(row, rows), pl.ds(col, cols)],
                dst.at[pl.ds(start, rows), pl.ds(dst_col, cols)],
                sems.at[len(copies)],
            )
            copy.start()
            copies.append(copy)
    return copies


def call(kernel, out_shape, inputs, in_any, scratch, flops, traffic):
    any_spec = pl.BlockSpec(memory_space=pl.ANY)
    vmem = pl.BlockSpec(memory_space=pltpu.VMEM)
    smem = pl.BlockSpec(memory_space=pltpu.SMEM)
    specs = [smem] + [vmem] * (len(inputs) - 1) + [any_spec] * len(in_any)
    return pl.pallas_call(
        kernel,
        out_shape=out_shape,
        in_specs=specs,
        out_specs=jax.tree.map(lambda _: vmem, out_shape),
        scratch_shapes=scratch,
        compiler_params=pltpu.CompilerParams(vmem_limit_bytes=VMEM_BYTES),
        cost_estimate=pl.CostEstimate(flops=flops, bytes_accessed=traffic, transcendentals=0),
    )(*inputs, *in_any)


def shaped(shape, dtype):
    return jax.ShapeDtypeStruct(shape, dtype)


def pack_qkv_kernel(half):
    def body(info, weight, gains, out):
        width = 2 * half

        def pick(first):
            for i in range(3):
                out[:, i * half : (i + 1) * half] = weight[
                    :, i * width + first : i * width + first + half
                ]

        @pl.when(info[1] == 0)
        def _():
            pick(0)

        @pl.when(info[1] != 0)
        def _():
            pick(half)

        out[:, 3 * half :] = gains[...]

    return body


def pack_mlp_kernel(count, down_rows, take):
    def body(info, attn, glu, down, out):
        rows, width = attn.shape
        units = count * take
        hidden = count * down_rows
        out[:, 0:width] = attn[...]
        last = width + 2 * units

        def pick(first):
            for part in range(2):
                for s in range(count):
                    at = part * hidden + s * down_rows + first
                    to = width + part * units + s * take
                    out[:, to : to + take] = glu[:, at : at + take]
            out[0:take, last:] = down[first : first + take, :]

        @pl.when(info[1] == 0)
        def _():
            pick(0)

        @pl.when(info[1] != 0)
        def _():
            pick(down_rows - take)

        if rows > take:
            out[take:, last:] = jnp.zeros((rows - take, width), BF)

    return body


def around_kernel(info, own, dy_own, partner, near, far, tok, dy):
    mine = slice(0, BLOCK)

    def arrange(first, first_dy, second, second_dy, before, after):
        tok[0:BLOCK, :] = before[mine, :]
        tok[BLOCK : 2 * BLOCK, :] = first
        tok[2 * BLOCK : 3 * BLOCK, :] = second
        tok[3 * BLOCK :, :] = after[mine, :]
        halo = slice(BLOCK, BLOCK + RADIUS)
        dy[0:RADIUS, :] = before[halo, :]
        dy[RADIUS : RADIUS + BLOCK, :] = first_dy
        dy[RADIUS + BLOCK : RADIUS + 2 * BLOCK, :] = second_dy
        dy[RADIUS + 2 * BLOCK :, :] = after[halo, :]

    other = partner[mine, :]
    other_dy = partner[BLOCK : 2 * BLOCK, :]

    @pl.when(info[1] == 0)
    def _():
        arrange(own[...], dy_own[...], other, other_dy, near, far)

    @pl.when(info[1] != 0)
    def _():
        arrange(other, other_dy, own[...], dy_own[...], far, near)


def qkv_layout(rows, half, split, weight, gains):
    wide = 3 * half
    first = (0, rows, 0, split, weight, 0)
    second = ((0, rows, 0, wide - split, weight, split), (0, rows, wide - split, 128, gains, 0))
    whole = ((0, rows, 0, wide, weight, 0), (0, rows, wide, 128, gains, 0))
    return ((first,), second, whole)


def project_kernel(pieces, rows, width, split):
    half = width // 2
    span = 4 * BLOCK

    def body(info, tok, cosine, sine, bias, *rest):
        refs, rest = rest[: len(pieces)], rest[len(pieces) :]
        q_out, k_out, v_out, p_out, ctx_out, normed_out, gains_out = rest[:7]
        weight, gain_cols, normed, sems = rest[7:]
        layout = qkv_layout(rows, half, split, weight, gain_cols)
        copies = place(info[0], pieces, refs, layout, sems)
        hats = [
            standardize(tok[i * BLOCK : (i + 1) * BLOCK, :].astype(F32))[0] for i in range(4)
        ]
        for copy in copies:
            copy.wait()
        pick = jnp.where(
            lax.broadcasted_iota(jnp.int32, (8, 128), 0)
            == lax.broadcasted_iota(jnp.int32, (8, 128), 1),
            1.0,
            0.0,
        ).astype(BF)
        gains = dot_cols(pick, gain_cols[...])
        gains_out[...] = gains
        for i, hat in enumerate(hats):
            normed[i * BLOCK : (i + 1) * BLOCK, :] = (hat * gains[0:1]).astype(BF)
        normed_out[...] = normed[BLOCK : 3 * BLOCK, :]
        cos3 = jnp.concatenate([cosine[...]] * 3, axis=1)
        sin3 = jnp.concatenate([sine[...]] * 3, axis=1)
        mid = slice(RADIUS, span - RADIUS)
        joined = dot(normed[mid, :], weight[:, 0:half])
        q_out[...] = (joined * cos3[mid] + turned(joined) * sin3[mid]).astype(BF)
        joined = dot(normed[...], weight[:, half : 2 * half])
        k_out[...] = (joined * cos3 + turned(joined) * sin3).astype(BF)
        v_out[...] = dot(normed[...], weight[:, 2 * half : 3 * half]).astype(BF)
        lane = lax.broadcasted_iota(jnp.int32, (BLOCK, 128), 1)
        scale = 1.0 / math.sqrt(HEAD)
        for pair in range(half // 128):
            cols = slice(pair * 128, pair * 128 + 128)
            for b in range(3):
                rows_q = slice(b * BLOCK, (b + 1) * BLOCK)
                rows_k = slice(b * BLOCK, (b + 2) * BLOCK)
                queries, keys, values = q_out[rows_q, cols], k_out[rows_k, cols], v_out[rows_k, cols]
                parts = []
                for h in range(2):
                    mine = (lane < HEAD) if h == 0 else (lane >= HEAD)
                    masked = jnp.where(mine, queries.astype(F32) * scale, 0.0).astype(BF)
                    scores = dot_cols(masked, keys) + bias[rows_q, :]
                    exponent = jnp.exp(scores - jnp.max(scores, axis=1, keepdims=True))
                    total = jnp.sum(exponent, axis=1, keepdims=True)
                    shares = (exponent * (1.0 / total)).astype(BF)
                    p_out[(pair * 2 + h) * 3 + b] = shares
                    parts.append(dot(shares, values))
                ctx_out[rows_q, cols] = jnp.where(lane < HEAD, parts[0], parts[1]).astype(BF)

    return body


def mlp_layout(rows, take, width, units, attn, glu, down):
    one = (0, rows, 0, width, attn, 0)
    gate = (0, rows, width, units, glu, 0)
    up = (0, rows, 0, units, glu, units)
    low = (0, take, units, width, down, 0)
    whole = (one, (0, rows, width, 2 * units, glu, 0), (0, take, width + 2 * units, width, down, 0))
    return ((one, gate), (up, low), whole)


def mlp_kernel(pieces, rows, take, width, units):
    half = width // 2
    pair = slice(RADIUS, RADIUS + 2 * BLOCK)

    def body(info, tok, ctx_own, ctx_other, dy, gains, mask, *rest):
        refs, rest = rest[: len(pieces)], rest[len(pieces) :]
        mix_keep, mix_send, shared, ctx_pair, hidden, gn_out, fgain_out = rest[:7]
        attn, glu, down, ggu, mix, sems = rest[7:]
        layout = mlp_layout(rows, take, width, units, attn, glu, down)
        copies = place(info[0], pieces, refs, layout, sems)
        at = info[1]
        inputs = tok[RADIUS : RADIUS + 3 * BLOCK, :].astype(F32)
        own_rows = pl.ds(pl.multiple_of(at * half, 128), half)
        other_rows = pl.ds(pl.multiple_of((1 - at) * half, 128), half)

        @pl.when(at == 0)
        def _():
            ctx_pair[:, 0:half] = ctx_own[pair, :]
            ctx_pair[:, half:] = ctx_other[pair, :]

        @pl.when(at != 0)
        def _():
            ctx_pair[:, 0:half] = ctx_other[pair, :]
            ctx_pair[:, half:] = ctx_own[pair, :]

        for copy in copies:
            copy.wait()
        lifted = dot(ctx_own[...], attn[own_rows, :]) + dot(ctx_other[...], attn[other_rows, :])
        hidden[...] = inputs + lifted
        hat, _ = standardize(hidden[...])
        normed = (hat * gains[1:2, :]).astype(BF)
        shared[:, 0:width] = normed[pair]
        partial = jnp.zeros((2 * BLOCK, width), F32)
        for c in range(0, units, 256):
            wide = min(256, units - c)
            cols = slice(c, c + wide)
            gate = dot(normed, glu[:, cols])
            up = dot(normed, glu[:, units + c : units + c + wide])
            grad_act = dot_cols(dy[...], down[cols, :]) * mask[0:1, cols]
            share = 0.5 * (1.0 + lax.erf(gate * (1.0 / math.sqrt(2.0))))
            density = jnp.exp(-0.5 * gate * gate) * (1.0 / math.sqrt(2.0 * math.pi))
            gelu = gate * share
            act = (gelu[pair] * up[pair] * mask[0:1, cols]).astype(BF)
            shared[:, width + c : width + c + wide] = act
            partial = partial + dot(act, down[cols, :])
            ggu[:, cols] = (grad_act * up * (share + gate * density)).astype(BF)
            ggu[:, units + c : units + c + wide] = (grad_act * gelu).astype(BF)
        mix[...] = partial
        mine = pl.ds(pl.multiple_of(at * BLOCK, BLOCK), BLOCK)
        theirs = pl.ds(pl.multiple_of((1 - at) * BLOCK, BLOCK), BLOCK)
        mix_keep[...] = mix[mine, :] + hidden[pl.ds(pl.multiple_of(RADIUS + at * BLOCK, 8), BLOCK), :]
        mix_send[...] = mix[theirs, :].astype(BF)
        shared[:, width + units :] = ggu[pair, :]
        grad = dot_cols(ggu[...], glu[...])
        gn_out[...] = grad.astype(BF)
        fgain = jnp.sum(grad[pair] * hat[pair], axis=0, keepdims=True)
        fgain_out[...] = jnp.broadcast_to(fgain, fgain_out.shape)

    return body


def pair_back(pair, gctx, q, k, v, p, cos, sin):
    lane = lax.broadcasted_iota(jnp.int32, (BLOCK, 128), 1)
    lane2 = lax.broadcasted_iota(jnp.int32, (2 * BLOCK, 128), 1)
    scale = 1.0 / math.sqrt(HEAD)
    cols = slice(pair * 128, pair * 128 + 128)
    first, second = slice(0, BLOCK), slice(BLOCK, 2 * BLOCK)
    low, high = slice(0, RADIUS), slice(RADIUS, BLOCK)
    grad_q = jnp.zeros((2 * BLOCK, 128), F32)
    grad_k, grad_v = [0.0, 0.0], [0.0, 0.0]
    for h in range(2):
        mine = (lane < HEAD) if h == 0 else (lane >= HEAD)
        mine2 = (lane2 < HEAD) if h == 0 else (lane2 >= HEAD)
        scores, shares, queries, grads, parts = [], [], [], [], []
        for b in range(3):
            rows_q = slice(b * BLOCK, (b + 1) * BLOCK)
            rows_k = slice(b * BLOCK, (b + 2) * BLOCK)
            keys, values = k[rows_k, cols], v[rows_k, cols]
            lowered = jnp.where(mine, gctx[rows_q, cols].astype(F32), 0.0).astype(BF)
            query = jnp.where(mine, q[rows_q, cols].astype(F32) * scale, 0.0).astype(BF)
            share = p[(pair * 2 + h) * 3 + b]
            wide = share.astype(F32)
            grad_share = dot_cols(lowered, values)
            row = jnp.sum(wide * grad_share, axis=1, keepdims=True)
            grad_score = (wide * (grad_share - row)).astype(BF)
            scores.append(grad_score)
            shares.append(share)
            queries.append(query)
            grads.append(lowered)
            part = (high, first, low)[b]
            parts.append(dot(grad_score[part], keys))
        grad_q = grad_q + jnp.where(mine2, jnp.concatenate(parts, axis=0) * scale, 0.0)
        for i in range(2):
            two = slice(i, i + 2)
            for total, left, right in ((grad_k, scores, queries), (grad_v, shares, grads)):
                upper, lower = left[i][:, second], left[i + 1][:, first]
                total[i] = total[i] + dot_rows(
                    jnp.concatenate([upper, lower], axis=0), jnp.concatenate(right[two], axis=0)
                )
    grad_k, grad_v = jnp.concatenate(grad_k, axis=0), jnp.concatenate(grad_v, axis=0)
    return (
        (grad_q * cos - turned(grad_q) * sin).astype(BF),
        (grad_k * cos - turned(grad_k) * sin).astype(BF),
        grad_v.astype(BF),
    )


def back_kernel(qkv_pieces, mlp_pieces, rows, width, split):
    half = width // 2
    pair = slice(RADIUS, RADIUS + 2 * BLOCK)

    def body(info, tok, gn_own, gn_other, hidden, dy, gains, fgain, q, k, v, p, cosine, sine, *rest):
        refs = rest[1:]
        n_qkv, n_mlp = len(qkv_pieces), len(mlp_pieces)
        qkv_refs, mlp_refs, rest = refs[:n_qkv], refs[n_qkv : n_qkv + n_mlp], refs[n_qkv + n_mlp :]
        gj_out, keep_out, send_out, ghid_out = rest[:4]
        weight, gain_cols, attn, gctx, held, sems, attn_sems = rest[4:]
        one = (0, rows, 0, width, attn, 0)
        attn_copies = place(info[0], mlp_pieces, mlp_refs, ((one,), (), (one,)), attn_sems)
        layout = qkv_layout(rows, half, split, weight, gain_cols)
        copies = place(info[0], qkv_pieces, qkv_refs, layout, sems)
        at = info[1]
        mine = pl.ds(pl.multiple_of(at * BLOCK, BLOCK), BLOCK)
        theirs = pl.ds(pl.multiple_of((1 - at) * BLOCK, BLOCK), BLOCK)
        hat, inverse = standardize(hidden[...])
        grad = gn_own[...].astype(F32) + gn_other[...].astype(F32)
        grad_hidden = dy[...].astype(F32) + norm_back(grad, gains[1:2, :], hat, inverse)
        held[...] = grad_hidden[pair]
        ghid_out[...] = held[mine, :]
        halves = jnp.where(at == 0, grad_hidden[pair, 0:half], grad_hidden[pair, half:])
        tokens_in = 2 * BLOCK
        gj_out[0:tokens_in, 3 * half :] = halves.astype(BF)
        grad_low = grad_hidden.astype(BF)
        for copy in attn_copies:
            copy.wait()
        own_rows = pl.ds(pl.multiple_of(at * half, 128), half)
        gctx[...] = dot_cols(grad_low, attn[own_rows, :]).astype(BF)
        cos, sin = cosine[BLOCK : 3 * BLOCK, :], sine[BLOCK : 3 * BLOCK, :]
        for i in range(half // 128):
            for part, grad in enumerate(pair_back(i, gctx, q, k, v, p, cos, sin)):
                col = part * half + i * 128
                gj_out[0:tokens_in, col : col + 128] = grad
        for copy in copies:
            copy.wait()
        grad = dot_cols(gj_out[0:tokens_in, 0 : 3 * half], weight[...])
        hat, _ = standardize(tok[BLOCK : 3 * BLOCK, :].astype(F32))
        again = jnp.sum(grad * hat, axis=0, keepdims=True)
        held[...] = grad
        keep_out[...] = held[mine, :]
        send_out[...] = held[theirs, :].astype(BF)
        tail = gj_out.shape[0] - tokens_in
        line = lax.broadcasted_iota(jnp.int32, (tail, width), 0)
        gain_rows = jnp.where(line == 0, again, jnp.where(line == 1, fgain[0:1, :], 0.0))
        gj_out[tokens_in:, 0:width] = gain_rows.astype(BF)
        gj_out[tokens_in:, width:] = jnp.zeros((tail, width), BF)

    return body


def final_kernel(info, tok, keep, other, ghid, gains, out):
    hat, inverse = standardize(tok[...].astype(F32))
    grad = keep[...] + other[...].astype(F32)
    out[...] = (ghid[...] + norm_back(grad, gains[0:1, :], hat, inverse)).astype(BF)


def slots_of(count, chip_bits):
    streams = []
    for order in (chip_bits, chip_bits[::-1]):
        kept = [0]
        for bit in order[1:][::-1]:
            kept = kept + [j | bit for j in kept]
        table = {j: (1, i) for i, j in enumerate(kept)}
        table.update({j | order[0]: (0, i) for i, j in enumerate(kept)})
        streams.append(table)
    return streams


def owner_rows(me, js, lhs_t, rows):
    return jnp.concatenate(
        [lhs_t[pl.ds(pl.multiple_of((me ^ j) * rows, 16), rows), :] for j in js], axis=0
    )


def emit(outs, slots, stream, js, rows, grad, start):
    grad = grad.astype(BF)
    for i, j in enumerate(js):
        kept, at = slots[stream][j]
        for c in range(grad.shape[1] // 128):
            row = start + c * rows
            outs[2 * stream + kept][at, row : row + rows, :] = grad[
                i * rows : (i + 1) * rows, c * 128 : (c + 1) * 128
            ]


def mlp_grad_kernel(js, slots, rows, take, width, units):
    half = width // 2

    def body(info, own, other, dy_own, dy_other, *rest):
        outs, (normed_t, act_t, ggu, dy) = rest[:4], rest[4:]
        me = info[0]
        pair = slice(RADIUS, RADIUS + 2 * BLOCK)
        for i, (ref, dref) in enumerate(((own, dy_own), (other, dy_other))):
            tok = slice(i * 2 * BLOCK, (i + 1) * 2 * BLOCK)
            normed_t[:, tok] = ref[:, 0:width].T
            act_t[:, tok] = ref[:, width : width + units].T
            ggu[tok, :] = ref[:, width + units :]
            dy[tok, :] = dref[pair, :]
        left = owner_rows(me, js, normed_t, rows)
        act = owner_rows(me, js, act_t, take)
        for s in range(2):
            grad = dot(left, ggu[:, s * units : (s + 1) * units])
            emit(outs, slots, s, js, rows, grad, 0)
            grad = dot(act, dy[:, s * half : (s + 1) * half])
            emit(outs, slots, s, js, take, grad, rows * (units // 128))

    return body


def qkv_grad_kernel(js, slots, rows, width):
    half = width // 2

    def body(info, normed_own, normed_other, ctx_own, ctx_other, own, other, *rest):
        outs, (normed_t, ctx_t, gj) = rest[:4], rest[4:]
        me = info[0]
        count = 2 * BLOCK
        each = ((normed_own, ctx_own, own), (normed_other, ctx_other, other))
        for i, (nref, cref, ref) in enumerate(each):
            tok = slice(i * count, (i + 1) * count)
            normed_t[:, tok] = nref[...].T
            ctx_t[:, tok] = cref[...].T
            gj[tok, :] = ref[0:count, :]
        left = owner_rows(me, js, normed_t, rows)
        ctx = owner_rows(me, js, ctx_t, rows)
        emit(outs, slots, 0, js, rows, dot(left, gj[:, 0 : 2 * half]), 0)
        emit(outs, slots, 1, js, rows, dot(left, gj[:, 2 * half : 3 * half]), 0)
        emit(outs, slots, 1, js, rows, dot(ctx, gj[:, 3 * half :]), 3 * rows)
        gains = own[count:, 0:width].astype(F32) + other[count:, 0:width].astype(F32)
        for s in range(2):
            for j in js:
                kept, i = slots[s][j]
                moved = pltpu.roll(gains, lax.rem(width - (me ^ j) * rows, width), 1)
                outs[2 * s + kept][i, 6 * rows : 6 * rows + 16, :] = moved[:, 0:128].astype(BF)

    return body


def mlp_unpack_kernel(rows, down_rows, take, width, units, count):
    hidden = count * down_rows
    spare = 2 * take - down_rows

    def body(info, mine, other, glu, down, held, wide):
        at = info[1]
        held[at] = mine[...].astype(F32)
        held[1 - at] = other[...].astype(F32)
        height = mine.shape[0] // 2
        tiles = units // 128
        for s in range(2):
            for t in range(2):
                for c in range(tiles):
                    row = s * height + c * rows
                    wide[:, c * 128 : (c + 1) * 128] = held[t, row : row + rows, :]
                skip = 0 if t == 0 else spare
                for i in range(count):
                    col = s * hidden + i * down_rows + t * take
                    glu[:, col : col + take - skip] = wide[:, i * take + skip : (i + 1) * take]
                for c in range(width // 256):
                    row = s * height + tiles * rows + c * take
                    col = s * (width // 2) + c * 128
                    down[t * take : (t + 1) * take - skip, col : col + 128] = held[
                        t, row + skip : row + take, :
                    ]

    return body


def qkv_unpack_kernel(rows, width):
    half = width // 2

    def body(info, mine, other, qkv, attn, gains, held):
        at = info[1]
        held[at] = mine[...].astype(F32)
        held[1 - at] = other[...].astype(F32)
        height = mine.shape[0] // 2
        for t in range(2):
            for i in range(3):
                for c in range(half // 128):
                    row = i // 2 * height + (i % 2 * (half // 128) + c) * rows
                    col = i * width + t * half + c * 128
                    qkv[:, col : col + 128] = held[t, row : row + rows, :]
            for c in range(half // 128):
                row = height + (half // 128 + c) * rows
                attn[:, t * half + c * 128 : t * half + (c + 1) * 128] = held[t, row : row + rows, :]
        gains[...] = held[0, 6 * rows : 6 * rows + 8, :] + held[1, 6 * rows : 6 * rows + 8, :]

    return body


def on_device(
    tokens,
    positions,
    qkv_weight,
    attn_weight,
    glu_weight,
    down_weight,
    attn_gain,
    ffn_gain,
    cotangent,
):
    block, width = tokens.shape
    half = width // 2
    rows, down_rows = qkv_weight.shape[0], down_weight.shape[0]
    count, replicas = lax.axis_size("shard"), lax.axis_size("replica")
    everyone = count * replicas
    take = -(-down_rows // 32) * 16
    units = count * take
    me = lax.axis_index("shard").astype(jnp.int32)
    side = lax.axis_index("replica").astype(jnp.int32) & 1
    info = jnp.stack([me, side])
    chip_bits = bits_of(count)[1:]

    gain_cols = jnp.pad(jnp.stack([attn_gain, ffn_gain], axis=1), ((0, 0), (0, 126)))
    own = call(
        pack_qkv_kernel(half),
        shaped((rows, 3 * half + 128), BF),
        (info, qkv_weight, gain_cols),
        [],
        [],
        1_000_000,
        1_000_000,
    )
    qkv_split = (3 * half + 128) // 2
    qkv_parts = gather_pieces(own, qkv_split, chip_bits)

    places = jnp.stack([positions >> 8, positions & 255]).astype(BF)
    places = jnp.pad(places, ((0, 14), (0, width - block)))
    rim = jnp.where(side == 0, cotangent[:RADIUS], cotangent[block - RADIUS :])
    rim = jnp.concatenate([tokens, rim, places], axis=0)
    step = [1 if i & 1 else -1 for i in range(everyone)]
    both = ("shard", "replica")

    def outward(array, length):
        moves = [(i, i + length * step[i]) for i in range(everyone)]
        return lax.ppermute(array, both, [(a, b) for a, b in moves if 0 <= b < everyone])

    near, far = outward(rim, 1), outward(rim, 2)
    partner = xor_send(jnp.concatenate([tokens, cotangent, places], axis=0), "replica", 1)

    own = call(
        pack_mlp_kernel(count, down_rows, take),
        shaped((rows, 2 * width + 2 * units), BF),
        (info, attn_weight, glu_weight, down_weight),
        [],
        [],
        1_000_000,
        2_000_000,
    )
    mlp_parts = gather_pieces(own, width + units, chip_bits)

    tok, dy = call(
        around_kernel,
        (shaped((4 * BLOCK, width), BF), shaped((3 * BLOCK, width), BF)),
        (info, tokens, cotangent, partner, near, far),
        [],
        [],
        1_000_000,
        2_000_000,
    )

    def places_of(packed, row):
        return packed[row, :block].astype(F32) * 256.0 + packed[row + 1, :block].astype(F32)

    mine, theirs = positions.astype(F32), places_of(partner, 2 * block)
    inner, outer = places_of(near, block + RADIUS), places_of(far, block + RADIUS)
    where = jnp.where(
        side == 0,
        jnp.concatenate([inner, mine, theirs, outer]),
        jnp.concatenate([outer, theirs, mine, inner]),
    )
    middle = HEAD // 2
    inverse = THETA_BASE ** (-(jnp.arange(middle, dtype=F32) * 2.0 / HEAD))
    phases = where[:, None] * inverse[None, :]
    cosine, sine = jnp.cos(phases), jnp.sin(phases)
    cosine = jnp.concatenate([cosine] * 4, axis=1)
    sine = jnp.concatenate([-sine, sine, -sine, sine], axis=1)
    offset = (
        jnp.arange(2 * BLOCK, dtype=jnp.int32)[None, :]
        - RADIUS
        - jnp.arange(BLOCK, dtype=jnp.int32)[:, None]
    )
    bias = []
    for b in range(3):
        later_key = where[None, b * BLOCK : (b + 2) * BLOCK] >= offset.astype(F32)
        start = RADIUS + b * BLOCK
        later_query = where[start : start + BLOCK, None] >= -offset.astype(F32)
        allowed = (jnp.abs(offset) <= RADIUS) & jnp.where(offset >= 0, later_key, later_query)
        bias.append(jnp.where(allowed, 0.0, NEGATIVE))
    bias = jnp.concatenate(bias, axis=0).astype(F32)
    unit = jnp.arange(units, dtype=jnp.int32) % take
    mask = jnp.where(unit >= side * (2 * take - down_rows), 1.0, 0.0).astype(F32)
    mask = jnp.broadcast_to(mask, (8, units))

    qkv_parts = with_core(qkv_parts)
    qkv_names = [(j, s) for j, s, _ in qkv_parts]
    qkv_arrays = [a for _, _, a in qkv_parts]
    weight_bytes = width * 3 * width * 2

    q, k, v, p, ctx, normed, gains = call(
        project_kernel(qkv_names, rows, width, qkv_split),
        (
            shaped((3 * BLOCK, half), BF),
            shaped((4 * BLOCK, half), BF),
            shaped((4 * BLOCK, half), BF),
            shaped((3 * half // HEAD, BLOCK, 2 * BLOCK), BF),
            shaped((3 * BLOCK, half), BF),
            shaped((2 * BLOCK, width), BF),
            shaped((8, width), F32),
        ),
        (info, tok, cosine, sine, bias),
        qkv_arrays,
        [
            pltpu.VMEM((width, 3 * half), BF),
            pltpu.VMEM((width, 128), BF),
            pltpu.VMEM((4 * BLOCK, width), BF),
            pltpu.SemaphoreType.DMA((2 * len(qkv_arrays),)),
        ],
        7_000_000_000,
        weight_bytes,
    )
    ctx_other = xor_send(ctx, "replica", 1)
    normed_other = xor_send(normed, "shard", 1)
    dy_other = xor_send(dy, "shard", 1)

    mlp_parts = with_core(mlp_parts, ctx)
    mlp_names = [(j, s) for j, s, _ in mlp_parts]
    mlp_arrays = [a for _, _, a in mlp_parts]
    mix_keep, mix_send, shared, ctx_pair, hidden, gn, fgain = call(
        mlp_kernel(mlp_names, rows, take, width, units),
        (
            shaped((BLOCK, width), F32),
            shaped((BLOCK, width), BF),
            shaped((2 * BLOCK, width + 3 * units), BF),
            shaped((2 * BLOCK, width), BF),
            shaped((3 * BLOCK, width), F32),
            shaped((3 * BLOCK, width), BF),
            shaped((8, width), F32),
        ),
        (info, tok, ctx, ctx_other, dy, gains, mask),
        mlp_arrays,
        [
            pltpu.VMEM((width, width), BF),
            pltpu.VMEM((width, 2 * units), BF),
            pltpu.VMEM((units, width), BF),
            pltpu.VMEM((3 * BLOCK, 2 * units), BF),
            pltpu.VMEM((2 * BLOCK, width), F32),
            pltpu.SemaphoreType.DMA((3 * len(mlp_arrays),)),
        ],
        8_000_000_000,
        2 * weight_bytes,
    )
    gn_other = xor_send(gn, "replica", 1)
    shared_other = xor_send(shared, "shard", 1)
    ctx_pair_other = xor_send(ctx_pair, "shard", 1)

    js = [2 * i for i in range(count // 2)]
    slots = slots_of(count, chip_bits)
    portion = count // 4

    def stack(height):
        return (shaped((portion, height, 128), BF),) * 4

    height = rows * (units // 128) + take * (half // 128)
    sums = call(
        mlp_grad_kernel(js, slots, rows, take, width, units),
        stack(height),
        (info, shared, shared_other, dy, dy_other),
        [],
        [
            pltpu.VMEM((width, 4 * BLOCK), BF),
            pltpu.VMEM((units, 4 * BLOCK), BF),
            pltpu.VMEM((4 * BLOCK, 2 * units), BF),
            pltpu.VMEM((4 * BLOCK, width), BF),
        ],
        4_000_000_000,
        weight_bytes,
    )

    gj, norm_keep, norm_send, ghid = call(
        back_kernel(qkv_names, mlp_names, rows, width, qkv_split),
        (
            shaped((2 * BLOCK + 16, 4 * half), BF),
            shaped((BLOCK, width), F32),
            shaped((BLOCK, width), BF),
            shaped((BLOCK, width), F32),
        ),
        (info, tok, gn, gn_other, hidden, dy, gains, fgain, q, k, v, p, cosine, sine),
        [sums[1]] + qkv_arrays + mlp_arrays,
        [
            pltpu.VMEM((width, 3 * half), BF),
            pltpu.VMEM((width, 128), BF),
            pltpu.VMEM((width, width), BF),
            pltpu.VMEM((3 * BLOCK, half), BF),
            pltpu.VMEM((2 * BLOCK, width), F32),
            pltpu.SemaphoreType.DMA((2 * len(qkv_arrays),)),
            pltpu.SemaphoreType.DMA((len(mlp_arrays),)),
        ],
        9_000_000_000,
        weight_bytes,
    )
    mlp_sums = (
        scatter_sum(sums[0], sums[1], chip_bits, gj),
        scatter_sum(sums[2], sums[3], chip_bits[::-1], gj),
    )
    gj_other = xor_send(gj, "shard", 1)
    sums = call(
        qkv_grad_kernel(js, slots, rows, width),
        stack(6 * rows + 16),
        (info, normed, normed_other, ctx_pair, ctx_pair_other, gj, gj_other),
        [],
        [
            pltpu.VMEM((width, 4 * BLOCK), BF),
            pltpu.VMEM((width, 4 * BLOCK), BF),
            pltpu.VMEM((4 * BLOCK, 4 * half), BF),
        ],
        3_000_000_000,
        weight_bytes,
    )
    qkv_sums = (
        scatter_sum(sums[0], sums[1], chip_bits),
        scatter_sum(sums[2], sums[3], chip_bits[::-1]),
    )
    mlp_total = replica_sum(both_sums(*mlp_sums))
    qkv_total = replica_sum(both_sums(*qkv_sums))

    mix_send, norm_send, _ = lax.optimization_barrier((mix_send, norm_send, gj))
    mix_other = xor_send(mix_send, "replica", 1)
    norm_other = xor_send(norm_send, "replica", 1)
    mixed = (mix_keep + mix_other.astype(F32)).astype(BF)
    grad_tokens = call(
        final_kernel,
        shaped((block, width), BF),
        (info, tokens, norm_keep, norm_other, ghid, gains),
        [],
        [],
        1_000_000,
        1_000_000,
    )
    grad_glu, grad_down = call(
        mlp_unpack_kernel(rows, down_rows, take, width, units, count),
        (shaped((rows, 2 * count * down_rows), F32), shaped((down_rows, width), F32)),
        (info,) + mlp_total,
        [],
        [pltpu.VMEM((2, 2 * height, 128), F32), pltpu.VMEM((rows, units), F32)],
        1_000_000,
        4_000_000,
    )
    grad_qkv, grad_attn, grad_gains = call(
        qkv_unpack_kernel(rows, width),
        (shaped((rows, 3 * width), F32), shaped((rows, width), F32), shaped((8, 128), F32)),
        (info,) + qkv_total,
        [],
        [pltpu.VMEM((2, 2 * (6 * rows + 16), 128), F32)],
        1_000_000,
        4_000_000,
    )
    return (
        mixed,
        grad_tokens,
        grad_qkv,
        grad_attn,
        grad_glu,
        grad_down,
        grad_gains[0, :rows],
        grad_gains[1, :rows],
    )


def solution(mesh):
    in_specs = (
        P(("shard", "replica"), None),
        P(("shard", "replica")),
        P("shard", None),
        P("shard", None),
        P("shard", None),
        P("shard", None),
        P("shard"),
        P("shard"),
        P(("shard", "replica"), None),
    )
    out_specs = (
        P(("shard", "replica"), None),
        P(("shard", "replica"), None),
        P("shard", None),
        P("shard", None),
        P("shard", None),
        P("shard", None),
        P("shard"),
        P("shard"),
    )
    return jax.shard_map(
        on_device, mesh=mesh, in_specs=in_specs, out_specs=out_specs, check_vma=False
    )
```

time: 223 us -> 179 us (0.80)
  waiting for transfers between devices: 103 us -> 64.6 us
  starting transfers between devices: 57.7 us -> 45.2 us
  Pallas kernels: 39.9 us -> 49.3 us
  other arithmetic: 11.1 us -> 8.73 us
    ppermute x48 -> x40, waiting for transfers between devices: 101 us -> 64 us  [xor_send(): return lax.ppermute(array, axis, [(i, i ^ bit) for i in range(count)])]
    pallas_call x5 -> x11, Pallas kernels: 39.9 us -> 49.3 us  [call(): pl.pallas_call(kernel, out_shape=out_shape, in_specs=specs, out_specs=jax...]
    ppermute x48 -> x40, starting transfers between devices: 51.9 us -> 43.3 us  [xor_send(): return lax.ppermute(array, axis, [(i, i ^ bit) for i in range(count)])]
    slice x12 -> x5, local copies, waits for them, and re-layouts: 4.96 us -> 0.07 us  [the longest x2 0.03 us: gather_pieces(): pieces.append((x | y, 1, xor_send(from_y[:, split:], 'shard', x)))]
    ppermute x2, starting transfers between devices: 5.86 us -> 1.97 us  [outward(): lax.ppermute(array, both, [(a, b) for a, b in moves if 0 <= b < everyone])]
    unnamed x100 -> x84, local copies, waits for them, and re-layouts: 3.8 us -> 6.61 us
    convert_element_type x8 -> x2, other arithmetic: 4.21 us -> 1.45 us  [the longest x1 0.74 us: on_device(): mine, theirs = (positions.astype(F32), places_of(partner, 2 * block))]
  transfers between devices with their start and end apart: 50 -> 42, of which waited for: 23 -> 18; matrix products, arithmetic and copies ran while one was open for 6% -> 4% of each run, Pallas kernels for 6% -> 21%
where the time goes in v2:
time: 179 us; the launch traced here: 178 us
  waiting for transfers between devices  64.6 us (36%)
  Pallas kernels  49.3 us (28%)
  starting transfers between devices  45.2 us (25%)
  local copies, waits for them, and re-layouts  9.46 us (5%)
  other arithmetic  8.73 us (5%)
    ppermute x40, waiting for transfers between devices, xor_send(): return lax.ppermute(array, axis, [(i, i ^ bit) for i in range(count)])  64 us
    pallas_call x11, Pallas kernels, call(): pl.pallas_call(kernel, out_shape=out_shape, in_specs=specs, out_specs=jax...  49.3 us
    ppermute x40, starting transfers between devices, xor_send(): return lax.ppermute(array, axis, [(i, i ^ bit) for i in range(count)])  43.3 us
    unnamed x84, local copies, waits for them, and re-layouts  6.61 us
  transfers between devices with their start and end apart: 42, of which 18 were waited for; matrix products, arithmetic and copies ran while one was open for 4% of the time, Pallas kernels for 21%

profile of v2, /device:TPU:0, one launch (start us, length us, event | category | flops | bytes accessed | tf_op | source)
XLA Modules:
  0.0 178.4 jit_solution(10880380386397355326)
XLA Ops:
  7.4 1.8 shard_map.153.rest_0_.rest_1_
  9.2 9.3 %collective-permute-start.3 = (bf16[96,1280]{1,0:T(8,128)(2,1)}, bf16[96,1280]{1,0:T(8,128)(2,1)S(1)}, u32[]{:S(2)}, u32[]{:S(2)}) collective-permute-start(bf16[96,1280]{1,0:T(8,128)(2,1)} %shard_map.153.rest_0_.rest_1_), channel_id=1, source_target_pairs={{0,8},{4,12},{8,0},{12,4},{16,24},{20,28},{24,16},{28,20},{1,9},{5... | collective-permute-start | bytes 737288 | tf_op jit(solution)/shard_map/ppermute | solution.py:23
  18.5 1.5 collective-permute-start.4
  20.1 2.2 %shard_map.155.rest_0_.rest_11_ = bf16[96,2816]{1,0:T(8,128)(2,1)} custom-call(s32[2]{0:T(128)} %pad_add_fusion.info, bf16[96,768]{1,0:T(8,128)(2,1)} %attn.1, bf16[96,2304]{1,0:T(8,128)(2,1)} %glu.1, bf16[144,768]{1,0:T(8,128)(2,1)} %down.1), custom_call_target="tpu_custom_call" | custom-call | flops 1000000 | bytes 2000000 | tf_op jit(solution)/shard_map/pallas_call | solution.py:143
  22.3 5.4 %collective-permute-done.3.rest_1_.rest_2_ = bf16[96,1280]{1,0:T(8,128)(2,1)S(1)} collective-permute-done((bf16[96,1280]{1,0:T(8,128)(2,1)}, bf16[96,1280]{1,0:T(8,128)(2,1)S(1)}, u32[]{:S(2)}, u32[]{:S(2)}) %collective-permute-start.3) | collective-permute-done | bytes 245792 | tf_op jit(solution)/shard_map/ppermute | solution.py:23
  27.7 1.5 collective-permute-start.13
  29.2 1.6 collective-permute-start.14
  31.4 2.1 %collective-permute-start.5 = (bf16[96,640]{1,0:T(8,128)(2,1)S(1)}, bf16[96,640]{1,0:T(8,128)(2,1)S(1)}, u32[]{:S(2)}, u32[]{:S(2)}) collective-permute-start(bf16[96,640]{1,0:T(8,128)(2,1)S(1)} %slice.150), channel_id=1, source_target_pairs={{0,16},{4,20},{8,24},{12,28},{16,0},{20,4},{24,8},{28,12},{1,17},{... | collective-permute-start | bytes 368648 | tf_op jit(solution)/shard_map/ppermute | solution.py:23
  33.5 7.8 %collective-permute-done.partner = bf16[272,768]{1,0:T(8,128)(2,1)S(1)} collective-permute-done((bf16[272,768]{1,0:T(8,128)(2,1)S(1)}, bf16[272,768]{1,0:T(8,128)(2,1)S(1)}, u32[]{:S(2)}, u32[]{:S(2)}) %collective-permute-start) | collective-permute-done | bytes 417824 | tf_op jit(solution)/shard_map/ppermute | solution.py:23
  48.2 2.7 %shard_map.152 = (bf16[512,768]{1,0:T(8,128)(2,1)}, bf16[384,768]{1,0:T(8,128)(2,1)}) custom-call(s32[2]{0:T(128)} %pad_add_fusion.info, bf16[128,768]{1,0:T(8,128)(2,1)} %tok.1, bf16[128,768]{1,0:T(8,128)(2,1)} %dy_own.1, bf16[272,768]{1,0:T(8,128)(2,1)} %copy-done.5, bf16[208,768]{1,0:T(8,128)(2,1)} %copy-done.11, bf16[208,768]{1,0:T(8,128)(2,1)} %copy-done.10), custom_call_target="tpu_custom_call" | custom-call | flops 1000000 | bytes 2000000 | tf_op jit(solution)/shard_map/pallas_call | solution.py:143
  55.4 6.8 %shard_map.154 = (bf16[384,384]{1,0:T(8,128)(2,1)}, bf16[512,384]{1,0:T(8,128)(2,1)}, bf16[512,384]{1,0:T(8,128)(2,1)}, bf16[18,128,256]{2,1,0:T(8,128)(2,1)}, b...) custom-call(s32[2]{0:T(128)} %pad_add_fusion.info, bf16[512,768]{1,0:T(8,128)(2,1)} %get-tuple-element.47.tok, ...), custom_call_target="tpu_custom_call" | custom-call | flops 7000000000 | bytes 3538944 | tf_op jit(solution)/shard_map/pallas_call | solution.py:143
  62.2 1.8 %collective-permute-start.12 = (bf16[384,384]{1,0:T(8,128)(2,1)}, bf16[384,384]{1,0:T(8,128)(2,1)S(1)}, u32[]{:S(2)}, u32[]{:S(2)}) collective-permute-start(bf16[384,384]{1,0:T(8,128)(2,1)} %get-tuple-element.48.ctx_own), channel_id=1, source_target_pairs={{0,1},{1,0},{2,3},{3,2},{4,5},{5,4},{6,7},{7,6},{8,9},{9,8},{10,11... | collective-permute-start | bytes 884744 | tf_op jit(solution)/shard_map/ppermute | solution.py:23
  64.6 7.3 %collective-permute-done.12.ctx_other = bf16[384,384]{1,0:T(8,128)(2,1)S(1)} collective-permute-done((bf16[384,384]{1,0:T(8,128)(2,1)}, bf16[384,384]{1,0:T(8,128)(2,1)S(1)}, u32[]{:S(2)}, u32[]{:S(2)}) %collective-permute-start.12) | collective-permute-done | bytes 294944 | tf_op jit(solution)/shard_map/ppermute | solution.py:23
  72.9 9.5 %shard_map.156 = (f32[128,768]{1,0:T(8,128)}, bf16[128,768]{1,0:T(8,128)(2,1)}, bf16[256,2688]{1,0:T(8,128)(2,1)}, bf16[256,768]{1,0:T(8,128)(2,1)}, f32[384,768...) custom-call(s32[2]{0:T(128)} %pad_add_fusion.info, bf16[512,768]{1,0:T(8,128)(2,1)} %get-tuple-element.47.tok, ...), custom_call_target="tpu_custom_call" | custom-call | flops 8000000000 | bytes 7077888 | tf_op jit(solution)/shard_map/pallas_call | solution.py:143
  83.0 1.7 collective-permute-start.22
  88.1 4.3 %shard_map.157 = (bf16[2,720,128]{2,1,0:T(8,128)(2,1)}, bf16[2,720,128]{2,1,0:T(8,128)(2,1)}, bf16[2,720,128]{2,1,0:T(8,128)(2,1)}, bf16[2,720,128]{2,1,0:T(8,128)(2,1)}) custom-call(s32[2]{0:T(128)} %pad_add_fusion.info, bf16[256,2688]{1,0:T(8,128)(2,1)} %get-tuple-element.62.own, bf16[256,2688]{1,0:T(8,128)(2,1)} %copy-done.20, ...), custom_call_target="tpu_custom_call" | custom-call | flops 4000000000 | bytes 3538944 | tf_op jit(solution)/shard_map/pallas_call | solution.py:143
  94.1 4.4 %collective-permute-done.22.gn_other = bf16[384,768]{1,0:T(8,128)(2,1)S(1)} collective-permute-done((bf16[384,768]{1,0:T(8,128)(2,1)}, bf16[384,768]{1,0:T(8,128)(2,1)S(1)}, u32[]{:S(2)}, u32[]{:S(2)}) %collective-permute-start.22) | collective-permute-done | bytes 589856 | tf_op jit(solution)/shard_map/ppermute | solution.py:23
  99.4 11.1 %shard_map.158 = (bf16[272,1536]{1,0:T(8,128)(2,1)}, f32[128,768]{1,0:T(8,128)}, bf16[128,768]{1,0:T(8,128)(2,1)}, f32[128,768]{1,0:T(8,128)}) custom-call(s32[2]{0:T(128)} %pad_add_fusion.info, bf16[512,768]{1,0:T(8,128)(2,1)} %get-tuple-element.47.tok, bf16[384,768]{1,0:T(8,128)(2,1)} %get-tuple-element.55.gn_own, bf16[384,768]{1,0:T(8,128)(2,1)} %copy-done.23, ...), custom_call_target="tpu_custom_call" | custom-call | flops 8999999488 | bytes 3538944 | tf_op jit(solution)/shard_map/pallas_call | solution.py:143
  111.2 1.7 collective-permute-start.26
  113.6 6.1 %collective-permute-done.37 = bf16[1,720,128]{2,1,0:T(8,128)(2,1)S(1)} collective-permute-done((bf16[1,720,128]{2,1,0:T(8,128)(2,1)S(1)}, bf16[1,720,128]{2,1,0:T(8,128)(2,1)S(1)}, u32[]{:S(2)}, u32[]{:S(2)}) %collective-permute-start.37) | collective-permute-done | bytes 184352 | tf_op jit(solution)/shard_map/ppermute | solution.py:23
  122.7 3.9 %shard_map.160 = (bf16[2,592,128]{2,1,0:T(8,128)(2,1)}, bf16[2,592,128]{2,1,0:T(8,128)(2,1)}, bf16[2,592,128]{2,1,0:T(8,128)(2,1)}, bf16[2,592,128]{2,1,0:T(8,128)(2,1)}) custom-call(s32[2]{0:T(128)} %pad_add_fusion.info, bf16[256,768]{1,0:T(8,128)(2,1)} %get-tuple-element.70.normed_own, bf16[256,768]{1,0:T(8,128)(2,1)} %copy-done.29, ...), custom_call_target="tpu_custom_call" | custom-call | flops 3000000000 | bytes 3538944 | tf_op jit(solution)/shard_map/pallas_call | solution.py:143
  128.9 3.1 %collective-permute-start.40 = (bf16[1440,128]{1,0:T(8,128)(2,1)S(1)}, bf16[1440,128]{1,0:T(8,128)(2,1)S(1)}, u32[]{:S(2)}, u32[]{:S(2)}) collective-permute-start(bf16[1440,128]{1,0:T(8,128)(2,1)S(1)} %pad_maximum_fusion.2), channel_id=1, source_target_pairs={{0,2},{1,3},{2,0},{3,1},{4,6},{5,7},{6,4},{7,5},{8,10},{9,11},{10,... | collective-permute-start | bytes 1105928 | tf_op jit(solution)/shard_map/ppermute | solution.py:23
  132.0 2.8 %collective-permute-done.30 = bf16[2,592,128]{2,1,0:T(8,128)(2,1)S(1)} collective-permute-done((bf16[2,592,128]{2,1,0:T(8,128)(2,1)}, bf16[2,592,128]{2,1,0:T(8,128)(2,1)S(1)}, u32[]{:S(2)}, u32[]{:S(2)}) %collective-permute-start.30) | collective-permute-done | bytes 303136 | tf_op jit(solution)/shard_map/ppermute | solution.py:23
  137.1 3.1 %collective-permute-done.31 = bf16[1,592,128]{2,1,0:T(8,128)(2,1)S(1)} collective-permute-done((bf16[1,592,128]{2,1,0:T(8,128)(2,1)S(1)}, bf16[1,592,128]{2,1,0:T(8,128)(2,1)S(1)}, u32[]{:S(2)}, u32[]{:S(2)}) %collective-permute-start.31) | collective-permute-done | bytes 151584 | tf_op jit(solution)/shard_map/ppermute | solution.py:23
  141.6 3.8 %collective-permute-start.34 = (bf16[1184,128]{1,0:T(8,128)(2,1)S(1)}, bf16[1184,128]{1,0:T(8,128)(2,1)S(1)}, u32[]{:S(2)}, u32[]{:S(2)}) collective-permute-start(bf16[1184,128]{1,0:T(8,128)(2,1)S(1)} %pad_maximum_fusion.4), channel_id=1, source_target_pairs={{0,2},{1,3},{2,0},{3,1},{4,6},{5,7},{6,4},{7,5},{8,10},{9,11},{10,... | collective-permute-start | bytes 909320 | tf_op jit(solution)/shard_map/ppermute | solution.py:23
  145.4 9.3 %collective-permute-done.40 = bf16[1440,128]{1,0:T(8,128)(2,1)S(1)} collective-permute-done((bf16[1440,128]{1,0:T(8,128)(2,1)S(1)}, bf16[1440,128]{1,0:T(8,128)(2,1)S(1)}, u32[]{:S(2)}, u32[]{:S(2)}) %collective-permute-start.40) | collective-permute-done | bytes 368672 | tf_op jit(solution)/shard_map/ppermute | solution.py:23
  154.9 5.1 %collective-permute-done.34 = bf16[1184,128]{1,0:T(8,128)(2,1)S(1)} collective-permute-done((bf16[1184,128]{1,0:T(8,128)(2,1)S(1)}, bf16[1184,128]{1,0:T(8,128)(2,1)S(1)}, u32[]{:S(2)}, u32[]{:S(2)}) %collective-permute-start.34) | collective-permute-done | bytes 303136 | tf_op jit(solution)/shard_map/ppermute | solution.py:23
  161.5 2.2 %shard_map.159 = bf16[128,768]{1,0:T(8,128)(2,1)} custom-call(s32[2]{0:T(128)} %pad_add_fusion.info, bf16[128,768]{1,0:T(8,128)(2,1)} %tok.1, f32[128,768]{1,0:T(8,128)} %get-tuple-element.67.keep, bf16[128,768]{1,0:T(8,128)(2,1)} %copy-done.15, f32[128,768]{1,0:T(8,128)} %get-tuple-element.69.ghid, f32[8,768]{1,0:T(8,128)} %get-tuple-element.50.gains), custom_call_target="tpu_custom_call" | custom-call | flops 1000000 | bytes 1000000 | tf_op jit(solution)/shard_map/pallas_call | solution.py:143
  164.5 3.4 %collective-permute-done.41.other = bf16[1440,128]{1,0:T(8,128)(2,1)S(1)} collective-permute-done((bf16[1440,128]{1,0:T(8,128)(2,1)S(1)}, bf16[1440,128]{1,0:T(8,128)(2,1)S(1)}, u32[]{:S(2)}, u32[]{:S(2)}) %collective-permute-start.41) | collective-permute-done | bytes 368672 | tf_op jit(solution)/shard_map/ppermute | solution.py:23
  168.6 2.6 %shard_map.162 = (f32[96,2304]{1,0:T(8,128)}, f32[144,768]{1,0:T(8,128)}) custom-call(s32[2]{0:T(128)} %pad_add_fusion.info, bf16[1440,128]{1,0:T(8,128)(2,1)} %copy-done.2, bf16[1440,128]{1,0:T(8,128)(2,1)} %copy-done.7), custom_call_target="tpu_custom_call" | custom-call | flops 1000000 | bytes 4000000 | tf_op jit(solution)/shard_map/pallas_call | solution.py:143
  171.2 3.1 %collective-permute-done.35.other = bf16[1184,128]{1,0:T(8,128)(2,1)S(1)} collective-permute-done((bf16[1184,128]{1,0:T(8,128)(2,1)S(1)}, bf16[1184,128]{1,0:T(8,128)(2,1)S(1)}, u32[]{:S(2)}, u32[]{:S(2)}) %collective-permute-start.35) | collective-permute-done | bytes 303136 | tf_op jit(solution)/shard_map/ppermute | solution.py:23
  175.0 2.2 %shard_map.161 = (f32[96,2304]{1,0:T(8,128)}, f32[96,768]{1,0:T(8,128)}, f32[8,128]{1,0:T(8,128)}) custom-call(s32[2]{0:T(128)} %pad_add_fusion.info, bf16[1184,128]{1,0:T(8,128)(2,1)} %copy-done.3, bf16[1184,128]{1,0:T(8,128)(2,1)} %copy-done.14), custom_call_target="tpu_custom_call" | custom-call | flops 1000000 | bytes 4000000 | tf_op jit(solution)/shard_map/pallas_call | solution.py:143
  (188 shorter events, 41.9 us)
Async XLA Ops:
  3.4 28.0 %collective-permute-start.2 = (bf16[208,768]{1,0:T(8,128)(2,1)S(1)}, bf16[208,768]{1,0:T(8,128)(2,1)S(1)}, u32[]{:S(2)}, u32[]{:S(2)}) collective-permute-start(bf16[208,768]{1,0:T(8,128)(2,1)S(1)} %pad_maximum_fusion.3), channel_id=1, source_target_pairs={{1,3},{2,0},{3,5},{4,2},{5,7},{6,4},{7,9},{8,6},{9,11},{10,8},{11,... | collective-permute-start | bytes 958472 | tf_op jit(solution)/shard_map/ppermute | solution.py:653
  4.7 26.7 %collective-permute-start.1 = (bf16[208,768]{1,0:T(8,128)(2,1)S(1)}, bf16[208,768]{1,0:T(8,128)(2,1)S(1)}, u32[]{:S(2)}, u32[]{:S(2)}) collective-permute-start(bf16[208,768]{1,0:T(8,128)(2,1)S(1)} %pad_maximum_fusion.3), channel_id=1, source_target_pairs={{1,2},{2,1},{3,4},{4,3},{5,6},{6,5},{7,8},{8,7},{9,10},{10,9},{11,... | collective-permute-start | bytes 958472 | tf_op jit(solution)/shard_map/ppermute | solution.py:653
  9.2 18.5 %collective-permute-start.3 = (bf16[96,1280]{1,0:T(8,128)(2,1)}, bf16[96,1280]{1,0:T(8,128)(2,1)S(1)}, u32[]{:S(2)}, u32[]{:S(2)}) collective-permute-start(bf16[96,1280]{1,0:T(8,128)(2,1)} %shard_map.153.rest_0_.rest_1_), channel_id=1, source_target_pairs={{0,8},{4,12},{8,0},{12,4},{16,24},{20,28},{24,16},{28,20},{1,9},{5... | collective-permute-start | bytes 737288 | tf_op jit(solution)/shard_map/ppermute | solution.py:23
  18.5 10.7 %collective-permute-start.4 = (bf16[96,1280]{1,0:T(8,128)(2,1)}, bf16[96,1280]{1,0:T(8,128)(2,1)S(1)}, u32[]{:S(2)}, u32[]{:S(2)}) collective-permute-start(bf16[96,1280]{1,0:T(8,128)(2,1)} %shard_map.153.rest_0_.rest_1_), channel_id=1, source_target_pairs={{0,16},{4,20},{8,24},{12,28},{16,0},{20,4},{24,8},{28,12},{1,17},{... | collective-permute-start | bytes 737288 | tf_op jit(solution)/shard_map/ppermute | solution.py:23
  20.1 31.6 %collective-permute-start.7 = (bf16[96,1280]{1,0:T(8,128)(2,1)}, bf16[96,1280]{1,0:T(8,128)(2,1)S(1)}, u32[]{:S(2)}, u32[]{:S(2)}) collective-permute-start(bf16[96,1280]{1,0:T(8,128)(2,1)} %shard_map.153.rest_0_.rest_1_), channel_id=1, source_target_pairs={{0,4},{4,0},{8,12},{12,8},{16,20},{20,16},{24,28},{28,24},{1,5},{5... | collective-permute-start | bytes 737288 | tf_op jit(solution)/shard_map/ppermute | solution.py:23
  27.7 18.5 %collective-permute-start.13 = (bf16[96,2816]{1,0:T(8,128)(2,1)}, bf16[96,2816]{1,0:T(8,128)(2,1)S(1)}, u32[]{:S(2)}, u32[]{:S(2)}) collective-permute-start(bf16[96,2816]{1,0:T(8,128)(2,1)} %shard_map.155.rest_0_.rest_11_), channel_id=1, source_target_pairs={{0,8},{4,12},{8,0},{12,4},{16,24},{20,28},{24,16},{28,20},{1,9},{5... | collective-permute-start | bytes 1622024 | tf_op jit(solution)/shard_map/ppermute | solution.py:23
  29.2 17.5 %collective-permute-start.14 = (bf16[96,2816]{1,0:T(8,128)(2,1)}, bf16[96,2816]{1,0:T(8,128)(2,1)S(1)}, u32[]{:S(2)}, u32[]{:S(2)}) collective-permute-start(bf16[96,2816]{1,0:T(8,128)(2,1)} %shard_map.155.rest_0_.rest_11_), channel_id=1, source_target_pairs={{0,16},{4,20},{8,24},{12,28},{16,0},{20,4},{24,8},{28,12},{1,17},{... | collective-permute-start | bytes 1622024 | tf_op jit(solution)/shard_map/ppermute | solution.py:23
  31.4 10.0 %collective-permute-start = (bf16[272,768]{1,0:T(8,128)(2,1)S(1)}, bf16[272,768]{1,0:T(8,128)(2,1)S(1)}, u32[]{:S(2)}, u32[]{:S(2)}) collective-permute-start(bf16[272,768]{1,0:T(8,128)(2,1)S(1)} %pad_maximum_fusion), channel_id=1, source_target_pairs={{0,1},{1,0},{2,3},{3,2},{4,5},{5,4},{6,7},{7,6},{8,9},{9,8},{10,11... | collective-permute-start | bytes 1253384 | tf_op jit(solution)/shard_map/ppermute | solution.py:23
  31.4 13.6 %collective-permute-start.5 = (bf16[96,640]{1,0:T(8,128)(2,1)S(1)}, bf16[96,640]{1,0:T(8,128)(2,1)S(1)}, u32[]{:S(2)}, u32[]{:S(2)}) collective-permute-start(bf16[96,640]{1,0:T(8,128)(2,1)S(1)} %slice.150), channel_id=1, source_target_pairs={{0,16},{4,20},{8,24},{12,28},{16,0},{20,4},{24,8},{28,12},{1,17},{... | collective-permute-start | bytes 368648 | tf_op jit(solution)/shard_map/ppermute | solution.py:23
  45.0 9.6 %collective-permute-start.8 = (bf16[96,1280]{1,0:T(8,128)(2,1)S(1)}, bf16[96,1280]{1,0:T(8,128)(2,1)S(1)}, u32[]{:S(2)}, u32[]{:S(2)}) collective-permute-start(bf16[96,1280]{1,0:T(8,128)(2,1)S(1)} %collective-permute-done.3.rest_1_.rest_2_), channel_id=1, source_target_pairs={{0,4},{4,0},{8,12},{12,8},{16,20},{20,16},{24,28},{28,24},{1,5},{5... | collective-permute-start | bytes 737288 | tf_op jit(solution)/shard_map/ppermute | solution.py:23
  46.3 8.4 %collective-permute-start.9 = (bf16[96,1280]{1,0:T(8,128)(2,1)S(1)}, bf16[96,1280]{1,0:T(8,128)(2,1)S(1)}, u32[]{:S(2)}, u32[]{:S(2)}) collective-permute-start(bf16[96,1280]{1,0:T(8,128)(2,1)S(1)} %collective-permute-done.4.rest_2_.rest_3_), channel_id=1, source_target_pairs={{0,4},{4,0},{8,12},{12,8},{16,20},{20,16},{24,28},{28,24},{1,5},{5... | collective-permute-start | bytes 737288 | tf_op jit(solution)/shard_map/ppermute | solution.py:23
  51.7 12.5 %collective-permute-start.17 = (bf16[96,2816]{1,0:T(8,128)(2,1)S(1)}, bf16[96,2816]{1,0:T(8,128)(2,1)S(1)}, u32[]{:S(2)}, u32[]{:S(2)}) collective-permute-start(bf16[96,2816]{1,0:T(8,128)(2,1)S(1)} %copy-done.4), channel_id=1, source_target_pairs={{0,4},{4,0},{8,12},{12,8},{16,20},{20,16},{24,28},{28,24},{1,5},{5... | collective-permute-start | bytes 1622024 | tf_op jit(solution)/shard_map/ppermute | solution.py:23
  52.2 10.0 %collective-permute-start.15 = (bf16[96,1408]{1,0:T(8,128)(2,1)S(1)}, bf16[96,1408]{1,0:T(8,128)(2,1)S(1)}, u32[]{:S(2)}, u32[]{:S(2)}) collective-permute-start(bf16[96,1408]{1,0:T(8,128)(2,1)S(1)} %slice.152), channel_id=1, source_target_pairs={{0,16},{4,20},{8,24},{12,28},{16,0},{20,4},{24,8},{28,12},{1,17},{... | collective-permute-start | bytes 811016 | tf_op jit(solution)/shard_map/ppermute | solution.py:23
  53.4 10.6 %collective-permute-start.16 = (bf16[96,1408]{1,0:T(8,128)(2,1)S(1)}, bf16[96,1408]{1,0:T(8,128)(2,1)}, u32[]{:S(2)}, u32[]{:S(2)}) collective-permute-start(bf16[96,1408]{1,0:T(8,128)(2,1)S(1)} %slice.153), channel_id=1, source_target_pairs={{0,8},{4,12},{8,0},{12,4},{16,24},{20,28},{24,16},{28,20},{1,9},{5... | collective-permute-start | bytes 811016 | tf_op jit(solution)/shard_map/ppermute | solution.py:23
  54.6 17.3 %collective-permute-start.18 = (bf16[96,2816]{1,0:T(8,128)(2,1)S(1)}, bf16[96,2816]{1,0:T(8,128)(2,1)S(1)}, u32[]{:S(2)}, u32[]{:S(2)}) collective-permute-start(bf16[96,2816]{1,0:T(8,128)(2,1)S(1)} %collective-permute-done.13.rest_1_.rest_12_), channel_id=1, source_target_pairs={{0,4},{4,0},{8,12},{12,8},{16,20},{20,16},{24,28},{28,24},{1,5},{5... | collective-permute-start | bytes 1622024 | tf_op jit(solution)/shard_map/ppermute | solution.py:23
  54.7 17.2 %collective-permute-start.19 = (bf16[96,2816]{1,0:T(8,128)(2,1)S(1)}, bf16[96,2816]{1,0:T(8,128)(2,1)}, u32[]{:S(2)}, u32[]{:S(2)}) collective-permute-start(bf16[96,2816]{1,0:T(8,128)(2,1)S(1)} %collective-permute-done.14.rest_2_.rest_13_), channel_id=1, source_target_pairs={{0,4},{4,0},{8,12},{12,8},{16,20},{20,16},{24,28},{28,24},{1,5},{5... | collective-permute-start | bytes 1622024 | tf_op jit(solution)/shard_map/ppermute | solution.py:23
  62.2 9.7 %collective-permute-start.12 = (bf16[384,384]{1,0:T(8,128)(2,1)}, bf16[384,384]{1,0:T(8,128)(2,1)S(1)}, u32[]{:S(2)}, u32[]{:S(2)}) collective-permute-start(bf16[384,384]{1,0:T(8,128)(2,1)} %get-tuple-element.48.ctx_own), channel_id=1, source_target_pairs={{0,1},{1,0},{2,3},{3,2},{4,5},{5,4},{6,7},{7,6},{8,9},{9,8},{10,11... | collective-permute-start | bytes 884744 | tf_op jit(solution)/shard_map/ppermute | solution.py:23
  64.0 7.9 %collective-permute-start.20 = (bf16[96,1408]{1,0:T(8,128)(2,1)S(1)}, bf16[96,1408]{1,0:T(8,128)(2,1)S(1)}, u32[]{:S(2)}, u32[]{:S(2)}) collective-permute-start(bf16[96,1408]{1,0:T(8,128)(2,1)S(1)} %collective-permute-done.15.rest_3_.rest_14_), channel_id=1, source_target_pairs={{0,4},{4,0},{8,12},{12,8},{16,20},{20,16},{24,28},{28,24},{1,5},{5... | collective-permute-start | bytes 811016 | tf_op jit(solution)/shard_map/ppermute | solution.py:23
  83.0 15.5 %collective-permute-start.22 = (bf16[384,768]{1,0:T(8,128)(2,1)}, bf16[384,768]{1,0:T(8,128)(2,1)S(1)}, u32[]{:S(2)}, u32[]{:S(2)}) collective-permute-start(bf16[384,768]{1,0:T(8,128)(2,1)} %get-tuple-element.55.gn_own), channel_id=1, source_target_pairs={{0,1},{1,0},{2,3},{3,2},{4,5},{5,4},{6,7},{7,6},{8,9},{9,8},{10,11... | collective-permute-start | bytes 1769480 | tf_op jit(solution)/shard_map/ppermute | solution.py:23
  92.4 18.7 %collective-permute-start.36 = (bf16[2,720,128]{2,1,0:T(8,128)(2,1)}, bf16[2,720,128]{2,1,0:T(8,128)(2,1)S(1)}, u32[]{:S(2)}, u32[]{:S(2)}) collective-permute-start(bf16[2,720,128]{2,1,0:T(8,128)(2,1)} %get-tuple-element.78), channel_id=1, source_target_pairs={{0,8},{4,12},{8,0},{12,4},{16,24},{20,28},{24,16},{28,20},{1,9},{5... | collective-permute-start | bytes 1105928 | tf_op jit(solution)/shard_map/ppermute | solution.py:23
  93.3 19.6 %collective-permute-start.38 = (bf16[2,720,128]{2,1,0:T(8,128)(2,1)}, bf16[2,720,128]{2,1,0:T(8,128)(2,1)S(1)}, u32[]{:S(2)}, u32[]{:S(2)}) collective-permute-start(bf16[2,720,128]{2,1,0:T(8,128)(2,1)} %get-tuple-element.81), channel_id=1, source_target_pairs={{0,16},{4,20},{8,24},{12,28},{16,0},{20,4},{24,8},{28,12},{1,17},{... | collective-permute-start | bytes 1105928 | tf_op jit(solution)/shard_map/ppermute | solution.py:23
  110.5 10.6 %collective-permute-start.29 = (bf16[272,1536]{1,0:T(8,128)(2,1)}, bf16[272,1536]{1,0:T(8,128)(2,1)S(1)}, u32[]{:S(2)}, u32[]{:S(2)}) collective-permute-start(bf16[272,1536]{1,0:T(8,128)(2,1)} %get-tuple-element.65.own), channel_id=1, source_target_pairs={{0,4},{4,0},{8,12},{12,8},{16,20},{20,16},{24,28},{28,24},{1,5},{5... | collective-permute-start | bytes 2506760 | tf_op jit(solution)/shard_map/ppermute | solution.py:23
  110.6 9.5 %collective-permute-start.27 = (bf16[256,768]{1,0:T(8,128)(2,1)S(1)}, bf16[256,768]{1,0:T(8,128)(2,1)S(1)}, u32[]{:S(2)}, u32[]{:S(2)}) collective-permute-start(bf16[256,768]{1,0:T(8,128)(2,1)S(1)} %copy-done.27), channel_id=1, source_target_pairs={{0,4},{4,0},{8,12},{12,8},{16,20},{20,16},{24,28},{28,24},{1,5},{5... | collective-permute-start | bytes 1179656 | tf_op jit(solution)/shard_map/ppermute | solution.py:23
  111.1 10.0 %collective-permute-start.28 = (bf16[256,768]{1,0:T(8,128)(2,1)S(1)}, bf16[256,768]{1,0:T(8,128)(2,1)S(1)}, u32[]{:S(2)}, u32[]{:S(2)}) collective-permute-start(bf16[256,768]{1,0:T(8,128)(2,1)S(1)} %copy-done.28), channel_id=1, source_target_pairs={{0,4},{4,0},{8,12},{12,8},{16,20},{20,16},{24,28},{28,24},{1,5},{5... | collective-permute-start | bytes 1179656 | tf_op jit(solution)/shard_map/ppermute | solution.py:23
  111.2 49.6 %collective-permute-start.26 = (bf16[128,768]{1,0:T(8,128)(2,1)}, bf16[128,768]{1,0:T(8,128)(2,1)S(1)}, u32[]{:S(2)}, u32[]{:S(2)}) collective-permute-start(bf16[128,768]{1,0:T(8,128)(2,1)} %get-tuple-element.68), channel_id=1, source_target_pairs={{0,1},{1,0},{2,3},{3,2},{4,5},{5,4},{6,7},{7,6},{8,9},{9,8},{10,11... | collective-permute-start | bytes 589832 | tf_op jit(solution)/shard_map/ppermute | solution.py:23
  119.7 44.0 %collective-permute-start.25 = (bf16[128,768]{1,0:T(8,128)(2,1)S(1)}, bf16[128,768]{1,0:T(8,128)(2,1)S(1)}, u32[]{:S(2)}, u32[]{:S(2)}) collective-permute-start(bf16[128,768]{1,0:T(8,128)(2,1)S(1)} %copy-done.37), channel_id=1, source_target_pairs={{0,1},{1,0},{2,3},{3,2},{4,5},{5,4},{6,7},{7,6},{8,9},{9,8},{10,11... | collective-permute-start | bytes 589832 | tf_op jit(solution)/shard_map/ppermute | solution.py:23
  126.7 8.1 %collective-permute-start.30 = (bf16[2,592,128]{2,1,0:T(8,128)(2,1)}, bf16[2,592,128]{2,1,0:T(8,128)(2,1)S(1)}, u32[]{:S(2)}, u32[]{:S(2)}) collective-permute-start(bf16[2,592,128]{2,1,0:T(8,128)(2,1)} %get-tuple-element.73), channel_id=1, source_target_pairs={{0,8},{4,12},{8,0},{12,4},{16,24},{20,28},{24,16},{28,20},{1,9},{5... | collective-permute-start | bytes 909320 | tf_op jit(solution)/shard_map/ppermute | solution.py:23
  128.0 8.2 %collective-permute-start.32 = (bf16[2,592,128]{2,1,0:T(8,128)(2,1)}, bf16[2,592,128]{2,1,0:T(8,128)(2,1)S(1)}, u32[]{:S(2)}, u32[]{:S(2)}) collective-permute-start(bf16[2,592,128]{2,1,0:T(8,128)(2,1)} %get-tuple-element.75), channel_id=1, source_target_pairs={{0,16},{4,20},{8,24},{12,28},{16,0},{20,4},{24,8},{28,12},{1,17},{... | collective-permute-start | bytes 909320 | tf_op jit(solution)/shard_map/ppermute | solution.py:23
  128.9 25.8 %collective-permute-start.40 = (bf16[1440,128]{1,0:T(8,128)(2,1)S(1)}, bf16[1440,128]{1,0:T(8,128)(2,1)S(1)}, u32[]{:S(2)}, u32[]{:S(2)}) collective-permute-start(bf16[1440,128]{1,0:T(8,128)(2,1)S(1)} %pad_maximum_fusion.2), channel_id=1, source_target_pairs={{0,2},{1,3},{2,0},{3,1},{4,6},{5,7},{6,4},{7,5},{8,10},{9,11},{10,... | collective-permute-start | bytes 1105928 | tf_op jit(solution)/shard_map/ppermute | solution.py:23
  141.6 18.4 %collective-permute-start.34 = (bf16[1184,128]{1,0:T(8,128)(2,1)S(1)}, bf16[1184,128]{1,0:T(8,128)(2,1)S(1)}, u32[]{:S(2)}, u32[]{:S(2)}) collective-permute-start(bf16[1184,128]{1,0:T(8,128)(2,1)S(1)} %pad_maximum_fusion.4), channel_id=1, source_target_pairs={{0,2},{1,3},{2,0},{3,1},{4,6},{5,7},{6,4},{7,5},{8,10},{9,11},{10,... | collective-permute-start | bytes 909320 | tf_op jit(solution)/shard_map/ppermute | solution.py:23
  154.8 13.0 %collective-permute-start.41 = (bf16[1440,128]{1,0:T(8,128)(2,1)S(1)}, bf16[1440,128]{1,0:T(8,128)(2,1)S(1)}, u32[]{:S(2)}, u32[]{:S(2)}) collective-permute-start(bf16[1440,128]{1,0:T(8,128)(2,1)S(1)} %add_convert_fusion.mine), channel_id=1, source_target_pairs={{0,1},{1,0},{2,3},{3,2},{4,5},{5,4},{6,7},{7,6},{8,9},{9,8},{10,11... | collective-permute-start | bytes 1105928 | tf_op jit(solution)/shard_map/ppermute | solution.py:23
  160.1 14.2 %collective-permute-start.35 = (bf16[1184,128]{1,0:T(8,128)(2,1)S(1)}, bf16[1184,128]{1,0:T(8,128)(2,1)S(1)}, u32[]{:S(2)}, u32[]{:S(2)}) collective-permute-start(bf16[1184,128]{1,0:T(8,128)(2,1)S(1)} %add_convert_fusion.1.mine), channel_id=1, source_target_pairs={{0,1},{1,0},{2,3},{3,2},{4,5},{5,4},{6,7},{7,6},{8,9},{9,8},{10,11... | collective-permute-start | bytes 909320 | tf_op jit(solution)/shard_map/ppermute | solution.py:23
  (52 other events, 374.5 us)

commit v3 on v2

v3 whole, which is shorter than its diff:
```python
import math

import jax
import jax.numpy as jnp
from jax import lax
from jax.experimental import pallas as pl
from jax.experimental.pallas import tpu as pltpu
from jax.sharding import PartitionSpec as P

HEAD = 64
RADIUS = 64
BLOCK = 128
EPSILON = 1e-05
THETA_BASE = 10000.0
NEGATIVE = -1e30
VMEM_BYTES = 56 * 1024 * 1024
BF = jnp.bfloat16
F32 = jnp.float32


def xor_send(array, axis, bit):
    count = lax.axis_size(axis)
    return lax.ppermute(array, axis, [(i, i ^ bit) for i in range(count)])


def bits_of(count):
    return [1 << i for i in range(count.bit_length() - 1)]


def gather_pieces(own, split, chip_bits, before):
    if len(chip_bits) == 2:
        x, y = chip_bits
        from_x, from_y = xor_send(own, "shard", x), xor_send(own, "shard", y)
        (from_x, from_y), before = lax.optimization_barrier(((from_x, from_y), before))
        pieces = [(0, 2, own), (x, 2, from_x), (y, 2, from_y)]
        pieces.append((x | y, 0, xor_send(from_x[:, :split], "shard", y)))
        pieces.append((x | y, 1, xor_send(from_y[:, split:], "shard", x)))
    else:
        streams = ([(0, 0, own[:, :split])], [(0, 1, own[:, split:])])
        for stage in range(len(chip_bits)):
            grown = []
            for which, bit in ((0, chip_bits[stage]), (1, chip_bits[-1 - stage])):
                grown.append(
                    [(j ^ bit, s, xor_send(a, "shard", bit)) for j, s, a in streams[which]]
                )
            for held, more in zip(streams, grown):
                held.extend(more)
        pieces = streams[0] + streams[1]
    return pieces, before


def with_core(pieces, after=None):
    rows = pieces[0][2].shape[0]
    arrays = [a for _, _, a in pieces]
    names = [(j, s, i, 0) for i, (j, s, _) in enumerate(pieces)]
    whole = [p for p in pieces if p[1] == 2]
    if whole:
        arrays.append(xor_send(jnp.concatenate([a for _, _, a in whole], axis=0), "shard", 1))
        names += [(p[0] ^ 1, 2, len(arrays) - 1, i * rows) for i, p in enumerate(whole)]
    for j, s, a in pieces[len(whole) :]:
        if after is not None:
            a, _ = lax.optimization_barrier((a, after))
        arrays.append(xor_send(a, "shard", 1))
        names.append((j ^ 1, s, len(arrays) - 1, 0))
    return names, arrays


def add_low(left, right):
    return (left.astype(F32) + right.astype(F32)).astype(BF)


def halve(keep, other):
    middle = keep.shape[0] // 2
    return add_low(keep[middle:], other[middle:]), add_low(keep[:middle], other[:middle])


def scatter_sums(sums, chip_bits, before_add=None, before_last=None):
    send, keep = [sums[0], sums[2]], [sums[1], sums[3]]
    orders = (chip_bits, chip_bits[::-1])
    for step in range(len(chip_bits) - 1):
        others = [xor_send(send[s], "shard", orders[s][step]) for s in range(2)]
        if before_add is not None:
            others, _ = lax.optimization_barrier((others, before_add))
        for s in range(2):
            send[s], keep[s] = halve(keep[s], others[s])
        if before_last is not None:
            send, _ = lax.optimization_barrier((send, before_last))
    return [
        (keep[s], xor_send(send[s], "shard", orders[s][-1]), send[s]) for s in range(2)
    ]


def last_sum(stream):
    keep, other, _ = stream
    return add_low(keep[0], other[0])


def side_sum(total, after=None):
    for bit in bits_of(lax.axis_size("replica"))[1:]:
        other = xor_send(total, "replica", bit)
        if after is not None:
            other, _ = lax.optimization_barrier((other, after))
        total = add_low(total, other)
    return total


def dot(left, right):
    return jnp.dot(left, right, preferred_element_type=F32)


def dot_cols(left, right):
    return lax.dot_general(left, right, (((1,), (1,)), ((), ())), preferred_element_type=F32)


def dot_rows(left, right):
    return lax.dot_general(left, right, (((0,), (0,)), ((), ())), preferred_element_type=F32)


def standardize(vector):
    average = jnp.mean(vector, axis=-1, keepdims=True)
    centred = vector - average
    spread = jnp.mean(centred * centred, axis=-1, keepdims=True)
    inverse = lax.rsqrt(spread + EPSILON)
    return centred * inverse, inverse


def norm_back(grad, gain, hat, inverse):
    dhat = grad * gain
    mean = jnp.mean(dhat, axis=-1, keepdims=True)
    along = jnp.mean(dhat * hat, axis=-1, keepdims=True)
    return (dhat - mean - hat * along) * inverse


def turned(vector):
    width = vector.shape[-1]
    lane = lax.broadcasted_iota(jnp.int32, vector.shape, 1)
    return jnp.where(
        (lane & 63) < 32, pltpu.roll(vector, width - 32, 1), pltpu.roll(vector, 32, 1)
    )


def place(me, pieces, refs, layout, sems):
    copies = []
    for j, stream, which, base in pieces:
        owner = me ^ j
        ref = refs[which]
        for row, rows, col, cols, dst, dst_col in layout[stream]:
            start = owner * rows
            if rows % 16 == 0:
                start = pl.multiple_of(start, 16)
            copy = pltpu.make_async_copy(
                ref.at[pl.ds(base + row, rows), pl.ds(col, cols)],
                dst.at[pl.ds(start, rows), pl.ds(dst_col, cols)],
                sems.at[len(copies)],
            )
            copy.start()
            copies.append(copy)
    return copies


def call(kernel, out_shape, inputs, in_any, scratch, flops, traffic):
    any_spec = pl.BlockSpec(memory_space=pl.ANY)
    vmem = pl.BlockSpec(memory_space=pltpu.VMEM)
    specs = [vmem] * len(inputs) + [any_spec] * len(in_any)
    return pl.pallas_call(
        kernel,
        out_shape=out_shape,
        in_specs=specs,
        out_specs=jax.tree.map(lambda _: vmem, out_shape),
        scratch_shapes=scratch,
        compiler_params=pltpu.CompilerParams(vmem_limit_bytes=VMEM_BYTES),
        cost_estimate=pl.CostEstimate(flops=flops, bytes_accessed=traffic, transcendentals=0),
    )(*inputs, *in_any)


def shard_at():
    return lax.axis_index("shard").astype(jnp.int32)


def side_at():
    return lax.axis_index("replica").astype(jnp.int32) & 1


def shaped(shape, dtype):
    return jax.ShapeDtypeStruct(shape, dtype)


def pack_kernel(count, down_rows, take):
    def body(qkv, attn, glu, down, attn_gain, ffn_gain, out):
        rows, width = attn.shape
        half = width // 2
        units = count * take
        hidden = count * down_rows
        first = 3 * half + 128
        middle = first + width
        last = middle + 2 * units

        def pick(side):
            for i in range(3):
                at = i * width + side * half
                out[:, i * half : (i + 1) * half] = qkv[:, at : at + half]
            skip = side * (down_rows - take)
            for part in range(2):
                for s in range(count):
                    at = part * hidden + s * down_rows + skip
                    to = middle + part * units + s * take
                    out[:, to : to + take] = glu[:, at : at + take]
            out[0:take, last:] = down[skip : skip + take, :]

        @pl.when(side_at() == 0)
        def _():
            pick(0)

        @pl.when(side_at() != 0)
        def _():
            pick(1)

        out[:, first:middle] = attn[...]
        if rows > take:
            out[take:, last:] = jnp.zeros((rows - take, width), BF)
        gains = [ref[...].astype(F32) for ref in (attn_gain, ffn_gain)]
        gains = jnp.concatenate(gains + [jnp.zeros((6, rows), F32)], axis=0)
        gains = jnp.concatenate([gains, jnp.zeros((8, 128 - rows), F32)], axis=1)
        square = jnp.concatenate([gains, jnp.zeros((120, 128), F32)], axis=0)
        out[:, 3 * half : first] = square.T[0:rows, :].astype(BF)

    return body


def around_kernel(own, dy_own, partner, near, far, tok, dy):
    mine = slice(0, BLOCK)

    def arrange(first, first_dy, second, second_dy, before, after):
        tok[0:BLOCK, :] = before[mine, :]
        tok[BLOCK : 2 * BLOCK, :] = first
        tok[2 * BLOCK : 3 * BLOCK, :] = second
        tok[3 * BLOCK :, :] = after[mine, :]
        halo = slice(BLOCK, BLOCK + RADIUS)
        dy[0:RADIUS, :] = before[halo, :]
        dy[RADIUS : RADIUS + BLOCK, :] = first_dy
        dy[RADIUS + BLOCK : RADIUS + 2 * BLOCK, :] = second_dy
        dy[RADIUS + 2 * BLOCK :, :] = after[halo, :]

    other = partner[mine, :]
    other_dy = partner[BLOCK : 2 * BLOCK, :]

    @pl.when(side_at() == 0)
    def _():
        arrange(own[...], dy_own[...], other, other_dy, near, far)

    @pl.when(side_at() != 0)
    def _():
        arrange(other, other_dy, own[...], dy_own[...], far, near)


def qkv_layout(rows, half, weight, gains=None):
    parts = [(0, rows, 0, 3 * half, weight, 0)]
    if gains is not None:
        parts.append((0, rows, 3 * half, 128, gains, 0))
    return (parts, (), parts)


def project_kernel(pieces, n_refs, rows, width):
    half = width // 2
    span = 4 * BLOCK

    def body(tok, cosine, sine, bias, *rest):
        refs, rest = rest[:n_refs], rest[n_refs:]
        q_out, k_out, v_out, p_out, ctx_out, normed_out, gains_out = rest[:7]
        weight, gain_cols, normed, sems = rest[7:]
        layout = qkv_layout(rows, half, weight, gain_cols)
        copies = place(shard_at(), pieces, refs, layout, sems)
        hats = [
            standardize(tok[i * BLOCK : (i + 1) * BLOCK, :].astype(F32))[0] for i in range(4)
        ]
        for copy in copies:
            copy.wait()
        pick = jnp.where(
            lax.broadcasted_iota(jnp.int32, (8, 128), 0)
            == lax.broadcasted_iota(jnp.int32, (8, 128), 1),
            1.0,
            0.0,
        ).astype(BF)
        gains = dot_cols(pick, gain_cols[...])
        gains_out[...] = gains
        for i, hat in enumerate(hats):
            normed[i * BLOCK : (i + 1) * BLOCK, :] = (hat * gains[0:1]).astype(BF)
        normed_out[...] = normed[BLOCK : 3 * BLOCK, :]
        cos3 = jnp.concatenate([cosine[...]] * 3, axis=1)
        sin3 = jnp.concatenate([sine[...]] * 3, axis=1)
        mid = slice(RADIUS, span - RADIUS)
        joined = dot(normed[mid, :], weight[:, 0:half])
        q_out[...] = (joined * cos3[mid] + turned(joined) * sin3[mid]).astype(BF)
        joined = dot(normed[...], weight[:, half : 2 * half])
        k_out[...] = (joined * cos3 + turned(joined) * sin3).astype(BF)
        v_out[...] = dot(normed[...], weight[:, 2 * half : 3 * half]).astype(BF)
        lane = lax.broadcasted_iota(jnp.int32, (BLOCK, 128), 1)
        scale = 1.0 / math.sqrt(HEAD)
        for pair in range(half // 128):
            cols = slice(pair * 128, pair * 128 + 128)
            for b in range(3):
                rows_q = slice(b * BLOCK, (b + 1) * BLOCK)
                rows_k = slice(b * BLOCK, (b + 2) * BLOCK)
                queries, keys, values = q_out[rows_q, cols], k_out[rows_k, cols], v_out[rows_k, cols]
                parts = []
                for h in range(2):
                    mine = (lane < HEAD) if h == 0 else (lane >= HEAD)
                    masked = jnp.where(mine, queries.astype(F32) * scale, 0.0).astype(BF)
                    scores = dot_cols(masked, keys) + bias[rows_q, :]
                    exponent = jnp.exp(scores - jnp.max(scores, axis=1, keepdims=True))
                    total = jnp.sum(exponent, axis=1, keepdims=True)
                    shares = (exponent * (1.0 / total)).astype(BF)
                    p_out[(pair * 2 + h) * 3 + b] = shares
                    parts.append(dot(shares, values))
                ctx_out[rows_q, cols] = jnp.where(lane < HEAD, parts[0], parts[1]).astype(BF)

    return body


def attn_layout(rows, width, attn):
    parts = [(0, rows, 3 * width // 2 + 128, width, attn, 0)]
    return (parts, (), parts)


def mlp_layout(rows, take, width, units, attn, glu, down):
    split = 3 * width // 2 + 128 + width
    first = attn_layout(rows, width, attn)[0]
    streams = [first]
    for start in (0, split):
        parts = [(0, rows, start, 2 * units, glu, 0)]
        parts.append((0, take, start + 2 * units, width, down, 0))
        streams.append(parts if start == 0 else first + parts)
    return streams


def mlp_kernel(pieces, n_refs, rows, down_rows, take, width, units):
    half = width // 2
    pair = slice(RADIUS, RADIUS + 2 * BLOCK)

    def body(tok, ctx_own, ctx_other, dy, gains, *rest):
        refs, rest = rest[2 : n_refs + 2], rest[n_refs + 2 :]
        mix_keep, mix_send, shared, ctx_pair, hidden, gn_out = rest[:6]
        attn, glu, down, ggu, mix, sems = rest[6:]
        layout = mlp_layout(rows, take, width, units, attn, glu, down)
        copies = place(shard_at(), pieces, refs, layout, sems)
        at = side_at()
        inputs = tok[RADIUS : RADIUS + 3 * BLOCK, :].astype(F32)
        own_rows = pl.ds(pl.multiple_of(at * half, 128), half)
        other_rows = pl.ds(pl.multiple_of((1 - at) * half, 128), half)

        @pl.when(at == 0)
        def _():
            ctx_pair[:, 0:half] = ctx_own[pair, :]
            ctx_pair[:, half:] = ctx_other[pair, :]

        @pl.when(at != 0)
        def _():
            ctx_pair[:, 0:half] = ctx_other[pair, :]
            ctx_pair[:, half:] = ctx_own[pair, :]

        for copy in copies:
            copy.wait()
        lifted = dot(ctx_own[...], attn[own_rows, :]) + dot(ctx_other[...], attn[other_rows, :])
        hidden[...] = inputs + lifted
        hat, _ = standardize(hidden[...])
        normed = (hat * gains[1:2, :]).astype(BF)
        shared[:, 0:width] = normed[pair]
        partial = jnp.zeros((2 * BLOCK, width), F32)
        unit = lax.rem(lax.broadcasted_iota(jnp.int32, (1, units), 1), take)
        mask = jnp.where(unit >= at * (2 * take - down_rows), 1.0, 0.0)
        for c in range(0, units, 256):
            wide = min(256, units - c)
            cols = slice(c, c + wide)
            gate = dot(normed, glu[:, cols])
            up = dot(normed, glu[:, units + c : units + c + wide])
            grad_act = dot_cols(dy[...], down[cols, :]) * mask[:, cols]
            share = 0.5 * (1.0 + lax.erf(gate * (1.0 / math.sqrt(2.0))))
            density = jnp.exp(-0.5 * gate * gate) * (1.0 / math.sqrt(2.0 * math.pi))
            gelu = gate * share
            act = (gelu[pair] * up[pair] * mask[:, cols]).astype(BF)
            shared[:, width + c : width + c + wide] = act
            partial = partial + dot(act, down[cols, :])
            ggu[:, cols] = (grad_act * up * (share + gate * density)).astype(BF)
            ggu[:, units + c : units + c + wide] = (grad_act * gelu).astype(BF)
        mix[...] = partial
        mine = pl.ds(pl.multiple_of(at * BLOCK, BLOCK), BLOCK)
        theirs = pl.ds(pl.multiple_of((1 - at) * BLOCK, BLOCK), BLOCK)
        mix_keep[...] = mix[mine, :] + hidden[pl.ds(pl.multiple_of(RADIUS + at * BLOCK, 8), BLOCK), :]
        mix_send[...] = mix[theirs, :].astype(BF)
        shared[:, width + units :] = ggu[pair, :]
        grad = dot_cols(ggu[...], glu[...])
        gn_out[...] = grad.astype(BF)

    return body


def pair_back(pair, gctx, q, k, v, p, cos, sin):
    lane = lax.broadcasted_iota(jnp.int32, (BLOCK, 128), 1)
    lane2 = lax.broadcasted_iota(jnp.int32, (2 * BLOCK, 128), 1)
    scale = 1.0 / math.sqrt(HEAD)
    cols = slice(pair * 128, pair * 128 + 128)
    first, second = slice(0, BLOCK), slice(BLOCK, 2 * BLOCK)
    low, high = slice(0, RADIUS), slice(RADIUS, BLOCK)
    grad_q = jnp.zeros((2 * BLOCK, 128), F32)
    grad_k, grad_v = [0.0, 0.0], [0.0, 0.0]
    for h in range(2):
        mine = (lane < HEAD) if h == 0 else (lane >= HEAD)
        mine2 = (lane2 < HEAD) if h == 0 else (lane2 >= HEAD)
        scores, shares, queries, grads, parts = [], [], [], [], []
        for b in range(3):
            rows_q = slice(b * BLOCK, (b + 1) * BLOCK)
            rows_k = slice(b * BLOCK, (b + 2) * BLOCK)
            keys, values = k[rows_k, cols], v[rows_k, cols]
            lowered = jnp.where(mine, gctx[rows_q, cols].astype(F32), 0.0).astype(BF)
            query = jnp.where(mine, q[rows_q, cols].astype(F32) * scale, 0.0).astype(BF)
            share = p[(pair * 2 + h) * 3 + b]
            wide = share.astype(F32)
            grad_share = dot_cols(lowered, values)
            row = jnp.sum(wide * grad_share, axis=1, keepdims=True)
            grad_score = (wide * (grad_share - row)).astype(BF)
            scores.append(grad_score)
            shares.append(share)
            queries.append(query)
            grads.append(lowered)
            part = (high, first, low)[b]
            parts.append(dot(grad_score[part], keys))
        grad_q = grad_q + jnp.where(mine2, jnp.concatenate(parts, axis=0) * scale, 0.0)
        for i in range(2):
            two = slice(i, i + 2)
            for total, left, right in ((grad_k, scores, queries), (grad_v, shares, grads)):
                upper, lower = left[i][:, second], left[i + 1][:, first]
                total[i] = total[i] + dot_rows(
                    jnp.concatenate([upper, lower], axis=0), jnp.concatenate(right[two], axis=0)
                )
    grad_k, grad_v = jnp.concatenate(grad_k, axis=0), jnp.concatenate(grad_v, axis=0)
    return (
        (grad_q * cos - turned(grad_q) * sin).astype(BF),
        (grad_k * cos - turned(grad_k) * sin).astype(BF),
        grad_v.astype(BF),
    )


def hidden_back_kernel(mlp_pieces, n_mlp, rows, width):
    half = width // 2
    pair = slice(RADIUS, RADIUS + 2 * BLOCK)

    def body(gn_own, gn_other, hidden, dy, gains, q, k, v, p, cosine, sine, *rest):
        mlp_refs, rest = rest[1 : n_mlp + 1], rest[n_mlp + 1 :]
        ghid_out, halves_out, gctx, first_out, attn, held, attn_sems = rest
        copies = place(shard_at(), mlp_pieces, mlp_refs, attn_layout(rows, width, attn), attn_sems)
        at = side_at()
        hat, inverse = standardize(hidden[...])
        grad = gn_own[...].astype(F32) + gn_other[...].astype(F32)
        grad_hidden = dy[...].astype(F32) + norm_back(grad, gains[1:2, :], hat, inverse)
        held[...] = grad_hidden[pair]
        ghid_out[...] = held[pl.ds(pl.multiple_of(at * BLOCK, BLOCK), BLOCK), :]
        halves = jnp.where(at == 0, grad_hidden[pair, 0:half], grad_hidden[pair, half:])
        halves_out[...] = halves.astype(BF)
        grad_low = grad_hidden.astype(BF)
        for copy in copies:
            copy.wait()
        own_rows = pl.ds(pl.multiple_of(at * half, 128), half)
        gctx[...] = dot_cols(grad_low, attn[own_rows, :]).astype(BF)
        cos, sin = cosine[BLOCK : 3 * BLOCK, :], sine[BLOCK : 3 * BLOCK, :]
        for part, grad in enumerate(pair_back(0, gctx, q, k, v, p, cos, sin)):
            first_out[:, part * 128 : (part + 1) * 128] = grad

    return body


def back_kernel(width):
    half = width // 2

    def body(first, halves, gctx, q, k, v, p, cosine, sine, sent_0, sent_1, mixed, gj_out):
        gj_out[:, 3 * half :] = halves[...]
        cos, sin = cosine[BLOCK : 3 * BLOCK, :], sine[BLOCK : 3 * BLOCK, :]
        for part in range(3):
            gj_out[:, part * half : part * half + 128] = first[:, part * 128 : (part + 1) * 128]
        for i in range(1, half // 128):
            for part, grad in enumerate(pair_back(i, gctx, q, k, v, p, cos, sin)):
                col = part * half + i * 128
                gj_out[:, col : col + 128] = grad

    return body


def norm_back_kernel(pieces, n_refs, rows, width):
    half = width // 2

    def body(gj, *rest):
        refs, rest = rest[:n_refs], rest[n_refs:]
        keep_out, send_out, weight, held, sems = rest
        copies = place(shard_at(), pieces, refs, qkv_layout(rows, half, weight), sems)
        at = side_at()
        for copy in copies:
            copy.wait()
        held[...] = dot_cols(gj[:, 0 : 3 * half], weight[...])
        keep_out[...] = held[pl.ds(pl.multiple_of(at * BLOCK, BLOCK), BLOCK), :]
        theirs = pl.ds(pl.multiple_of((1 - at) * BLOCK, BLOCK), BLOCK)
        send_out[...] = held[theirs, :].astype(BF)

    return body


def final_kernel(tok, keep, other, ghid, gains, out):
    hat, inverse = standardize(tok[...].astype(F32))
    grad = keep[...] + other[...].astype(F32)
    out[...] = (ghid[...] + norm_back(grad, gains[0:1, :], hat, inverse)).astype(BF)


def slots_of(count, chip_bits):
    streams = []
    for order in (chip_bits, chip_bits[::-1]):
        kept = [0]
        for bit in order[1:][::-1]:
            kept = kept + [j | bit for j in kept]
        table = {j: (1, i) for i, j in enumerate(kept)}
        table.update({j | order[0]: (0, i) for i, j in enumerate(kept)})
        streams.append(table)
    return streams


def owner_rows(me, js, lhs_t, rows):
    return jnp.concatenate(
        [lhs_t[pl.ds(pl.multiple_of((me ^ j) * rows, 16), rows), :] for j in js], axis=0
    )


def emit(outs, slots, stream, js, rows, grad, start):
    grad = grad.astype(BF)
    for i, j in enumerate(js):
        kept, at = slots[stream][j]
        for c in range(grad.shape[1] // 128):
            row = start + c * rows
            outs[2 * stream + kept][at, row : row + rows, :] = grad[
                i * rows : (i + 1) * rows, c * 128 : (c + 1) * 128
            ]


def mlp_grad_kernel(js, slots, rows, take, width, units):
    half = width // 2

    def body(own, other, dy_own, dy_other, *rest):
        outs, (normed_t, act_t, ggu, dy) = rest[1:5], rest[5:]
        me = shard_at()
        pair = slice(RADIUS, RADIUS + 2 * BLOCK)
        for i, (ref, dref) in enumerate(((own, dy_own), (other, dy_other))):
            tok = slice(i * 2 * BLOCK, (i + 1) * 2 * BLOCK)
            normed_t[:, tok] = ref[:, 0:width].T
            act_t[:, tok] = ref[:, width : width + units].T
            ggu[tok, :] = ref[:, width + units :]
            dy[tok, :] = dref[pair, :]
        left = owner_rows(me, js, normed_t, rows)
        act = owner_rows(me, js, act_t, take)
        for s in range(2):
            grad = dot(left, ggu[:, s * units : (s + 1) * units])
            emit(outs, slots, s, js, rows, grad, 0)
            grad = dot(act, dy[:, s * half : (s + 1) * half])
            emit(outs, slots, s, js, take, grad, rows * (units // 128))

    return body


def qkv_grad_kernel(js, slots, rows, width):
    half = width // 2

    def body(normed_own, normed_other, ctx_own, ctx_other, own, other, *rest):
        outs, (normed_t, ctx_t, gj) = rest[1:5], rest[5:]
        me = shard_at()
        count = 2 * BLOCK
        each = ((normed_own, ctx_own, own), (normed_other, ctx_other, other))
        for i, (nref, cref, ref) in enumerate(each):
            tok = slice(i * count, (i + 1) * count)
            normed_t[:, tok] = nref[...].T
            ctx_t[:, tok] = cref[...].T
            gj[tok, :] = ref[...]
        left = owner_rows(me, js, normed_t, rows)
        ctx = owner_rows(me, js, ctx_t, rows)
        emit(outs, slots, 0, js, rows, dot(left, gj[:, 0 : 2 * half]), 0)
        emit(outs, slots, 1, js, rows, dot(left, gj[:, 2 * half : 3 * half]), 0)
        emit(outs, slots, 1, js, rows, dot(ctx, gj[:, 3 * half :]), 3 * rows)

    return body


def gain_grad(weight, grad, gain):
    total = jnp.sum(weight[...].astype(F32) * grad[...], axis=1, keepdims=True)
    rows = total.shape[0]
    total = jnp.concatenate([total, jnp.zeros((128 - rows, 1), F32)], axis=0)
    return jnp.broadcast_to(total, (128, 128)).T[0:1, 0:rows] / gain[...].astype(F32)


def mlp_unpack_kernel(rows, down_rows, take, width, units, count):
    hidden = count * down_rows
    spare = 2 * take - down_rows

    def body(mine_0, mine_1, other_0, other_1, weight, gain, glu, down, gain_out, held, wide):
        at = side_at()
        tiles = units // 128
        for s, (mine, other) in enumerate(((mine_0, other_0), (mine_1, other_1))):
            held[at, s] = mine[...].astype(F32)
            held[1 - at, s] = other[...].astype(F32)
        for s in range(2):
            for t in range(2):
                for c in range(tiles):
                    row = c * rows
                    wide[:, c * 128 : (c + 1) * 128] = held[t, s, row : row + rows, :]
                skip = 0 if t == 0 else spare
                for i in range(count):
                    col = s * hidden + i * down_rows + t * take
                    glu[:, col : col + take - skip] = wide[:, i * take + skip : (i + 1) * take]
                for c in range(width // 256):
                    row = tiles * rows + c * take
                    col = s * (width // 2) + c * 128
                    down[t * take : (t + 1) * take - skip, col : col + 128] = held[
                        t, s, row + skip : row + take, :
                    ]
        gain_out[...] = gain_grad(weight, glu, gain)

    return body


def qkv_unpack_kernel(rows, width):
    half = width // 2
    tiles = half // 128

    def body(mine_0, mine_1, other_0, other_1, weight, gain, qkv, attn, gain_out, held):
        at = side_at()
        for s, (mine, other) in enumerate(((mine_0, other_0), (mine_1, other_1))):
            held[at, s] = mine[...].astype(F32)
            held[1 - at, s] = other[...].astype(F32)
        for t in range(2):
            for i in range(3):
                for c in range(tiles):
                    row = (i % 2 * tiles + c) * rows
                    col = i * width + t * half + c * 128
                    qkv[:, col : col + 128] = held[t, i // 2, row : row + rows, :]
            for c in range(tiles):
                row = (tiles + c) * rows
                attn[:, t * half + c * 128 : t * half + (c + 1) * 128] = held[t, 1, row : row + rows, :]
        gain_out[...] = gain_grad(weight, qkv, gain)

    return body


def on_device(
    tokens,
    positions,
    qkv_weight,
    attn_weight,
    glu_weight,
    down_weight,
    attn_gain,
    ffn_gain,
    cotangent,
):
    block, width = tokens.shape
    half = width // 2
    rows, down_rows = qkv_weight.shape[0], down_weight.shape[0]
    count, replicas = lax.axis_size("shard"), lax.axis_size("replica")
    everyone = count * replicas
    take = -(-down_rows // 32) * 16
    units = count * take
    me = lax.axis_index("shard").astype(jnp.int32)
    side = lax.axis_index("replica").astype(jnp.int32) & 1
    chip_bits = bits_of(count)[1:]

    own = call(
        pack_kernel(count, down_rows, take),
        shaped((rows, 3 * half + 128 + 2 * width + 2 * units), BF),
        (qkv_weight, attn_weight, glu_weight, down_weight, attn_gain[None], ffn_gain[None]),
        [],
        [],
        1_000_000,
        2_000_000,
    )

    places = jnp.stack([positions >> 8, positions & 255]).astype(BF)
    places = jnp.pad(places, ((0, 14), (0, width - block)))
    rim = jnp.where(side == 0, cotangent[:RADIUS], cotangent[block - RADIUS :])
    rim = jnp.concatenate([tokens, rim, places], axis=0)
    packed = jnp.concatenate([tokens, cotangent, places], axis=0)
    rim, packed, _ = lax.optimization_barrier((rim, packed, own))
    step = [1 if i & 1 else -1 for i in range(everyone)]
    both = ("shard", "replica")

    def outward(array):
        moves = [(i, i + step[i]) for i in range(everyone)]
        return lax.ppermute(array, both, [(a, b) for a, b in moves if 0 <= b < everyone])

    near, partner = outward(rim), xor_send(packed, "replica", 1)
    parts, (near, partner) = gather_pieces(
        own, 3 * half + 128 + width, chip_bits, (near, partner)
    )
    far = xor_send(near, "replica", 1)

    tok, dy = call(
        around_kernel,
        (shaped((4 * BLOCK, width), BF), shaped((3 * BLOCK, width), BF)),
        (tokens, cotangent, partner, near, far),
        [],
        [],
        1_000_000,
        2_000_000,
    )

    def places_of(packed, row):
        return packed[row, :block].astype(F32) * 256.0 + packed[row + 1, :block].astype(F32)

    mine, theirs = positions.astype(F32), places_of(partner, 2 * block)
    inner, outer = places_of(near, block + RADIUS), places_of(far, block + RADIUS)
    where = jnp.where(
        side == 0,
        jnp.concatenate([inner, mine, theirs, outer]),
        jnp.concatenate([outer, theirs, mine, inner]),
    )
    middle = HEAD // 2
    inverse = THETA_BASE ** (-(jnp.arange(middle, dtype=F32) * 2.0 / HEAD))
    phases = where[:, None] * inverse[None, :]
    cosine, sine = jnp.cos(phases), jnp.sin(phases)
    cosine = jnp.concatenate([cosine] * 4, axis=1)
    sine = jnp.concatenate([-sine, sine, -sine, sine], axis=1)
    offset = (
        jnp.arange(2 * BLOCK, dtype=jnp.int32)[None, :]
        - RADIUS
        - jnp.arange(BLOCK, dtype=jnp.int32)[:, None]
    )
    bias = []
    for b in range(3):
        later_key = where[None, b * BLOCK : (b + 2) * BLOCK] >= offset.astype(F32)
        start = RADIUS + b * BLOCK
        later_query = where[start : start + BLOCK, None] >= -offset.astype(F32)
        allowed = (jnp.abs(offset) <= RADIUS) & jnp.where(offset >= 0, later_key, later_query)
        bias.append(jnp.where(allowed, 0.0, NEGATIVE))
    bias = jnp.concatenate(bias, axis=0).astype(F32)
    names, arrays = with_core(parts)
    weight_bytes = width * 3 * width * 2

    q, k, v, p, ctx, normed, gains = call(
        project_kernel(names, len(arrays), rows, width),
        (
            shaped((3 * BLOCK, half), BF),
            shaped((4 * BLOCK, half), BF),
            shaped((4 * BLOCK, half), BF),
            shaped((3 * half // HEAD, BLOCK, 2 * BLOCK), BF),
            shaped((3 * BLOCK, half), BF),
            shaped((2 * BLOCK, width), BF),
            shaped((8, width), F32),
        ),
        (tok, cosine, sine, bias),
        arrays,
        [
            pltpu.VMEM((width, 3 * half), BF),
            pltpu.VMEM((width, 128), BF),
            pltpu.VMEM((4 * BLOCK, width), BF),
            pltpu.SemaphoreType.DMA((2 * len(names),)),
        ],
        7_000_000_000,
        weight_bytes,
    )
    ctx_other = xor_send(ctx, "replica", 1)
    normed_other = xor_send(normed, "shard", 1)
    dy_other = xor_send(dy, "shard", 1)

    mix_keep, mix_send, shared, ctx_pair, hidden, gn = call(
        mlp_kernel(names, len(arrays), rows, down_rows, take, width, units),
        (
            shaped((BLOCK, width), F32),
            shaped((BLOCK, width), BF),
            shaped((2 * BLOCK, width + 3 * units), BF),
            shaped((2 * BLOCK, width), BF),
            shaped((3 * BLOCK, width), F32),
            shaped((3 * BLOCK, width), BF),
        ),
        (tok, ctx, ctx_other, dy, gains),
        [normed_other, dy_other] + arrays,
        [
            pltpu.VMEM((width, width), BF),
            pltpu.VMEM((width, 2 * units), BF),
            pltpu.VMEM((units, width), BF),
            pltpu.VMEM((3 * BLOCK, 2 * units), BF),
            pltpu.VMEM((2 * BLOCK, width), F32),
            pltpu.SemaphoreType.DMA((3 * len(names),)),
        ],
        8_000_000_000,
        2 * weight_bytes,
    )
    gn_other = xor_send(gn, "replica", 1)
    shared_other = xor_send(shared, "shard", 1)
    ctx_pair_other = xor_send(ctx_pair, "shard", 1)

    js = [2 * i for i in range(count // 2)]
    slots = slots_of(count, chip_bits)
    portion = count // 4

    def stack(height):
        return (shaped((portion, height, 128), BF),) * 4

    height = rows * (units // 128) + take * (half // 128)
    sums = call(
        mlp_grad_kernel(js, slots, rows, take, width, units),
        stack(height),
        (shared, shared_other, dy, dy_other),
        [ctx_pair_other],
        [
            pltpu.VMEM((width, 4 * BLOCK), BF),
            pltpu.VMEM((units, 4 * BLOCK), BF),
            pltpu.VMEM((4 * BLOCK, 2 * units), BF),
            pltpu.VMEM((4 * BLOCK, width), BF),
        ],
        4_000_000_000,
        weight_bytes,
    )

    ghid, halves, gctx, gj_first = call(
        hidden_back_kernel(names, len(arrays), rows, width),
        (
            shaped((BLOCK, width), F32),
            shaped((2 * BLOCK, half), BF),
            shaped((3 * BLOCK, half), BF),
            shaped((2 * BLOCK, 3 * 128), BF),
        ),
        (gn, gn_other, hidden, dy, gains, q, k, v, p, cosine, sine),
        [sums[1]] + arrays,
        [
            pltpu.VMEM((width, width), BF),
            pltpu.VMEM((2 * BLOCK, width), F32),
            pltpu.SemaphoreType.DMA((len(names),)),
        ],
        5_000_000_000,
        weight_bytes,
    )
    mlp_sums = scatter_sums(sums, chip_bits, gctx)
    mix_other = xor_send(mix_send, "replica", 1)
    gj = call(
        back_kernel(width),
        shaped((2 * BLOCK, 4 * half), BF),
        (gj_first, halves, gctx, q, k, v, p, cosine, sine),
        [mlp_sums[0][2], mlp_sums[1][2], mix_other],
        [],
        6_000_000_000,
        weight_bytes,
    )
    gj, _ = lax.optimization_barrier((gj, (mlp_sums[0][1], mlp_sums[1][1])))
    mlp_sums = [last_sum(stream) for stream in mlp_sums]
    gj, mlp_sums = lax.optimization_barrier((gj, mlp_sums))
    gj_other = xor_send(gj, "shard", 1)
    norm_keep, norm_send = call(
        norm_back_kernel(names, len(arrays), rows, width),
        (shaped((BLOCK, width), F32), shaped((BLOCK, width), BF)),
        (gj,),
        arrays,
        [
            pltpu.VMEM((width, 3 * half), BF),
            pltpu.VMEM((2 * BLOCK, width), F32),
            pltpu.SemaphoreType.DMA((len(names),)),
        ],
        3_000_000_000,
        weight_bytes,
    )
    sums = call(
        qkv_grad_kernel(js, slots, rows, width),
        stack(6 * rows),
        (normed, normed_other, ctx_pair, ctx_pair_other, gj, gj_other),
        [norm_keep],
        [
            pltpu.VMEM((width, 4 * BLOCK), BF),
            pltpu.VMEM((width, 4 * BLOCK), BF),
            pltpu.VMEM((4 * BLOCK, 4 * half), BF),
        ],
        3_000_000_000,
        weight_bytes,
    )
    mlp_mine = [side_sum(mlp_sums[0], sums[1])]
    qkv_sums = scatter_sums(sums, chip_bits, None, mlp_mine[0])
    mlp_mine.append(side_sum(mlp_sums[1], (qkv_sums[0][2], qkv_sums[1][2])))
    mlp_other = [xor_send(part, "replica", 1) for part in mlp_mine]
    sent = (qkv_sums[0][1], qkv_sums[1][1])
    norm_send, _ = lax.optimization_barrier((norm_send, sums[1]))
    norm_other = xor_send(norm_send, "replica", 1)
    norm_other, mix_other, _ = lax.optimization_barrier((norm_other, mix_other, sent))
    mixed = (mix_keep + mix_other.astype(F32)).astype(BF)
    grad_tokens = call(
        final_kernel,
        shaped((block, width), BF),
        (tokens, norm_keep, norm_other, ghid, gains),
        [],
        [],
        1_000_000,
        1_000_000,
    )
    grad_glu, grad_down, grad_ffn_gain = call(
        mlp_unpack_kernel(rows, down_rows, take, width, units, count),
        (
            shaped((rows, 2 * count * down_rows), F32),
            shaped((down_rows, width), F32),
            shaped((1, rows), F32),
        ),
        (*mlp_mine, *mlp_other, glu_weight, ffn_gain[None]),
        [],
        [pltpu.VMEM((2, 2, height, 128), F32), pltpu.VMEM((rows, units), F32)],
        1_000_000,
        4_000_000,
    )
    done = (mixed, grad_tokens, grad_glu)
    qkv_mine = [side_sum(last_sum(stream), done) for stream in qkv_sums]
    qkv_other = [xor_send(part, "replica", 1) for part in qkv_mine]
    grad_qkv, grad_attn, grad_attn_gain = call(
        qkv_unpack_kernel(rows, width),
        (
            shaped((rows, 3 * width), F32),
            shaped((rows, width), F32),
            shaped((1, rows), F32),
        ),
        (*qkv_mine, *qkv_other, qkv_weight, attn_gain[None]),
        [],
        [pltpu.VMEM((2, 2, 6 * rows, 128), F32)],
        1_000_000,
        4_000_000,
    )
    return (
        mixed,
        grad_tokens,
        grad_qkv,
        grad_attn,
        grad_glu,
        grad_down,
        grad_attn_gain.reshape(rows),
        grad_ffn_gain.reshape(rows),
    )


def solution(mesh):
    in_specs = (
        P(("shard", "replica"), None),
        P(("shard", "replica")),
        P("shard", None),
        P("shard", None),
        P("shard", None),
        P("shard", None),
        P("shard"),
        P("shard"),
        P(("shard", "replica"), None),
    )
    out_specs = (
        P(("shard", "replica"), None),
        P(("shard", "replica"), None),
        P("shard", None),
        P("shard", None),
        P("shard", None),
        P("shard", None),
        P("shard"),
        P("shard"),
    )
    return jax.shard_map(
        on_device, mesh=mesh, in_specs=in_specs, out_specs=out_specs, check_vma=False
    )
```

time: 179 us -> 162 us (0.905)
  starting transfers between devices: 45.2 us -> 31.8 us
  waiting for transfers between devices: 64.6 us -> 55.9 us
  Pallas kernels: 49.3 us -> 53.6 us
  other arithmetic: 8.73 us -> 11.3 us
    ppermute x40 -> x34, starting transfers between devices: 43.3 us -> 31.1 us  [xor_send(): return lax.ppermute(array, axis, [(i, i ^ bit) for i in range(count)])]
    ppermute x40 -> x34, waiting for transfers between devices: 64 us -> 55.9 us  [xor_send(): return lax.ppermute(array, axis, [(i, i ^ bit) for i in range(count)])]
    pallas_call x11 -> x12, Pallas kernels: 49.3 us -> 53.6 us  [call(): pl.pallas_call(kernel, out_shape=out_shape, in_specs=specs, out_specs=jax...]
    convert_element_type x10 -> x12, other arithmetic: 0.65 us -> 3.39 us  [add_low(): return (left.astype(F32) + right.astype(F32)).astype(BF)]
    concatenate x3, other arithmetic: 0.07 us -> 2.57 us  [the longest x1 1.57 us: with_core(): jnp.concatenate([a for _, _, a in whole], axis=0)]
    unnamed x84 -> x72, local copies, waits for them, and re-layouts: 6.61 us -> 7.99 us
  transfers between devices with their start and end apart: 42 -> 35, of which waited for: 18 -> 14; matrix products, arithmetic and copies ran while one was open for 4% -> 6% of each run, Pallas kernels for 21% -> 24%
where the time goes in v3:
time: 162 us
  waiting for transfers between devices  55.9 us (35%)
  Pallas kernels  53.6 us (33%)
  starting transfers between devices  31.8 us (20%)
  other arithmetic  11.3 us (7%)
  local copies, waits for them, and re-layouts  8.12 us (5%)
    ppermute x34, waiting for transfers between devices, xor_send(): return lax.ppermute(array, axis, [(i, i ^ bit) for i in range(count)])  55.9 us
    pallas_call x12, Pallas kernels, call(): pl.pallas_call(kernel, out_shape=out_shape, in_specs=specs, out_specs=jax...  53.6 us
    ppermute x34, starting transfers between devices, xor_send(): return lax.ppermute(array, axis, [(i, i ^ bit) for i in range(count)])  31.1 us
    unnamed x72, local copies, waits for them, and re-layouts  7.99 us
    convert_element_type x12, other arithmetic, add_low(): return (left.astype(F32) + right.astype(F32)).astype(BF)  3.39 us
  transfers between devices with their start and end apart: 35, of which 14 were waited for; matrix products, arithmetic and copies ran while one was open for 6% of the time, Pallas kernels for 24%

profile of v3, /device:TPU:0, one launch (start us, length us, event | category | flops | bytes accessed | tf_op | source)
XLA Modules:
  0.0 161.8 jit_solution(10074232289310038759)
XLA Ops:
  0.7 2.6 %shard_map.152.rest_0_.rest_2_.rest_1_ = bf16[96,4096]{1,0:T(8,128)(2,1)} custom-call(bf16[96,2304]{1,0:T(8,128)(2,1)} %weight.3, bf16[96,768]{1,0:T(8,128)(2,1)} %attn.1, bf16[96,2304]{1,0:T(8,128)(2,1)} %weight.2, bf16[144,768]{1,0:T(8,128)(2,1)} %down.1, bf16[1,96]{1,0:T(2,128)(2,1)} %bitcast.22, bf16[1,96]{1,0:T(2,128)(2,1)} %bitcast.24), custom_call_target="tpu_custom_call" | custom-call | flops 1000000 | bytes 2000000 | tf_op jit(solution)/shard_map/pallas_call | solution.py:165
  3.2 2.9 %collective-permute-start = (bf16[96,4096]{1,0:T(8,128)(2,1)}, bf16[96,4096]{1,0:T(8,128)(2,1)S(1)}, u32[]{:S(2)}, u32[]{:S(2)}) collective-permute-start(bf16[96,4096]{1,0:T(8,128)(2,1)} %shard_map.152.rest_0_.rest_2_.rest_1_), channel_id=1, source_target_pairs={{0,8},{4,12},{8,0},{12,4},{16,24},{20,28},{24,16},{28,20},{1,9},{5... | collective-permute-start | bytes 2359304 | tf_op jit(solution)/shard_map/ppermute | solution.py:23
  6.2 1.5 collective-permute-start.1
  9.5 1.6 %collective-permute-start.3 = (bf16[272,768]{1,0:T(8,128)(2,1)S(1)}, bf16[272,768]{1,0:T(8,128)(2,1)S(1)}, u32[]{:S(2)}, u32[]{:S(2)}) collective-permute-start(bf16[272,768]{1,0:T(8,128)(2,1)S(1)} %pad_maximum_fusion.1), channel_id=1, source_target_pairs={{0,1},{1,0},{2,3},{3,2},{4,5},{5,4},{6,7},{7,6},{8,9},{9,8},{10,11... | collective-permute-start | bytes 1253384 | tf_op jit(solution)/shard_map/ppermute | solution.py:23
  11.8 9.4 %collective-permute-done.3.partner = bf16[272,768]{1,0:T(8,128)(2,1)S(1)} collective-permute-done((bf16[272,768]{1,0:T(8,128)(2,1)S(1)}, bf16[272,768]{1,0:T(8,128)(2,1)S(1)}, u32[]{:S(2)}, u32[]{:S(2)}) %collective-permute-start.3) | collective-permute-done | bytes 417824 | tf_op jit(solution)/shard_map/ppermute | solution.py:23
  21.2 6.0 %collective-permute-done.rest_1_.rest_3_.rest_2_ = bf16[96,4096]{1,0:T(8,128)(2,1)S(1)} collective-permute-done((bf16[96,4096]{1,0:T(8,128)(2,1)}, bf16[96,4096]{1,0:T(8,128)(2,1)S(1)}, u32[]{:S(2)}, u32[]{:S(2)}) %collective-permute-start) | collective-permute-done | bytes 786464 | tf_op jit(solution)/shard_map/ppermute | solution.py:23
  27.9 1.6 pad_maximum_fusion
  29.5 1.5 collective-permute-start.7
  32.8 7.8 %collective-permute-done.4.far = bf16[208,768]{1,0:T(8,128)(2,1)S(1)} collective-permute-done((bf16[208,768]{1,0:T(8,128)(2,1)S(1)}, bf16[208,768]{1,0:T(8,128)(2,1)S(1)}, u32[]{:S(2)}, u32[]{:S(2)}) %collective-permute-start.4) | collective-permute-done | bytes 319520 | tf_op jit(solution)/shard_map/ppermute | solution.py:23
  41.7 2.6 %shard_map.153 = (bf16[512,768]{1,0:T(8,128)(2,1)}, bf16[384,768]{1,0:T(8,128)(2,1)}) custom-call(bf16[128,768]{1,0:T(8,128)(2,1)} %tok.1, bf16[128,768]{1,0:T(8,128)(2,1)} %dy_own.1, bf16[272,768]{1,0:T(8,128)(2,1)} %copy-done.8, bf16[208,768]{1,0:T(8,128)(2,1)} %copy-done.12, bf16[208,768]{1,0:T(8,128)(2,1)} %copy-done.13), custom_call_target="tpu_custom_call" | custom-call | flops 1000000 | bytes 2000000 | tf_op jit(solution)/shard_map/pallas_call | solution.py:165
  48.7 6.9 %shard_map.154 = (bf16[384,384]{1,0:T(8,128)(2,1)}, bf16[512,384]{1,0:T(8,128)(2,1)}, bf16[512,384]{1,0:T(8,128)(2,1)}, bf16[18,128,256]{2,1,0:T(8,128)(2,1)}, b...) custom-call(bf16[512,768]{1,0:T(8,128)(2,1)} %get-tuple-element.68.tok, ...), custom_call_target="tpu_custom_call" | custom-call | flops 7000000000 | bytes 3538944 | tf_op jit(solution)/shard_map/pallas_call | solution.py:165
  56.4 8.9 %collective-permute-done.10.ctx_other = bf16[384,384]{1,0:T(8,128)(2,1)S(1)} collective-permute-done((bf16[384,384]{1,0:T(8,128)(2,1)}, bf16[384,384]{1,0:T(8,128)(2,1)S(1)}, u32[]{:S(2)}, u32[]{:S(2)}) %collective-permute-start.10) | collective-permute-done | bytes 294944 | tf_op jit(solution)/shard_map/ppermute | solution.py:23
  66.2 9.5 %shard_map.155 = (f32[128,768]{1,0:T(8,128)}, bf16[128,768]{1,0:T(8,128)(2,1)}, bf16[256,2688]{1,0:T(8,128)(2,1)}, bf16[256,768]{1,0:T(8,128)(2,1)}, f32[384,768]{1,0:T(8,128)}, /*index=5*/bf16[384,768]{1,0:T(8,128)(2,1)}) custom-call(bf16[512,768]{1,0:T(8,128)(2,1)} %get-tuple-element.68.tok, bf16[384,384]{1,0:T(8,128)(2,1)} %get-tuple-element.71.ctx_own, ...), custom_call_target="tpu_custom_call" | custom-call | flops 8000000000 | bytes 7077888 | tf_op jit(solution)/shard_map/pallas_call | solution.py:165
  76.5 1.7 %collective-permute-start.18 = (bf16[128,768]{1,0:T(8,128)(2,1)}, bf16[128,768]{1,0:T(8,128)(2,1)S(1)}, u32[]{:S(2)}, u32[]{:S(2)}) collective-permute-start(bf16[128,768]{1,0:T(8,128)(2,1)} %get-tuple-element.93), channel_id=1, source_target_pairs={{0,1},{1,0},{2,3},{3,2},{4,5},{5,4},{6,7},{7,6},{8,9},{9,8},{10,11... | collective-permute-start | bytes 589832 | tf_op jit(solution)/shard_map/ppermute | solution.py:23
  81.5 4.3 %shard_map.156 = (bf16[2,720,128]{2,1,0:T(8,128)(2,1)}, bf16[2,720,128]{2,1,0:T(8,128)(2,1)}, bf16[2,720,128]{2,1,0:T(8,128)(2,1)}, bf16[2,720,128]{2,1,0:T(8,128)(2,1)}) custom-call(bf16[256,2688]{1,0:T(8,128)(2,1)} %get-tuple-element.82.own, bf16[256,2688]{1,0:T(8,128)(2,1)} %copy-done.24, bf16[384,768]{1,0:T(8,128)(2,1)} %get-tuple-element.72.dy.dy_own, ...), custom_call_target="tpu_custom_call" | custom-call | flops 4000000000 | bytes 3538944 | tf_op jit(solution)/shard_map/pallas_call | solution.py:165
  87.7 4.9 %collective-permute-done.13.gn_other = bf16[384,768]{1,0:T(8,128)(2,1)S(1)} collective-permute-done((bf16[384,768]{1,0:T(8,128)(2,1)}, bf16[384,768]{1,0:T(8,128)(2,1)S(1)}, u32[]{:S(2)}, u32[]{:S(2)}) %collective-permute-start.13) | collective-permute-done | bytes 589856 | tf_op jit(solution)/shard_map/ppermute | solution.py:23
  93.5 6.8 %shard_map.157 = (f32[128,768]{1,0:T(8,128)}, bf16[256,384]{1,0:T(8,128)(2,1)}, bf16[384,384]{1,0:T(8,128)(2,1)}, bf16[256,384]{1,0:T(8,128)(2,1)}) custom-call(bf16[384,768]{1,0:T(8,128)(2,1)} %get-tuple-element.76.gn_own, bf16[384,768]{1,0:T(8,128)(2,1)} %copy-done.27, f32[384,768]{1,0:T(8,128)} %get-tuple-element.77.hidden, ...), custom_call_target="tpu_custom_call" | custom-call | flops 5000000000 | bytes 3538944 | tf_op jit(solution)/shard_map/pallas_call | solution.py:165
  103.2 5.0 %shard_map.158.gj.own = bf16[256,1536]{1,0:T(8,128)(2,1)} custom-call(bf16[256,384]{1,0:T(8,128)(2,1)} %get-tuple-element.85.first, bf16[256,384]{1,0:T(8,128)(2,1)} %get-tuple-element.86.halves, bf16[384,384]{1,0:T(8,128)(2,1)} %get-tuple-element.87.gctx, bf16[384,384]{1,0:T(8,128)(2,1)} %get-tuple-element.78.q, bf16[512,384]{1,0:T(8,128)(2,1)} %get-tuple-element.79.k, ...), custom_call_target="tpu_custom_call" | custom-call | flops 6000000000 | bytes 3538944 | tf_op jit(solution)/shard_map/pallas_call | solution.py:165
  108.5 2.5 %collective-permute-start.25 = (bf16[720,128]{1,0:T(8,128)(2,1)S(1)}, bf16[720,128]{1,0:T(8,128)(2,1)S(1)}, u32[]{:S(2)}, u32[]{:S(2)}) collective-permute-start(bf16[720,128]{1,0:T(8,128)(2,1)S(1)} %fusion), channel_id=1, source_target_pairs={{0,2},{1,3},{2,0},{3,1},{4,6},{5,7},{6,4},{7,5},{8,10},{9,11},{10,... | collective-permute-start | bytes 552968 | tf_op jit(solution)/shard_map/ppermute | solution.py:23
  110.9 4.4 %shard_map.159 = (f32[128,768]{1,0:T(8,128)}, bf16[128,768]{1,0:T(8,128)(2,1)}) custom-call(bf16[256,1536]{1,0:T(8,128)(2,1)} %shard_map.158.gj.own, bf16[96,4096]{1,0:T(8,128)(2,1)} %shard_map.152.rest_0_.rest_2_.rest_1_, bf16[96,4096]{1,0:T(8,128)(2,1)} %copy-done.1, bf16[96,4096]{1,0:T(8,128)(2,1)} %copy-done.2, bf16[96,2048]{1,0:T(8,128)(2,1)} %copy-done.28, ...), custom_call_target="tpu_custom_call" | custom-call | flops 3000000000 | bytes 3538944 | tf_op jit(solution)/shard_map/pallas_call | solution.py:165
  116.2 3.8 %shard_map.160 = (bf16[2,576,128]{2,1,0:T(8,128)(2,1)}, bf16[2,576,128]{2,1,0:T(8,128)(2,1)}, bf16[2,576,128]{2,1,0:T(8,128)(2,1)}, bf16[2,576,128]{2,1,0:T(8,128)(2,1)}) custom-call(bf16[256,768]{1,0:T(8,128)(2,1)} %get-tuple-element.74.normed_own, bf16[256,768]{1,0:T(8,128)(2,1)} %copy-done.32, bf16[256,768]{1,0:T(8,128)(2,1)} %get-tuple-element.83.ctx_own, ...), custom_call_target="tpu_custom_call" | custom-call | flops 3000000000 | bytes 3538944 | tf_op jit(solution)/shard_map/pallas_call | solution.py:165
  123.2 1.7 %collective-permute-start.22 = (bf16[128,768]{1,0:T(8,128)(2,1)S(1)}, bf16[128,768]{1,0:T(8,128)(2,1)S(1)}, u32[]{:S(2)}, u32[]{:S(2)}) collective-permute-start(bf16[128,768]{1,0:T(8,128)(2,1)S(1)} %copy-done.35), channel_id=1, source_target_pairs={{0,1},{1,0},{2,3},{3,2},{4,5},{5,4},{6,7},{7,6},{8,9},{9,8},{10,11... | collective-permute-start | bytes 589832 | tf_op jit(solution)/shard_map/ppermute | solution.py:23
  124.9 4.5 %collective-permute-done.23 = bf16[2,576,128]{2,1,0:T(8,128)(2,1)S(1)} collective-permute-done((bf16[2,576,128]{2,1,0:T(8,128)(2,1)}, bf16[2,576,128]{2,1,0:T(8,128)(2,1)S(1)}, u32[]{:S(2)}, u32[]{:S(2)}) %collective-permute-start.23) | collective-permute-done | bytes 294944 | tf_op jit(solution)/shard_map/ppermute | solution.py:23
  134.6 2.4 %collective-permute-done.27 = bf16[1,576,128]{2,1,0:T(8,128)(2,1)S(1)} collective-permute-done((bf16[1,576,128]{2,1,0:T(8,128)(2,1)S(1)}, bf16[1,576,128]{2,1,0:T(8,128)(2,1)S(1)}, u32[]{:S(2)}, u32[]{:S(2)}) %collective-permute-start.27) | collective-permute-done | bytes 147488 | tf_op jit(solution)/shard_map/ppermute | solution.py:23
  138.0 1.6 collective-permute-start.32
  139.6 1.5 collective-permute-start.28
  141.1 2.2 %shard_map.161 = bf16[128,768]{1,0:T(8,128)(2,1)} custom-call(bf16[128,768]{1,0:T(8,128)(2,1)} %tok.1, f32[128,768]{1,0:T(8,128)} %get-tuple-element.97.rest_0_.keep, bf16[128,768]{1,0:T(8,128)(2,1)} %copy-done.17, f32[128,768]{1,0:T(8,128)} %get-tuple-element.109.ghid, f32[8,768]{1,0:T(8,128)} %get-tuple-element.73.gains), custom_call_target="tpu_custom_call" | custom-call | flops 1000000 | bytes 1000000 | tf_op jit(solution)/shard_map/pallas_call | solution.py:165
  145.4 2.9 %shard_map.162 = (f32[96,2304]{1,0:T(8,128)}, f32[144,768]{1,0:T(8,128)}, f32[1,96]{1,0:T(1,128)}) custom-call(bf16[720,128]{1,0:T(8,128)(2,1)} %copy-done.4, bf16[720,128]{1,0:T(8,128)(2,1)} %copy-done.5, bf16[720,128]{1,0:T(8,128)(2,1)} %copy-done.18, bf16[720,128]{1,0:T(8,128)(2,1)} %copy-done.19, bf16[96,2304]{1,0:T(8,128)(2,1)} %weight.2, ...), custom_call_target="tpu_custom_call" | custom-call | flops 1000000 | bytes 4000000 | tf_op jit(solution)/shard_map/pallas_call | solution.py:165
  148.4 2.4 %collective-permute-done.32 = bf16[576,128]{1,0:T(8,128)(2,1)S(1)} collective-permute-done((bf16[576,128]{1,0:T(8,128)(2,1)S(1)}, bf16[576,128]{1,0:T(8,128)(2,1)S(1)}, u32[]{:S(2)}, u32[]{:S(2)}) %collective-permute-start.32) | collective-permute-done | bytes 147488 | tf_op jit(solution)/shard_map/ppermute | solution.py:23
  153.0 3.9 %collective-permute-done.34.other_1 = bf16[576,128]{1,0:T(8,128)(2,1)S(1)} collective-permute-done((bf16[576,128]{1,0:T(8,128)(2,1)S(1)}, bf16[576,128]{1,0:T(8,128)(2,1)S(1)}, u32[]{:S(2)}, u32[]{:S(2)}) %collective-permute-start.34) | collective-permute-done | bytes 147488 | tf_op jit(solution)/shard_map/ppermute | solution.py:23
  157.0 1.6 collective-permute-done.33.other_0
  159.2 2.6 %shard_map.163 = (f32[96,2304]{1,0:T(8,128)}, f32[96,768]{1,0:T(8,128)}, f32[1,96]{1,0:T(1,128)}) custom-call(bf16[576,128]{1,0:T(8,128)(2,1)} %copy-done.7, bf16[576,128]{1,0:T(8,128)(2,1)} %copy-done.6, bf16[576,128]{1,0:T(8,128)(2,1)} %copy-done.23, bf16[576,128]{1,0:T(8,128)(2,1)} %copy-done.22, bf16[96,2304]{1,0:T(8,128)(2,1)} %weight.3, ...), custom_call_target="tpu_custom_call" | custom-call | flops 1000000 | bytes 4000000 | tf_op jit(solution)/shard_map/pallas_call | solution.py:165
  (155 shorter events, 37.0 us)
Async XLA Ops:
  3.2 24.0 %collective-permute-start = (bf16[96,4096]{1,0:T(8,128)(2,1)}, bf16[96,4096]{1,0:T(8,128)(2,1)S(1)}, u32[]{:S(2)}, u32[]{:S(2)}) collective-permute-start(bf16[96,4096]{1,0:T(8,128)(2,1)} %shard_map.152.rest_0_.rest_2_.rest_1_), channel_id=1, source_target_pairs={{0,8},{4,12},{8,0},{12,4},{16,24},{20,28},{24,16},{28,20},{1,9},{5... | collective-permute-start | bytes 2359304 | tf_op jit(solution)/shard_map/ppermute | solution.py:23
  6.2 21.8 %collective-permute-start.1 = (bf16[96,4096]{1,0:T(8,128)(2,1)}, bf16[96,4096]{1,0:T(8,128)(2,1)S(1)}, u32[]{:S(2)}, u32[]{:S(2)}) collective-permute-start(bf16[96,4096]{1,0:T(8,128)(2,1)} %shard_map.152.rest_0_.rest_2_.rest_1_), channel_id=1, source_target_pairs={{0,16},{4,20},{8,24},{12,28},{16,0},{20,4},{24,8},{28,12},{1,17},{... | collective-permute-start | bytes 2359304 | tf_op jit(solution)/shard_map/ppermute | solution.py:23
  9.5 11.8 %collective-permute-start.3 = (bf16[272,768]{1,0:T(8,128)(2,1)S(1)}, bf16[272,768]{1,0:T(8,128)(2,1)S(1)}, u32[]{:S(2)}, u32[]{:S(2)}) collective-permute-start(bf16[272,768]{1,0:T(8,128)(2,1)S(1)} %pad_maximum_fusion.1), channel_id=1, source_target_pairs={{0,1},{1,0},{2,3},{3,2},{4,5},{5,4},{6,7},{7,6},{8,9},{9,8},{10,11... | collective-permute-start | bytes 1253384 | tf_op jit(solution)/shard_map/ppermute | solution.py:23
  29.5 18.3 %collective-permute-start.7 = (bf16[288,4096]{1,0:T(8,128)(2,1)S(1)}, bf16[288,4096]{1,0:T(8,128)(2,1)}, u32[]{:S(2)}, u32[]{:S(2)}) collective-permute-start(bf16[288,4096]{1,0:T(8,128)(2,1)S(1)} %pad_maximum_fusion), channel_id=1, source_target_pairs={{0,4},{4,0},{8,12},{12,8},{16,20},{20,16},{24,28},{28,24},{1,5},{5... | collective-permute-start | bytes 7077896 | tf_op jit(solution)/shard_map/ppermute | solution.py:23
  31.0 9.5 %collective-permute-start.4 = (bf16[208,768]{1,0:T(8,128)(2,1)S(1)}, bf16[208,768]{1,0:T(8,128)(2,1)S(1)}, u32[]{:S(2)}, u32[]{:S(2)}) collective-permute-start(bf16[208,768]{1,0:T(8,128)(2,1)S(1)} %collective-permute-done.2.near), channel_id=1, source_target_pairs={{0,1},{1,0},{2,3},{3,2},{4,5},{5,4},{6,7},{7,6},{8,9},{9,8},{10,11... | collective-permute-start | bytes 958472 | tf_op jit(solution)/shard_map/ppermute | solution.py:23
  31.1 14.1 %collective-permute-start.5 = (bf16[96,2048]{1,0:T(8,128)(2,1)S(1)}, bf16[96,2048]{1,0:T(8,128)(2,1)S(1)}, u32[]{:S(2)}, u32[]{:S(2)}) collective-permute-start(bf16[96,2048]{1,0:T(8,128)(2,1)S(1)} %slice.110), channel_id=1, source_target_pairs={{0,16},{4,20},{8,24},{12,28},{16,0},{20,4},{24,8},{28,12},{1,17},{... | collective-permute-start | bytes 1179656 | tf_op jit(solution)/shard_map/ppermute | solution.py:23
  32.2 13.6 %collective-permute-start.6 = (bf16[96,2048]{1,0:T(8,128)(2,1)S(1)}, bf16[96,2048]{1,0:T(8,128)(2,1)S(1)}, u32[]{:S(2)}, u32[]{:S(2)}) collective-permute-start(bf16[96,2048]{1,0:T(8,128)(2,1)S(1)} %slice.111), channel_id=1, source_target_pairs={{0,8},{4,12},{8,0},{12,4},{16,24},{20,28},{24,16},{28,20},{1,9},{5... | collective-permute-start | bytes 1179656 | tf_op jit(solution)/shard_map/ppermute | solution.py:23
  44.3 12.1 %collective-permute-start.12 = (bf16[384,768]{1,0:T(8,128)(2,1)}, bf16[384,768]{1,0:T(8,128)(2,1)S(1)}, u32[]{:S(2)}, u32[]{:S(2)}) collective-permute-start(bf16[384,768]{1,0:T(8,128)(2,1)} %get-tuple-element.72.dy.dy_own), channel_id=1, source_target_pairs={{0,4},{4,0},{8,12},{12,8},{16,20},{20,16},{24,28},{28,24},{1,5},{5... | collective-permute-start | bytes 1769480 | tf_op jit(solution)/shard_map/ppermute | solution.py:23
  55.6 9.7 %collective-permute-start.11 = (bf16[256,768]{1,0:T(8,128)(2,1)}, bf16[256,768]{1,0:T(8,128)(2,1)S(1)}, u32[]{:S(2)}, u32[]{:S(2)}) collective-permute-start(bf16[256,768]{1,0:T(8,128)(2,1)} %get-tuple-element.74.normed_own), channel_id=1, source_target_pairs={{0,4},{4,0},{8,12},{12,8},{16,20},{20,16},{24,28},{28,24},{1,5},{5... | collective-permute-start | bytes 1179656 | tf_op jit(solution)/shard_map/ppermute | solution.py:23
  56.1 9.2 %collective-permute-start.10 = (bf16[384,384]{1,0:T(8,128)(2,1)}, bf16[384,384]{1,0:T(8,128)(2,1)S(1)}, u32[]{:S(2)}, u32[]{:S(2)}) collective-permute-start(bf16[384,384]{1,0:T(8,128)(2,1)} %get-tuple-element.71.ctx_own), channel_id=1, source_target_pairs={{0,1},{1,0},{2,3},{3,2},{4,5},{5,4},{6,7},{7,6},{8,9},{9,8},{10,11... | collective-permute-start | bytes 884744 | tf_op jit(solution)/shard_map/ppermute | solution.py:23
  75.7 4.0 %collective-permute-start.14 = (bf16[256,2688]{1,0:T(8,128)(2,1)}, bf16[256,2688]{1,0:T(8,128)(2,1)S(1)}, u32[]{:S(2)}, u32[]{:S(2)}) collective-permute-start(bf16[256,2688]{1,0:T(8,128)(2,1)} %get-tuple-element.82.own), channel_id=1, source_target_pairs={{0,4},{4,0},{8,12},{12,8},{16,20},{20,16},{24,28},{28,24},{1,5},{5... | collective-permute-start | bytes 4128776 | tf_op jit(solution)/shard_map/ppermute | solution.py:23
  75.8 3.9 %collective-permute-start.15 = (bf16[256,768]{1,0:T(8,128)(2,1)}, bf16[256,768]{1,0:T(8,128)(2,1)S(1)}, u32[]{:S(2)}, u32[]{:S(2)}) collective-permute-start(bf16[256,768]{1,0:T(8,128)(2,1)} %get-tuple-element.83.ctx_own), channel_id=1, source_target_pairs={{0,4},{4,0},{8,12},{12,8},{16,20},{20,16},{24,28},{28,24},{1,5},{5... | collective-permute-start | bytes 1179656 | tf_op jit(solution)/shard_map/ppermute | solution.py:23
  76.3 16.4 %collective-permute-start.13 = (bf16[384,768]{1,0:T(8,128)(2,1)}, bf16[384,768]{1,0:T(8,128)(2,1)S(1)}, u32[]{:S(2)}, u32[]{:S(2)}) collective-permute-start(bf16[384,768]{1,0:T(8,128)(2,1)} %get-tuple-element.76.gn_own), channel_id=1, source_target_pairs={{0,1},{1,0},{2,3},{3,2},{4,5},{5,4},{6,7},{7,6},{8,9},{9,8},{10,11... | collective-permute-start | bytes 1769480 | tf_op jit(solution)/shard_map/ppermute | solution.py:23
  76.5 26.0 %collective-permute-start.18 = (bf16[128,768]{1,0:T(8,128)(2,1)}, bf16[128,768]{1,0:T(8,128)(2,1)S(1)}, u32[]{:S(2)}, u32[]{:S(2)}) collective-permute-start(bf16[128,768]{1,0:T(8,128)(2,1)} %get-tuple-element.93), channel_id=1, source_target_pairs={{0,1},{1,0},{2,3},{3,2},{4,5},{5,4},{6,7},{7,6},{8,9},{9,8},{10,11... | collective-permute-start | bytes 589832 | tf_op jit(solution)/shard_map/ppermute | solution.py:23
  85.8 14.5 %collective-permute-start.16 = (bf16[2,720,128]{2,1,0:T(8,128)(2,1)}, bf16[2,720,128]{2,1,0:T(8,128)(2,1)S(1)}, u32[]{:S(2)}, u32[]{:S(2)}) collective-permute-start(bf16[2,720,128]{2,1,0:T(8,128)(2,1)} %get-tuple-element.88), channel_id=1, source_target_pairs={{0,8},{4,12},{8,0},{12,4},{16,24},{20,28},{24,16},{28,20},{1,9},{5... | collective-permute-start | bytes 1105928 | tf_op jit(solution)/shard_map/ppermute | solution.py:23
  86.3 14.0 %collective-permute-start.17 = (bf16[2,720,128]{2,1,0:T(8,128)(2,1)}, bf16[2,720,128]{2,1,0:T(8,128)(2,1)S(1)}, u32[]{:S(2)}, u32[]{:S(2)}) collective-permute-start(bf16[2,720,128]{2,1,0:T(8,128)(2,1)} %get-tuple-element.89), channel_id=1, source_target_pairs={{0,16},{4,20},{8,24},{12,28},{16,0},{20,4},{24,8},{28,12},{1,17},{... | collective-permute-start | bytes 1105928 | tf_op jit(solution)/shard_map/ppermute | solution.py:23
  100.4 7.8 %collective-permute-start.20 = (bf16[1,720,128]{2,1,0:T(8,128)(2,1)S(1)}, bf16[1,720,128]{2,1,0:T(8,128)(2,1)S(1)}, u32[]{:S(2)}, u32[]{:S(2)}) collective-permute-start(bf16[1,720,128]{2,1,0:T(8,128)(2,1)S(1)} %add_convert_fusion.7.sent_1), channel_id=1, source_target_pairs={{0,8},{4,12},{8,0},{12,4},{16,24},{20,28},{24,16},{28,20},{1,9},{5... | collective-permute-start | bytes 552968 | tf_op jit(solution)/shard_map/ppermute | solution.py:23
  101.0 7.2 %collective-permute-start.19 = (bf16[1,720,128]{2,1,0:T(8,128)(2,1)S(1)}, bf16[1,720,128]{2,1,0:T(8,128)(2,1)S(1)}, u32[]{:S(2)}, u32[]{:S(2)}) collective-permute-start(bf16[1,720,128]{2,1,0:T(8,128)(2,1)S(1)} %add_convert_fusion.8.sent_0), channel_id=1, source_target_pairs={{0,16},{4,20},{8,24},{12,28},{16,0},{20,4},{24,8},{28,12},{1,17},{... | collective-permute-start | bytes 552968 | tf_op jit(solution)/shard_map/ppermute | solution.py:23
  108.4 7.0 %collective-permute-start.21 = (bf16[256,1536]{1,0:T(8,128)(2,1)}, bf16[256,1536]{1,0:T(8,128)(2,1)S(1)}, u32[]{:S(2)}, u32[]{:S(2)}) collective-permute-start(bf16[256,1536]{1,0:T(8,128)(2,1)} %shard_map.158.gj.own), channel_id=1, source_target_pairs={{0,4},{4,0},{8,12},{12,8},{16,20},{20,16},{24,28},{28,24},{1,5},{5... | collective-permute-start | bytes 2359304 | tf_op jit(solution)/shard_map/ppermute | solution.py:23
  108.5 13.6 %collective-permute-start.25 = (bf16[720,128]{1,0:T(8,128)(2,1)S(1)}, bf16[720,128]{1,0:T(8,128)(2,1)S(1)}, u32[]{:S(2)}, u32[]{:S(2)}) collective-permute-start(bf16[720,128]{1,0:T(8,128)(2,1)S(1)} %fusion), channel_id=1, source_target_pairs={{0,2},{1,3},{2,0},{3,1},{4,6},{5,7},{6,4},{7,5},{8,10},{9,11},{10,... | collective-permute-start | bytes 552968 | tf_op jit(solution)/shard_map/ppermute | solution.py:23
  120.1 9.3 %collective-permute-start.23 = (bf16[2,576,128]{2,1,0:T(8,128)(2,1)}, bf16[2,576,128]{2,1,0:T(8,128)(2,1)S(1)}, u32[]{:S(2)}, u32[]{:S(2)}) collective-permute-start(bf16[2,576,128]{2,1,0:T(8,128)(2,1)} %get-tuple-element.100), channel_id=1, source_target_pairs={{0,8},{4,12},{8,0},{12,4},{16,24},{20,28},{24,16},{28,20},{1,9},{5... | collective-permute-start | bytes 884744 | tf_op jit(solution)/shard_map/ppermute | solution.py:23
  120.7 12.4 %collective-permute-start.29 = (bf16[720,128]{1,0:T(8,128)(2,1)S(1)}, bf16[720,128]{1,0:T(8,128)(2,1)S(1)}, u32[]{:S(2)}, u32[]{:S(2)}) collective-permute-start(bf16[720,128]{1,0:T(8,128)(2,1)S(1)} %fusion.1), channel_id=1, source_target_pairs={{0,2},{1,3},{2,0},{3,1},{4,6},{5,7},{6,4},{7,5},{8,10},{9,11},{10,... | collective-permute-start | bytes 552968 | tf_op jit(solution)/shard_map/ppermute | solution.py:23
  122.1 8.7 %collective-permute-start.24 = (bf16[2,576,128]{2,1,0:T(8,128)(2,1)}, bf16[2,576,128]{2,1,0:T(8,128)(2,1)S(1)}, u32[]{:S(2)}, u32[]{:S(2)}) collective-permute-start(bf16[2,576,128]{2,1,0:T(8,128)(2,1)} %get-tuple-element.102), channel_id=1, source_target_pairs={{0,16},{4,20},{8,24},{12,28},{16,0},{20,4},{24,8},{28,12},{1,17},{... | collective-permute-start | bytes 884744 | tf_op jit(solution)/shard_map/ppermute | solution.py:23
  122.8 21.2 %collective-permute-start.30 = (bf16[720,128]{1,0:T(8,128)(2,1)S(1)}, bf16[720,128]{1,0:T(8,128)(2,1)S(1)}, u32[]{:S(2)}, u32[]{:S(2)}) collective-permute-start(bf16[720,128]{1,0:T(8,128)(2,1)S(1)} %add_convert_fusion.2.mine_0), channel_id=1, source_target_pairs={{0,1},{1,0},{2,3},{3,2},{4,5},{5,4},{6,7},{7,6},{8,9},{9,8},{10,11... | collective-permute-start | bytes 552968 | tf_op jit(solution)/shard_map/ppermute | solution.py:23
  123.2 16.3 %collective-permute-start.22 = (bf16[128,768]{1,0:T(8,128)(2,1)S(1)}, bf16[128,768]{1,0:T(8,128)(2,1)S(1)}, u32[]{:S(2)}, u32[]{:S(2)}) collective-permute-start(bf16[128,768]{1,0:T(8,128)(2,1)S(1)} %copy-done.35), channel_id=1, source_target_pairs={{0,1},{1,0},{2,3},{3,2},{4,5},{5,4},{6,7},{7,6},{8,9},{9,8},{10,11... | collective-permute-start | bytes 589832 | tf_op jit(solution)/shard_map/ppermute | solution.py:23
  131.8 5.2 %collective-permute-start.27 = (bf16[1,576,128]{2,1,0:T(8,128)(2,1)S(1)}, bf16[1,576,128]{2,1,0:T(8,128)(2,1)S(1)}, u32[]{:S(2)}, u32[]{:S(2)}) collective-permute-start(bf16[1,576,128]{2,1,0:T(8,128)(2,1)S(1)} %add_convert_fusion.15), channel_id=1, source_target_pairs={{0,8},{4,12},{8,0},{12,4},{16,24},{20,28},{24,16},{28,20},{1,9},{5... | collective-permute-start | bytes 442376 | tf_op jit(solution)/shard_map/ppermute | solution.py:23
  132.4 7.1 %collective-permute-start.26 = (bf16[1,576,128]{2,1,0:T(8,128)(2,1)S(1)}, bf16[1,576,128]{2,1,0:T(8,128)(2,1)S(1)}, u32[]{:S(2)}, u32[]{:S(2)}) collective-permute-start(bf16[1,576,128]{2,1,0:T(8,128)(2,1)S(1)} %add_convert_fusion.16), channel_id=1, source_target_pairs={{0,16},{4,20},{8,24},{12,28},{16,0},{20,4},{24,8},{28,12},{1,17},{... | collective-permute-start | bytes 442376 | tf_op jit(solution)/shard_map/ppermute | solution.py:23
  133.1 11.0 %collective-permute-start.31 = (bf16[720,128]{1,0:T(8,128)(2,1)S(1)}, bf16[720,128]{1,0:T(8,128)(2,1)S(1)}, u32[]{:S(2)}, u32[]{:S(2)}) collective-permute-start(bf16[720,128]{1,0:T(8,128)(2,1)S(1)} %add_convert_fusion.1.mine_1), channel_id=1, source_target_pairs={{0,1},{1,0},{2,3},{3,2},{4,5},{5,4},{6,7},{7,6},{8,9},{9,8},{10,11... | collective-permute-start | bytes 552968 | tf_op jit(solution)/shard_map/ppermute | solution.py:23
  138.0 12.8 %collective-permute-start.32 = (bf16[576,128]{1,0:T(8,128)(2,1)S(1)}, bf16[576,128]{1,0:T(8,128)(2,1)S(1)}, u32[]{:S(2)}, u32[]{:S(2)}) collective-permute-start(bf16[576,128]{1,0:T(8,128)(2,1)S(1)} %fusion.3), channel_id=1, source_target_pairs={{0,2},{1,3},{2,0},{3,1},{4,6},{5,7},{6,4},{7,5},{8,10},{9,11},{10,... | collective-permute-start | bytes 442376 | tf_op jit(solution)/shard_map/ppermute | solution.py:23
  139.6 12.7 %collective-permute-start.28 = (bf16[576,128]{1,0:T(8,128)(2,1)S(1)}, bf16[576,128]{1,0:T(8,128)(2,1)S(1)}, u32[]{:S(2)}, u32[]{:S(2)}) collective-permute-start(bf16[576,128]{1,0:T(8,128)(2,1)S(1)} %fusion.2), channel_id=1, source_target_pairs={{0,2},{1,3},{2,0},{3,1},{4,6},{5,7},{6,4},{7,5},{8,10},{9,11},{10,... | collective-permute-start | bytes 442376 | tf_op jit(solution)/shard_map/ppermute | solution.py:23
  150.8 6.2 %collective-permute-start.34 = (bf16[576,128]{1,0:T(8,128)(2,1)S(1)}, bf16[576,128]{1,0:T(8,128)(2,1)S(1)}, u32[]{:S(2)}, u32[]{:S(2)}) collective-permute-start(bf16[576,128]{1,0:T(8,128)(2,1)S(1)} %add_convert_fusion.9.mine_1), channel_id=1, source_target_pairs={{0,1},{1,0},{2,3},{3,2},{4,5},{5,4},{6,7},{7,6},{8,9},{9,8},{10,11... | collective-permute-start | bytes 442376 | tf_op jit(solution)/shard_map/ppermute | solution.py:23
  152.4 6.2 %collective-permute-start.33 = (bf16[576,128]{1,0:T(8,128)(2,1)S(1)}, bf16[576,128]{1,0:T(8,128)(2,1)S(1)}, u32[]{:S(2)}, u32[]{:S(2)}) collective-permute-start(bf16[576,128]{1,0:T(8,128)(2,1)S(1)} %add_convert_fusion.12.mine_0), channel_id=1, source_target_pairs={{0,1},{1,0},{2,3},{3,2},{4,5},{5,4},{6,7},{7,6},{8,9},{9,8},{10,11... | collective-permute-start | bytes 442376 | tf_op jit(solution)/shard_map/ppermute | solution.py:23
  (39 other events, 226.8 us)

commit v4 on v3

--- a/solution.py
+++ b/solution.py
@@ -13,7 +13,7 @@
 EPSILON = 1e-05
 THETA_BASE = 10000.0
 NEGATIVE = -1e30
-VMEM_BYTES = 56 * 1024 * 1024
+VMEM_BYTES = 24 * 1024 * 1024
 BF = jnp.bfloat16
 F32 = jnp.float32
 
@@ -27,14 +27,16 @@
     return [1 << i for i in range(count.bit_length() - 1)]
 
 
-def gather_pieces(own, split, chip_bits, before):
+def gather_pieces(own, split, chip_bits, before=None):
     if len(chip_bits) == 2:
         x, y = chip_bits
         from_x, from_y = xor_send(own, "shard", x), xor_send(own, "shard", y)
-        (from_x, from_y), before = lax.optimization_barrier(((from_x, from_y), before))
+        if before is not None:
+            (from_x, from_y), _ = lax.optimization_barrier(((from_x, from_y), before))
         pieces = [(0, 2, own), (x, 2, from_x), (y, 2, from_y)]
-        pieces.append((x | y, 0, xor_send(from_x[:, :split], "shard", y)))
-        pieces.append((x | y, 1, xor_send(from_y[:, split:], "shard", x)))
+        forward = [from_x[:, :split], from_y[:, split:]]
+        pieces.append((x | y, 0, xor_send(forward[0], "shard", y)))
+        pieces.append((x | y, 1, xor_send(forward[1], "shard", x)))
     else:
         streams = ([(0, 0, own[:, :split])], [(0, 1, own[:, split:])])
         for stage in range(len(chip_bits)):
@@ -46,22 +48,25 @@
             for held, more in zip(streams, grown):
                 held.extend(more)
         pieces = streams[0] + streams[1]
-    return pieces, before
-
-
-def with_core(pieces, after=None):
+        forward = []
+    return pieces, forward
+
+
+def with_core(pieces, joined):
     rows = pieces[0][2].shape[0]
     arrays = [a for _, _, a in pieces]
     names = [(j, s, i, 0) for i, (j, s, _) in enumerate(pieces)]
     whole = [p for p in pieces if p[1] == 2]
-    if whole:
-        arrays.append(xor_send(jnp.concatenate([a for _, _, a in whole], axis=0), "shard", 1))
-        names += [(p[0] ^ 1, 2, len(arrays) - 1, i * rows) for i, p in enumerate(whole)]
-    for j, s, a in pieces[len(whole) :]:
-        if after is not None:
-            a, _ = lax.optimization_barrier((a, after))
-        arrays.append(xor_send(a, "shard", 1))
-        names.append((j ^ 1, s, len(arrays) - 1, 0))
+    others = pieces[len(whole) :]
+    if joined and whole:
+        whole.append((others[0][0], 2, jnp.concatenate([a for _, _, a in others], axis=1)))
+        others = []
+    groups = ([whole] if whole else []) + [[p] for p in others]
+    for group in groups:
+        sent = [a for _, _, a in group]
+        sent = jnp.concatenate(sent, axis=0) if len(sent) > 1 else sent[0]
+        arrays.append(xor_send(sent, "shard", 1))
+        names += [(p[0] ^ 1, p[1], len(arrays) - 1, i * rows) for i, p in enumerate(group)]
     return names, arrays
 
 
@@ -185,27 +190,16 @@
     return jax.ShapeDtypeStruct(shape, dtype)
 
 
-def pack_kernel(count, down_rows, take):
-    def body(qkv, attn, glu, down, attn_gain, ffn_gain, out):
-        rows, width = attn.shape
-        half = width // 2
-        units = count * take
-        hidden = count * down_rows
-        first = 3 * half + 128
-        middle = first + width
-        last = middle + 2 * units
-
-        def pick(side):
+def pack_qkv_kernel(half):
+    def body(weight, attn_gain, ffn_gain, out):
+        width = 2 * half
+        rows = weight.shape[0]
+
+        def pick(first):
             for i in range(3):
-                at = i * width + side * half
-                out[:, i * half : (i + 1) * half] = qkv[:, at : at + half]
-            skip = side * (down_rows - take)
-            for part in range(2):
-                for s in range(count):
-                    at = part * hidden + s * down_rows + skip
-                    to = middle + part * units + s * take
-                    out[:, to : to + take] = glu[:, at : at + take]
-            out[0:take, last:] = down[skip : skip + take, :]
+                out[:, i * half : (i + 1) * half] = weight[
+                    :, i * width + first : i * width + first + half
+                ]
 
         @pl.when(side_at() == 0)
         def _():
@@ -213,59 +207,131 @@
 
         @pl.when(side_at() != 0)
         def _():
-            pick(1)
-
-        out[:, first:middle] = attn[...]
-        if rows > take:
-            out[take:, last:] = jnp.zeros((rows - take, width), BF)
+            pick(half)
+
         gains = [ref[...].astype(F32) for ref in (attn_gain, ffn_gain)]
         gains = jnp.concatenate(gains + [jnp.zeros((6, rows), F32)], axis=0)
         gains = jnp.concatenate([gains, jnp.zeros((8, 128 - rows), F32)], axis=1)
         square = jnp.concatenate([gains, jnp.zeros((120, 128), F32)], axis=0)
-        out[:, 3 * half : first] = square.T[0:rows, :].astype(BF)
+        out[:, 3 * half :] = square.T[0:rows, :].astype(BF)
 
     return body
 
 
-def around_kernel(own, dy_own, partner, near, far, tok, dy):
-    mine = slice(0, BLOCK)
-
-    def arrange(first, first_dy, second, second_dy, before, after):
-        tok[0:BLOCK, :] = before[mine, :]
-        tok[BLOCK : 2 * BLOCK, :] = first
-        tok[2 * BLOCK : 3 * BLOCK, :] = second
-        tok[3 * BLOCK :, :] = after[mine, :]
-        halo = slice(BLOCK, BLOCK + RADIUS)
-        dy[0:RADIUS, :] = before[halo, :]
-        dy[RADIUS : RADIUS + BLOCK, :] = first_dy
-        dy[RADIUS + BLOCK : RADIUS + 2 * BLOCK, :] = second_dy
-        dy[RADIUS + 2 * BLOCK :, :] = after[halo, :]
-
-    other = partner[mine, :]
-    other_dy = partner[BLOCK : 2 * BLOCK, :]
+def pack_mlp_kernel(count, down_rows, take):
+    def body(attn, glu, down, out):
+        rows, width = attn.shape
+        units = count * take
+        hidden = count * down_rows
+        out[:, 0:width] = attn[...]
+        last = width + 2 * units
+
+        def pick(first):
+            for part in range(2):
+                for s in range(count):
+                    at = part * hidden + s * down_rows + first
+                    to = width + part * units + s * take
+                    out[:, to : to + take] = glu[:, at : at + take]
+            out[0:take, last:] = down[first : first + take, :]
+
+        @pl.when(side_at() == 0)
+        def _():
+            pick(0)
+
+        @pl.when(side_at() != 0)
+        def _():
+            pick(down_rows - take)
+
+        if rows > take:
+            out[take:, last:] = jnp.zeros((rows - take, width), BF)
+
+    return body
+
+
+def around_kernel(own, places, partner, near, far, out, cosine, sine, bias):
+    def arrange(*blocks):
+        for i, ref in enumerate(blocks):
+            out[i * BLOCK : (i + 1) * BLOCK, :] = ref[0:BLOCK, :]
 
     @pl.when(side_at() == 0)
     def _():
-        arrange(own[...], dy_own[...], other, other_dy, near, far)
+        arrange(near, own, partner, far)
 
     @pl.when(side_at() != 0)
     def _():
-        arrange(other, other_dy, own[...], dy_own[...], far, near)
+        arrange(far, partner, own, near)
+
+    def places_of(ref):
+        first = ref.shape[0] - 16
+        return ref[first : first + 1, 0:BLOCK].astype(F32) * 256.0 + ref[
+            first + 1 : first + 2, 0:BLOCK
+        ].astype(F32)
+
+    mine, theirs = places[...].astype(F32), places_of(partner)
+    inner, outer = places_of(near), places_of(far)
+    even = side_at() == 0
+    lines = [
+        jnp.where(even, inner, outer),
+        jnp.where(even, mine, theirs),
+        jnp.where(even, theirs, mine),
+        jnp.where(even, outer, inner),
+    ]
+    stacked = jnp.concatenate([jnp.broadcast_to(line, (BLOCK, BLOCK)).T for line in lines], axis=0)
+    lane = lax.broadcasted_iota(jnp.int32, (1, 128), 1)
+    power = lax.rem(lane, HEAD // 2).astype(F32) * (2.0 / HEAD)
+    phases = stacked * jnp.exp(power * -math.log(THETA_BASE))
+    cosine[...] = jnp.cos(phases)
+    sine[...] = jnp.where((lane & 63) < 32, -1.0, 1.0) * jnp.sin(phases)
+    offset = (
+        lax.broadcasted_iota(jnp.int32, (BLOCK, 2 * BLOCK), 1)
+        - RADIUS
+        - lax.broadcasted_iota(jnp.int32, (BLOCK, 2 * BLOCK), 0)
+    )
+    distance = offset.astype(F32)
+    for b in range(3):
+        start = RADIUS + b * BLOCK
+        key = jnp.concatenate([lines[b], lines[b + 1]], axis=1)
+        query = jnp.concatenate([stacked[start : start + BLOCK, :]] * 2, axis=1)
+        later = jnp.where(offset >= 0, key - distance, query + distance)
+        allowed = (jnp.abs(offset) <= RADIUS) & (later >= 0.0)
+        bias[b * BLOCK : (b + 1) * BLOCK, :] = jnp.where(allowed, 0.0, NEGATIVE)
+
+
+def around_back_kernel(own, partner, near, far, out):
+    def arrange(before, first, second, after):
+        out[0:RADIUS, :] = before[...]
+        out[RADIUS : RADIUS + BLOCK, :] = first
+        out[RADIUS + BLOCK : RADIUS + 2 * BLOCK, :] = second
+        out[RADIUS + 2 * BLOCK :, :] = after[...]
+
+    theirs = partner[...]
+
+    @pl.when(side_at() == 0)
+    def _():
+        arrange(near, own[...], theirs, far)
+
+    @pl.when(side_at() != 0)
+    def _():
+        arrange(far, theirs, own[...], near)
 
 
 def qkv_layout(rows, half, weight, gains=None):
-    parts = [(0, rows, 0, 3 * half, weight, 0)]
+    wide = 3 * half
+    split = (wide + 128) // 2
+    streams = [[(0, rows, 0, split, weight, 0)], [(0, rows, 0, wide - split, weight, split)]]
+    streams.append([(0, rows, 0, wide, weight, 0)])
     if gains is not None:
-        parts.append((0, rows, 3 * half, 128, gains, 0))
-    return (parts, (), parts)
-
-
-def project_kernel(pieces, n_refs, rows, width):
+        streams[1].append((0, rows, wide - split, 128, gains, 0))
+        streams[2].append((0, rows, wide, 128, gains, 0))
+    return streams
+
+
+def project_kernel(pieces, n_refs, rows, width, skip):
     half = width // 2
     span = 4 * BLOCK
 
     def body(tok, cosine, sine, bias, *rest):
-        refs, rest = rest[:n_refs], rest[n_refs:]
+        refs, rest = rest[skip : n_refs + skip], rest[n_refs + skip :]
         q_out, k_out, v_out, p_out, ctx_out, normed_out, gains_out = rest[:7]
         weight, gain_cols, normed, sems = rest[7:]
         layout = qkv_layout(rows, half, weight, gain_cols)
@@ -318,19 +384,17 @@
 
 
 def attn_layout(rows, width, attn):
-    parts = [(0, rows, 3 * width // 2 + 128, width, attn, 0)]
+    parts = [(0, rows, 0, width, attn, 0)]
     return (parts, (), parts)
 
 
 def mlp_layout(rows, take, width, units, attn, glu, down):
-    split = 3 * width // 2 + 128 + width
-    first = attn_layout(rows, width, attn)[0]
-    streams = [first]
-    for start in (0, split):
-        parts = [(0, rows, start, 2 * units, glu, 0)]
-        parts.append((0, take, start + 2 * units, width, down, 0))
-        streams.append(parts if start == 0 else first + parts)
-    return streams
+    one = (0, rows, 0, width, attn, 0)
+    gate = (0, rows, width, units, glu, 0)
+    up = (0, rows, 0, units, glu, units)
+    low = (0, take, units, width, down, 0)
+    whole = (one, (0, rows, width, 2 * units, glu, 0), (0, take, width + 2 * units, width, down, 0))
+    return ((one, gate), (up, low), whole)
 
 
 def mlp_kernel(pieces, n_refs, rows, down_rows, take, width, units):
@@ -338,7 +402,7 @@
     pair = slice(RADIUS, RADIUS + 2 * BLOCK)
 
     def body(tok, ctx_own, ctx_other, dy, gains, *rest):
-        refs, rest = rest[2 : n_refs + 2], rest[n_refs + 2 :]
+        refs, rest = rest[1 : n_refs + 1], rest[n_refs + 1 :]
         mix_keep, mix_send, shared, ctx_pair, hidden, gn_out = rest[:6]
         attn, glu, down, ggu, mix, sems = rest[6:]
         layout = mlp_layout(rows, take, width, units, attn, glu, down)
@@ -666,21 +730,19 @@
     chip_bits = bits_of(count)[1:]
 
     own = call(
-        pack_kernel(count, down_rows, take),
-        shaped((rows, 3 * half + 128 + 2 * width + 2 * units), BF),
-        (qkv_weight, attn_weight, glu_weight, down_weight, attn_gain[None], ffn_gain[None]),
+        pack_qkv_kernel(half),
+        shaped((rows, 3 * half + 128), BF),
+        (qkv_weight, attn_gain[None], ffn_gain[None]),
         [],
         [],
         1_000_000,
-        2_000_000,
+        1_000_000,
     )
 
     places = jnp.stack([positions >> 8, positions & 255]).astype(BF)
     places = jnp.pad(places, ((0, 14), (0, width - block)))
-    rim = jnp.where(side == 0, cotangent[:RADIUS], cotangent[block - RADIUS :])
-    rim = jnp.concatenate([tokens, rim, places], axis=0)
-    packed = jnp.concatenate([tokens, cotangent, places], axis=0)
-    rim, packed, _ = lax.optimization_barrier((rim, packed, own))
+    rim = jnp.concatenate([tokens, places], axis=0)
+    rim, _ = lax.optimization_barrier((rim, own))
     step = [1 if i & 1 else -1 for i in range(everyone)]
     both = ("shard", "replica")
 
@@ -688,56 +750,50 @@
         moves = [(i, i + step[i]) for i in range(everyone)]
         return lax.ppermute(array, both, [(a, b) for a, b in moves if 0 <= b < everyone])
 
-    near, partner = outward(rim), xor_send(packed, "replica", 1)
-    parts, (near, partner) = gather_pieces(
-        own, 3 * half + 128 + width, chip_bits, (near, partner)
-    )
-    far = xor_send(near, "replica", 1)
-
-    tok, dy = call(
-        around_kernel,
-        (shaped((4 * BLOCK, width), BF), shaped((3 * BLOCK, width), BF)),
-        (tokens, cotangent, partner, near, far),
+    own_mlp = call(
+        pack_mlp_kernel(count, down_rows, take),
+        shaped((rows, 2 * width + 2 * units), BF),
+        (attn_weight, glu_weight, down_weight),
         [],
         [],
         1_000_000,
         2_000_000,
     )
-
-    def places_of(packed, row):
-        return packed[row, :block].astype(F32) * 256.0 + packed[row + 1, :block].astype(F32)
-
-    mine, theirs = positions.astype(F32), places_of(partner, 2 * block)
-    inner, outer = places_of(near, block + RADIUS), places_of(far, block + RADIUS)
-    where = jnp.where(
-        side == 0,
-        jnp.concatenate([inner, mine, theirs, outer]),
-        jnp.concatenate([outer, theirs, mine, inner]),
-    )
-    middle = HEAD // 2
-    inverse = THETA_BASE ** (-(jnp.arange(middle, dtype=F32) * 2.0 / HEAD))
-    phases = where[:, None] * inverse[None, :]
-    cosine, sine = jnp.cos(phases), jnp.sin(phases)
-    cosine = jnp.concatenate([cosine] * 4, axis=1)
-    sine = jnp.concatenate([-sine, sine, -sine, sine], axis=1)
-    offset = (
-        jnp.arange(2 * BLOCK, dtype=jnp.int32)[None, :]
-        - RADIUS
-        - jnp.arange(BLOCK, dtype=jnp.int32)[:, None]
-    )
-    bias = []
-    for b in range(3):
-        later_key = where[None, b * BLOCK : (b + 2) * BLOCK] >= offset.astype(F32)
-        start = RADIUS + b * BLOCK
-        later_query = where[start : start + BLOCK, None] >= -offset.astype(F32)
-        allowed = (jnp.abs(offset) <= RADIUS) & jnp.where(offset >= 0, later_key, later_query)
-        bias.append(jnp.where(allowed, 0.0, NEGATIVE))
-    bias = jnp.concatenate(bias, axis=0).astype(F32)
-    names, arrays = with_core(parts)
+    qkv_parts, _ = gather_pieces(
+        own, (3 * half + 128) // 2, chip_bits, rim
+    )
+    near, partner = outward(rim), xor_send(rim, "replica", 1)
+    arrived = [a for _, _, a in qkv_parts]
+    own, near, partner, arrived = lax.optimization_barrier((own_mlp, near, partner, arrived))
+    qkv_parts = [(j, s, a) for (j, s, _), a in zip(qkv_parts, arrived)]
+    far = xor_send(near, "replica", 1)
+    mlp_parts, forward = gather_pieces(own, width + units, chip_bits)
+
+    tok, cosine, sine, bias = call(
+        around_kernel,
+        (
+            shaped((4 * BLOCK, width), BF),
+            shaped((4 * BLOCK, 128), F32),
+            shaped((4 * BLOCK, 128), F32),
+            shaped((3 * BLOCK, 2 * BLOCK), F32),
+        ),
+        (tokens, positions[None], partner, near, far),
+        [],
+        [],
+        1_000_000,
+        2_000_000,
+    )
+    rim = jnp.where(side == 0, cotangent[:RADIUS], cotangent[block - RADIUS :])
+    rim, _ = lax.optimization_barrier((rim, near))
+    near_dy = outward(rim)
+    sent, near_dy = lax.optimization_barrier((cotangent, near_dy))
+    partner_dy = xor_send(sent, "replica", 1)
+    far_dy = xor_send(near_dy, "replica", 1)
+    qkv_names, qkv_arrays = with_core(qkv_parts, True)
     weight_bytes = width * 3 * width * 2
 
     q, k, v, p, ctx, normed, gains = call(
-        project_kernel(names, len(arrays), rows, width),
+        project_kernel(qkv_names, len(qkv_arrays), rows, width, 2 + len(forward)),
         (
             shaped((3 * BLOCK, half), BF),
             shaped((4 * BLOCK, half), BF),
@@ -748,19 +804,34 @@
             shaped((8, width), F32),
         ),
         (tok, cosine, sine, bias),
-        arrays,
+        [far_dy, partner_dy] + forward + qkv_arrays,
         [
             pltpu.VMEM((width, 3 * half), BF),
             pltpu.VMEM((width, 128), BF),
             pltpu.VMEM((4 * BLOCK, width), BF),
-            pltpu.SemaphoreType.DMA((2 * len(names),)),
+            pltpu.SemaphoreType.DMA((2 * len(qkv_names),)),
         ],
         7_000_000_000,
         weight_bytes,
     )
     ctx_other = xor_send(ctx, "replica", 1)
     normed_other = xor_send(normed, "shard", 1)
+    near_dy, far_dy, partner_dy, _ = lax.optimization_barrier(
+        (near_dy, far_dy, partner_dy, ctx)
+    )
+    dy = call(
+        around_back_kernel,
+        shaped((3 * BLOCK, width), BF),
+        (cotangent, partner_dy, near_dy, far_dy),
+        [],
+        [],
+        1_000_000,
+        2_000_000,
+    )
     dy_other = xor_send(dy, "shard", 1)
+    held, _ = lax.optimization_barrier(([a for _, _, a in mlp_parts], ctx))
+    mlp_parts = [(j, s, a) for (j, s, _), a in zip(mlp_parts, held)]
+    names, arrays = with_core(mlp_parts, False)
 
     mix_keep, mix_send, shared, ctx_pair, hidden, gn = call(
         mlp_kernel(names, len(arrays), rows, down_rows, take, width, units),
@@ -773,7 +844,7 @@
             shaped((3 * BLOCK, width), BF),
         ),
         (tok, ctx, ctx_other, dy, gains),
-        [normed_other, dy_other] + arrays,
+        [normed_other] + arrays,
         [
             pltpu.VMEM((width, width), BF),
             pltpu.VMEM((width, 2 * units), BF),
@@ -846,14 +917,14 @@
     gj, mlp_sums = lax.optimization_barrier((gj, mlp_sums))
     gj_other = xor_send(gj, "shard", 1)
     norm_keep, norm_send = call(
-        norm_back_kernel(names, len(arrays), rows, width),
+        norm_back_kernel(qkv_names, len(qkv_arrays), rows, width),
         (shaped((BLOCK, width), F32), shaped((BLOCK, width), BF)),
         (gj,),
-        arrays,
+        qkv_arrays,
         [
             pltpu.VMEM((width, 3 * half), BF),
             pltpu.VMEM((2 * BLOCK, width), F32),
-            pltpu.SemaphoreType.DMA((len(names),)),
+            pltpu.SemaphoreType.DMA((len(qkv_names),)),
         ],
         3_000_000_000,
         weight_bytes,

time: 162 us -> 145 us (0.90)
  Pallas kernels: 53.6 us -> 24.8 us
  starting transfers between devices: 31.8 us -> 47.4 us
  waiting for transfers between devices: 55.9 us -> 63.5 us
  other arithmetic: 11.3 us -> 4.2 us
  local copies, waits for them, and re-layouts: 8.12 us -> 3.38 us
    pallas_call x12 -> x14, Pallas kernels: 53.6 us -> 24.8 us  [call(): pl.pallas_call(kernel, out_shape=out_shape, in_specs=specs, out_specs=jax...]
    ppermute x34 -> x41, starting transfers between devices: 31.1 us -> 46.1 us  [xor_send(): return lax.ppermute(array, axis, [(i, i ^ bit) for i in range(count)])]
    ppermute x34 -> x41, waiting for transfers between devices: 55.9 us -> 63.5 us  [xor_send(): return lax.ppermute(array, axis, [(i, i ^ bit) for i in range(count)])]
    unnamed x72 -> x32, local copies, waits for them, and re-layouts: 7.99 us -> 3.31 us
    convert_element_type x12, other arithmetic: 3.39 us -> 0.65 us  [add_low(): return (left.astype(F32) + right.astype(F32)).astype(BF)]
    concatenate x6 -> x3, other arithmetic: 4.34 us -> 2.15 us  [the longest x2 1.2 us: with_core(): sent = jnp.concatenate(sent, axis=0) if len(sent) > 1 else sent[0]]
  transfers between devices with their start and end apart: 35 -> 43, of which waited for: 14 -> 21; matrix products, arithmetic and copies ran while one was open for 6% -> 2% of each run, Pallas kernels for 24% -> 12%
where the time goes in v4:
time: 145 us; the launch traced here: 144 us
  waiting for transfers between devices  63.5 us (44%)
  starting transfers between devices  47.4 us (33%)
  Pallas kernels  24.8 us (17%)
  other arithmetic  4.2 us (3%)
  local copies, waits for them, and re-layouts  3.38 us (2%)
    ppermute x41, waiting for transfers between devices, xor_send(): return lax.ppermute(array, axis, [(i, i ^ bit) for i in range(count)])  63.5 us
    ppermute x41, starting transfers between devices, xor_send(): return lax.ppermute(array, axis, [(i, i ^ bit) for i in range(count)])  46.1 us
    pallas_call x14, Pallas kernels, call(): pl.pallas_call(kernel, out_shape=out_shape, in_specs=specs, out_specs=jax...  24.8 us
    unnamed x32, local copies, waits for them, and re-layouts  3.31 us
  transfers between devices with their start and end apart: 43, of which 21 were waited for; matrix products, arithmetic and copies ran while one was open for 2% of the time, Pallas kernels for 12%

profile of v4, /device:TPU:0, one launch (start us, length us, event | category | flops | bytes accessed | tf_op | source)
XLA Modules:
  0.0 144.4 jit_solution(8125812834175822119)
XLA Ops:
  3.1 3.0 %collective-permute-start.2 = (bf16[96,1280]{1,0:T(8,128)(2,1)S(1)}, bf16[96,1280]{1,0:T(8,128)(2,1)S(1)}, u32[]{:S(2)}, u32[]{:S(2)}) collective-permute-start(bf16[96,1280]{1,0:T(8,128)(2,1)S(1)} %shard_map.153.rest_4_.rest_0_), channel_id=1, source_target_pairs={{0,8},{4,12},{8,0},{12,4},{16,24},{20,28},{24,16},{28,20},{1,9},{5... | collective-permute-start | bytes 737288 | tf_op jit(solution)/shard_map/ppermute | solution.py:23
  6.1 1.5 %collective-permute-start.3 = (bf16[96,1280]{1,0:T(8,128)(2,1)S(1)}, bf16[96,1280]{1,0:T(8,128)(2,1)S(1)}, u32[]{:S(2)}, u32[]{:S(2)}) collective-permute-start(bf16[96,1280]{1,0:T(8,128)(2,1)S(1)} %shard_map.153.rest_4_.rest_0_), channel_id=1, source_target_pairs={{0,16},{4,20},{8,24},{12,28},{16,0},{20,4},{24,8},{28,12},{1,17},{... | collective-permute-start | bytes 737288 | tf_op jit(solution)/shard_map/ppermute | solution.py:23
  9.9 4.5 %collective-permute-start.1 = (bf16[144,768]{1,0:T(8,128)(2,1)S(1)}, bf16[144,768]{1,0:T(8,128)(2,1)S(1)}, u32[]{:S(2)}, u32[]{:S(2)}) collective-permute-start(bf16[144,768]{1,0:T(8,128)(2,1)S(1)} %pad_maximum_fusion.1), channel_id=1, source_target_pairs={{0,1},{1,0},{2,3},{3,2},{4,5},{5,4},{6,7},{7,6},{8,9},{9,8},{10,11... | collective-permute-start | bytes 663560 | tf_op jit(solution)/shard_map/ppermute | solution.py:23
  16.1 9.1 %collective-permute-done.1.partner = bf16[144,768]{1,0:T(8,128)(2,1)S(1)} collective-permute-done((bf16[144,768]{1,0:T(8,128)(2,1)S(1)}, bf16[144,768]{1,0:T(8,128)(2,1)S(1)}, u32[]{:S(2)}, u32[]{:S(2)}) %collective-permute-start.1) | collective-permute-done | bytes 221216 | tf_op jit(solution)/shard_map/ppermute | solution.py:23
  27.6 1.8 %collective-permute-start.6 = (bf16[144,768]{1,0:T(8,128)(2,1)S(1)}, bf16[144,768]{1,0:T(8,128)(2,1)S(1)}, u32[]{:S(2)}, u32[]{:S(2)}) collective-permute-start(bf16[144,768]{1,0:T(8,128)(2,1)S(1)} %collective-permute-done.near), channel_id=1, source_target_pairs={{0,1},{1,0},{2,3},{3,2},{4,5},{5,4},{6,7},{7,6},{8,9},{9,8},{10,11... | collective-permute-start | bytes 663560 | tf_op jit(solution)/shard_map/ppermute | solution.py:23
  30.1 6.1 %collective-permute-start.9 = (bf16[128,768]{1,0:T(8,128)(2,1)S(1)}, bf16[128,768]{1,0:T(8,128)(2,1)S(1)}, u32[]{:S(2)}, u32[]{:S(2)}) collective-permute-start(bf16[128,768]{1,0:T(8,128)(2,1)S(1)} %copy-done.4), channel_id=1, source_target_pairs={{0,1},{1,0},{2,3},{3,2},{4,5},{5,4},{6,7},{7,6},{8,9},{9,8},{10,11... | collective-permute-start | bytes 589832 | tf_op jit(solution)/shard_map/ppermute | solution.py:23
  36.2 1.5 %collective-permute-start.8 = (bf16[64,768]{1,0:T(8,128)(2,1)S(1)}, bf16[64,768]{1,0:T(8,128)(2,1)S(1)}, u32[]{:S(2)}, u32[]{:S(2)}) collective-permute-start(bf16[64,768]{1,0:T(8,128)(2,1)S(1)} %collective-permute-done.7.near), channel_id=1, source_target_pairs={{0,1},{1,0},{2,3},{3,2},{4,5},{5,4},{6,7},{7,6},{8,9},{9,8},{10,11... | collective-permute-start | bytes 294920 | tf_op jit(solution)/shard_map/ppermute | solution.py:23
  39.8 2.2 %collective-permute-done.10.rest_2_ = bf16[96,2816]{1,0:T(8,128)(2,1)S(1)} collective-permute-done((bf16[96,2816]{1,0:T(8,128)(2,1)S(1)}, bf16[96,2816]{1,0:T(8,128)(2,1)S(1)}, u32[]{:S(2)}, u32[]{:S(2)}) %collective-permute-start.10) | collective-permute-done | bytes 540704 | tf_op jit(solution)/shard_map/ppermute | solution.py:23
  42.1 2.8 %collective-permute-start.15 = (bf16[96,1408]{1,0:T(8,128)(2,1)S(1)}, bf16[96,1408]{1,0:T(8,128)(2,1)S(1)}, u32[]{:S(2)}, u32[]{:S(2)}) collective-permute-start(bf16[96,1408]{1,0:T(8,128)(2,1)S(1)} %slice.88.rest_2_), channel_id=1, source_target_pairs={{0,16},{4,20},{8,24},{12,28},{16,0},{20,4},{24,8},{28,12},{1,17},{... | collective-permute-start | bytes 811016 | tf_op jit(solution)/shard_map/ppermute | solution.py:23
  45.0 4.3 %shard_map.155 = (bf16[384,384]{1,0:T(8,128)(2,1)S(1)}, bf16[512,384]{1,0:T(8,128)(2,1)S(1)}, bf16[512,384]{1,0:T(8,128)(2,1)S(1)}, bf16[18,128,256]{2,1,0:T(8,1...) custom-call(bf16[512,768]{1,0:T(8,128)(2,1)S(1)} %get-tuple-element.87.tok, ...), custom_call_target="tpu_custom_call" | custom-call | flops 7000000000 | bytes 3538944 | tf_op jit(solution)/shard_map/pallas_call | solution.py:170
  52.8 3.2 %collective-permute-done.18.rest_7_ = bf16[96,1408]{1,0:T(8,128)(2,1)S(1)} collective-permute-done((bf16[96,1408]{1,0:T(8,128)(2,1)S(1)}, bf16[96,1408]{1,0:T(8,128)(2,1)S(1)}, u32[]{:S(2)}, u32[]{:S(2)}) %collective-permute-start.18) | collective-permute-done | bytes 270368 | tf_op jit(solution)/shard_map/ppermute | solution.py:23
  56.4 4.7 %collective-permute-done.13.ctx_other = bf16[384,384]{1,0:T(8,128)(2,1)S(1)} collective-permute-done((bf16[384,384]{1,0:T(8,128)(2,1)S(1)}, bf16[384,384]{1,0:T(8,128)(2,1)S(1)}, u32[]{:S(2)}, u32[]{:S(2)}) %collective-permute-start.13) | collective-permute-done | bytes 294944 | tf_op jit(solution)/shard_map/ppermute | solution.py:23
  61.1 5.4 %shard_map.157 = (f32[128,768]{1,0:T(8,128)S(1)}, bf16[128,768]{1,0:T(8,128)(2,1)S(1)}, bf16[256,2688]{1,0:T(8,128)(2,1)S(1)}, bf16[256,768]{1,0:T(8,128)(2,1)S(...) custom-call(bf16[512,768]{1,0:T(8,128)(2,1)S(1)} %get-tuple-element.87.tok, ...), custom_call_target="tpu_custom_call" | custom-call | flops 8000000000 | bytes 7077888 | tf_op jit(solution)/shard_map/pallas_call | solution.py:170
  67.5 1.7 %collective-permute-start.26 = (bf16[128,768]{1,0:T(8,128)(2,1)S(1)}, bf16[128,768]{1,0:T(8,128)(2,1)S(1)}, u32[]{:S(2)}, u32[]{:S(2)}) collective-permute-start(bf16[128,768]{1,0:T(8,128)(2,1)S(1)} %get-tuple-element.129), channel_id=1, source_target_pairs={{0,1},{1,0},{2,3},{3,2},{4,5},{5,4},{6,7},{7,6},{8,9},{9,8},{10,11... | collective-permute-start | bytes 589832 | tf_op jit(solution)/shard_map/ppermute | solution.py:23
  74.5 8.9 %collective-permute-done.20.gn_other = bf16[384,768]{1,0:T(8,128)(2,1)S(1)} collective-permute-done((bf16[384,768]{1,0:T(8,128)(2,1)S(1)}, bf16[384,768]{1,0:T(8,128)(2,1)S(1)}, u32[]{:S(2)}, u32[]{:S(2)}) %collective-permute-start.20) | collective-permute-done | bytes 589856 | tf_op jit(solution)/shard_map/ppermute | solution.py:23
  83.3 2.6 %shard_map.159 = (f32[128,768]{1,0:T(8,128)S(1)}, bf16[256,384]{1,0:T(8,128)(2,1)S(1)}, bf16[384,384]{1,0:T(8,128)(2,1)S(1)}, bf16[256,384]{1,0:T(8,128)(2,1)S(1)}) custom-call(bf16[384,768]{1,0:T(8,128)(2,1)S(1)} %get-tuple-element.112.gn_own, bf16[384,768]{1,0:T(8,128)(2,1)S(1)} %collective-permute-done.20.gn_other, ...), custom_call_target="tpu_custom_call" | custom-call | flops 5000000000 | bytes 3538944 | tf_op jit(solution)/shard_map/pallas_call | solution.py:170
  86.5 1.5 %collective-permute-start.27 = (bf16[1,720,128]{2,1,0:T(8,128)(2,1)S(1)}, bf16[1,720,128]{2,1,0:T(8,128)(2,1)S(1)}, u32[]{:S(2)}, u32[]{:S(2)}) collective-permute-start(bf16[1,720,128]{2,1,0:T(8,128)(2,1)S(1)} %add_convert_fusion.8.sent_0), channel_id=1, source_target_pairs={{0,16},{4,20},{8,24},{12,28},{16,0},{20,4},{24,8},{28,12},{1,17},{... | collective-permute-start | bytes 552968 | tf_op jit(solution)/shard_map/ppermute | solution.py:23
  88.0 2.2 %shard_map.160.gj.own = bf16[256,1536]{1,0:T(8,128)(2,1)S(1)} custom-call(bf16[256,384]{1,0:T(8,128)(2,1)S(1)} %get-tuple-element.121.first, bf16[256,384]{1,0:T(8,128)(2,1)S(1)} %get-tuple-element.122.halves, bf16[384,384]{1,0:T(8,128)(2,1)S(1)} %get-tuple-element.123.gctx, bf16[384,384]{1,0:T(8,128)(2,1)S(1)} %get-tuple-element.114.q, ...), custom_call_target="tpu_custom_call" | custom-call | flops 6000000000 | bytes 3538944 | tf_op jit(solution)/shard_map/pallas_call | solution.py:170
  90.2 1.6 %collective-permute-done.28 = bf16[1,720,128]{2,1,0:T(8,128)(2,1)S(1)} collective-permute-done((bf16[1,720,128]{2,1,0:T(8,128)(2,1)S(1)}, bf16[1,720,128]{2,1,0:T(8,128)(2,1)S(1)}, u32[]{:S(2)}, u32[]{:S(2)}) %collective-permute-start.28) | collective-permute-done | bytes 184352 | tf_op jit(solution)/shard_map/ppermute | solution.py:23
  92.4 2.3 %collective-permute-start.33 = (bf16[720,128]{1,0:T(8,128)(2,1)S(1)}, bf16[720,128]{1,0:T(8,128)(2,1)S(1)}, u32[]{:S(2)}, u32[]{:S(2)}) collective-permute-start(bf16[720,128]{1,0:T(8,128)(2,1)S(1)} %fusion), channel_id=1, source_target_pairs={{0,2},{1,3},{2,0},{3,1},{4,6},{5,7},{6,4},{7,5},{8,10},{9,11},{10,... | collective-permute-start | bytes 552968 | tf_op jit(solution)/shard_map/ppermute | solution.py:23
  94.7 2.3 %shard_map.161 = (f32[128,768]{1,0:T(8,128)S(1)}, bf16[128,768]{1,0:T(8,128)(2,1)S(1)}) custom-call(bf16[256,1536]{1,0:T(8,128)(2,1)S(1)} %shard_map.160.gj.own, bf16[96,1280]{1,0:T(8,128)(2,1)S(1)} %shard_map.153.rest_4_.rest_0_, bf16[96,1280]{1,0:T(8,128)(2,1)S(1)} %collective-permute-done.2.rest_5_.rest_1_, ...), custom_call_target="tpu_custom_call" | custom-call | flops 3000000000 | bytes 3538944 | tf_op jit(solution)/shard_map/pallas_call | solution.py:170
  98.8 1.7 %collective-permute-start.37 = (bf16[720,128]{1,0:T(8,128)(2,1)S(1)}, bf16[720,128]{1,0:T(8,128)(2,1)S(1)}, u32[]{:S(2)}, u32[]{:S(2)}) collective-permute-start(bf16[720,128]{1,0:T(8,128)(2,1)S(1)} %fusion.1), channel_id=1, source_target_pairs={{0,2},{1,3},{2,0},{3,1},{4,6},{5,7},{6,4},{7,5},{8,10},{9,11},{10,... | collective-permute-start | bytes 552968 | tf_op jit(solution)/shard_map/ppermute | solution.py:23
  100.5 8.2 %collective-permute-done.33 = bf16[720,128]{1,0:T(8,128)(2,1)S(1)} collective-permute-done((bf16[720,128]{1,0:T(8,128)(2,1)S(1)}, bf16[720,128]{1,0:T(8,128)(2,1)S(1)}, u32[]{:S(2)}, u32[]{:S(2)}) %collective-permute-start.33) | collective-permute-done | bytes 184352 | tf_op jit(solution)/shard_map/ppermute | solution.py:23
  110.2 2.0 %collective-permute-start.30 = (bf16[128,768]{1,0:T(8,128)(2,1)S(1)}, bf16[128,768]{1,0:T(8,128)(2,1)S(1)}, u32[]{:S(2)}, u32[]{:S(2)}) collective-permute-start(bf16[128,768]{1,0:T(8,128)(2,1)S(1)} %get-tuple-element.135), channel_id=1, source_target_pairs={{0,1},{1,0},{2,3},{3,2},{4,5},{5,4},{6,7},{7,6},{8,9},{9,8},{10,11... | collective-permute-start | bytes 589832 | tf_op jit(solution)/shard_map/ppermute | solution.py:23
  112.3 4.5 %collective-permute-done.32 = bf16[2,576,128]{2,1,0:T(8,128)(2,1)S(1)} collective-permute-done((bf16[2,576,128]{2,1,0:T(8,128)(2,1)S(1)}, bf16[2,576,128]{2,1,0:T(8,128)(2,1)S(1)}, u32[]{:S(2)}, u32[]{:S(2)}) %collective-permute-start.32) | collective-permute-done | bytes 294944 | tf_op jit(solution)/shard_map/ppermute | solution.py:23
  116.8 1.8 %collective-permute-start.35 = (bf16[1,576,128]{2,1,0:T(8,128)(2,1)S(1)}, bf16[1,576,128]{2,1,0:T(8,128)(2,1)S(1)}, u32[]{:S(2)}, u32[]{:S(2)}) collective-permute-start(bf16[1,576,128]{2,1,0:T(8,128)(2,1)S(1)} %add_convert_fusion.15), channel_id=1, source_target_pairs={{0,8},{4,12},{8,0},{12,4},{16,24},{20,28},{24,16},{28,20},{1,9},{5... | collective-permute-start | bytes 442376 | tf_op jit(solution)/shard_map/ppermute | solution.py:23
  119.9 2.2 %collective-permute-done.35 = bf16[1,576,128]{2,1,0:T(8,128)(2,1)S(1)} collective-permute-done((bf16[1,576,128]{2,1,0:T(8,128)(2,1)S(1)}, bf16[1,576,128]{2,1,0:T(8,128)(2,1)S(1)}, u32[]{:S(2)}, u32[]{:S(2)}) %collective-permute-start.35) | collective-permute-done | bytes 147488 | tf_op jit(solution)/shard_map/ppermute | solution.py:23
  127.3 1.6 %shard_map.164 = (f32[96,2304]{1,0:T(8,128)}, f32[144,768]{1,0:T(8,128)}, f32[1,96]{1,0:T(1,128)}) custom-call(bf16[720,128]{1,0:T(8,128)(2,1)S(1)} %add_convert_fusion.2.mine_0, bf16[720,128]{1,0:T(8,128)(2,1)S(1)} %add_convert_fusion.1.mine_1, bf16[720,128]{1,0:T(8,128)(2,1)S(1)} %collective-permute-done.38.other_0, ...), custom_call_target="tpu_custom_call" | custom-call | flops 1000000 | bytes 4000000 | tf_op jit(solution)/shard_map/pallas_call | solution.py:170
  128.9 6.2 %collective-permute-done.40 = bf16[576,128]{1,0:T(8,128)(2,1)S(1)} collective-permute-done((bf16[576,128]{1,0:T(8,128)(2,1)S(1)}, bf16[576,128]{1,0:T(8,128)(2,1)S(1)}, u32[]{:S(2)}, u32[]{:S(2)}) %collective-permute-start.40) | collective-permute-done | bytes 147488 | tf_op jit(solution)/shard_map/ppermute | solution.py:23
  135.3 1.5 %collective-permute-done.36 = bf16[576,128]{1,0:T(8,128)(2,1)S(1)} collective-permute-done((bf16[576,128]{1,0:T(8,128)(2,1)S(1)}, bf16[576,128]{1,0:T(8,128)(2,1)S(1)}, u32[]{:S(2)}, u32[]{:S(2)}) %collective-permute-start.36) | collective-permute-done | bytes 147488 | tf_op jit(solution)/shard_map/ppermute | solution.py:23
  137.4 4.0 %collective-permute-done.42.other_1 = bf16[576,128]{1,0:T(8,128)(2,1)S(1)} collective-permute-done((bf16[576,128]{1,0:T(8,128)(2,1)S(1)}, bf16[576,128]{1,0:T(8,128)(2,1)S(1)}, u32[]{:S(2)}, u32[]{:S(2)}) %collective-permute-start.42) | collective-permute-done | bytes 147488 | tf_op jit(solution)/shard_map/ppermute | solution.py:23
  141.4 1.6 %collective-permute-done.41.other_0 = bf16[576,128]{1,0:T(8,128)(2,1)S(1)} collective-permute-done((bf16[576,128]{1,0:T(8,128)(2,1)S(1)}, bf16[576,128]{1,0:T(8,128)(2,1)S(1)}, u32[]{:S(2)}, u32[]{:S(2)}) %collective-permute-start.41) | collective-permute-done | bytes 147488 | tf_op jit(solution)/shard_map/ppermute | solution.py:23
  (123 shorter events, 34.9 us)
Async XLA Ops:
  3.1 11.3 %collective-permute-start.2 = (bf16[96,1280]{1,0:T(8,128)(2,1)S(1)}, bf16[96,1280]{1,0:T(8,128)(2,1)S(1)}, u32[]{:S(2)}, u32[]{:S(2)}) collective-permute-start(bf16[96,1280]{1,0:T(8,128)(2,1)S(1)} %shard_map.153.rest_4_.rest_0_), channel_id=1, source_target_pairs={{0,8},{4,12},{8,0},{12,4},{16,24},{20,28},{24,16},{28,20},{1,9},{5... | collective-permute-start | bytes 737288 | tf_op jit(solution)/shard_map/ppermute | solution.py:23
  6.1 8.3 %collective-permute-start.3 = (bf16[96,1280]{1,0:T(8,128)(2,1)S(1)}, bf16[96,1280]{1,0:T(8,128)(2,1)S(1)}, u32[]{:S(2)}, u32[]{:S(2)}) collective-permute-start(bf16[96,1280]{1,0:T(8,128)(2,1)S(1)} %shard_map.153.rest_4_.rest_0_), channel_id=1, source_target_pairs={{0,16},{4,20},{8,24},{12,28},{16,0},{20,4},{24,8},{28,12},{1,17},{... | collective-permute-start | bytes 737288 | tf_op jit(solution)/shard_map/ppermute | solution.py:23
  9.2 6.9 %collective-permute-start = (bf16[144,768]{1,0:T(8,128)(2,1)S(1)}, bf16[144,768]{1,0:T(8,128)(2,1)S(1)}, u32[]{:S(2)}, u32[]{:S(2)}) collective-permute-start(bf16[144,768]{1,0:T(8,128)(2,1)S(1)} %pad_maximum_fusion.1), channel_id=1, source_target_pairs={{1,2},{2,1},{3,4},{4,3},{5,6},{6,5},{7,8},{8,7},{9,10},{10,9},{11,... | collective-permute-start | bytes 663560 | tf_op jit(solution)/shard_map/ppermute | solution.py:751
  9.9 15.3 %collective-permute-start.1 = (bf16[144,768]{1,0:T(8,128)(2,1)S(1)}, bf16[144,768]{1,0:T(8,128)(2,1)S(1)}, u32[]{:S(2)}, u32[]{:S(2)}) collective-permute-start(bf16[144,768]{1,0:T(8,128)(2,1)S(1)} %pad_maximum_fusion.1), channel_id=1, source_target_pairs={{0,1},{1,0},{2,3},{3,2},{4,5},{5,4},{6,7},{7,6},{8,9},{9,8},{10,11... | collective-permute-start | bytes 663560 | tf_op jit(solution)/shard_map/ppermute | solution.py:23
  14.4 10.8 %collective-permute-start.4 = (bf16[96,640]{1,0:T(8,128)(2,1)S(1)}, bf16[96,640]{1,0:T(8,128)(2,1)S(1)}, u32[]{:S(2)}, u32[]{:S(2)}) collective-permute-start(bf16[96,640]{1,0:T(8,128)(2,1)S(1)} %slice.66), channel_id=1, source_target_pairs={{0,16},{4,20},{8,24},{12,28},{16,0},{20,4},{24,8},{28,12},{1,17},{... | collective-permute-start | bytes 368648 | tf_op jit(solution)/shard_map/ppermute | solution.py:23
  15.3 9.9 %collective-permute-start.5 = (bf16[96,640]{1,0:T(8,128)(2,1)S(1)}, bf16[96,640]{1,0:T(8,128)(2,1)S(1)}, u32[]{:S(2)}, u32[]{:S(2)}) collective-permute-start(bf16[96,640]{1,0:T(8,128)(2,1)S(1)} %slice.67), channel_id=1, source_target_pairs={{0,8},{4,12},{8,0},{12,4},{16,24},{20,28},{24,16},{28,20},{1,9},{5... | collective-permute-start | bytes 368648 | tf_op jit(solution)/shard_map/ppermute | solution.py:23
  26.3 18.7 %collective-permute-start.12 = (bf16[384,1280]{1,0:T(8,128)(2,1)}, bf16[384,1280]{1,0:T(8,128)(2,1)}, u32[]{:S(2)}, u32[]{:S(2)}) collective-permute-start(bf16[384,1280]{1,0:T(8,128)(2,1)} %maximum_maximum_fusion), channel_id=1, source_target_pairs={{0,4},{4,0},{8,12},{12,8},{16,20},{20,16},{24,28},{28,24},{1,5},{5... | collective-permute-start | bytes 2949128 | tf_op jit(solution)/shard_map/ppermute | solution.py:23
  26.4 15.6 %collective-permute-start.10 = (bf16[96,2816]{1,0:T(8,128)(2,1)S(1)}, bf16[96,2816]{1,0:T(8,128)(2,1)S(1)}, u32[]{:S(2)}, u32[]{:S(2)}) collective-permute-start(bf16[96,2816]{1,0:T(8,128)(2,1)S(1)} %shard_map.152.rest_1_), channel_id=1, source_target_pairs={{0,8},{4,12},{8,0},{12,4},{16,24},{20,28},{24,16},{28,20},{1,9},{5... | collective-permute-start | bytes 1622024 | tf_op jit(solution)/shard_map/ppermute | solution.py:23
  27.6 17.3 %collective-permute-start.11 = (bf16[96,2816]{1,0:T(8,128)(2,1)S(1)}, bf16[96,2816]{1,0:T(8,128)(2,1)S(1)}, u32[]{:S(2)}, u32[]{:S(2)}) collective-permute-start(bf16[96,2816]{1,0:T(8,128)(2,1)S(1)} %shard_map.152.rest_1_), channel_id=1, source_target_pairs={{0,16},{4,20},{8,24},{12,28},{16,0},{20,4},{24,8},{28,12},{1,17},{... | collective-permute-start | bytes 1622024 | tf_op jit(solution)/shard_map/ppermute | solution.py:23
  27.6 8.6 %collective-permute-start.6 = (bf16[144,768]{1,0:T(8,128)(2,1)S(1)}, bf16[144,768]{1,0:T(8,128)(2,1)S(1)}, u32[]{:S(2)}, u32[]{:S(2)}) collective-permute-start(bf16[144,768]{1,0:T(8,128)(2,1)S(1)} %collective-permute-done.near), channel_id=1, source_target_pairs={{0,1},{1,0},{2,3},{3,2},{4,5},{5,4},{6,7},{7,6},{8,9},{9,8},{10,11... | collective-permute-start | bytes 663560 | tf_op jit(solution)/shard_map/ppermute | solution.py:23
  30.1 14.9 %collective-permute-start.9 = (bf16[128,768]{1,0:T(8,128)(2,1)S(1)}, bf16[128,768]{1,0:T(8,128)(2,1)S(1)}, u32[]{:S(2)}, u32[]{:S(2)}) collective-permute-start(bf16[128,768]{1,0:T(8,128)(2,1)S(1)} %copy-done.4), channel_id=1, source_target_pairs={{0,1},{1,0},{2,3},{3,2},{4,5},{5,4},{6,7},{7,6},{8,9},{9,8},{10,11... | collective-permute-start | bytes 589832 | tf_op jit(solution)/shard_map/ppermute | solution.py:23
  36.2 8.8 %collective-permute-start.8 = (bf16[64,768]{1,0:T(8,128)(2,1)S(1)}, bf16[64,768]{1,0:T(8,128)(2,1)S(1)}, u32[]{:S(2)}, u32[]{:S(2)}) collective-permute-start(bf16[64,768]{1,0:T(8,128)(2,1)S(1)} %collective-permute-done.7.near), channel_id=1, source_target_pairs={{0,1},{1,0},{2,3},{3,2},{4,5},{5,4},{6,7},{7,6},{8,9},{9,8},{10,11... | collective-permute-start | bytes 294920 | tf_op jit(solution)/shard_map/ppermute | solution.py:23
  42.1 8.0 %collective-permute-start.15 = (bf16[96,1408]{1,0:T(8,128)(2,1)S(1)}, bf16[96,1408]{1,0:T(8,128)(2,1)S(1)}, u32[]{:S(2)}, u32[]{:S(2)}) collective-permute-start(bf16[96,1408]{1,0:T(8,128)(2,1)S(1)} %slice.88.rest_2_), channel_id=1, source_target_pairs={{0,16},{4,20},{8,24},{12,28},{16,0},{20,4},{24,8},{28,12},{1,17},{... | collective-permute-start | bytes 811016 | tf_op jit(solution)/shard_map/ppermute | solution.py:23
  44.9 6.5 %collective-permute-start.16 = (bf16[96,1408]{1,0:T(8,128)(2,1)S(1)}, bf16[96,1408]{1,0:T(8,128)(2,1)S(1)}, u32[]{:S(2)}, u32[]{:S(2)}) collective-permute-start(bf16[96,1408]{1,0:T(8,128)(2,1)S(1)} %slice.89.rest_3_), channel_id=1, source_target_pairs={{0,8},{4,12},{8,0},{12,4},{16,24},{20,28},{24,16},{28,20},{1,9},{5... | collective-permute-start | bytes 811016 | tf_op jit(solution)/shard_map/ppermute | solution.py:23
  51.5 9.6 %collective-permute-start.17 = (bf16[288,2816]{1,0:T(8,128)(2,1)S(1)}, bf16[288,2816]{1,0:T(8,128)(2,1)S(1)}, u32[]{:S(2)}, u32[]{:S(2)}) collective-permute-start(bf16[288,2816]{1,0:T(8,128)(2,1)S(1)} %pad_maximum_fusion), channel_id=1, source_target_pairs={{0,4},{4,0},{8,12},{12,8},{16,20},{20,16},{24,28},{28,24},{1,5},{5... | collective-permute-start | bytes 4866056 | tf_op jit(solution)/shard_map/ppermute | solution.py:23
  51.6 9.5 %collective-permute-start.14 = (bf16[256,768]{1,0:T(8,128)(2,1)S(1)}, bf16[256,768]{1,0:T(8,128)(2,1)S(1)}, u32[]{:S(2)}, u32[]{:S(2)}) collective-permute-start(bf16[256,768]{1,0:T(8,128)(2,1)S(1)} %get-tuple-element.105.normed_own), channel_id=1, source_target_pairs={{0,4},{4,0},{8,12},{12,8},{16,20},{20,16},{24,28},{28,24},{1,5},{5... | collective-permute-start | bytes 1179656 | tf_op jit(solution)/shard_map/ppermute | solution.py:23
  52.1 9.0 %collective-permute-start.13 = (bf16[384,384]{1,0:T(8,128)(2,1)S(1)}, bf16[384,384]{1,0:T(8,128)(2,1)S(1)}, u32[]{:S(2)}, u32[]{:S(2)}) collective-permute-start(bf16[384,384]{1,0:T(8,128)(2,1)S(1)} %get-tuple-element.100.ctx_own), channel_id=1, source_target_pairs={{0,1},{1,0},{2,3},{3,2},{4,5},{5,4},{6,7},{7,6},{8,9},{9,8},{10,11... | collective-permute-start | bytes 884744 | tf_op jit(solution)/shard_map/ppermute | solution.py:23
  67.2 16.1 %collective-permute-start.20 = (bf16[384,768]{1,0:T(8,128)(2,1)S(1)}, bf16[384,768]{1,0:T(8,128)(2,1)S(1)}, u32[]{:S(2)}, u32[]{:S(2)}) collective-permute-start(bf16[384,768]{1,0:T(8,128)(2,1)S(1)} %get-tuple-element.112.gn_own), channel_id=1, source_target_pairs={{0,1},{1,0},{2,3},{3,2},{4,5},{5,4},{6,7},{7,6},{8,9},{9,8},{10,11... | collective-permute-start | bytes 1769480 | tf_op jit(solution)/shard_map/ppermute | solution.py:23
  67.5 20.5 %collective-permute-start.26 = (bf16[128,768]{1,0:T(8,128)(2,1)S(1)}, bf16[128,768]{1,0:T(8,128)(2,1)S(1)}, u32[]{:S(2)}, u32[]{:S(2)}) collective-permute-start(bf16[128,768]{1,0:T(8,128)(2,1)S(1)} %get-tuple-element.129), channel_id=1, source_target_pairs={{0,1},{1,0},{2,3},{3,2},{4,5},{5,4},{6,7},{7,6},{8,9},{9,8},{10,11... | collective-permute-start | bytes 589832 | tf_op jit(solution)/shard_map/ppermute | solution.py:23
  72.6 13.3 %collective-permute-start.24 = (bf16[2,720,128]{2,1,0:T(8,128)(2,1)S(1)}, bf16[2,720,128]{2,1,0:T(8,128)(2,1)S(1)}, u32[]{:S(2)}, u32[]{:S(2)}) collective-permute-start(bf16[2,720,128]{2,1,0:T(8,128)(2,1)S(1)} %get-tuple-element.124), channel_id=1, source_target_pairs={{0,8},{4,12},{8,0},{12,4},{16,24},{20,28},{24,16},{28,20},{1,9},{5... | collective-permute-start | bytes 1105928 | tf_op jit(solution)/shard_map/ppermute | solution.py:23
  73.1 12.9 %collective-permute-start.25 = (bf16[2,720,128]{2,1,0:T(8,128)(2,1)S(1)}, bf16[2,720,128]{2,1,0:T(8,128)(2,1)S(1)}, u32[]{:S(2)}, u32[]{:S(2)}) collective-permute-start(bf16[2,720,128]{2,1,0:T(8,128)(2,1)S(1)} %get-tuple-element.125), channel_id=1, source_target_pairs={{0,16},{4,20},{8,24},{12,28},{16,0},{20,4},{24,8},{28,12},{1,17},{... | collective-permute-start | bytes 1105928 | tf_op jit(solution)/shard_map/ppermute | solution.py:23
  92.4 16.3 %collective-permute-start.33 = (bf16[720,128]{1,0:T(8,128)(2,1)S(1)}, bf16[720,128]{1,0:T(8,128)(2,1)S(1)}, u32[]{:S(2)}, u32[]{:S(2)}) collective-permute-start(bf16[720,128]{1,0:T(8,128)(2,1)S(1)} %fusion), channel_id=1, source_target_pairs={{0,2},{1,3},{2,0},{3,1},{4,6},{5,7},{6,4},{7,5},{8,10},{9,11},{10,... | collective-permute-start | bytes 552968 | tf_op jit(solution)/shard_map/ppermute | solution.py:23
  98.2 14.0 %collective-permute-start.31 = (bf16[2,576,128]{2,1,0:T(8,128)(2,1)S(1)}, bf16[2,576,128]{2,1,0:T(8,128)(2,1)S(1)}, u32[]{:S(2)}, u32[]{:S(2)}) collective-permute-start(bf16[2,576,128]{2,1,0:T(8,128)(2,1)S(1)} %get-tuple-element.136), channel_id=1, source_target_pairs={{0,8},{4,12},{8,0},{12,4},{16,24},{20,28},{24,16},{28,20},{1,9},{5... | collective-permute-start | bytes 884744 | tf_op jit(solution)/shard_map/ppermute | solution.py:23
  98.8 20.9 %collective-permute-start.37 = (bf16[720,128]{1,0:T(8,128)(2,1)S(1)}, bf16[720,128]{1,0:T(8,128)(2,1)S(1)}, u32[]{:S(2)}, u32[]{:S(2)}) collective-permute-start(bf16[720,128]{1,0:T(8,128)(2,1)S(1)} %fusion.1), channel_id=1, source_target_pairs={{0,2},{1,3},{2,0},{3,1},{4,6},{5,7},{6,4},{7,5},{8,10},{9,11},{10,... | collective-permute-start | bytes 552968 | tf_op jit(solution)/shard_map/ppermute | solution.py:23
  108.7 8.1 %collective-permute-start.32 = (bf16[2,576,128]{2,1,0:T(8,128)(2,1)S(1)}, bf16[2,576,128]{2,1,0:T(8,128)(2,1)S(1)}, u32[]{:S(2)}, u32[]{:S(2)}) collective-permute-start(bf16[2,576,128]{2,1,0:T(8,128)(2,1)S(1)} %get-tuple-element.138), channel_id=1, source_target_pairs={{0,16},{4,20},{8,24},{12,28},{16,0},{20,4},{24,8},{28,12},{1,17},{... | collective-permute-start | bytes 884744 | tf_op jit(solution)/shard_map/ppermute | solution.py:23
  110.1 16.9 %collective-permute-start.38 = (bf16[720,128]{1,0:T(8,128)(2,1)S(1)}, bf16[720,128]{1,0:T(8,128)(2,1)S(1)}, u32[]{:S(2)}, u32[]{:S(2)}) collective-permute-start(bf16[720,128]{1,0:T(8,128)(2,1)S(1)} %add_convert_fusion.2.mine_0), channel_id=1, source_target_pairs={{0,1},{1,0},{2,3},{3,2},{4,5},{5,4},{6,7},{7,6},{8,9},{9,8},{10,11... | collective-permute-start | bytes 552968 | tf_op jit(solution)/shard_map/ppermute | solution.py:23
  110.2 13.0 %collective-permute-start.30 = (bf16[128,768]{1,0:T(8,128)(2,1)S(1)}, bf16[128,768]{1,0:T(8,128)(2,1)S(1)}, u32[]{:S(2)}, u32[]{:S(2)}) collective-permute-start(bf16[128,768]{1,0:T(8,128)(2,1)S(1)} %get-tuple-element.135), channel_id=1, source_target_pairs={{0,1},{1,0},{2,3},{3,2},{4,5},{5,4},{6,7},{7,6},{8,9},{9,8},{10,11... | collective-permute-start | bytes 589832 | tf_op jit(solution)/shard_map/ppermute | solution.py:23
  119.8 7.6 %collective-permute-start.39 = (bf16[720,128]{1,0:T(8,128)(2,1)S(1)}, bf16[720,128]{1,0:T(8,128)(2,1)S(1)}, u32[]{:S(2)}, u32[]{:S(2)}) collective-permute-start(bf16[720,128]{1,0:T(8,128)(2,1)S(1)} %add_convert_fusion.1.mine_1), channel_id=1, source_target_pairs={{0,1},{1,0},{2,3},{3,2},{4,5},{5,4},{6,7},{7,6},{8,9},{9,8},{10,11... | collective-permute-start | bytes 552968 | tf_op jit(solution)/shard_map/ppermute | solution.py:23
  122.1 13.0 %collective-permute-start.40 = (bf16[576,128]{1,0:T(8,128)(2,1)S(1)}, bf16[576,128]{1,0:T(8,128)(2,1)S(1)}, u32[]{:S(2)}, u32[]{:S(2)}) collective-permute-start(bf16[576,128]{1,0:T(8,128)(2,1)S(1)} %fusion.3), channel_id=1, source_target_pairs={{0,2},{1,3},{2,0},{3,1},{4,6},{5,7},{6,4},{7,5},{8,10},{9,11},{10,... | collective-permute-start | bytes 442376 | tf_op jit(solution)/shard_map/ppermute | solution.py:23
  123.9 12.9 %collective-permute-start.36 = (bf16[576,128]{1,0:T(8,128)(2,1)S(1)}, bf16[576,128]{1,0:T(8,128)(2,1)S(1)}, u32[]{:S(2)}, u32[]{:S(2)}) collective-permute-start(bf16[576,128]{1,0:T(8,128)(2,1)S(1)} %fusion.2), channel_id=1, source_target_pairs={{0,2},{1,3},{2,0},{3,1},{4,6},{5,7},{6,4},{7,5},{8,10},{9,11},{10,... | collective-permute-start | bytes 442376 | tf_op jit(solution)/shard_map/ppermute | solution.py:23
  135.2 6.2 %collective-permute-start.42 = (bf16[576,128]{1,0:T(8,128)(2,1)S(1)}, bf16[576,128]{1,0:T(8,128)(2,1)S(1)}, u32[]{:S(2)}, u32[]{:S(2)}) collective-permute-start(bf16[576,128]{1,0:T(8,128)(2,1)S(1)} %add_convert_fusion.9.mine_1), channel_id=1, source_target_pairs={{0,1},{1,0},{2,3},{3,2},{4,5},{5,4},{6,7},{7,6},{8,9},{9,8},{10,11... | collective-permute-start | bytes 442376 | tf_op jit(solution)/shard_map/ppermute | solution.py:23
  136.8 6.2 %collective-permute-start.41 = (bf16[576,128]{1,0:T(8,128)(2,1)S(1)}, bf16[576,128]{1,0:T(8,128)(2,1)S(1)}, u32[]{:S(2)}, u32[]{:S(2)}) collective-permute-start(bf16[576,128]{1,0:T(8,128)(2,1)S(1)} %add_convert_fusion.12.mine_0), channel_id=1, source_target_pairs={{0,1},{1,0},{2,3},{3,2},{4,5},{5,4},{6,7},{7,6},{8,9},{9,8},{10,11... | collective-permute-start | bytes 442376 | tf_op jit(solution)/shard_map/ppermute | solution.py:23
  (27 other events, 210.8 us)

commit v5 on v4

--- a/solution.py
+++ b/solution.py
@@ -14,6 +14,7 @@
 THETA_BASE = 10000.0
 NEGATIVE = -1e30
 VMEM_BYTES = 24 * 1024 * 1024
+VMEM_ALL = 60 * 1024 * 1024
 BF = jnp.bfloat16
 F32 = jnp.float32
 
@@ -25,6 +26,11 @@
 
 def bits_of(count):
     return [1 << i for i in range(count.bit_length() - 1)]
+
+
+def core_send(array, bits):
+    count = lax.axis_size("shard")
+    return lax.ppermute(array, "shard", [(i, i ^ bits[i & 1]) for i in range(count)])
 
 
 def gather_pieces(own, split, chip_bits, before=None):
@@ -80,24 +86,24 @@
 
 
 def scatter_sums(sums, chip_bits, before_add=None, before_last=None):
-    send, keep = [sums[0], sums[2]], [sums[1], sums[3]]
-    orders = (chip_bits, chip_bits[::-1])
-    for step in range(len(chip_bits) - 1):
-        others = [xor_send(send[s], "shard", orders[s][step]) for s in range(2)]
+    send, keep = sums
+    orders = list(zip(chip_bits, chip_bits[::-1]))
+    for bits in orders[:-1]:
+        other = core_send(send, bits)
         if before_add is not None:
-            others, _ = lax.optimization_barrier((others, before_add))
-        for s in range(2):
-            send[s], keep[s] = halve(keep[s], others[s])
-        if before_last is not None:
-            send, _ = lax.optimization_barrier((send, before_last))
+            other, _ = lax.optimization_barrier((other, before_add))
+        send, keep = halve(keep, other)
+    if before_last is not None:
+        send, _ = lax.optimization_barrier((send, before_last))
+    return keep, core_send(send, orders[-1]), send
+
+
+def last_sums(keep, other, _):
+    middle = keep.shape[1] // 2
     return [
-        (keep[s], xor_send(send[s], "shard", orders[s][-1]), send[s]) for s in range(2)
+        add_low(keep[0, :middle], other[0, :middle]),
+        add_low(keep[0, middle:], other[0, middle:]),
     ]
-
-
-def last_sum(stream):
-    keep, other, _ = stream
-    return add_low(keep[0], other[0])
 
 
 def side_sum(total, after=None):
@@ -163,7 +169,7 @@
     return copies
 
 
-def call(kernel, out_shape, inputs, in_any, scratch, flops, traffic):
+def call(kernel, out_shape, inputs, in_any, scratch, flops, traffic, vmem_bytes=VMEM_BYTES):
     any_spec = pl.BlockSpec(memory_space=pl.ANY)
     vmem = pl.BlockSpec(memory_space=pltpu.VMEM)
     specs = [vmem] * len(inputs) + [any_spec] * len(in_any)
@@ -173,7 +179,7 @@
         in_specs=specs,
         out_specs=jax.tree.map(lambda _: vmem, out_shape),
         scratch_shapes=scratch,
-        compiler_params=pltpu.CompilerParams(vmem_limit_bytes=VMEM_BYTES),
+        compiler_params=pltpu.CompilerParams(vmem_limit_bytes=vmem_bytes),
         cost_estimate=pl.CostEstimate(flops=flops, bytes_accessed=traffic, transcendentals=0),
     )(*inputs, *in_any)
 
@@ -191,29 +197,33 @@
 
 
 def pack_qkv_kernel(half):
-    def body(weight, attn_gain, ffn_gain, out):
-        width = 2 * half
+    def body(weight, attn_gain, ffn_gain, out, attn_held, ffn_held, sems):
         rows = weight.shape[0]
-
-        def pick(first):
-            for i in range(3):
-                out[:, i * half : (i + 1) * half] = weight[
-                    :, i * width + first : i * width + first + half
-                ]
-
-        @pl.when(side_at() == 0)
-        def _():
-            pick(0)
-
-        @pl.when(side_at() != 0)
-        def _():
-            pick(half)
-
-        gains = [ref[...].astype(F32) for ref in (attn_gain, ffn_gain)]
+        first = side_at() * half
+        copies = [
+            pltpu.make_async_copy(attn_gain, attn_held, sems.at[0]),
+            pltpu.make_async_copy(ffn_gain, ffn_held, sems.at[1]),
+        ]
+        for i in range(3):
+            start = pl.multiple_of(i * 2 * half + first, 128)
+            copies.append(
+                pltpu.make_async_copy(
+                    weight.at[:, pl.ds(start, half)],
+                    out.at[:, pl.ds(i * half, half)],
+                    sems.at[2 + i],
+                )
+            )
+        for copy in copies:
+            copy.start()
+        copies[0].wait()
+        copies[1].wait()
+        gains = [ref[...].astype(F32) for ref in (attn_held, ffn_held)]
         gains = jnp.concatenate(gains + [jnp.zeros((6, rows), F32)], axis=0)
         gains = jnp.concatenate([gains, jnp.zeros((8, 128 - rows), F32)], axis=1)
         square = jnp.concatenate([gains, jnp.zeros((120, 128), F32)], axis=0)
         out[:, 3 * half :] = square.T[0:rows, :].astype(BF)
+        for copy in copies[2:]:
+            copy.wait()
 
     return body
 
@@ -535,7 +545,7 @@
 def back_kernel(width):
     half = width // 2
 
-    def body(first, halves, gctx, q, k, v, p, cosine, sine, sent_0, sent_1, mixed, gj_out):
+    def body(first, halves, gctx, q, k, v, p, cosine, sine, sent, mixed, gj_out):
         gj_out[:, 3 * half :] = halves[...]
         cos, sin = cosine[BLOCK : 3 * BLOCK, :], sine[BLOCK : 3 * BLOCK, :]
         for part in range(3):
@@ -572,40 +582,40 @@
     out[...] = (ghid[...] + norm_back(grad, gains[0:1, :], hat, inverse)).astype(BF)
 
 
-def slots_of(count, chip_bits):
-    streams = []
+def slots_of(chip_bits):
+    tables = []
     for order in (chip_bits, chip_bits[::-1]):
         kept = [0]
         for bit in order[1:][::-1]:
             kept = kept + [j | bit for j in kept]
-        table = {j: (1, i) for i, j in enumerate(kept)}
-        table.update({j | order[0]: (0, i) for i, j in enumerate(kept)})
-        streams.append(table)
-    return streams
-
-
-def owner_rows(me, js, lhs_t, rows):
-    return jnp.concatenate(
-        [lhs_t[pl.ds(pl.multiple_of((me ^ j) * rows, 16), rows), :] for j in js], axis=0
-    )
-
-
-def emit(outs, slots, stream, js, rows, grad, start):
+        tables.append([(1, i, j) for i, j in enumerate(kept)])
+        tables[-1] += [(0, i, j | order[0]) for i, j in enumerate(kept)]
+    return [(kept, i, j, k) for (kept, i, j), (_, _, k) in zip(*tables)]
+
+
+def owner_rows(me, slots, lhs_t, rows):
+    parts = []
+    for _, _, even, odd in slots:
+        owner = me ^ jnp.where((me & 1) == 0, even, odd)
+        parts.append(lhs_t[pl.ds(pl.multiple_of(owner * rows, 16), rows), :])
+    return jnp.concatenate(parts, axis=0)
+
+
+def emit(outs, slots, rows, grad, start):
     grad = grad.astype(BF)
-    for i, j in enumerate(js):
-        kept, at = slots[stream][j]
+    for i, (kept, at, _, _) in enumerate(slots):
         for c in range(grad.shape[1] // 128):
             row = start + c * rows
-            outs[2 * stream + kept][at, row : row + rows, :] = grad[
+            outs[kept][at, row : row + rows, :] = grad[
                 i * rows : (i + 1) * rows, c * 128 : (c + 1) * 128
             ]
 
 
-def mlp_grad_kernel(js, slots, rows, take, width, units):
+def mlp_grad_kernel(slots, rows, take, width, units):
     half = width // 2
 
     def body(own, other, dy_own, dy_other, *rest):
-        outs, (normed_t, act_t, ggu, dy) = rest[1:5], rest[5:]
+        outs, (normed_t, act_t, ggu, dy) = rest[1:3], rest[3:]
         me = shard_at()
         pair = slice(RADIUS, RADIUS + 2 * BLOCK)
         for i, (ref, dref) in enumerate(((own, dy_own), (other, dy_other))):
@@ -614,22 +624,23 @@
             act_t[:, tok] = ref[:, width : width + units].T
             ggu[tok, :] = ref[:, width + units :]
             dy[tok, :] = dref[pair, :]
-        left = owner_rows(me, js, normed_t, rows)
-        act = owner_rows(me, js, act_t, take)
+        left = owner_rows(me, slots, normed_t, rows)
+        act = owner_rows(me, slots, act_t, take)
+        height = outs[0].shape[1] // 2
         for s in range(2):
             grad = dot(left, ggu[:, s * units : (s + 1) * units])
-            emit(outs, slots, s, js, rows, grad, 0)
+            emit(outs, slots, rows, grad, s * height)
             grad = dot(act, dy[:, s * half : (s + 1) * half])
-            emit(outs, slots, s, js, take, grad, rows * (units // 128))
+            emit(outs, slots, take, grad, s * height + rows * (units // 128))
 
     return body
 
 
-def qkv_grad_kernel(js, slots, rows, width):
+def qkv_grad_kernel(slots, rows, width):
     half = width // 2
 
     def body(normed_own, normed_other, ctx_own, ctx_other, own, other, *rest):
-        outs, (normed_t, ctx_t, gj) = rest[1:5], rest[5:]
+        outs, (normed_t, ctx_t, gj) = rest[1:3], rest[3:]
         me = shard_at()
         count = 2 * BLOCK
         each = ((normed_own, ctx_own, own), (normed_other, ctx_other, other))
@@ -638,11 +649,10 @@
             normed_t[:, tok] = nref[...].T
             ctx_t[:, tok] = cref[...].T
             gj[tok, :] = ref[...]
-        left = owner_rows(me, js, normed_t, rows)
-        ctx = owner_rows(me, js, ctx_t, rows)
-        emit(outs, slots, 0, js, rows, dot(left, gj[:, 0 : 2 * half]), 0)
-        emit(outs, slots, 1, js, rows, dot(left, gj[:, 2 * half : 3 * half]), 0)
-        emit(outs, slots, 1, js, rows, dot(ctx, gj[:, 3 * half :]), 3 * rows)
+        left = owner_rows(me, slots, normed_t, rows)
+        ctx = owner_rows(me, slots, ctx_t, rows)
+        emit(outs, slots, rows, dot(left, gj[:, 0 : 3 * half]), 0)
+        emit(outs, slots, rows, dot(ctx, gj[:, 3 * half :]), 9 * rows)
 
     return body
 
@@ -658,7 +668,7 @@
     hidden = count * down_rows
     spare = 2 * take - down_rows
 
-    def body(mine_0, mine_1, other_0, other_1, weight, gain, glu, down, gain_out, held, wide):
+    def body(mine_0, mine_1, other_0, other_1, weight, gain, sent, glu, down, gain_out, held, wide):
         at = side_at()
         tiles = units // 128
         for s, (mine, other) in enumerate(((mine_0, other_0), (mine_1, other_1))):
@@ -732,11 +742,16 @@
     own = call(
         pack_qkv_kernel(half),
         shaped((rows, 3 * half + 128), BF),
-        (qkv_weight, attn_gain[None], ffn_gain[None]),
-        [],
-        [],
+        (),
+        [qkv_weight, attn_gain[None], ffn_gain[None]],
+        [
+            pltpu.VMEM((1, rows), BF),
+            pltpu.VMEM((1, rows), BF),
+            pltpu.SemaphoreType.DMA((5,)),
+        ],
         1_000_000,
         1_000_000,
+        VMEM_ALL,
     )
 
     places = jnp.stack([positions >> 8, positions & 255]).astype(BF)
@@ -860,16 +875,15 @@
     shared_other = xor_send(shared, "shard", 1)
     ctx_pair_other = xor_send(ctx_pair, "shard", 1)
 
-    js = [2 * i for i in range(count // 2)]
-    slots = slots_of(count, chip_bits)
+    slots = slots_of(chip_bits)
     portion = count // 4
 
     def stack(height):
-        return (shaped((portion, height, 128), BF),) * 4
+        return (shaped((portion, 2 * height, 128), BF),) * 2
 
     height = rows * (units // 128) + take * (half // 128)
     sums = call(
-        mlp_grad_kernel(js, slots, rows, take, width, units),
+        mlp_grad_kernel(slots, rows, take, width, units),
         stack(height),
         (shared, shared_other, dy, dy_other),
         [ctx_pair_other],
@@ -907,14 +921,11 @@
         back_kernel(width),
         shaped((2 * BLOCK, 4 * half), BF),
         (gj_first, halves, gctx, q, k, v, p, cosine, sine),
-        [mlp_sums[0][2], mlp_sums[1][2], mix_other],
+        [mlp_sums[2], mix_other],
         [],
         6_000_000_000,
         weight_bytes,
     )
-    gj, _ = lax.optimization_barrier((gj, (mlp_sums[0][1], mlp_sums[1][1])))
-    mlp_sums = [last_sum(stream) for stream in mlp_sums]
-    gj, mlp_sums = lax.optimization_barrier((gj, mlp_sums))
     gj_other = xor_send(gj, "shard", 1)
     norm_keep, norm_send = call(
         norm_back_kernel(qkv_names, len(qkv_arrays), rows, width),
@@ -930,7 +941,7 @@
         weight_bytes,
     )
     sums = call(
-        qkv_grad_kernel(js, slots, rows, width),
+        qkv_grad_kernel(slots, rows, width),
         stack(6 * rows),
         (normed, normed_other, ctx_pair, ctx_pair_other, gj, gj_other),
         [norm_keep],
@@ -942,11 +953,12 @@
         3_000_000_000,
         weight_bytes,
     )
-    mlp_mine = [side_sum(mlp_sums[0], sums[1])]
-    qkv_sums = scatter_sums(sums, chip_bits, None, mlp_mine[0])
-    mlp_mine.append(side_sum(mlp_sums[1], (qkv_sums[0][2], qkv_sums[1][2])))
+    mlp_sums, _ = lax.optimization_barrier((mlp_sums, sums[1]))
+    mlp_sums = last_sums(*mlp_sums)
+    qkv_sums = scatter_sums(sums, chip_bits)
+    mlp_mine = [side_sum(part, qkv_sums[2]) for part in mlp_sums]
     mlp_other = [xor_send(part, "replica", 1) for part in mlp_mine]
-    sent = (qkv_sums[0][1], qkv_sums[1][1])
+    sent = qkv_sums[1]
     norm_send, _ = lax.optimization_barrier((norm_send, sums[1]))
     norm_other = xor_send(norm_send, "replica", 1)
     norm_other, mix_other, _ = lax.optimization_barrier((norm_other, mix_other, sent))
@@ -968,13 +980,13 @@
             shaped((1, rows), F32),
         ),
         (*mlp_mine, *mlp_other, glu_weight, ffn_gain[None]),
-        [],
+        [sent],
         [pltpu.VMEM((2, 2, height, 128), F32), pltpu.VMEM((rows, units), F32)],
         1_000_000,
         4_000_000,
     )
     done = (mixed, grad_tokens, grad_glu)
-    qkv_mine = [side_sum(last_sum(stream), done) for stream in qkv_sums]
+    qkv_mine = [side_sum(part, done) for part in last_sums(*qkv_sums)]
     qkv_other = [xor_send(part, "replica", 1) for part in qkv_mine]
     grad_qkv, grad_attn, grad_attn_gain = call(
         qkv_unpack_kernel(rows, width),

time: 145 us -> 140 us (0.966)
  starting transfers between devices: 47.4 us -> 37.7 us
  waiting for transfers between devices: 63.5 us -> 68.9 us
  local copies, waits for them, and re-layouts: 3.38 us -> 1.07 us
  Pallas kernels: 24.8 us -> 26.5 us
    ppermute x41 -> x33, starting transfers between devices: 46.1 us -> 33.3 us  [xor_send(): return lax.ppermute(array, axis, [(i, i ^ bit) for i in range(count)])]
    ppermute x0 -> x4, waiting for transfers between devices: none -> 5.77 us  [core_send(): lax.ppermute(array, 'shard', [(i, i ^ bits[i & 1]) for i in range(count)])]
    ppermute x0 -> x4, starting transfers between devices: none -> 3.08 us  [core_send(): lax.ppermute(array, 'shard', [(i, i ^ bits[i & 1]) for i in range(count)])]
    unnamed x32 -> x28, local copies, waits for them, and re-layouts: 3.31 us -> 1 us
    pallas_call x14, Pallas kernels: 24.8 us -> 26.5 us  [call(): pl.pallas_call(kernel, out_shape=out_shape, in_specs=specs, out_specs=jax...]
    ppermute x41 -> x33, waiting for transfers between devices: 63.5 us -> 63.1 us  [xor_send(): return lax.ppermute(array, axis, [(i, i ^ bit) for i in range(count)])]
  transfers between devices with their start and end apart: 43 -> 39, of which waited for: 21 -> 21; matrix products, arithmetic and copies ran while one was open for 2% -> 2% of each run, Pallas kernels for 12% -> 11%
where the time goes in v5:
time: 140 us; the launch traced here: 139 us
  waiting for transfers between devices  68.9 us (49%)
  starting transfers between devices  37.7 us (27%)
  Pallas kernels  26.5 us (19%)
  other arithmetic  4.26 us (3%)
    ppermute x33, waiting for transfers between devices, xor_send(): return lax.ppermute(array, axis, [(i, i ^ bit) for i in range(count)])  63.1 us
    ppermute x33, starting transfers between devices, xor_send(): return lax.ppermute(array, axis, [(i, i ^ bit) for i in range(count)])  33.3 us
    pallas_call x14, Pallas kernels, call(): pl.pallas_call(kernel, out_shape=out_shape, in_specs=specs, out_specs=jax...  26.5 us
    ppermute x4, waiting for transfers between devices, core_send(): lax.ppermute(array, 'shard', [(i, i ^ bits[i & 1]) for i in range(count)])  5.77 us
    ppermute x4, starting transfers between devices, core_send(): lax.ppermute(array, 'shard', [(i, i ^ bits[i & 1]) for i in range(count)])  3.08 us
  transfers between devices with their start and end apart: 39, of which 21 were waited for; matrix products, arithmetic and copies ran while one was open for 2% of the time, Pallas kernels for 11%

profile of v5, /device:TPU:0, one launch (start us, length us, event | category | flops | bytes accessed | tf_op | source)
XLA Modules:
  0.0 139.5 jit_solution(695407440839372423)
XLA Ops:
  0.7 1.8 %shard_map.153.rest_4_.rest_0_ = bf16[96,1280]{1,0:T(8,128)(2,1)} custom-call(bf16[96,2304]{1,0:T(8,128)(2,1)} %weight.5, bf16[1,96]{1,0:T(2,128)(2,1)} %bitcast.17, bf16[1,96]{1,0:T(2,128)(2,1)} %bitcast.19), custom_call_target="tpu_custom_call" | custom-call | flops 1000000 | bytes 1000000 | tf_op jit(solution)/shard_map/pallas_call | solution.py:176
  2.5 3.0 %collective-permute-start.2 = (bf16[96,1280]{1,0:T(8,128)(2,1)}, bf16[96,1280]{1,0:T(8,128)(2,1)S(1)}, u32[]{:S(2)}, u32[]{:S(2)}) collective-permute-start(bf16[96,1280]{1,0:T(8,128)(2,1)} %shard_map.153.rest_4_.rest_0_), channel_id=1, source_target_pairs={{0,8},{4,12},{8,0},{12,4},{16,24},{20,28},{24,16},{28,20},{1,9},{5... | collective-permute-start | bytes 737288 | tf_op jit(solution)/shard_map/ppermute | solution.py:24
  5.5 1.5 %collective-permute-start.3 = (bf16[96,1280]{1,0:T(8,128)(2,1)}, bf16[96,1280]{1,0:T(8,128)(2,1)S(1)}, u32[]{:S(2)}, u32[]{:S(2)}) collective-permute-start(bf16[96,1280]{1,0:T(8,128)(2,1)} %shard_map.153.rest_4_.rest_0_), channel_id=1, source_target_pairs={{0,16},{4,20},{8,24},{12,28},{16,0},{20,4},{24,8},{28,12},{1,17},{... | collective-permute-start | bytes 737288 | tf_op jit(solution)/shard_map/ppermute | solution.py:24
  9.3 4.5 %collective-permute-start.1 = (bf16[144,768]{1,0:T(8,128)(2,1)S(1)}, bf16[144,768]{1,0:T(8,128)(2,1)S(1)}, u32[]{:S(2)}, u32[]{:S(2)}) collective-permute-start(bf16[144,768]{1,0:T(8,128)(2,1)S(1)} %pad_maximum_fusion.1), channel_id=1, source_target_pairs={{0,1},{1,0},{2,3},{3,2},{4,5},{5,4},{6,7},{7,6},{8,9},{9,8},{10,11... | collective-permute-start | bytes 663560 | tf_op jit(solution)/shard_map/ppermute | solution.py:24
  15.6 9.0 %collective-permute-done.1.partner = bf16[144,768]{1,0:T(8,128)(2,1)S(1)} collective-permute-done((bf16[144,768]{1,0:T(8,128)(2,1)S(1)}, bf16[144,768]{1,0:T(8,128)(2,1)S(1)}, u32[]{:S(2)}, u32[]{:S(2)}) %collective-permute-start.1) | collective-permute-done | bytes 221216 | tf_op jit(solution)/shard_map/ppermute | solution.py:24
  27.0 1.9 %collective-permute-start.6 = (bf16[144,768]{1,0:T(8,128)(2,1)S(1)}, bf16[144,768]{1,0:T(8,128)(2,1)S(1)}, u32[]{:S(2)}, u32[]{:S(2)}) collective-permute-start(bf16[144,768]{1,0:T(8,128)(2,1)S(1)} %collective-permute-done.near), channel_id=1, source_target_pairs={{0,1},{1,0},{2,3},{3,2},{4,5},{5,4},{6,7},{7,6},{8,9},{9,8},{10,11... | collective-permute-start | bytes 663560 | tf_op jit(solution)/shard_map/ppermute | solution.py:24
  29.6 6.0 %collective-permute-start.9 = (bf16[128,768]{1,0:T(8,128)(2,1)S(1)}, bf16[128,768]{1,0:T(8,128)(2,1)S(1)}, u32[]{:S(2)}, u32[]{:S(2)}) collective-permute-start(bf16[128,768]{1,0:T(8,128)(2,1)S(1)} %copy-done.4), channel_id=1, source_target_pairs={{0,1},{1,0},{2,3},{3,2},{4,5},{5,4},{6,7},{7,6},{8,9},{9,8},{10,11... | collective-permute-start | bytes 589832 | tf_op jit(solution)/shard_map/ppermute | solution.py:24
  35.6 1.6 %collective-permute-start.8 = (bf16[64,768]{1,0:T(8,128)(2,1)S(1)}, bf16[64,768]{1,0:T(8,128)(2,1)S(1)}, u32[]{:S(2)}, u32[]{:S(2)}) collective-permute-start(bf16[64,768]{1,0:T(8,128)(2,1)S(1)} %collective-permute-done.7.near), channel_id=1, source_target_pairs={{0,1},{1,0},{2,3},{3,2},{4,5},{5,4},{6,7},{7,6},{8,9},{9,8},{10,11... | collective-permute-start | bytes 294920 | tf_op jit(solution)/shard_map/ppermute | solution.py:24
  39.2 2.2 %collective-permute-done.10.rest_2_ = bf16[96,2816]{1,0:T(8,128)(2,1)S(1)} collective-permute-done((bf16[96,2816]{1,0:T(8,128)(2,1)S(1)}, bf16[96,2816]{1,0:T(8,128)(2,1)S(1)}, u32[]{:S(2)}, u32[]{:S(2)}) %collective-permute-start.10) | collective-permute-done | bytes 540704 | tf_op jit(solution)/shard_map/ppermute | solution.py:24
  41.5 2.9 %collective-permute-start.15 = (bf16[96,1408]{1,0:T(8,128)(2,1)S(1)}, bf16[96,1408]{1,0:T(8,128)(2,1)S(1)}, u32[]{:S(2)}, u32[]{:S(2)}) collective-permute-start(bf16[96,1408]{1,0:T(8,128)(2,1)S(1)} %slice.88.rest_2_), channel_id=1, source_target_pairs={{0,16},{4,20},{8,24},{12,28},{16,0},{20,4},{24,8},{28,12},{1,17},{... | collective-permute-start | bytes 811016 | tf_op jit(solution)/shard_map/ppermute | solution.py:24
  44.5 4.3 %shard_map.155 = (bf16[384,384]{1,0:T(8,128)(2,1)S(1)}, bf16[512,384]{1,0:T(8,128)(2,1)S(1)}, bf16[512,384]{1,0:T(8,128)(2,1)S(1)}, bf16[18,128,256]{2,1,0:T(8,1...) custom-call(bf16[512,768]{1,0:T(8,128)(2,1)S(1)} %get-tuple-element.78.tok, ...), custom_call_target="tpu_custom_call" | custom-call | flops 7000000000 | bytes 3538944 | tf_op jit(solution)/shard_map/pallas_call | solution.py:176
  49.5 1.4 %collective-permute-done.16.rest_5_ = bf16[96,1408]{1,0:T(8,128)(2,1)S(1)} collective-permute-done((bf16[96,1408]{1,0:T(8,128)(2,1)S(1)}, bf16[96,1408]{1,0:T(8,128)(2,1)S(1)}, u32[]{:S(2)}, u32[]{:S(2)}) %collective-permute-start.16) | collective-permute-done | bytes 270368 | tf_op jit(solution)/shard_map/ppermute | solution.py:24
  52.2 3.3 %collective-permute-done.18.rest_7_ = bf16[96,1408]{1,0:T(8,128)(2,1)S(1)} collective-permute-done((bf16[96,1408]{1,0:T(8,128)(2,1)S(1)}, bf16[96,1408]{1,0:T(8,128)(2,1)S(1)}, u32[]{:S(2)}, u32[]{:S(2)}) %collective-permute-start.18) | collective-permute-done | bytes 270368 | tf_op jit(solution)/shard_map/ppermute | solution.py:24
  55.9 4.7 %collective-permute-done.13.ctx_other = bf16[384,384]{1,0:T(8,128)(2,1)S(1)} collective-permute-done((bf16[384,384]{1,0:T(8,128)(2,1)S(1)}, bf16[384,384]{1,0:T(8,128)(2,1)S(1)}, u32[]{:S(2)}, u32[]{:S(2)}) %collective-permute-start.13) | collective-permute-done | bytes 294944 | tf_op jit(solution)/shard_map/ppermute | solution.py:24
  60.6 5.5 %shard_map.157 = (f32[128,768]{1,0:T(8,128)S(1)}, bf16[128,768]{1,0:T(8,128)(2,1)S(1)}, bf16[256,2688]{1,0:T(8,128)(2,1)S(1)}, bf16[256,768]{1,0:T(8,128)(2,1)S(...) custom-call(bf16[512,768]{1,0:T(8,128)(2,1)S(1)} %get-tuple-element.78.tok, ...), custom_call_target="tpu_custom_call" | custom-call | flops 8000000000 | bytes 7077888 | tf_op jit(solution)/shard_map/pallas_call | solution.py:176
  67.0 3.1 %collective-permute-done.22.dy_other = bf16[384,768]{1,0:T(8,128)(2,1)S(1)} collective-permute-done((bf16[384,768]{1,0:T(8,128)(2,1)S(1)}, bf16[384,768]{1,0:T(8,128)(2,1)S(1)}, u32[]{:S(2)}, u32[]{:S(2)}) %collective-permute-start.22) | collective-permute-done | bytes 589856 | tf_op jit(solution)/shard_map/ppermute | solution.py:24
  72.7 10.2 %collective-permute-done.20.gn_other = bf16[384,768]{1,0:T(8,128)(2,1)S(1)} collective-permute-done((bf16[384,768]{1,0:T(8,128)(2,1)S(1)}, bf16[384,768]{1,0:T(8,128)(2,1)S(1)}, u32[]{:S(2)}, u32[]{:S(2)}) %collective-permute-start.20) | collective-permute-done | bytes 589856 | tf_op jit(solution)/shard_map/ppermute | solution.py:24
  82.8 2.6 %shard_map.159 = (f32[128,768]{1,0:T(8,128)S(1)}, bf16[256,384]{1,0:T(8,128)(2,1)S(1)}, bf16[384,384]{1,0:T(8,128)(2,1)S(1)}, bf16[256,384]{1,0:T(8,128)(2,1)S(1)}) custom-call(bf16[384,768]{1,0:T(8,128)(2,1)S(1)} %get-tuple-element.103.gn_own, bf16[384,768]{1,0:T(8,128)(2,1)S(1)} %collective-permute-done.20.gn_other, ...), custom_call_target="tpu_custom_call" | custom-call | flops 5000000000 | bytes 3538944 | tf_op jit(solution)/shard_map/pallas_call | solution.py:176
  86.6 2.2 %shard_map.160.gj.own = bf16[256,1536]{1,0:T(8,128)(2,1)S(1)} custom-call(bf16[256,384]{1,0:T(8,128)(2,1)S(1)} %get-tuple-element.112.first, bf16[256,384]{1,0:T(8,128)(2,1)S(1)} %get-tuple-element.113.halves, bf16[384,384]{1,0:T(8,128)(2,1)S(1)} %get-tuple-element.114.gctx, bf16[384,384]{1,0:T(8,128)(2,1)S(1)} %get-tuple-element.105.q, ...), custom_call_target="tpu_custom_call" | custom-call | flops 6000000000 | bytes 3538944 | tf_op jit(solution)/shard_map/pallas_call | solution.py:176
  90.0 2.3 %shard_map.161 = (f32[128,768]{1,0:T(8,128)S(1)}, bf16[128,768]{1,0:T(8,128)(2,1)S(1)}) custom-call(bf16[256,1536]{1,0:T(8,128)(2,1)S(1)} %shard_map.160.gj.own, bf16[96,1280]{1,0:T(8,128)(2,1)S(1)} %copy-done.3, bf16[96,1280]{1,0:T(8,128)(2,1)S(1)} %collective-permute-done.2.rest_5_.rest_1_, bf16[96,1280]{1,0:T(8,128)(2,1)S(1)} %collective-permute-done.3.rest_6_.rest_2_, ...), custom_call_target="tpu_custom_call" | custom-call | flops 3000000000 | bytes 3538944 | tf_op jit(solution)/shard_map/pallas_call | solution.py:176
  94.2 3.2 %collective-permute-done.31 = bf16[1,1440,128]{2,1,0:T(8,128)(2,1)S(1)} collective-permute-done((bf16[1,1440,128]{2,1,0:T(8,128)(2,1)S(1)}, bf16[1,1440,128]{2,1,0:T(8,128)(2,1)S(1)}, u32[]{:S(2)}, u32[]{:S(2)}) %collective-permute-start.31) | collective-permute-done | bytes 368672 | tf_op jit(solution)/shard_map/ppermute | solution.py:33
  97.7 2.7 %collective-permute-start.32 = (bf16[720,128]{1,0:T(8,128)(2,1)S(1)}, bf16[720,128]{1,0:T(8,128)(2,1)S(1)}, u32[]{:S(2)}, u32[]{:S(2)}) collective-permute-start(bf16[720,128]{1,0:T(8,128)(2,1)S(1)} %get-tuple-element.143), channel_id=1, source_target_pairs={{0,2},{1,3},{2,0},{3,1},{4,6},{5,7},{6,4},{7,5},{8,10},{9,11},{10,... | collective-permute-start | bytes 552968 | tf_op jit(solution)/shard_map/ppermute | solution.py:24
  100.8 2.6 %collective-permute-done.28 = bf16[2,1152,128]{2,1,0:T(8,128)(2,1)S(1)} collective-permute-done((bf16[2,1152,128]{2,1,0:T(8,128)(2,1)S(1)}, bf16[2,1152,128]{2,1,0:T(8,128)(2,1)S(1)}, u32[]{:S(2)}, u32[]{:S(2)}) %collective-permute-start.28) | collective-permute-done | bytes 589856 | tf_op jit(solution)/shard_map/ppermute | solution.py:33
  104.6 6.9 %collective-permute-done.33 = bf16[720,128]{1,0:T(8,128)(2,1)S(1)} collective-permute-done((bf16[720,128]{1,0:T(8,128)(2,1)S(1)}, bf16[720,128]{1,0:T(8,128)(2,1)S(1)}, u32[]{:S(2)}, u32[]{:S(2)}) %collective-permute-start.33) | collective-permute-done | bytes 184352 | tf_op jit(solution)/shard_map/ppermute | solution.py:24
  111.7 3.7 %collective-permute-done.32 = bf16[720,128]{1,0:T(8,128)(2,1)S(1)} collective-permute-done((bf16[720,128]{1,0:T(8,128)(2,1)S(1)}, bf16[720,128]{1,0:T(8,128)(2,1)S(1)}, u32[]{:S(2)}, u32[]{:S(2)}) %collective-permute-start.32) | collective-permute-done | bytes 184352 | tf_op jit(solution)/shard_map/ppermute | solution.py:24
  115.6 2.9 %collective-permute-start.36 = (bf16[576,128]{1,0:T(8,128)(2,1)S(1)}, bf16[576,128]{1,0:T(8,128)(2,1)S(1)}, u32[]{:S(2)}, u32[]{:S(2)}) collective-permute-start(bf16[576,128]{1,0:T(8,128)(2,1)S(1)} %get-tuple-element.144), channel_id=1, source_target_pairs={{0,2},{1,3},{2,0},{3,1},{4,6},{5,7},{6,4},{7,5},{8,10},{9,11},{10,... | collective-permute-start | bytes 442376 | tf_op jit(solution)/shard_map/ppermute | solution.py:24
  119.6 2.7 %collective-permute-done.35.other_1 = bf16[720,128]{1,0:T(8,128)(2,1)S(1)} collective-permute-done((bf16[720,128]{1,0:T(8,128)(2,1)S(1)}, bf16[720,128]{1,0:T(8,128)(2,1)S(1)}, u32[]{:S(2)}, u32[]{:S(2)}) %collective-permute-start.35) | collective-permute-done | bytes 184352 | tf_op jit(solution)/shard_map/ppermute | solution.py:24
  122.3 4.4 %collective-permute-done.34.other_0 = bf16[720,128]{1,0:T(8,128)(2,1)S(1)} collective-permute-done((bf16[720,128]{1,0:T(8,128)(2,1)S(1)}, bf16[720,128]{1,0:T(8,128)(2,1)S(1)}, u32[]{:S(2)}, u32[]{:S(2)}) %collective-permute-start.34) | collective-permute-done | bytes 184352 | tf_op jit(solution)/shard_map/ppermute | solution.py:24
  126.7 1.6 %shard_map.164 = (f32[96,2304]{1,0:T(8,128)}, f32[144,768]{1,0:T(8,128)}, f32[1,96]{1,0:T(1,128)}) custom-call(bf16[720,128]{1,0:T(8,128)(2,1)S(1)} %add_convert_fusion.7.mine_0, bf16[720,128]{1,0:T(8,128)(2,1)S(1)} %add_convert_fusion.5.mine_1, bf16[720,128]{1,0:T(8,128)(2,1)S(1)} %collective-permute-done.34.other_0, ...), custom_call_target="tpu_custom_call" | custom-call | flops 1000000 | bytes 4000000 | tf_op jit(solution)/shard_map/pallas_call | solution.py:176
  129.4 2.2 %collective-permute-done.30 = bf16[576,128]{1,0:T(8,128)(2,1)S(1)} collective-permute-done((bf16[576,128]{1,0:T(8,128)(2,1)S(1)}, bf16[576,128]{1,0:T(8,128)(2,1)S(1)}, u32[]{:S(2)}, u32[]{:S(2)}) %collective-permute-start.30) | collective-permute-done | bytes 147488 | tf_op jit(solution)/shard_map/ppermute | solution.py:24
  131.7 4.4 %collective-permute-done.38.other_1 = bf16[576,128]{1,0:T(8,128)(2,1)S(1)} collective-permute-done((bf16[576,128]{1,0:T(8,128)(2,1)S(1)}, bf16[576,128]{1,0:T(8,128)(2,1)S(1)}, u32[]{:S(2)}, u32[]{:S(2)}) %collective-permute-start.38) | collective-permute-done | bytes 147488 | tf_op jit(solution)/shard_map/ppermute | solution.py:24
  136.1 2.0 %collective-permute-done.37.other_0 = bf16[576,128]{1,0:T(8,128)(2,1)S(1)} collective-permute-done((bf16[576,128]{1,0:T(8,128)(2,1)S(1)}, bf16[576,128]{1,0:T(8,128)(2,1)S(1)}, u32[]{:S(2)}, u32[]{:S(2)}) %collective-permute-start.37) | collective-permute-done | bytes 147488 | tf_op jit(solution)/shard_map/ppermute | solution.py:24
  (107 shorter events, 25.4 us)
Async XLA Ops:
  2.5 11.3 %collective-permute-start.2 = (bf16[96,1280]{1,0:T(8,128)(2,1)}, bf16[96,1280]{1,0:T(8,128)(2,1)S(1)}, u32[]{:S(2)}, u32[]{:S(2)}) collective-permute-start(bf16[96,1280]{1,0:T(8,128)(2,1)} %shard_map.153.rest_4_.rest_0_), channel_id=1, source_target_pairs={{0,8},{4,12},{8,0},{12,4},{16,24},{20,28},{24,16},{28,20},{1,9},{5... | collective-permute-start | bytes 737288 | tf_op jit(solution)/shard_map/ppermute | solution.py:24
  5.5 8.3 %collective-permute-start.3 = (bf16[96,1280]{1,0:T(8,128)(2,1)}, bf16[96,1280]{1,0:T(8,128)(2,1)S(1)}, u32[]{:S(2)}, u32[]{:S(2)}) collective-permute-start(bf16[96,1280]{1,0:T(8,128)(2,1)} %shard_map.153.rest_4_.rest_0_), channel_id=1, source_target_pairs={{0,16},{4,20},{8,24},{12,28},{16,0},{20,4},{24,8},{28,12},{1,17},{... | collective-permute-start | bytes 737288 | tf_op jit(solution)/shard_map/ppermute | solution.py:24
  8.6 6.9 %collective-permute-start = (bf16[144,768]{1,0:T(8,128)(2,1)S(1)}, bf16[144,768]{1,0:T(8,128)(2,1)S(1)}, u32[]{:S(2)}, u32[]{:S(2)}) collective-permute-start(bf16[144,768]{1,0:T(8,128)(2,1)S(1)} %pad_maximum_fusion.1), channel_id=1, source_target_pairs={{1,2},{2,1},{3,4},{4,3},{5,6},{6,5},{7,8},{8,7},{9,10},{10,9},{11,... | collective-permute-start | bytes 663560 | tf_op jit(solution)/shard_map/ppermute | solution.py:766
  9.3 15.3 %collective-permute-start.1 = (bf16[144,768]{1,0:T(8,128)(2,1)S(1)}, bf16[144,768]{1,0:T(8,128)(2,1)S(1)}, u32[]{:S(2)}, u32[]{:S(2)}) collective-permute-start(bf16[144,768]{1,0:T(8,128)(2,1)S(1)} %pad_maximum_fusion.1), channel_id=1, source_target_pairs={{0,1},{1,0},{2,3},{3,2},{4,5},{5,4},{6,7},{7,6},{8,9},{9,8},{10,11... | collective-permute-start | bytes 663560 | tf_op jit(solution)/shard_map/ppermute | solution.py:24
  13.8 10.8 %collective-permute-start.4 = (bf16[96,640]{1,0:T(8,128)(2,1)S(1)}, bf16[96,640]{1,0:T(8,128)(2,1)S(1)}, u32[]{:S(2)}, u32[]{:S(2)}) collective-permute-start(bf16[96,640]{1,0:T(8,128)(2,1)S(1)} %slice.66), channel_id=1, source_target_pairs={{0,16},{4,20},{8,24},{12,28},{16,0},{20,4},{24,8},{28,12},{1,17},{... | collective-permute-start | bytes 368648 | tf_op jit(solution)/shard_map/ppermute | solution.py:24
  14.8 9.8 %collective-permute-start.5 = (bf16[96,640]{1,0:T(8,128)(2,1)S(1)}, bf16[96,640]{1,0:T(8,128)(2,1)S(1)}, u32[]{:S(2)}, u32[]{:S(2)}) collective-permute-start(bf16[96,640]{1,0:T(8,128)(2,1)S(1)} %slice.67), channel_id=1, source_target_pairs={{0,8},{4,12},{8,0},{12,4},{16,24},{20,28},{24,16},{28,20},{1,9},{5... | collective-permute-start | bytes 368648 | tf_op jit(solution)/shard_map/ppermute | solution.py:24
  25.7 18.8 %collective-permute-start.12 = (bf16[384,1280]{1,0:T(8,128)(2,1)}, bf16[384,1280]{1,0:T(8,128)(2,1)}, u32[]{:S(2)}, u32[]{:S(2)}) collective-permute-start(bf16[384,1280]{1,0:T(8,128)(2,1)} %maximum_maximum_fusion), channel_id=1, source_target_pairs={{0,4},{4,0},{8,12},{12,8},{16,20},{20,16},{24,28},{28,24},{1,5},{5... | collective-permute-start | bytes 2949128 | tf_op jit(solution)/shard_map/ppermute | solution.py:24
  25.8 15.6 %collective-permute-start.10 = (bf16[96,2816]{1,0:T(8,128)(2,1)S(1)}, bf16[96,2816]{1,0:T(8,128)(2,1)S(1)}, u32[]{:S(2)}, u32[]{:S(2)}) collective-permute-start(bf16[96,2816]{1,0:T(8,128)(2,1)S(1)} %shard_map.152.rest_1_), channel_id=1, source_target_pairs={{0,8},{4,12},{8,0},{12,4},{16,24},{20,28},{24,16},{28,20},{1,9},{5... | collective-permute-start | bytes 1622024 | tf_op jit(solution)/shard_map/ppermute | solution.py:24
  27.0 17.4 %collective-permute-start.11 = (bf16[96,2816]{1,0:T(8,128)(2,1)S(1)}, bf16[96,2816]{1,0:T(8,128)(2,1)S(1)}, u32[]{:S(2)}, u32[]{:S(2)}) collective-permute-start(bf16[96,2816]{1,0:T(8,128)(2,1)S(1)} %shard_map.152.rest_1_), channel_id=1, source_target_pairs={{0,16},{4,20},{8,24},{12,28},{16,0},{20,4},{24,8},{28,12},{1,17},{... | collective-permute-start | bytes 1622024 | tf_op jit(solution)/shard_map/ppermute | solution.py:24
  27.0 8.6 %collective-permute-start.6 = (bf16[144,768]{1,0:T(8,128)(2,1)S(1)}, bf16[144,768]{1,0:T(8,128)(2,1)S(1)}, u32[]{:S(2)}, u32[]{:S(2)}) collective-permute-start(bf16[144,768]{1,0:T(8,128)(2,1)S(1)} %collective-permute-done.near), channel_id=1, source_target_pairs={{0,1},{1,0},{2,3},{3,2},{4,5},{5,4},{6,7},{7,6},{8,9},{9,8},{10,11... | collective-permute-start | bytes 663560 | tf_op jit(solution)/shard_map/ppermute | solution.py:24
  29.6 14.9 %collective-permute-start.9 = (bf16[128,768]{1,0:T(8,128)(2,1)S(1)}, bf16[128,768]{1,0:T(8,128)(2,1)S(1)}, u32[]{:S(2)}, u32[]{:S(2)}) collective-permute-start(bf16[128,768]{1,0:T(8,128)(2,1)S(1)} %copy-done.4), channel_id=1, source_target_pairs={{0,1},{1,0},{2,3},{3,2},{4,5},{5,4},{6,7},{7,6},{8,9},{9,8},{10,11... | collective-permute-start | bytes 589832 | tf_op jit(solution)/shard_map/ppermute | solution.py:24
  35.6 8.9 %collective-permute-start.8 = (bf16[64,768]{1,0:T(8,128)(2,1)S(1)}, bf16[64,768]{1,0:T(8,128)(2,1)S(1)}, u32[]{:S(2)}, u32[]{:S(2)}) collective-permute-start(bf16[64,768]{1,0:T(8,128)(2,1)S(1)} %collective-permute-done.7.near), channel_id=1, source_target_pairs={{0,1},{1,0},{2,3},{3,2},{4,5},{5,4},{6,7},{7,6},{8,9},{9,8},{10,11... | collective-permute-start | bytes 294920 | tf_op jit(solution)/shard_map/ppermute | solution.py:24
  41.5 8.0 %collective-permute-start.15 = (bf16[96,1408]{1,0:T(8,128)(2,1)S(1)}, bf16[96,1408]{1,0:T(8,128)(2,1)S(1)}, u32[]{:S(2)}, u32[]{:S(2)}) collective-permute-start(bf16[96,1408]{1,0:T(8,128)(2,1)S(1)} %slice.88.rest_2_), channel_id=1, source_target_pairs={{0,16},{4,20},{8,24},{12,28},{16,0},{20,4},{24,8},{28,12},{1,17},{... | collective-permute-start | bytes 811016 | tf_op jit(solution)/shard_map/ppermute | solution.py:24
  44.4 6.5 %collective-permute-start.16 = (bf16[96,1408]{1,0:T(8,128)(2,1)S(1)}, bf16[96,1408]{1,0:T(8,128)(2,1)S(1)}, u32[]{:S(2)}, u32[]{:S(2)}) collective-permute-start(bf16[96,1408]{1,0:T(8,128)(2,1)S(1)} %slice.89.rest_3_), channel_id=1, source_target_pairs={{0,8},{4,12},{8,0},{12,4},{16,24},{20,28},{24,16},{28,20},{1,9},{5... | collective-permute-start | bytes 811016 | tf_op jit(solution)/shard_map/ppermute | solution.py:24
  51.0 9.6 %collective-permute-start.17 = (bf16[288,2816]{1,0:T(8,128)(2,1)S(1)}, bf16[288,2816]{1,0:T(8,128)(2,1)S(1)}, u32[]{:S(2)}, u32[]{:S(2)}) collective-permute-start(bf16[288,2816]{1,0:T(8,128)(2,1)S(1)} %pad_maximum_fusion), channel_id=1, source_target_pairs={{0,4},{4,0},{8,12},{12,8},{16,20},{20,16},{24,28},{28,24},{1,5},{5... | collective-permute-start | bytes 4866056 | tf_op jit(solution)/shard_map/ppermute | solution.py:24
  51.1 9.5 %collective-permute-start.14 = (bf16[256,768]{1,0:T(8,128)(2,1)S(1)}, bf16[256,768]{1,0:T(8,128)(2,1)S(1)}, u32[]{:S(2)}, u32[]{:S(2)}) collective-permute-start(bf16[256,768]{1,0:T(8,128)(2,1)S(1)} %get-tuple-element.96.normed_own), channel_id=1, source_target_pairs={{0,4},{4,0},{8,12},{12,8},{16,20},{20,16},{24,28},{28,24},{1,5},{5... | collective-permute-start | bytes 1179656 | tf_op jit(solution)/shard_map/ppermute | solution.py:24
  51.6 9.0 %collective-permute-start.13 = (bf16[384,384]{1,0:T(8,128)(2,1)S(1)}, bf16[384,384]{1,0:T(8,128)(2,1)S(1)}, u32[]{:S(2)}, u32[]{:S(2)}) collective-permute-start(bf16[384,384]{1,0:T(8,128)(2,1)S(1)} %get-tuple-element.91.ctx_own), channel_id=1, source_target_pairs={{0,1},{1,0},{2,3},{3,2},{4,5},{5,4},{6,7},{7,6},{8,9},{9,8},{10,11... | collective-permute-start | bytes 884744 | tf_op jit(solution)/shard_map/ppermute | solution.py:24
  66.7 16.1 %collective-permute-start.20 = (bf16[384,768]{1,0:T(8,128)(2,1)S(1)}, bf16[384,768]{1,0:T(8,128)(2,1)S(1)}, u32[]{:S(2)}, u32[]{:S(2)}) collective-permute-start(bf16[384,768]{1,0:T(8,128)(2,1)S(1)} %get-tuple-element.103.gn_own), channel_id=1, source_target_pairs={{0,1},{1,0},{2,3},{3,2},{4,5},{5,4},{6,7},{7,6},{8,9},{9,8},{10,11... | collective-permute-start | bytes 1769480 | tf_op jit(solution)/shard_map/ppermute | solution.py:24
  72.1 13.4 %collective-permute-start.24 = (bf16[2,1440,128]{2,1,0:T(8,128)(2,1)S(1)}, bf16[2,1440,128]{2,1,0:T(8,128)(2,1)S(1)}, u32[]{:S(2)}, u32[]{:S(2)}) collective-permute-start(bf16[2,1440,128]{2,1,0:T(8,128)(2,1)S(1)} %get-tuple-element.115), channel_id=1, source_target_pairs={{0,8},{4,20},{8,0},{12,28},{16,24},{20,4},{24,16},{28,12},{1,9},{5... | collective-permute-start | bytes 2211848 | tf_op jit(solution)/shard_map/ppermute | solution.py:33
  72.2 14.4 %collective-permute-start.25 = (bf16[128,768]{1,0:T(8,128)(2,1)S(1)}, bf16[128,768]{1,0:T(8,128)(2,1)S(1)}, u32[]{:S(2)}, u32[]{:S(2)}) collective-permute-start(bf16[128,768]{1,0:T(8,128)(2,1)S(1)} %get-tuple-element.117), channel_id=1, source_target_pairs={{0,1},{1,0},{2,3},{3,2},{4,5},{5,4},{6,7},{7,6},{8,9},{9,8},{10,11... | collective-permute-start | bytes 589832 | tf_op jit(solution)/shard_map/ppermute | solution.py:24
  88.9 8.5 %collective-permute-start.31 = (bf16[1,1440,128]{2,1,0:T(8,128)(2,1)S(1)}, bf16[1,1440,128]{2,1,0:T(8,128)(2,1)S(1)}, u32[]{:S(2)}, u32[]{:S(2)}) collective-permute-start(bf16[1,1440,128]{2,1,0:T(8,128)(2,1)S(1)} %get-tuple-element.139.sent), channel_id=1, source_target_pairs={{0,16},{4,12},{8,24},{12,4},{16,0},{20,28},{24,8},{28,20},{1,17},{... | collective-permute-start | bytes 1105928 | tf_op jit(solution)/shard_map/ppermute | solution.py:33
  93.4 9.9 %collective-permute-start.28 = (bf16[2,1152,128]{2,1,0:T(8,128)(2,1)S(1)}, bf16[2,1152,128]{2,1,0:T(8,128)(2,1)S(1)}, u32[]{:S(2)}, u32[]{:S(2)}) collective-permute-start(bf16[2,1152,128]{2,1,0:T(8,128)(2,1)S(1)} %get-tuple-element.122), channel_id=1, source_target_pairs={{0,8},{4,20},{8,0},{12,28},{16,24},{20,4},{24,16},{28,12},{1,9},{5... | collective-permute-start | bytes 1769480 | tf_op jit(solution)/shard_map/ppermute | solution.py:33
  97.5 14.1 %collective-permute-start.33 = (bf16[720,128]{1,0:T(8,128)(2,1)S(1)}, bf16[720,128]{1,0:T(8,128)(2,1)S(1)}, u32[]{:S(2)}, u32[]{:S(2)}) collective-permute-start(bf16[720,128]{1,0:T(8,128)(2,1)S(1)} %get-tuple-element.142), channel_id=1, source_target_pairs={{0,2},{1,3},{2,0},{3,1},{4,6},{5,7},{6,4},{7,5},{8,10},{9,11},{10,... | collective-permute-start | bytes 552968 | tf_op jit(solution)/shard_map/ppermute | solution.py:24
  97.7 17.6 %collective-permute-start.32 = (bf16[720,128]{1,0:T(8,128)(2,1)S(1)}, bf16[720,128]{1,0:T(8,128)(2,1)S(1)}, u32[]{:S(2)}, u32[]{:S(2)}) collective-permute-start(bf16[720,128]{1,0:T(8,128)(2,1)S(1)} %get-tuple-element.143), channel_id=1, source_target_pairs={{0,2},{1,3},{2,0},{3,1},{4,6},{5,7},{6,4},{7,5},{8,10},{9,11},{10,... | collective-permute-start | bytes 552968 | tf_op jit(solution)/shard_map/ppermute | solution.py:24
  100.5 18.0 %collective-permute-start.27 = (bf16[128,768]{1,0:T(8,128)(2,1)S(1)}, bf16[128,768]{1,0:T(8,128)(2,1)S(1)}, u32[]{:S(2)}, u32[]{:S(2)}) collective-permute-start(bf16[128,768]{1,0:T(8,128)(2,1)S(1)} %get-tuple-element.121), channel_id=1, source_target_pairs={{0,1},{1,0},{2,3},{3,2},{4,5},{5,4},{6,7},{7,6},{8,9},{9,8},{10,11... | collective-permute-start | bytes 589832 | tf_op jit(solution)/shard_map/ppermute | solution.py:24
  103.5 12.0 %collective-permute-start.29 = (bf16[1,1152,128]{2,1,0:T(8,128)(2,1)S(1)}, bf16[1,1152,128]{2,1,0:T(8,128)(2,1)S(1)}, u32[]{:S(2)}, u32[]{:S(2)}) collective-permute-start(bf16[1,1152,128]{2,1,0:T(8,128)(2,1)S(1)} %get-tuple-element.141), channel_id=1, source_target_pairs={{0,16},{4,12},{8,24},{12,4},{16,0},{20,28},{24,8},{28,20},{1,17},{... | collective-permute-start | bytes 884744 | tf_op jit(solution)/shard_map/ppermute | solution.py:33
  111.6 10.7 %collective-permute-start.35 = (bf16[720,128]{1,0:T(8,128)(2,1)S(1)}, bf16[720,128]{1,0:T(8,128)(2,1)S(1)}, u32[]{:S(2)}, u32[]{:S(2)}) collective-permute-start(bf16[720,128]{1,0:T(8,128)(2,1)S(1)} %add_convert_fusion.5.mine_1), channel_id=1, source_target_pairs={{0,1},{1,0},{2,3},{3,2},{4,5},{5,4},{6,7},{7,6},{8,9},{9,8},{10,11... | collective-permute-start | bytes 552968 | tf_op jit(solution)/shard_map/ppermute | solution.py:24
  115.4 11.3 %collective-permute-start.34 = (bf16[720,128]{1,0:T(8,128)(2,1)S(1)}, bf16[720,128]{1,0:T(8,128)(2,1)S(1)}, u32[]{:S(2)}, u32[]{:S(2)}) collective-permute-start(bf16[720,128]{1,0:T(8,128)(2,1)S(1)} %add_convert_fusion.7.mine_0), channel_id=1, source_target_pairs={{0,1},{1,0},{2,3},{3,2},{4,5},{5,4},{6,7},{7,6},{8,9},{9,8},{10,11... | collective-permute-start | bytes 552968 | tf_op jit(solution)/shard_map/ppermute | solution.py:24
  115.6 13.7 %collective-permute-start.36 = (bf16[576,128]{1,0:T(8,128)(2,1)S(1)}, bf16[576,128]{1,0:T(8,128)(2,1)S(1)}, u32[]{:S(2)}, u32[]{:S(2)}) collective-permute-start(bf16[576,128]{1,0:T(8,128)(2,1)S(1)} %get-tuple-element.144), channel_id=1, source_target_pairs={{0,2},{1,3},{2,0},{3,1},{4,6},{5,7},{6,4},{7,5},{8,10},{9,11},{10,... | collective-permute-start | bytes 442376 | tf_op jit(solution)/shard_map/ppermute | solution.py:24
  118.5 13.2 %collective-permute-start.30 = (bf16[576,128]{1,0:T(8,128)(2,1)S(1)}, bf16[576,128]{1,0:T(8,128)(2,1)S(1)}, u32[]{:S(2)}, u32[]{:S(2)}) collective-permute-start(bf16[576,128]{1,0:T(8,128)(2,1)S(1)} %get-tuple-element.145), channel_id=1, source_target_pairs={{0,2},{1,3},{2,0},{3,1},{4,6},{5,7},{6,4},{7,5},{8,10},{9,11},{10,... | collective-permute-start | bytes 442376 | tf_op jit(solution)/shard_map/ppermute | solution.py:24
  129.3 6.8 %collective-permute-start.38 = (bf16[576,128]{1,0:T(8,128)(2,1)S(1)}, bf16[576,128]{1,0:T(8,128)(2,1)S(1)}, u32[]{:S(2)}, u32[]{:S(2)}) collective-permute-start(bf16[576,128]{1,0:T(8,128)(2,1)S(1)} %add_convert_fusion.9.mine_1), channel_id=1, source_target_pairs={{0,1},{1,0},{2,3},{3,2},{4,5},{5,4},{6,7},{7,6},{8,9},{9,8},{10,11... | collective-permute-start | bytes 442376 | tf_op jit(solution)/shard_map/ppermute | solution.py:24
  131.7 6.4 %collective-permute-start.37 = (bf16[576,128]{1,0:T(8,128)(2,1)S(1)}, bf16[576,128]{1,0:T(8,128)(2,1)S(1)}, u32[]{:S(2)}, u32[]{:S(2)}) collective-permute-start(bf16[576,128]{1,0:T(8,128)(2,1)S(1)} %add_convert_fusion.11.mine_0), channel_id=1, source_target_pairs={{0,1},{1,0},{2,3},{3,2},{4,5},{5,4},{6,7},{7,6},{8,9},{9,8},{10,11... | collective-permute-start | bytes 442376 | tf_op jit(solution)/shard_map/ppermute | solution.py:24
  (21 other events, 231.1 us)

commit v6 on v5

--- a/solution.py
+++ b/solution.py
@@ -398,13 +398,12 @@
     return (parts, (), parts)
 
 
-def mlp_layout(rows, take, width, units, attn, glu, down):
-    one = (0, rows, 0, width, attn, 0)
+def mlp_layout(rows, take, width, units, glu, down):
     gate = (0, rows, width, units, glu, 0)
     up = (0, rows, 0, units, glu, units)
     low = (0, take, units, width, down, 0)
-    whole = (one, (0, rows, width, 2 * units, glu, 0), (0, take, width + 2 * units, width, down, 0))
-    return ((one, gate), (up, low), whole)
+    whole = ((0, rows, width, 2 * units, glu, 0), (0, take, width + 2 * units, width, down, 0))
+    return ((gate,), (up, low), whole)
 
 
 def mlp_kernel(pieces, n_refs, rows, down_rows, take, width, units):
@@ -414,8 +413,9 @@
     def body(tok, ctx_own, ctx_other, dy, gains, *rest):
         refs, rest = rest[1 : n_refs + 1], rest[n_refs + 1 :]
         mix_keep, mix_send, shared, ctx_pair, hidden, gn_out = rest[:6]
-        attn, glu, down, ggu, mix, sems = rest[6:]
-        layout = mlp_layout(rows, take, width, units, attn, glu, down)
+        attn, glu, down, ggu, mix, attn_sems, sems = rest[6:]
+        first = place(shard_at(), pieces, refs, attn_layout(rows, width, attn), attn_sems)
+        layout = mlp_layout(rows, take, width, units, glu, down)
         copies = place(shard_at(), pieces, refs, layout, sems)
         at = side_at()
         inputs = tok[RADIUS : RADIUS + 3 * BLOCK, :].astype(F32)
@@ -432,13 +432,15 @@
             ctx_pair[:, 0:half] = ctx_other[pair, :]
             ctx_pair[:, half:] = ctx_own[pair, :]
 
-        for copy in copies:
+        for copy in first:
             copy.wait()
         lifted = dot(ctx_own[...], attn[own_rows, :]) + dot(ctx_other[...], attn[other_rows, :])
         hidden[...] = inputs + lifted
         hat, _ = standardize(hidden[...])
         normed = (hat * gains[1:2, :]).astype(BF)
         shared[:, 0:width] = normed[pair]
+        for copy in copies:
+            copy.wait()
         partial = jnp.zeros((2 * BLOCK, width), F32)
         unit = lax.rem(lax.broadcasted_iota(jnp.int32, (1, units), 1), take)
         mask = jnp.where(unit >= at * (2 * take - down_rows), 1.0, 0.0)
@@ -866,7 +868,8 @@
             pltpu.VMEM((units, width), BF),
             pltpu.VMEM((3 * BLOCK, 2 * units), BF),
             pltpu.VMEM((2 * BLOCK, width), F32),
-            pltpu.SemaphoreType.DMA((3 * len(names),)),
+            pltpu.SemaphoreType.DMA((len(names),)),
+            pltpu.SemaphoreType.DMA((2 * len(names),)),
         ],
         8_000_000_000,
         2 * weight_bytes,
@@ -955,13 +958,8 @@
     )
     mlp_sums, _ = lax.optimization_barrier((mlp_sums, sums[1]))
     mlp_sums = last_sums(*mlp_sums)
-    qkv_sums = scatter_sums(sums, chip_bits)
-    mlp_mine = [side_sum(part, qkv_sums[2]) for part in mlp_sums]
-    mlp_other = [xor_send(part, "replica", 1) for part in mlp_mine]
-    sent = qkv_sums[1]
     norm_send, _ = lax.optimization_barrier((norm_send, sums[1]))
     norm_other = xor_send(norm_send, "replica", 1)
-    norm_other, mix_other, _ = lax.optimization_barrier((norm_other, mix_other, sent))
     mixed = (mix_keep + mix_other.astype(F32)).astype(BF)
     grad_tokens = call(
         final_kernel,
@@ -972,6 +970,10 @@
         1_000_000,
         1_000_000,
     )
+    qkv_sums = scatter_sums(sums, chip_bits, (mixed, grad_tokens))
+    mlp_mine = [side_sum(part, qkv_sums[2]) for part in mlp_sums]
+    mlp_other = [xor_send(part, "replica", 1) for part in mlp_mine]
+    sent = qkv_sums[1]
     grad_glu, grad_down, grad_ffn_gain = call(
         mlp_unpack_kernel(rows, down_rows, take, width, units, count),
         (
@@ -985,7 +987,7 @@
         1_000_000,
         4_000_000,
     )
-    done = (mixed, grad_tokens, grad_glu)
+    done = grad_glu
     qkv_mine = [side_sum(part, done) for part in last_sums(*qkv_sums)]
     qkv_other = [xor_send(part, "replica", 1) for part in qkv_mine]
     grad_qkv, grad_attn, grad_attn_gain = call(

time: 140 us -> 139 us (level)
  waiting for transfers between devices: 68.9 us -> 66.9 us
    ppermute x4, waiting for transfers between devices: 5.77 us -> 2.46 us  [core_send(): lax.ppermute(array, 'shard', [(i, i ^ bits[i & 1]) for i in range(count)])]
where the time goes in v6:
time: 139 us
  waiting for transfers between devices  66.9 us (48%)
  starting transfers between devices  38.7 us (28%)
  Pallas kernels  26.6 us (19%)
  other arithmetic  4.26 us (3%)
    ppermute x33, waiting for transfers between devices, xor_send(): return lax.ppermute(array, axis, [(i, i ^ bit) for i in range(count)])  64.4 us
    ppermute x33, starting transfers between devices, xor_send(): return lax.ppermute(array, axis, [(i, i ^ bit) for i in range(count)])  34 us
    pallas_call x14, Pallas kernels, call(): pl.pallas_call(kernel, out_shape=out_shape, in_specs=specs, out_specs=jax...  26.6 us
    ppermute x4, starting transfers between devices, core_send(): lax.ppermute(array, 'shard', [(i, i ^ bits[i & 1]) for i in range(count)])  3.33 us
  transfers between devices with their start and end apart: 39, of which 21 were waited for; matrix products, arithmetic and copies ran while one was open for 2% of the time, Pallas kernels for 11%

profile of v6, /device:TPU:0, one launch (start us, length us, event | category | flops | bytes accessed | tf_op | source)
XLA Modules:
  0.0 138.6 jit_solution(182566364322245509)
XLA Ops:
  0.7 1.8 %shard_map.153.rest_4_.rest_0_ = bf16[96,1280]{1,0:T(8,128)(2,1)} custom-call(bf16[96,2304]{1,0:T(8,128)(2,1)} %weight.5, bf16[1,96]{1,0:T(2,128)(2,1)} %bitcast.17, bf16[1,96]{1,0:T(2,128)(2,1)} %bitcast.19), custom_call_target="tpu_custom_call" | custom-call | flops 1000000 | bytes 1000000 | tf_op jit(solution)/shard_map/pallas_call | solution.py:176
  2.5 3.0 %collective-permute-start.2 = (bf16[96,1280]{1,0:T(8,128)(2,1)}, bf16[96,1280]{1,0:T(8,128)(2,1)S(1)}, u32[]{:S(2)}, u32[]{:S(2)}) collective-permute-start(bf16[96,1280]{1,0:T(8,128)(2,1)} %shard_map.153.rest_4_.rest_0_), channel_id=1, source_target_pairs={{0,8},{4,12},{8,0},{12,4},{16,24},{20,28},{24,16},{28,20},{1,9},{5... | collective-permute-start | bytes 737288 | tf_op jit(solution)/shard_map/ppermute | solution.py:24
  5.5 1.5 %collective-permute-start.3 = (bf16[96,1280]{1,0:T(8,128)(2,1)}, bf16[96,1280]{1,0:T(8,128)(2,1)S(1)}, u32[]{:S(2)}, u32[]{:S(2)}) collective-permute-start(bf16[96,1280]{1,0:T(8,128)(2,1)} %shard_map.153.rest_4_.rest_0_), channel_id=1, source_target_pairs={{0,16},{4,20},{8,24},{12,28},{16,0},{20,4},{24,8},{28,12},{1,17},{... | collective-permute-start | bytes 737288 | tf_op jit(solution)/shard_map/ppermute | solution.py:24
  9.3 4.5 %collective-permute-start.1 = (bf16[144,768]{1,0:T(8,128)(2,1)S(1)}, bf16[144,768]{1,0:T(8,128)(2,1)S(1)}, u32[]{:S(2)}, u32[]{:S(2)}) collective-permute-start(bf16[144,768]{1,0:T(8,128)(2,1)S(1)} %pad_maximum_fusion.1), channel_id=1, source_target_pairs={{0,1},{1,0},{2,3},{3,2},{4,5},{5,4},{6,7},{7,6},{8,9},{9,8},{10,11... | collective-permute-start | bytes 663560 | tf_op jit(solution)/shard_map/ppermute | solution.py:24
  15.6 9.0 %collective-permute-done.1.partner = bf16[144,768]{1,0:T(8,128)(2,1)S(1)} collective-permute-done((bf16[144,768]{1,0:T(8,128)(2,1)S(1)}, bf16[144,768]{1,0:T(8,128)(2,1)S(1)}, u32[]{:S(2)}, u32[]{:S(2)}) %collective-permute-start.1) | collective-permute-done | bytes 221216 | tf_op jit(solution)/shard_map/ppermute | solution.py:24
  27.0 1.9 %collective-permute-start.6 = (bf16[144,768]{1,0:T(8,128)(2,1)S(1)}, bf16[144,768]{1,0:T(8,128)(2,1)S(1)}, u32[]{:S(2)}, u32[]{:S(2)}) collective-permute-start(bf16[144,768]{1,0:T(8,128)(2,1)S(1)} %collective-permute-done.near), channel_id=1, source_target_pairs={{0,1},{1,0},{2,3},{3,2},{4,5},{5,4},{6,7},{7,6},{8,9},{9,8},{10,11... | collective-permute-start | bytes 663560 | tf_op jit(solution)/shard_map/ppermute | solution.py:24
  29.6 6.0 %collective-permute-start.9 = (bf16[128,768]{1,0:T(8,128)(2,1)S(1)}, bf16[128,768]{1,0:T(8,128)(2,1)S(1)}, u32[]{:S(2)}, u32[]{:S(2)}) collective-permute-start(bf16[128,768]{1,0:T(8,128)(2,1)S(1)} %copy-done.4), channel_id=1, source_target_pairs={{0,1},{1,0},{2,3},{3,2},{4,5},{5,4},{6,7},{7,6},{8,9},{9,8},{10,11... | collective-permute-start | bytes 589832 | tf_op jit(solution)/shard_map/ppermute | solution.py:24
  35.6 1.6 %collective-permute-start.8 = (bf16[64,768]{1,0:T(8,128)(2,1)S(1)}, bf16[64,768]{1,0:T(8,128)(2,1)S(1)}, u32[]{:S(2)}, u32[]{:S(2)}) collective-permute-start(bf16[64,768]{1,0:T(8,128)(2,1)S(1)} %collective-permute-done.7.near), channel_id=1, source_target_pairs={{0,1},{1,0},{2,3},{3,2},{4,5},{5,4},{6,7},{7,6},{8,9},{9,8},{10,11... | collective-permute-start | bytes 294920 | tf_op jit(solution)/shard_map/ppermute | solution.py:24
  39.2 2.2 %collective-permute-done.10.rest_2_ = bf16[96,2816]{1,0:T(8,128)(2,1)S(1)} collective-permute-done((bf16[96,2816]{1,0:T(8,128)(2,1)S(1)}, bf16[96,2816]{1,0:T(8,128)(2,1)S(1)}, u32[]{:S(2)}, u32[]{:S(2)}) %collective-permute-start.10) | collective-permute-done | bytes 540704 | tf_op jit(solution)/shard_map/ppermute | solution.py:24
  41.5 2.9 %collective-permute-start.15 = (bf16[96,1408]{1,0:T(8,128)(2,1)S(1)}, bf16[96,1408]{1,0:T(8,128)(2,1)S(1)}, u32[]{:S(2)}, u32[]{:S(2)}) collective-permute-start(bf16[96,1408]{1,0:T(8,128)(2,1)S(1)} %slice.88.rest_2_), channel_id=1, source_target_pairs={{0,16},{4,20},{8,24},{12,28},{16,0},{20,4},{24,8},{28,12},{1,17},{... | collective-permute-start | bytes 811016 | tf_op jit(solution)/shard_map/ppermute | solution.py:24
  44.5 4.3 %shard_map.155 = (bf16[384,384]{1,0:T(8,128)(2,1)S(1)}, bf16[512,384]{1,0:T(8,128)(2,1)S(1)}, bf16[512,384]{1,0:T(8,128)(2,1)S(1)}, bf16[18,128,256]{2,1,0:T(8,1...) custom-call(bf16[512,768]{1,0:T(8,128)(2,1)S(1)} %get-tuple-element.77.tok, ...), custom_call_target="tpu_custom_call" | custom-call | flops 7000000000 | bytes 3538944 | tf_op jit(solution)/shard_map/pallas_call | solution.py:176
  52.2 3.3 %collective-permute-done.18.rest_7_ = bf16[96,1408]{1,0:T(8,128)(2,1)S(1)} collective-permute-done((bf16[96,1408]{1,0:T(8,128)(2,1)S(1)}, bf16[96,1408]{1,0:T(8,128)(2,1)S(1)}, u32[]{:S(2)}, u32[]{:S(2)}) %collective-permute-start.18) | collective-permute-done | bytes 270368 | tf_op jit(solution)/shard_map/ppermute | solution.py:24
  55.9 4.7 %collective-permute-done.13.ctx_other = bf16[384,384]{1,0:T(8,128)(2,1)S(1)} collective-permute-done((bf16[384,384]{1,0:T(8,128)(2,1)S(1)}, bf16[384,384]{1,0:T(8,128)(2,1)S(1)}, u32[]{:S(2)}, u32[]{:S(2)}) %collective-permute-start.13) | collective-permute-done | bytes 294944 | tf_op jit(solution)/shard_map/ppermute | solution.py:24
  60.6 5.6 %shard_map.157 = (f32[128,768]{1,0:T(8,128)S(1)}, bf16[128,768]{1,0:T(8,128)(2,1)S(1)}, bf16[256,2688]{1,0:T(8,128)(2,1)S(1)}, bf16[256,768]{1,0:T(8,128)(2,1)S(...) custom-call(bf16[512,768]{1,0:T(8,128)(2,1)S(1)} %get-tuple-element.77.tok, ...), custom_call_target="tpu_custom_call" | custom-call | flops 8000000000 | bytes 7077888 | tf_op jit(solution)/shard_map/pallas_call | solution.py:176
  67.1 3.1 %collective-permute-done.23.dy_other = bf16[384,768]{1,0:T(8,128)(2,1)S(1)} collective-permute-done((bf16[384,768]{1,0:T(8,128)(2,1)S(1)}, bf16[384,768]{1,0:T(8,128)(2,1)S(1)}, u32[]{:S(2)}, u32[]{:S(2)}) %collective-permute-start.23) | collective-permute-done | bytes 589856 | tf_op jit(solution)/shard_map/ppermute | solution.py:24
  72.8 10.2 %collective-permute-done.21.gn_other = bf16[384,768]{1,0:T(8,128)(2,1)S(1)} collective-permute-done((bf16[384,768]{1,0:T(8,128)(2,1)S(1)}, bf16[384,768]{1,0:T(8,128)(2,1)S(1)}, u32[]{:S(2)}, u32[]{:S(2)}) %collective-permute-start.21) | collective-permute-done | bytes 589856 | tf_op jit(solution)/shard_map/ppermute | solution.py:24
  82.9 2.6 %shard_map.159 = (f32[128,768]{1,0:T(8,128)S(1)}, bf16[256,384]{1,0:T(8,128)(2,1)S(1)}, bf16[384,384]{1,0:T(8,128)(2,1)S(1)}, bf16[256,384]{1,0:T(8,128)(2,1)S(1)}) custom-call(bf16[384,768]{1,0:T(8,128)(2,1)S(1)} %get-tuple-element.103.gn_own, bf16[384,768]{1,0:T(8,128)(2,1)S(1)} %collective-permute-done.21.gn_other, ...), custom_call_target="tpu_custom_call" | custom-call | flops 5000000000 | bytes 3538944 | tf_op jit(solution)/shard_map/pallas_call | solution.py:176
  86.7 2.2 %shard_map.160.gj.own = bf16[256,1536]{1,0:T(8,128)(2,1)S(1)} custom-call(bf16[256,384]{1,0:T(8,128)(2,1)S(1)} %get-tuple-element.112.first, bf16[256,384]{1,0:T(8,128)(2,1)S(1)} %get-tuple-element.113.halves, bf16[384,384]{1,0:T(8,128)(2,1)S(1)} %get-tuple-element.114.gctx, bf16[384,384]{1,0:T(8,128)(2,1)S(1)} %get-tuple-element.105.q, ...), custom_call_target="tpu_custom_call" | custom-call | flops 6000000000 | bytes 3538944 | tf_op jit(solution)/shard_map/pallas_call | solution.py:176
  90.1 2.3 %shard_map.161 = (f32[128,768]{1,0:T(8,128)S(1)}, bf16[128,768]{1,0:T(8,128)(2,1)S(1)}) custom-call(bf16[256,1536]{1,0:T(8,128)(2,1)S(1)} %shard_map.160.gj.own, bf16[96,1280]{1,0:T(8,128)(2,1)S(1)} %copy-done.3, bf16[96,1280]{1,0:T(8,128)(2,1)S(1)} %collective-permute-done.2.rest_5_.rest_1_, bf16[96,1280]{1,0:T(8,128)(2,1)S(1)} %collective-permute-done.3.rest_6_.rest_2_, ...), custom_call_target="tpu_custom_call" | custom-call | flops 3000000000 | bytes 3538944 | tf_op jit(solution)/shard_map/pallas_call | solution.py:176
  95.0 2.5 %collective-permute-done.31 = bf16[1,1440,128]{2,1,0:T(8,128)(2,1)S(1)} collective-permute-done((bf16[1,1440,128]{2,1,0:T(8,128)(2,1)S(1)}, bf16[1,1440,128]{2,1,0:T(8,128)(2,1)S(1)}, u32[]{:S(2)}, u32[]{:S(2)}) %collective-permute-start.31) | collective-permute-done | bytes 368672 | tf_op jit(solution)/shard_map/ppermute | solution.py:33
  97.9 1.7 %collective-permute-start.33 = (bf16[720,128]{1,0:T(8,128)(2,1)S(1)}, bf16[720,128]{1,0:T(8,128)(2,1)S(1)}, u32[]{:S(2)}, u32[]{:S(2)}) collective-permute-start(bf16[720,128]{1,0:T(8,128)(2,1)S(1)} %get-tuple-element.140), channel_id=1, source_target_pairs={{0,2},{1,3},{2,0},{3,1},{4,6},{5,7},{6,4},{7,5},{8,10},{9,11},{10,... | collective-permute-start | bytes 552968 | tf_op jit(solution)/shard_map/ppermute | solution.py:24
  100.9 5.6 %collective-permute-done.27.other = bf16[128,768]{1,0:T(8,128)(2,1)S(1)} collective-permute-done((bf16[128,768]{1,0:T(8,128)(2,1)S(1)}, bf16[128,768]{1,0:T(8,128)(2,1)S(1)}, u32[]{:S(2)}, u32[]{:S(2)}) %collective-permute-start.27) | collective-permute-done | bytes 196640 | tf_op jit(solution)/shard_map/ppermute | solution.py:24
  109.0 4.9 %collective-permute-done.33 = bf16[720,128]{1,0:T(8,128)(2,1)S(1)} collective-permute-done((bf16[720,128]{1,0:T(8,128)(2,1)S(1)}, bf16[720,128]{1,0:T(8,128)(2,1)S(1)}, u32[]{:S(2)}, u32[]{:S(2)}) %collective-permute-start.33) | collective-permute-done | bytes 184352 | tf_op jit(solution)/shard_map/ppermute | solution.py:24
  114.0 1.8 %collective-permute-done.32 = bf16[720,128]{1,0:T(8,128)(2,1)S(1)} collective-permute-done((bf16[720,128]{1,0:T(8,128)(2,1)S(1)}, bf16[720,128]{1,0:T(8,128)(2,1)S(1)}, u32[]{:S(2)}, u32[]{:S(2)}) %collective-permute-start.32) | collective-permute-done | bytes 184352 | tf_op jit(solution)/shard_map/ppermute | solution.py:24
  116.3 2.5 %collective-permute-start.36 = (bf16[576,128]{1,0:T(8,128)(2,1)S(1)}, bf16[576,128]{1,0:T(8,128)(2,1)S(1)}, u32[]{:S(2)}, u32[]{:S(2)}) collective-permute-start(bf16[576,128]{1,0:T(8,128)(2,1)S(1)} %get-tuple-element.142), channel_id=1, source_target_pairs={{0,2},{1,3},{2,0},{3,1},{4,6},{5,7},{6,4},{7,5},{8,10},{9,11},{10,... | collective-permute-start | bytes 442376 | tf_op jit(solution)/shard_map/ppermute | solution.py:24
  119.3 5.5 %collective-permute-done.35.other_1 = bf16[720,128]{1,0:T(8,128)(2,1)S(1)} collective-permute-done((bf16[720,128]{1,0:T(8,128)(2,1)S(1)}, bf16[720,128]{1,0:T(8,128)(2,1)S(1)}, u32[]{:S(2)}, u32[]{:S(2)}) %collective-permute-start.35) | collective-permute-done | bytes 184352 | tf_op jit(solution)/shard_map/ppermute | solution.py:24
  124.8 2.0 %collective-permute-done.34.other_0 = bf16[720,128]{1,0:T(8,128)(2,1)S(1)} collective-permute-done((bf16[720,128]{1,0:T(8,128)(2,1)S(1)}, bf16[720,128]{1,0:T(8,128)(2,1)S(1)}, u32[]{:S(2)}, u32[]{:S(2)}) %collective-permute-start.34) | collective-permute-done | bytes 184352 | tf_op jit(solution)/shard_map/ppermute | solution.py:24
  126.8 1.6 %shard_map.164 = (f32[96,2304]{1,0:T(8,128)}, f32[144,768]{1,0:T(8,128)}, f32[1,96]{1,0:T(1,128)}) custom-call(bf16[720,128]{1,0:T(8,128)(2,1)S(1)} %add_convert_fusion.7.mine_0, bf16[720,128]{1,0:T(8,128)(2,1)S(1)} %add_convert_fusion.5.mine_1, bf16[720,128]{1,0:T(8,128)(2,1)S(1)} %collective-permute-done.34.other_0, ...), custom_call_target="tpu_custom_call" | custom-call | flops 1000000 | bytes 4000000 | tf_op jit(solution)/shard_map/pallas_call | solution.py:176
  128.4 1.6 %collective-permute-done.36 = bf16[576,128]{1,0:T(8,128)(2,1)S(1)} collective-permute-done((bf16[576,128]{1,0:T(8,128)(2,1)S(1)}, bf16[576,128]{1,0:T(8,128)(2,1)S(1)}, u32[]{:S(2)}, u32[]{:S(2)}) %collective-permute-start.36) | collective-permute-done | bytes 147488 | tf_op jit(solution)/shard_map/ppermute | solution.py:24
  130.0 1.5 %collective-permute-done.30 = bf16[576,128]{1,0:T(8,128)(2,1)S(1)} collective-permute-done((bf16[576,128]{1,0:T(8,128)(2,1)S(1)}, bf16[576,128]{1,0:T(8,128)(2,1)S(1)}, u32[]{:S(2)}, u32[]{:S(2)}) %collective-permute-start.30) | collective-permute-done | bytes 147488 | tf_op jit(solution)/shard_map/ppermute | solution.py:24
  132.2 3.4 %collective-permute-done.38.other_1 = bf16[576,128]{1,0:T(8,128)(2,1)S(1)} collective-permute-done((bf16[576,128]{1,0:T(8,128)(2,1)S(1)}, bf16[576,128]{1,0:T(8,128)(2,1)S(1)}, u32[]{:S(2)}, u32[]{:S(2)}) %collective-permute-start.38) | collective-permute-done | bytes 147488 | tf_op jit(solution)/shard_map/ppermute | solution.py:24
  135.6 1.6 %collective-permute-done.37.other_0 = bf16[576,128]{1,0:T(8,128)(2,1)S(1)} collective-permute-done((bf16[576,128]{1,0:T(8,128)(2,1)S(1)}, bf16[576,128]{1,0:T(8,128)(2,1)S(1)}, u32[]{:S(2)}, u32[]{:S(2)}) %collective-permute-start.37) | collective-permute-done | bytes 147488 | tf_op jit(solution)/shard_map/ppermute | solution.py:24
  (107 shorter events, 29.0 us)
Async XLA Ops:
  2.5 11.3 %collective-permute-start.2 = (bf16[96,1280]{1,0:T(8,128)(2,1)}, bf16[96,1280]{1,0:T(8,128)(2,1)S(1)}, u32[]{:S(2)}, u32[]{:S(2)}) collective-permute-start(bf16[96,1280]{1,0:T(8,128)(2,1)} %shard_map.153.rest_4_.rest_0_), channel_id=1, source_target_pairs={{0,8},{4,12},{8,0},{12,4},{16,24},{20,28},{24,16},{28,20},{1,9},{5... | collective-permute-start | bytes 737288 | tf_op jit(solution)/shard_map/ppermute | solution.py:24
  5.5 8.3 %collective-permute-start.3 = (bf16[96,1280]{1,0:T(8,128)(2,1)}, bf16[96,1280]{1,0:T(8,128)(2,1)S(1)}, u32[]{:S(2)}, u32[]{:S(2)}) collective-permute-start(bf16[96,1280]{1,0:T(8,128)(2,1)} %shard_map.153.rest_4_.rest_0_), channel_id=1, source_target_pairs={{0,16},{4,20},{8,24},{12,28},{16,0},{20,4},{24,8},{28,12},{1,17},{... | collective-permute-start | bytes 737288 | tf_op jit(solution)/shard_map/ppermute | solution.py:24
  8.6 6.9 %collective-permute-start = (bf16[144,768]{1,0:T(8,128)(2,1)S(1)}, bf16[144,768]{1,0:T(8,128)(2,1)S(1)}, u32[]{:S(2)}, u32[]{:S(2)}) collective-permute-start(bf16[144,768]{1,0:T(8,128)(2,1)S(1)} %pad_maximum_fusion.1), channel_id=1, source_target_pairs={{1,2},{2,1},{3,4},{4,3},{5,6},{6,5},{7,8},{8,7},{9,10},{10,9},{11,... | collective-permute-start | bytes 663560 | tf_op jit(solution)/shard_map/ppermute | solution.py:768
  9.3 15.3 %collective-permute-start.1 = (bf16[144,768]{1,0:T(8,128)(2,1)S(1)}, bf16[144,768]{1,0:T(8,128)(2,1)S(1)}, u32[]{:S(2)}, u32[]{:S(2)}) collective-permute-start(bf16[144,768]{1,0:T(8,128)(2,1)S(1)} %pad_maximum_fusion.1), channel_id=1, source_target_pairs={{0,1},{1,0},{2,3},{3,2},{4,5},{5,4},{6,7},{7,6},{8,9},{9,8},{10,11... | collective-permute-start | bytes 663560 | tf_op jit(solution)/shard_map/ppermute | solution.py:24
  13.8 10.8 %collective-permute-start.4 = (bf16[96,640]{1,0:T(8,128)(2,1)S(1)}, bf16[96,640]{1,0:T(8,128)(2,1)S(1)}, u32[]{:S(2)}, u32[]{:S(2)}) collective-permute-start(bf16[96,640]{1,0:T(8,128)(2,1)S(1)} %slice.66), channel_id=1, source_target_pairs={{0,16},{4,20},{8,24},{12,28},{16,0},{20,4},{24,8},{28,12},{1,17},{... | collective-permute-start | bytes 368648 | tf_op jit(solution)/shard_map/ppermute | solution.py:24
  14.8 9.8 %collective-permute-start.5 = (bf16[96,640]{1,0:T(8,128)(2,1)S(1)}, bf16[96,640]{1,0:T(8,128)(2,1)S(1)}, u32[]{:S(2)}, u32[]{:S(2)}) collective-permute-start(bf16[96,640]{1,0:T(8,128)(2,1)S(1)} %slice.67), channel_id=1, source_target_pairs={{0,8},{4,12},{8,0},{12,4},{16,24},{20,28},{24,16},{28,20},{1,9},{5... | collective-permute-start | bytes 368648 | tf_op jit(solution)/shard_map/ppermute | solution.py:24
  25.7 18.8 %collective-permute-start.12 = (bf16[384,1280]{1,0:T(8,128)(2,1)}, bf16[384,1280]{1,0:T(8,128)(2,1)}, u32[]{:S(2)}, u32[]{:S(2)}) collective-permute-start(bf16[384,1280]{1,0:T(8,128)(2,1)} %maximum_maximum_fusion), channel_id=1, source_target_pairs={{0,4},{4,0},{8,12},{12,8},{16,20},{20,16},{24,28},{28,24},{1,5},{5... | collective-permute-start | bytes 2949128 | tf_op jit(solution)/shard_map/ppermute | solution.py:24
  25.8 15.6 %collective-permute-start.10 = (bf16[96,2816]{1,0:T(8,128)(2,1)S(1)}, bf16[96,2816]{1,0:T(8,128)(2,1)S(1)}, u32[]{:S(2)}, u32[]{:S(2)}) collective-permute-start(bf16[96,2816]{1,0:T(8,128)(2,1)S(1)} %shard_map.152.rest_1_), channel_id=1, source_target_pairs={{0,8},{4,12},{8,0},{12,4},{16,24},{20,28},{24,16},{28,20},{1,9},{5... | collective-permute-start | bytes 1622024 | tf_op jit(solution)/shard_map/ppermute | solution.py:24
  27.0 17.4 %collective-permute-start.11 = (bf16[96,2816]{1,0:T(8,128)(2,1)S(1)}, bf16[96,2816]{1,0:T(8,128)(2,1)S(1)}, u32[]{:S(2)}, u32[]{:S(2)}) collective-permute-start(bf16[96,2816]{1,0:T(8,128)(2,1)S(1)} %shard_map.152.rest_1_), channel_id=1, source_target_pairs={{0,16},{4,20},{8,24},{12,28},{16,0},{20,4},{24,8},{28,12},{1,17},{... | collective-permute-start | bytes 1622024 | tf_op jit(solution)/shard_map/ppermute | solution.py:24
  27.0 8.6 %collective-permute-start.6 = (bf16[144,768]{1,0:T(8,128)(2,1)S(1)}, bf16[144,768]{1,0:T(8,128)(2,1)S(1)}, u32[]{:S(2)}, u32[]{:S(2)}) collective-permute-start(bf16[144,768]{1,0:T(8,128)(2,1)S(1)} %collective-permute-done.near), channel_id=1, source_target_pairs={{0,1},{1,0},{2,3},{3,2},{4,5},{5,4},{6,7},{7,6},{8,9},{9,8},{10,11... | collective-permute-start | bytes 663560 | tf_op jit(solution)/shard_map/ppermute | solution.py:24
  29.6 14.9 %collective-permute-start.9 = (bf16[128,768]{1,0:T(8,128)(2,1)S(1)}, bf16[128,768]{1,0:T(8,128)(2,1)S(1)}, u32[]{:S(2)}, u32[]{:S(2)}) collective-permute-start(bf16[128,768]{1,0:T(8,128)(2,1)S(1)} %copy-done.4), channel_id=1, source_target_pairs={{0,1},{1,0},{2,3},{3,2},{4,5},{5,4},{6,7},{7,6},{8,9},{9,8},{10,11... | collective-permute-start | bytes 589832 | tf_op jit(solution)/shard_map/ppermute | solution.py:24
  35.6 8.9 %collective-permute-start.8 = (bf16[64,768]{1,0:T(8,128)(2,1)S(1)}, bf16[64,768]{1,0:T(8,128)(2,1)S(1)}, u32[]{:S(2)}, u32[]{:S(2)}) collective-permute-start(bf16[64,768]{1,0:T(8,128)(2,1)S(1)} %collective-permute-done.7.near), channel_id=1, source_target_pairs={{0,1},{1,0},{2,3},{3,2},{4,5},{5,4},{6,7},{7,6},{8,9},{9,8},{10,11... | collective-permute-start | bytes 294920 | tf_op jit(solution)/shard_map/ppermute | solution.py:24
  41.5 8.0 %collective-permute-start.15 = (bf16[96,1408]{1,0:T(8,128)(2,1)S(1)}, bf16[96,1408]{1,0:T(8,128)(2,1)S(1)}, u32[]{:S(2)}, u32[]{:S(2)}) collective-permute-start(bf16[96,1408]{1,0:T(8,128)(2,1)S(1)} %slice.88.rest_2_), channel_id=1, source_target_pairs={{0,16},{4,20},{8,24},{12,28},{16,0},{20,4},{24,8},{28,12},{1,17},{... | collective-permute-start | bytes 811016 | tf_op jit(solution)/shard_map/ppermute | solution.py:24
  44.4 6.5 %collective-permute-start.16 = (bf16[96,1408]{1,0:T(8,128)(2,1)S(1)}, bf16[96,1408]{1,0:T(8,128)(2,1)S(1)}, u32[]{:S(2)}, u32[]{:S(2)}) collective-permute-start(bf16[96,1408]{1,0:T(8,128)(2,1)S(1)} %slice.89.rest_3_), channel_id=1, source_target_pairs={{0,8},{4,12},{8,0},{12,4},{16,24},{20,28},{24,16},{28,20},{1,9},{5... | collective-permute-start | bytes 811016 | tf_op jit(solution)/shard_map/ppermute | solution.py:24
  51.0 9.6 %collective-permute-start.17 = (bf16[288,2816]{1,0:T(8,128)(2,1)S(1)}, bf16[288,2816]{1,0:T(8,128)(2,1)S(1)}, u32[]{:S(2)}, u32[]{:S(2)}) collective-permute-start(bf16[288,2816]{1,0:T(8,128)(2,1)S(1)} %pad_maximum_fusion), channel_id=1, source_target_pairs={{0,4},{4,0},{8,12},{12,8},{16,20},{20,16},{24,28},{28,24},{1,5},{5... | collective-permute-start | bytes 4866056 | tf_op jit(solution)/shard_map/ppermute | solution.py:24
  51.1 9.5 %collective-permute-start.14 = (bf16[256,768]{1,0:T(8,128)(2,1)S(1)}, bf16[256,768]{1,0:T(8,128)(2,1)S(1)}, u32[]{:S(2)}, u32[]{:S(2)}) collective-permute-start(bf16[256,768]{1,0:T(8,128)(2,1)S(1)} %get-tuple-element.95.normed_own), channel_id=1, source_target_pairs={{0,4},{4,0},{8,12},{12,8},{16,20},{20,16},{24,28},{28,24},{1,5},{5... | collective-permute-start | bytes 1179656 | tf_op jit(solution)/shard_map/ppermute | solution.py:24
  51.6 9.0 %collective-permute-start.13 = (bf16[384,384]{1,0:T(8,128)(2,1)S(1)}, bf16[384,384]{1,0:T(8,128)(2,1)S(1)}, u32[]{:S(2)}, u32[]{:S(2)}) collective-permute-start(bf16[384,384]{1,0:T(8,128)(2,1)S(1)} %get-tuple-element.90.ctx_own), channel_id=1, source_target_pairs={{0,1},{1,0},{2,3},{3,2},{4,5},{5,4},{6,7},{7,6},{8,9},{9,8},{10,11... | collective-permute-start | bytes 884744 | tf_op jit(solution)/shard_map/ppermute | solution.py:24
  66.8 16.1 %collective-permute-start.21 = (bf16[384,768]{1,0:T(8,128)(2,1)S(1)}, bf16[384,768]{1,0:T(8,128)(2,1)S(1)}, u32[]{:S(2)}, u32[]{:S(2)}) collective-permute-start(bf16[384,768]{1,0:T(8,128)(2,1)S(1)} %get-tuple-element.103.gn_own), channel_id=1, source_target_pairs={{0,1},{1,0},{2,3},{3,2},{4,5},{5,4},{6,7},{7,6},{8,9},{9,8},{10,11... | collective-permute-start | bytes 1769480 | tf_op jit(solution)/shard_map/ppermute | solution.py:24
  72.2 13.4 %collective-permute-start.25 = (bf16[2,1440,128]{2,1,0:T(8,128)(2,1)S(1)}, bf16[2,1440,128]{2,1,0:T(8,128)(2,1)S(1)}, u32[]{:S(2)}, u32[]{:S(2)}) collective-permute-start(bf16[2,1440,128]{2,1,0:T(8,128)(2,1)S(1)} %get-tuple-element.115), channel_id=1, source_target_pairs={{0,8},{4,20},{8,0},{12,28},{16,24},{20,4},{24,16},{28,12},{1,9},{5... | collective-permute-start | bytes 2211848 | tf_op jit(solution)/shard_map/ppermute | solution.py:33
  72.3 14.4 %collective-permute-start.20 = (bf16[128,768]{1,0:T(8,128)(2,1)S(1)}, bf16[128,768]{1,0:T(8,128)(2,1)S(1)}, u32[]{:S(2)}, u32[]{:S(2)}) collective-permute-start(bf16[128,768]{1,0:T(8,128)(2,1)S(1)} %get-tuple-element.102), channel_id=1, source_target_pairs={{0,1},{1,0},{2,3},{3,2},{4,5},{5,4},{6,7},{7,6},{8,9},{9,8},{10,11... | collective-permute-start | bytes 589832 | tf_op jit(solution)/shard_map/ppermute | solution.py:24
  89.0 8.5 %collective-permute-start.31 = (bf16[1,1440,128]{2,1,0:T(8,128)(2,1)S(1)}, bf16[1,1440,128]{2,1,0:T(8,128)(2,1)S(1)}, u32[]{:S(2)}, u32[]{:S(2)}) collective-permute-start(bf16[1,1440,128]{2,1,0:T(8,128)(2,1)S(1)} %get-tuple-element.137.sent), channel_id=1, source_target_pairs={{0,16},{4,12},{8,24},{12,4},{16,0},{20,28},{24,8},{28,20},{1,17},{... | collective-permute-start | bytes 1105928 | tf_op jit(solution)/shard_map/ppermute | solution.py:33
  93.5 14.0 %collective-permute-start.28 = (bf16[2,1152,128]{2,1,0:T(8,128)(2,1)S(1)}, bf16[2,1152,128]{2,1,0:T(8,128)(2,1)S(1)}, u32[]{:S(2)}, u32[]{:S(2)}) collective-permute-start(bf16[2,1152,128]{2,1,0:T(8,128)(2,1)S(1)} %get-tuple-element.122), channel_id=1, source_target_pairs={{0,8},{4,20},{8,0},{12,28},{16,24},{20,4},{24,16},{28,12},{1,9},{5... | collective-permute-start | bytes 1769480 | tf_op jit(solution)/shard_map/ppermute | solution.py:33
  97.5 9.0 %collective-permute-start.27 = (bf16[128,768]{1,0:T(8,128)(2,1)S(1)}, bf16[128,768]{1,0:T(8,128)(2,1)S(1)}, u32[]{:S(2)}, u32[]{:S(2)}) collective-permute-start(bf16[128,768]{1,0:T(8,128)(2,1)S(1)} %get-tuple-element.120), channel_id=1, source_target_pairs={{0,1},{1,0},{2,3},{3,2},{4,5},{5,4},{6,7},{7,6},{8,9},{9,8},{10,11... | collective-permute-start | bytes 589832 | tf_op jit(solution)/shard_map/ppermute | solution.py:24
  97.9 16.0 %collective-permute-start.33 = (bf16[720,128]{1,0:T(8,128)(2,1)S(1)}, bf16[720,128]{1,0:T(8,128)(2,1)S(1)}, u32[]{:S(2)}, u32[]{:S(2)}) collective-permute-start(bf16[720,128]{1,0:T(8,128)(2,1)S(1)} %get-tuple-element.140), channel_id=1, source_target_pairs={{0,2},{1,3},{2,0},{3,1},{4,6},{5,7},{6,4},{7,5},{8,10},{9,11},{10,... | collective-permute-start | bytes 552968 | tf_op jit(solution)/shard_map/ppermute | solution.py:24
  99.6 16.3 %collective-permute-start.32 = (bf16[720,128]{1,0:T(8,128)(2,1)S(1)}, bf16[720,128]{1,0:T(8,128)(2,1)S(1)}, u32[]{:S(2)}, u32[]{:S(2)}) collective-permute-start(bf16[720,128]{1,0:T(8,128)(2,1)S(1)} %get-tuple-element.141), channel_id=1, source_target_pairs={{0,2},{1,3},{2,0},{3,1},{4,6},{5,7},{6,4},{7,5},{8,10},{9,11},{10,... | collective-permute-start | bytes 552968 | tf_op jit(solution)/shard_map/ppermute | solution.py:24
  107.7 8.5 %collective-permute-start.29 = (bf16[1,1152,128]{2,1,0:T(8,128)(2,1)S(1)}, bf16[1,1152,128]{2,1,0:T(8,128)(2,1)S(1)}, u32[]{:S(2)}, u32[]{:S(2)}) collective-permute-start(bf16[1,1152,128]{2,1,0:T(8,128)(2,1)S(1)} %get-tuple-element.139), channel_id=1, source_target_pairs={{0,16},{4,12},{8,24},{12,4},{16,0},{20,28},{24,8},{28,20},{1,17},{... | collective-permute-start | bytes 884744 | tf_op jit(solution)/shard_map/ppermute | solution.py:33
  114.0 10.8 %collective-permute-start.35 = (bf16[720,128]{1,0:T(8,128)(2,1)S(1)}, bf16[720,128]{1,0:T(8,128)(2,1)S(1)}, u32[]{:S(2)}, u32[]{:S(2)}) collective-permute-start(bf16[720,128]{1,0:T(8,128)(2,1)S(1)} %add_convert_fusion.5.mine_1), channel_id=1, source_target_pairs={{0,1},{1,0},{2,3},{3,2},{4,5},{5,4},{6,7},{7,6},{8,9},{9,8},{10,11... | collective-permute-start | bytes 552968 | tf_op jit(solution)/shard_map/ppermute | solution.py:24
  115.9 10.8 %collective-permute-start.34 = (bf16[720,128]{1,0:T(8,128)(2,1)S(1)}, bf16[720,128]{1,0:T(8,128)(2,1)S(1)}, u32[]{:S(2)}, u32[]{:S(2)}) collective-permute-start(bf16[720,128]{1,0:T(8,128)(2,1)S(1)} %add_convert_fusion.7.mine_0), channel_id=1, source_target_pairs={{0,1},{1,0},{2,3},{3,2},{4,5},{5,4},{6,7},{7,6},{8,9},{9,8},{10,11... | collective-permute-start | bytes 552968 | tf_op jit(solution)/shard_map/ppermute | solution.py:24
  116.3 13.6 %collective-permute-start.36 = (bf16[576,128]{1,0:T(8,128)(2,1)S(1)}, bf16[576,128]{1,0:T(8,128)(2,1)S(1)}, u32[]{:S(2)}, u32[]{:S(2)}) collective-permute-start(bf16[576,128]{1,0:T(8,128)(2,1)S(1)} %get-tuple-element.142), channel_id=1, source_target_pairs={{0,2},{1,3},{2,0},{3,1},{4,6},{5,7},{6,4},{7,5},{8,10},{9,11},{10,... | collective-permute-start | bytes 442376 | tf_op jit(solution)/shard_map/ppermute | solution.py:24
  118.8 12.7 %collective-permute-start.30 = (bf16[576,128]{1,0:T(8,128)(2,1)S(1)}, bf16[576,128]{1,0:T(8,128)(2,1)S(1)}, u32[]{:S(2)}, u32[]{:S(2)}) collective-permute-start(bf16[576,128]{1,0:T(8,128)(2,1)S(1)} %get-tuple-element.143), channel_id=1, source_target_pairs={{0,2},{1,3},{2,0},{3,1},{4,6},{5,7},{6,4},{7,5},{8,10},{9,11},{10,... | collective-permute-start | bytes 442376 | tf_op jit(solution)/shard_map/ppermute | solution.py:24
  130.0 5.6 %collective-permute-start.38 = (bf16[576,128]{1,0:T(8,128)(2,1)S(1)}, bf16[576,128]{1,0:T(8,128)(2,1)S(1)}, u32[]{:S(2)}, u32[]{:S(2)}) collective-permute-start(bf16[576,128]{1,0:T(8,128)(2,1)S(1)} %add_convert_fusion.9.mine_1), channel_id=1, source_target_pairs={{0,1},{1,0},{2,3},{3,2},{4,5},{5,4},{6,7},{7,6},{8,9},{9,8},{10,11... | collective-permute-start | bytes 442376 | tf_op jit(solution)/shard_map/ppermute | solution.py:24
  131.5 5.6 %collective-permute-start.37 = (bf16[576,128]{1,0:T(8,128)(2,1)S(1)}, bf16[576,128]{1,0:T(8,128)(2,1)S(1)}, u32[]{:S(2)}, u32[]{:S(2)}) collective-permute-start(bf16[576,128]{1,0:T(8,128)(2,1)S(1)} %add_convert_fusion.11.mine_0), channel_id=1, source_target_pairs={{0,1},{1,0},{2,3},{3,2},{4,5},{5,4},{6,7},{7,6},{8,9},{9,8},{10,11... | collective-permute-start | bytes 442376 | tf_op jit(solution)/shard_map/ppermute | solution.py:24
  (21 other events, 232.1 us)

commit v7 on v6

--- a/solution.py
+++ b/solution.py
@@ -444,8 +444,8 @@
         partial = jnp.zeros((2 * BLOCK, width), F32)
         unit = lax.rem(lax.broadcasted_iota(jnp.int32, (1, units), 1), take)
         mask = jnp.where(unit >= at * (2 * take - down_rows), 1.0, 0.0)
-        for c in range(0, units, 256):
-            wide = min(256, units - c)
+        for c in range(0, units, 640):
+            wide = min(640, units - c)
             cols = slice(c, c + wide)
             gate = dot(normed, glu[:, cols])
             up = dot(normed, glu[:, units + c : units + c + wide])
@@ -547,7 +547,7 @@
 def back_kernel(width):
     half = width // 2
 
-    def body(first, halves, gctx, q, k, v, p, cosine, sine, sent, mixed, gj_out):
+    def body(first, halves, gctx, q, k, v, p, cosine, sine, sent, gj_out):
         gj_out[:, 3 * half :] = halves[...]
         cos, sin = cosine[BLOCK : 3 * BLOCK, :], sine[BLOCK : 3 * BLOCK, :]
         for part in range(3):
@@ -924,7 +924,7 @@
         back_kernel(width),
         shaped((2 * BLOCK, 4 * half), BF),
         (gj_first, halves, gctx, q, k, v, p, cosine, sine),
-        [mlp_sums[2], mix_other],
+        [mlp_sums[2]],
         [],
         6_000_000_000,
         weight_bytes,
@@ -956,7 +956,7 @@
         3_000_000_000,
         weight_bytes,
     )
-    mlp_sums, _ = lax.optimization_barrier((mlp_sums, sums[1]))
+    mlp_sums, mix_other, _ = lax.optimization_barrier((mlp_sums, mix_other, sums[1]))
     mlp_sums = last_sums(*mlp_sums)
     norm_send, _ = lax.optimization_barrier((norm_send, sums[1]))
     norm_other = xor_send(norm_send, "replica", 1)

time: 139 us -> 137 us (0.986)
  waiting for transfers between devices: 66.9 us -> 62 us
  starting transfers between devices: 38.7 us -> 42.5 us
    ppermute x33, waiting for transfers between devices: 64.4 us -> 59.2 us  [xor_send(): return lax.ppermute(array, axis, [(i, i ^ bit) for i in range(count)])]
    ppermute x33, starting transfers between devices: 34 us -> 37.7 us  [xor_send(): return lax.ppermute(array, axis, [(i, i ^ bit) for i in range(count)])]
where the time goes in v7:
time: 137 us
  waiting for transfers between devices  62 us (45%)
  starting transfers between devices  42.5 us (31%)
  Pallas kernels  26.3 us (19%)
  other arithmetic  4.26 us (3%)
    ppermute x33, waiting for transfers between devices, xor_send(): return lax.ppermute(array, axis, [(i, i ^ bit) for i in range(count)])  59.2 us
    ppermute x33, starting transfers between devices, xor_send(): return lax.ppermute(array, axis, [(i, i ^ bit) for i in range(count)])  37.7 us
    pallas_call x14, Pallas kernels, call(): pl.pallas_call(kernel, out_shape=out_shape, in_specs=specs, out_specs=jax...  26.3 us
    ppermute x4, starting transfers between devices, core_send(): lax.ppermute(array, 'shard', [(i, i ^ bits[i & 1]) for i in range(count)])  3.4 us
    ppermute x4, waiting for transfers between devices, core_send(): lax.ppermute(array, 'shard', [(i, i ^ bits[i & 1]) for i in range(count)])  2.79 us
  transfers between devices with their start and end apart: 39, of which 21 were waited for; matrix products, arithmetic and copies ran while one was open for 2% of the time, Pallas kernels for 11%

profile of v7, /device:TPU:0, one launch (start us, length us, event | category | flops | bytes accessed | tf_op | source)
XLA Modules:
  0.0 137.2 jit_solution(14384004092874713666)
XLA Ops:
  0.7 1.8 %shard_map.153.rest_4_.rest_0_ = bf16[96,1280]{1,0:T(8,128)(2,1)} custom-call(bf16[96,2304]{1,0:T(8,128)(2,1)} %weight.5, bf16[1,96]{1,0:T(2,128)(2,1)} %bitcast.17, bf16[1,96]{1,0:T(2,128)(2,1)} %bitcast.19), custom_call_target="tpu_custom_call" | custom-call | flops 1000000 | bytes 1000000 | tf_op jit(solution)/shard_map/pallas_call | solution.py:176
  2.5 3.0 %collective-permute-start.2 = (bf16[96,1280]{1,0:T(8,128)(2,1)}, bf16[96,1280]{1,0:T(8,128)(2,1)S(1)}, u32[]{:S(2)}, u32[]{:S(2)}) collective-permute-start(bf16[96,1280]{1,0:T(8,128)(2,1)} %shard_map.153.rest_4_.rest_0_), channel_id=1, source_target_pairs={{0,8},{4,12},{8,0},{12,4},{16,24},{20,28},{24,16},{28,20},{1,9},{5... | collective-permute-start | bytes 737288 | tf_op jit(solution)/shard_map/ppermute | solution.py:24
  5.5 1.5 %collective-permute-start.3 = (bf16[96,1280]{1,0:T(8,128)(2,1)}, bf16[96,1280]{1,0:T(8,128)(2,1)S(1)}, u32[]{:S(2)}, u32[]{:S(2)}) collective-permute-start(bf16[96,1280]{1,0:T(8,128)(2,1)} %shard_map.153.rest_4_.rest_0_), channel_id=1, source_target_pairs={{0,16},{4,20},{8,24},{12,28},{16,0},{20,4},{24,8},{28,12},{1,17},{... | collective-permute-start | bytes 737288 | tf_op jit(solution)/shard_map/ppermute | solution.py:24
  9.3 4.5 %collective-permute-start.1 = (bf16[144,768]{1,0:T(8,128)(2,1)S(1)}, bf16[144,768]{1,0:T(8,128)(2,1)S(1)}, u32[]{:S(2)}, u32[]{:S(2)}) collective-permute-start(bf16[144,768]{1,0:T(8,128)(2,1)S(1)} %pad_maximum_fusion.1), channel_id=1, source_target_pairs={{0,1},{1,0},{2,3},{3,2},{4,5},{5,4},{6,7},{7,6},{8,9},{9,8},{10,11... | collective-permute-start | bytes 663560 | tf_op jit(solution)/shard_map/ppermute | solution.py:24
  15.6 9.0 %collective-permute-done.1.partner = bf16[144,768]{1,0:T(8,128)(2,1)S(1)} collective-permute-done((bf16[144,768]{1,0:T(8,128)(2,1)S(1)}, bf16[144,768]{1,0:T(8,128)(2,1)S(1)}, u32[]{:S(2)}, u32[]{:S(2)}) %collective-permute-start.1) | collective-permute-done | bytes 221216 | tf_op jit(solution)/shard_map/ppermute | solution.py:24
  27.0 1.9 %collective-permute-start.6 = (bf16[144,768]{1,0:T(8,128)(2,1)S(1)}, bf16[144,768]{1,0:T(8,128)(2,1)S(1)}, u32[]{:S(2)}, u32[]{:S(2)}) collective-permute-start(bf16[144,768]{1,0:T(8,128)(2,1)S(1)} %collective-permute-done.near), channel_id=1, source_target_pairs={{0,1},{1,0},{2,3},{3,2},{4,5},{5,4},{6,7},{7,6},{8,9},{9,8},{10,11... | collective-permute-start | bytes 663560 | tf_op jit(solution)/shard_map/ppermute | solution.py:24
  29.6 6.0 %collective-permute-start.9 = (bf16[128,768]{1,0:T(8,128)(2,1)S(1)}, bf16[128,768]{1,0:T(8,128)(2,1)S(1)}, u32[]{:S(2)}, u32[]{:S(2)}) collective-permute-start(bf16[128,768]{1,0:T(8,128)(2,1)S(1)} %copy-done.4), channel_id=1, source_target_pairs={{0,1},{1,0},{2,3},{3,2},{4,5},{5,4},{6,7},{7,6},{8,9},{9,8},{10,11... | collective-permute-start | bytes 589832 | tf_op jit(solution)/shard_map/ppermute | solution.py:24
  35.6 1.6 %collective-permute-start.8 = (bf16[64,768]{1,0:T(8,128)(2,1)S(1)}, bf16[64,768]{1,0:T(8,128)(2,1)S(1)}, u32[]{:S(2)}, u32[]{:S(2)}) collective-permute-start(bf16[64,768]{1,0:T(8,128)(2,1)S(1)} %collective-permute-done.7.near), channel_id=1, source_target_pairs={{0,1},{1,0},{2,3},{3,2},{4,5},{5,4},{6,7},{7,6},{8,9},{9,8},{10,11... | collective-permute-start | bytes 294920 | tf_op jit(solution)/shard_map/ppermute | solution.py:24
  39.2 2.2 %collective-permute-done.10.rest_2_ = bf16[96,2816]{1,0:T(8,128)(2,1)S(1)} collective-permute-done((bf16[96,2816]{1,0:T(8,128)(2,1)S(1)}, bf16[96,2816]{1,0:T(8,128)(2,1)S(1)}, u32[]{:S(2)}, u32[]{:S(2)}) %collective-permute-start.10) | collective-permute-done | bytes 540704 | tf_op jit(solution)/shard_map/ppermute | solution.py:24
  41.5 2.9 %collective-permute-start.15 = (bf16[96,1408]{1,0:T(8,128)(2,1)S(1)}, bf16[96,1408]{1,0:T(8,128)(2,1)S(1)}, u32[]{:S(2)}, u32[]{:S(2)}) collective-permute-start(bf16[96,1408]{1,0:T(8,128)(2,1)S(1)} %slice.88.rest_2_), channel_id=1, source_target_pairs={{0,16},{4,20},{8,24},{12,28},{16,0},{20,4},{24,8},{28,12},{1,17},{... | collective-permute-start | bytes 811016 | tf_op jit(solution)/shard_map/ppermute | solution.py:24
  44.5 4.3 %shard_map.155 = (bf16[384,384]{1,0:T(8,128)(2,1)S(1)}, bf16[512,384]{1,0:T(8,128)(2,1)S(1)}, bf16[512,384]{1,0:T(8,128)(2,1)S(1)}, bf16[18,128,256]{2,1,0:T(8,1...) custom-call(bf16[512,768]{1,0:T(8,128)(2,1)S(1)} %get-tuple-element.78.tok, ...), custom_call_target="tpu_custom_call" | custom-call | flops 7000000000 | bytes 3538944 | tf_op jit(solution)/shard_map/pallas_call | solution.py:176
  52.2 3.3 %collective-permute-done.18.rest_7_ = bf16[96,1408]{1,0:T(8,128)(2,1)S(1)} collective-permute-done((bf16[96,1408]{1,0:T(8,128)(2,1)S(1)}, bf16[96,1408]{1,0:T(8,128)(2,1)S(1)}, u32[]{:S(2)}, u32[]{:S(2)}) %collective-permute-start.18) | collective-permute-done | bytes 270368 | tf_op jit(solution)/shard_map/ppermute | solution.py:24
  55.9 4.7 %collective-permute-done.13.ctx_other = bf16[384,384]{1,0:T(8,128)(2,1)S(1)} collective-permute-done((bf16[384,384]{1,0:T(8,128)(2,1)S(1)}, bf16[384,384]{1,0:T(8,128)(2,1)S(1)}, u32[]{:S(2)}, u32[]{:S(2)}) %collective-permute-start.13) | collective-permute-done | bytes 294944 | tf_op jit(solution)/shard_map/ppermute | solution.py:24
  60.6 5.2 %shard_map.157 = (f32[128,768]{1,0:T(8,128)S(1)}, bf16[128,768]{1,0:T(8,128)(2,1)S(1)}, bf16[256,2688]{1,0:T(8,128)(2,1)S(1)}, bf16[256,768]{1,0:T(8,128)(2,1)S(...) custom-call(bf16[512,768]{1,0:T(8,128)(2,1)S(1)} %get-tuple-element.78.tok, ...), custom_call_target="tpu_custom_call" | custom-call | flops 8000000000 | bytes 7077888 | tf_op jit(solution)/shard_map/pallas_call | solution.py:176
  66.8 3.1 %collective-permute-done.21.dy_other = bf16[384,768]{1,0:T(8,128)(2,1)S(1)} collective-permute-done((bf16[384,768]{1,0:T(8,128)(2,1)S(1)}, bf16[384,768]{1,0:T(8,128)(2,1)S(1)}, u32[]{:S(2)}, u32[]{:S(2)}) %collective-permute-start.21) | collective-permute-done | bytes 589856 | tf_op jit(solution)/shard_map/ppermute | solution.py:24
  72.0 10.2 %collective-permute-done.24.gn_other = bf16[384,768]{1,0:T(8,128)(2,1)S(1)} collective-permute-done((bf16[384,768]{1,0:T(8,128)(2,1)S(1)}, bf16[384,768]{1,0:T(8,128)(2,1)S(1)}, u32[]{:S(2)}, u32[]{:S(2)}) %collective-permute-start.24) | collective-permute-done | bytes 589856 | tf_op jit(solution)/shard_map/ppermute | solution.py:24
  82.2 2.6 %shard_map.159 = (f32[128,768]{1,0:T(8,128)S(1)}, bf16[256,384]{1,0:T(8,128)(2,1)S(1)}, bf16[384,384]{1,0:T(8,128)(2,1)S(1)}, bf16[256,384]{1,0:T(8,128)(2,1)S(1)}) custom-call(bf16[384,768]{1,0:T(8,128)(2,1)S(1)} %get-tuple-element.107.gn_own, bf16[384,768]{1,0:T(8,128)(2,1)S(1)} %collective-permute-done.24.gn_other, ...), custom_call_target="tpu_custom_call" | custom-call | flops 5000000000 | bytes 3538944 | tf_op jit(solution)/shard_map/pallas_call | solution.py:176
  85.0 2.2 %shard_map.160.gj.own = bf16[256,1536]{1,0:T(8,128)(2,1)S(1)} custom-call(bf16[256,384]{1,0:T(8,128)(2,1)S(1)} %get-tuple-element.116.first, bf16[256,384]{1,0:T(8,128)(2,1)S(1)} %get-tuple-element.117.halves, bf16[384,384]{1,0:T(8,128)(2,1)S(1)} %get-tuple-element.113.gctx, bf16[384,384]{1,0:T(8,128)(2,1)S(1)} %get-tuple-element.109.q, ...), custom_call_target="tpu_custom_call" | custom-call | flops 6000000000 | bytes 3538944 | tf_op jit(solution)/shard_map/pallas_call | solution.py:176
  88.6 2.3 %shard_map.161 = (f32[128,768]{1,0:T(8,128)S(1)}, bf16[128,768]{1,0:T(8,128)(2,1)S(1)}) custom-call(bf16[256,1536]{1,0:T(8,128)(2,1)S(1)} %shard_map.160.gj.own, bf16[96,1280]{1,0:T(8,128)(2,1)S(1)} %copy-done.3, bf16[96,1280]{1,0:T(8,128)(2,1)S(1)} %collective-permute-done.2.rest_5_.rest_1_, bf16[96,1280]{1,0:T(8,128)(2,1)S(1)} %collective-permute-done.3.rest_6_.rest_2_, ...), custom_call_target="tpu_custom_call" | custom-call | flops 3000000000 | bytes 3538944 | tf_op jit(solution)/shard_map/pallas_call | solution.py:176
  93.0 1.7 %collective-permute-done.26 = bf16[128,768]{1,0:T(8,128)(2,1)S(1)} collective-permute-done((bf16[128,768]{1,0:T(8,128)(2,1)S(1)}, bf16[128,768]{1,0:T(8,128)(2,1)S(1)}, u32[]{:S(2)}, u32[]{:S(2)}) %collective-permute-start.26) | collective-permute-done | bytes 196640 | tf_op jit(solution)/shard_map/ppermute | solution.py:24
  94.6 1.7 %collective-permute-done.25 = bf16[1,1440,128]{2,1,0:T(8,128)(2,1)S(1)} collective-permute-done((bf16[1,1440,128]{2,1,0:T(8,128)(2,1)S(1)}, bf16[1,1440,128]{2,1,0:T(8,128)(2,1)S(1)}, u32[]{:S(2)}, u32[]{:S(2)}) %collective-permute-start.25) | collective-permute-done | bytes 368672 | tf_op jit(solution)/shard_map/ppermute | solution.py:33
  98.3 2.8 %collective-permute-start.32 = (bf16[720,128]{1,0:T(8,128)(2,1)S(1)}, bf16[720,128]{1,0:T(8,128)(2,1)S(1)}, u32[]{:S(2)}, u32[]{:S(2)}) collective-permute-start(bf16[720,128]{1,0:T(8,128)(2,1)S(1)} %get-tuple-element.143), channel_id=1, source_target_pairs={{0,2},{1,3},{2,0},{3,1},{4,6},{5,7},{6,4},{7,5},{8,10},{9,11},{10,... | collective-permute-start | bytes 552968 | tf_op jit(solution)/shard_map/ppermute | solution.py:24
  101.9 5.3 %collective-permute-done.28.other = bf16[128,768]{1,0:T(8,128)(2,1)S(1)} collective-permute-done((bf16[128,768]{1,0:T(8,128)(2,1)S(1)}, bf16[128,768]{1,0:T(8,128)(2,1)S(1)}, u32[]{:S(2)}, u32[]{:S(2)}) %collective-permute-start.28) | collective-permute-done | bytes 196640 | tf_op jit(solution)/shard_map/ppermute | solution.py:24
  109.8 2.5 %collective-permute-start.35 = (bf16[720,128]{1,0:T(8,128)(2,1)S(1)}, bf16[720,128]{1,0:T(8,128)(2,1)S(1)}, u32[]{:S(2)}, u32[]{:S(2)}) collective-permute-start(bf16[720,128]{1,0:T(8,128)(2,1)S(1)} %add_convert_fusion.5.mine_1), channel_id=1, source_target_pairs={{0,1},{1,0},{2,3},{3,2},{4,5},{5,4},{6,7},{7,6},{8,9},{9,8},{10,11... | collective-permute-start | bytes 552968 | tf_op jit(solution)/shard_map/ppermute | solution.py:24
  112.4 1.6 %collective-permute-done.32 = bf16[720,128]{1,0:T(8,128)(2,1)S(1)} collective-permute-done((bf16[720,128]{1,0:T(8,128)(2,1)S(1)}, bf16[720,128]{1,0:T(8,128)(2,1)S(1)}, u32[]{:S(2)}, u32[]{:S(2)}) %collective-permute-start.32) | collective-permute-done | bytes 184352 | tf_op jit(solution)/shard_map/ppermute | solution.py:24
  115.2 3.0 %collective-permute-start.36 = (bf16[576,128]{1,0:T(8,128)(2,1)S(1)}, bf16[576,128]{1,0:T(8,128)(2,1)S(1)}, u32[]{:S(2)}, u32[]{:S(2)}) collective-permute-start(bf16[576,128]{1,0:T(8,128)(2,1)S(1)} %get-tuple-element.144), channel_id=1, source_target_pairs={{0,2},{1,3},{2,0},{3,1},{4,6},{5,7},{6,4},{7,5},{8,10},{9,11},{10,... | collective-permute-start | bytes 442376 | tf_op jit(solution)/shard_map/ppermute | solution.py:24
  118.3 1.6 %collective-permute-done.35.other_1 = bf16[720,128]{1,0:T(8,128)(2,1)S(1)} collective-permute-done((bf16[720,128]{1,0:T(8,128)(2,1)S(1)}, bf16[720,128]{1,0:T(8,128)(2,1)S(1)}, u32[]{:S(2)}, u32[]{:S(2)}) %collective-permute-start.35) | collective-permute-done | bytes 184352 | tf_op jit(solution)/shard_map/ppermute | solution.py:24
  119.9 4.5 %collective-permute-done.34.other_0 = bf16[720,128]{1,0:T(8,128)(2,1)S(1)} collective-permute-done((bf16[720,128]{1,0:T(8,128)(2,1)S(1)}, bf16[720,128]{1,0:T(8,128)(2,1)S(1)}, u32[]{:S(2)}, u32[]{:S(2)}) %collective-permute-start.34) | collective-permute-done | bytes 184352 | tf_op jit(solution)/shard_map/ppermute | solution.py:24
  124.4 1.6 %shard_map.164 = (f32[96,2304]{1,0:T(8,128)}, f32[144,768]{1,0:T(8,128)}, f32[1,96]{1,0:T(1,128)}) custom-call(bf16[720,128]{1,0:T(8,128)(2,1)S(1)} %add_convert_fusion.7.mine_0, bf16[720,128]{1,0:T(8,128)(2,1)S(1)} %add_convert_fusion.5.mine_1, bf16[720,128]{1,0:T(8,128)(2,1)S(1)} %collective-permute-done.34.other_0, ...), custom_call_target="tpu_custom_call" | custom-call | flops 1000000 | bytes 4000000 | tf_op jit(solution)/shard_map/pallas_call | solution.py:176
  126.0 2.0 %collective-permute-done.36 = bf16[576,128]{1,0:T(8,128)(2,1)S(1)} collective-permute-done((bf16[576,128]{1,0:T(8,128)(2,1)S(1)}, bf16[576,128]{1,0:T(8,128)(2,1)S(1)}, u32[]{:S(2)}, u32[]{:S(2)}) %collective-permute-start.36) | collective-permute-done | bytes 147488 | tf_op jit(solution)/shard_map/ppermute | solution.py:24
  130.3 3.9 %collective-permute-done.38.other_1 = bf16[576,128]{1,0:T(8,128)(2,1)S(1)} collective-permute-done((bf16[576,128]{1,0:T(8,128)(2,1)S(1)}, bf16[576,128]{1,0:T(8,128)(2,1)S(1)}, u32[]{:S(2)}, u32[]{:S(2)}) %collective-permute-start.38) | collective-permute-done | bytes 147488 | tf_op jit(solution)/shard_map/ppermute | solution.py:24
  134.2 1.6 %collective-permute-done.37.other_0 = bf16[576,128]{1,0:T(8,128)(2,1)S(1)} collective-permute-done((bf16[576,128]{1,0:T(8,128)(2,1)S(1)}, bf16[576,128]{1,0:T(8,128)(2,1)S(1)}, u32[]{:S(2)}, u32[]{:S(2)}) %collective-permute-start.37) | collective-permute-done | bytes 147488 | tf_op jit(solution)/shard_map/ppermute | solution.py:24
  (107 shorter events, 30.1 us)
Async XLA Ops:
  2.5 11.3 %collective-permute-start.2 = (bf16[96,1280]{1,0:T(8,128)(2,1)}, bf16[96,1280]{1,0:T(8,128)(2,1)S(1)}, u32[]{:S(2)}, u32[]{:S(2)}) collective-permute-start(bf16[96,1280]{1,0:T(8,128)(2,1)} %shard_map.153.rest_4_.rest_0_), channel_id=1, source_target_pairs={{0,8},{4,12},{8,0},{12,4},{16,24},{20,28},{24,16},{28,20},{1,9},{5... | collective-permute-start | bytes 737288 | tf_op jit(solution)/shard_map/ppermute | solution.py:24
  5.5 8.3 %collective-permute-start.3 = (bf16[96,1280]{1,0:T(8,128)(2,1)}, bf16[96,1280]{1,0:T(8,128)(2,1)S(1)}, u32[]{:S(2)}, u32[]{:S(2)}) collective-permute-start(bf16[96,1280]{1,0:T(8,128)(2,1)} %shard_map.153.rest_4_.rest_0_), channel_id=1, source_target_pairs={{0,16},{4,20},{8,24},{12,28},{16,0},{20,4},{24,8},{28,12},{1,17},{... | collective-permute-start | bytes 737288 | tf_op jit(solution)/shard_map/ppermute | solution.py:24
  8.6 6.9 %collective-permute-start = (bf16[144,768]{1,0:T(8,128)(2,1)S(1)}, bf16[144,768]{1,0:T(8,128)(2,1)S(1)}, u32[]{:S(2)}, u32[]{:S(2)}) collective-permute-start(bf16[144,768]{1,0:T(8,128)(2,1)S(1)} %pad_maximum_fusion.1), channel_id=1, source_target_pairs={{1,2},{2,1},{3,4},{4,3},{5,6},{6,5},{7,8},{8,7},{9,10},{10,9},{11,... | collective-permute-start | bytes 663560 | tf_op jit(solution)/shard_map/ppermute | solution.py:768
  9.3 15.3 %collective-permute-start.1 = (bf16[144,768]{1,0:T(8,128)(2,1)S(1)}, bf16[144,768]{1,0:T(8,128)(2,1)S(1)}, u32[]{:S(2)}, u32[]{:S(2)}) collective-permute-start(bf16[144,768]{1,0:T(8,128)(2,1)S(1)} %pad_maximum_fusion.1), channel_id=1, source_target_pairs={{0,1},{1,0},{2,3},{3,2},{4,5},{5,4},{6,7},{7,6},{8,9},{9,8},{10,11... | collective-permute-start | bytes 663560 | tf_op jit(solution)/shard_map/ppermute | solution.py:24
  13.8 10.8 %collective-permute-start.4 = (bf16[96,640]{1,0:T(8,128)(2,1)S(1)}, bf16[96,640]{1,0:T(8,128)(2,1)S(1)}, u32[]{:S(2)}, u32[]{:S(2)}) collective-permute-start(bf16[96,640]{1,0:T(8,128)(2,1)S(1)} %slice.66), channel_id=1, source_target_pairs={{0,16},{4,20},{8,24},{12,28},{16,0},{20,4},{24,8},{28,12},{1,17},{... | collective-permute-start | bytes 368648 | tf_op jit(solution)/shard_map/ppermute | solution.py:24
  14.8 9.8 %collective-permute-start.5 = (bf16[96,640]{1,0:T(8,128)(2,1)S(1)}, bf16[96,640]{1,0:T(8,128)(2,1)S(1)}, u32[]{:S(2)}, u32[]{:S(2)}) collective-permute-start(bf16[96,640]{1,0:T(8,128)(2,1)S(1)} %slice.67), channel_id=1, source_target_pairs={{0,8},{4,12},{8,0},{12,4},{16,24},{20,28},{24,16},{28,20},{1,9},{5... | collective-permute-start | bytes 368648 | tf_op jit(solution)/shard_map/ppermute | solution.py:24
  25.7 18.8 %collective-permute-start.12 = (bf16[384,1280]{1,0:T(8,128)(2,1)}, bf16[384,1280]{1,0:T(8,128)(2,1)}, u32[]{:S(2)}, u32[]{:S(2)}) collective-permute-start(bf16[384,1280]{1,0:T(8,128)(2,1)} %maximum_maximum_fusion), channel_id=1, source_target_pairs={{0,4},{4,0},{8,12},{12,8},{16,20},{20,16},{24,28},{28,24},{1,5},{5... | collective-permute-start | bytes 2949128 | tf_op jit(solution)/shard_map/ppermute | solution.py:24
  25.8 15.6 %collective-permute-start.10 = (bf16[96,2816]{1,0:T(8,128)(2,1)S(1)}, bf16[96,2816]{1,0:T(8,128)(2,1)S(1)}, u32[]{:S(2)}, u32[]{:S(2)}) collective-permute-start(bf16[96,2816]{1,0:T(8,128)(2,1)S(1)} %shard_map.152.rest_1_), channel_id=1, source_target_pairs={{0,8},{4,12},{8,0},{12,4},{16,24},{20,28},{24,16},{28,20},{1,9},{5... | collective-permute-start | bytes 1622024 | tf_op jit(solution)/shard_map/ppermute | solution.py:24
  27.0 17.4 %collective-permute-start.11 = (bf16[96,2816]{1,0:T(8,128)(2,1)S(1)}, bf16[96,2816]{1,0:T(8,128)(2,1)S(1)}, u32[]{:S(2)}, u32[]{:S(2)}) collective-permute-start(bf16[96,2816]{1,0:T(8,128)(2,1)S(1)} %shard_map.152.rest_1_), channel_id=1, source_target_pairs={{0,16},{4,20},{8,24},{12,28},{16,0},{20,4},{24,8},{28,12},{1,17},{... | collective-permute-start | bytes 1622024 | tf_op jit(solution)/shard_map/ppermute | solution.py:24
  27.0 8.6 %collective-permute-start.6 = (bf16[144,768]{1,0:T(8,128)(2,1)S(1)}, bf16[144,768]{1,0:T(8,128)(2,1)S(1)}, u32[]{:S(2)}, u32[]{:S(2)}) collective-permute-start(bf16[144,768]{1,0:T(8,128)(2,1)S(1)} %collective-permute-done.near), channel_id=1, source_target_pairs={{0,1},{1,0},{2,3},{3,2},{4,5},{5,4},{6,7},{7,6},{8,9},{9,8},{10,11... | collective-permute-start | bytes 663560 | tf_op jit(solution)/shard_map/ppermute | solution.py:24
  29.6 14.9 %collective-permute-start.9 = (bf16[128,768]{1,0:T(8,128)(2,1)S(1)}, bf16[128,768]{1,0:T(8,128)(2,1)S(1)}, u32[]{:S(2)}, u32[]{:S(2)}) collective-permute-start(bf16[128,768]{1,0:T(8,128)(2,1)S(1)} %copy-done.4), channel_id=1, source_target_pairs={{0,1},{1,0},{2,3},{3,2},{4,5},{5,4},{6,7},{7,6},{8,9},{9,8},{10,11... | collective-permute-start | bytes 589832 | tf_op jit(solution)/shard_map/ppermute | solution.py:24
  35.6 8.9 %collective-permute-start.8 = (bf16[64,768]{1,0:T(8,128)(2,1)S(1)}, bf16[64,768]{1,0:T(8,128)(2,1)S(1)}, u32[]{:S(2)}, u32[]{:S(2)}) collective-permute-start(bf16[64,768]{1,0:T(8,128)(2,1)S(1)} %collective-permute-done.7.near), channel_id=1, source_target_pairs={{0,1},{1,0},{2,3},{3,2},{4,5},{5,4},{6,7},{7,6},{8,9},{9,8},{10,11... | collective-permute-start | bytes 294920 | tf_op jit(solution)/shard_map/ppermute | solution.py:24
  41.5 8.0 %collective-permute-start.15 = (bf16[96,1408]{1,0:T(8,128)(2,1)S(1)}, bf16[96,1408]{1,0:T(8,128)(2,1)S(1)}, u32[]{:S(2)}, u32[]{:S(2)}) collective-permute-start(bf16[96,1408]{1,0:T(8,128)(2,1)S(1)} %slice.88.rest_2_), channel_id=1, source_target_pairs={{0,16},{4,20},{8,24},{12,28},{16,0},{20,4},{24,8},{28,12},{1,17},{... | collective-permute-start | bytes 811016 | tf_op jit(solution)/shard_map/ppermute | solution.py:24
  44.4 6.5 %collective-permute-start.16 = (bf16[96,1408]{1,0:T(8,128)(2,1)S(1)}, bf16[96,1408]{1,0:T(8,128)(2,1)S(1)}, u32[]{:S(2)}, u32[]{:S(2)}) collective-permute-start(bf16[96,1408]{1,0:T(8,128)(2,1)S(1)} %slice.89.rest_3_), channel_id=1, source_target_pairs={{0,8},{4,12},{8,0},{12,4},{16,24},{20,28},{24,16},{28,20},{1,9},{5... | collective-permute-start | bytes 811016 | tf_op jit(solution)/shard_map/ppermute | solution.py:24
  51.0 9.6 %collective-permute-start.17 = (bf16[288,2816]{1,0:T(8,128)(2,1)S(1)}, bf16[288,2816]{1,0:T(8,128)(2,1)S(1)}, u32[]{:S(2)}, u32[]{:S(2)}) collective-permute-start(bf16[288,2816]{1,0:T(8,128)(2,1)S(1)} %pad_maximum_fusion), channel_id=1, source_target_pairs={{0,4},{4,0},{8,12},{12,8},{16,20},{20,16},{24,28},{28,24},{1,5},{5... | collective-permute-start | bytes 4866056 | tf_op jit(solution)/shard_map/ppermute | solution.py:24
  51.1 9.5 %collective-permute-start.14 = (bf16[256,768]{1,0:T(8,128)(2,1)S(1)}, bf16[256,768]{1,0:T(8,128)(2,1)S(1)}, u32[]{:S(2)}, u32[]{:S(2)}) collective-permute-start(bf16[256,768]{1,0:T(8,128)(2,1)S(1)} %get-tuple-element.96.normed_own), channel_id=1, source_target_pairs={{0,4},{4,0},{8,12},{12,8},{16,20},{20,16},{24,28},{28,24},{1,5},{5... | collective-permute-start | bytes 1179656 | tf_op jit(solution)/shard_map/ppermute | solution.py:24
  51.6 9.0 %collective-permute-start.13 = (bf16[384,384]{1,0:T(8,128)(2,1)S(1)}, bf16[384,384]{1,0:T(8,128)(2,1)S(1)}, u32[]{:S(2)}, u32[]{:S(2)}) collective-permute-start(bf16[384,384]{1,0:T(8,128)(2,1)S(1)} %get-tuple-element.91.ctx_own), channel_id=1, source_target_pairs={{0,1},{1,0},{2,3},{3,2},{4,5},{5,4},{6,7},{7,6},{8,9},{9,8},{10,11... | collective-permute-start | bytes 884744 | tf_op jit(solution)/shard_map/ppermute | solution.py:24
  66.5 15.7 %collective-permute-start.24 = (bf16[384,768]{1,0:T(8,128)(2,1)S(1)}, bf16[384,768]{1,0:T(8,128)(2,1)S(1)}, u32[]{:S(2)}, u32[]{:S(2)}) collective-permute-start(bf16[384,768]{1,0:T(8,128)(2,1)S(1)} %get-tuple-element.107.gn_own), channel_id=1, source_target_pairs={{0,1},{1,0},{2,3},{3,2},{4,5},{5,4},{6,7},{7,6},{8,9},{9,8},{10,11... | collective-permute-start | bytes 1769480 | tf_op jit(solution)/shard_map/ppermute | solution.py:24
  71.8 12.9 %collective-permute-start.23 = (bf16[2,1440,128]{2,1,0:T(8,128)(2,1)S(1)}, bf16[2,1440,128]{2,1,0:T(8,128)(2,1)S(1)}, u32[]{:S(2)}, u32[]{:S(2)}) collective-permute-start(bf16[2,1440,128]{2,1,0:T(8,128)(2,1)S(1)} %get-tuple-element.106), channel_id=1, source_target_pairs={{0,8},{4,20},{8,0},{12,28},{16,24},{20,4},{24,16},{28,12},{1,9},{5... | collective-permute-start | bytes 2211848 | tf_op jit(solution)/shard_map/ppermute | solution.py:33
  87.3 7.3 %collective-permute-start.26 = (bf16[128,768]{1,0:T(8,128)(2,1)S(1)}, bf16[128,768]{1,0:T(8,128)(2,1)S(1)}, u32[]{:S(2)}, u32[]{:S(2)}) collective-permute-start(bf16[128,768]{1,0:T(8,128)(2,1)S(1)} %get-tuple-element.115), channel_id=1, source_target_pairs={{0,1},{1,0},{2,3},{3,2},{4,5},{5,4},{6,7},{7,6},{8,9},{9,8},{10,11... | collective-permute-start | bytes 589832 | tf_op jit(solution)/shard_map/ppermute | solution.py:24
  87.7 8.7 %collective-permute-start.25 = (bf16[1,1440,128]{2,1,0:T(8,128)(2,1)S(1)}, bf16[1,1440,128]{2,1,0:T(8,128)(2,1)S(1)}, u32[]{:S(2)}, u32[]{:S(2)}) collective-permute-start(bf16[1,1440,128]{2,1,0:T(8,128)(2,1)S(1)} %get-tuple-element.138.sent), channel_id=1, source_target_pairs={{0,16},{4,12},{8,24},{12,4},{16,0},{20,28},{24,8},{28,20},{1,17},{... | collective-permute-start | bytes 1105928 | tf_op jit(solution)/shard_map/ppermute | solution.py:33
  92.1 16.1 %collective-permute-start.29 = (bf16[2,1152,128]{2,1,0:T(8,128)(2,1)S(1)}, bf16[2,1152,128]{2,1,0:T(8,128)(2,1)S(1)}, u32[]{:S(2)}, u32[]{:S(2)}) collective-permute-start(bf16[2,1152,128]{2,1,0:T(8,128)(2,1)S(1)} %get-tuple-element.124), channel_id=1, source_target_pairs={{0,8},{4,20},{8,0},{12,28},{16,24},{20,4},{24,16},{28,12},{1,9},{5... | collective-permute-start | bytes 1769480 | tf_op jit(solution)/shard_map/ppermute | solution.py:33
  96.4 13.3 %collective-permute-start.33 = (bf16[720,128]{1,0:T(8,128)(2,1)S(1)}, bf16[720,128]{1,0:T(8,128)(2,1)S(1)}, u32[]{:S(2)}, u32[]{:S(2)}) collective-permute-start(bf16[720,128]{1,0:T(8,128)(2,1)S(1)} %get-tuple-element.142), channel_id=1, source_target_pairs={{0,2},{1,3},{2,0},{3,1},{4,6},{5,7},{6,4},{7,5},{8,10},{9,11},{10,... | collective-permute-start | bytes 552968 | tf_op jit(solution)/shard_map/ppermute | solution.py:24
  97.9 9.3 %collective-permute-start.28 = (bf16[128,768]{1,0:T(8,128)(2,1)S(1)}, bf16[128,768]{1,0:T(8,128)(2,1)S(1)}, u32[]{:S(2)}, u32[]{:S(2)}) collective-permute-start(bf16[128,768]{1,0:T(8,128)(2,1)S(1)} %get-tuple-element.122), channel_id=1, source_target_pairs={{0,1},{1,0},{2,3},{3,2},{4,5},{5,4},{6,7},{7,6},{8,9},{9,8},{10,11... | collective-permute-start | bytes 589832 | tf_op jit(solution)/shard_map/ppermute | solution.py:24
  98.3 15.6 %collective-permute-start.32 = (bf16[720,128]{1,0:T(8,128)(2,1)S(1)}, bf16[720,128]{1,0:T(8,128)(2,1)S(1)}, u32[]{:S(2)}, u32[]{:S(2)}) collective-permute-start(bf16[720,128]{1,0:T(8,128)(2,1)S(1)} %get-tuple-element.143), channel_id=1, source_target_pairs={{0,2},{1,3},{2,0},{3,1},{4,6},{5,7},{6,4},{7,5},{8,10},{9,11},{10,... | collective-permute-start | bytes 552968 | tf_op jit(solution)/shard_map/ppermute | solution.py:24
  108.3 6.8 %collective-permute-start.30 = (bf16[1,1152,128]{2,1,0:T(8,128)(2,1)S(1)}, bf16[1,1152,128]{2,1,0:T(8,128)(2,1)S(1)}, u32[]{:S(2)}, u32[]{:S(2)}) collective-permute-start(bf16[1,1152,128]{2,1,0:T(8,128)(2,1)S(1)} %get-tuple-element.141), channel_id=1, source_target_pairs={{0,16},{4,12},{8,24},{12,4},{16,0},{20,28},{24,8},{28,20},{1,17},{... | collective-permute-start | bytes 884744 | tf_op jit(solution)/shard_map/ppermute | solution.py:33
  109.8 10.1 %collective-permute-start.35 = (bf16[720,128]{1,0:T(8,128)(2,1)S(1)}, bf16[720,128]{1,0:T(8,128)(2,1)S(1)}, u32[]{:S(2)}, u32[]{:S(2)}) collective-permute-start(bf16[720,128]{1,0:T(8,128)(2,1)S(1)} %add_convert_fusion.5.mine_1), channel_id=1, source_target_pairs={{0,1},{1,0},{2,3},{3,2},{4,5},{5,4},{6,7},{7,6},{8,9},{9,8},{10,11... | collective-permute-start | bytes 552968 | tf_op jit(solution)/shard_map/ppermute | solution.py:24
  114.0 10.4 %collective-permute-start.34 = (bf16[720,128]{1,0:T(8,128)(2,1)S(1)}, bf16[720,128]{1,0:T(8,128)(2,1)S(1)}, u32[]{:S(2)}, u32[]{:S(2)}) collective-permute-start(bf16[720,128]{1,0:T(8,128)(2,1)S(1)} %add_convert_fusion.7.mine_0), channel_id=1, source_target_pairs={{0,1},{1,0},{2,3},{3,2},{4,5},{5,4},{6,7},{7,6},{8,9},{9,8},{10,11... | collective-permute-start | bytes 552968 | tf_op jit(solution)/shard_map/ppermute | solution.py:24
  115.2 12.8 %collective-permute-start.36 = (bf16[576,128]{1,0:T(8,128)(2,1)S(1)}, bf16[576,128]{1,0:T(8,128)(2,1)S(1)}, u32[]{:S(2)}, u32[]{:S(2)}) collective-permute-start(bf16[576,128]{1,0:T(8,128)(2,1)S(1)} %get-tuple-element.144), channel_id=1, source_target_pairs={{0,2},{1,3},{2,0},{3,1},{4,6},{5,7},{6,4},{7,5},{8,10},{9,11},{10,... | collective-permute-start | bytes 442376 | tf_op jit(solution)/shard_map/ppermute | solution.py:24
  118.2 11.4 %collective-permute-start.31 = (bf16[576,128]{1,0:T(8,128)(2,1)S(1)}, bf16[576,128]{1,0:T(8,128)(2,1)S(1)}, u32[]{:S(2)}, u32[]{:S(2)}) collective-permute-start(bf16[576,128]{1,0:T(8,128)(2,1)S(1)} %get-tuple-element.145), channel_id=1, source_target_pairs={{0,2},{1,3},{2,0},{3,1},{4,6},{5,7},{6,4},{7,5},{8,10},{9,11},{10,... | collective-permute-start | bytes 442376 | tf_op jit(solution)/shard_map/ppermute | solution.py:24
  128.1 6.1 %collective-permute-start.38 = (bf16[576,128]{1,0:T(8,128)(2,1)S(1)}, bf16[576,128]{1,0:T(8,128)(2,1)S(1)}, u32[]{:S(2)}, u32[]{:S(2)}) collective-permute-start(bf16[576,128]{1,0:T(8,128)(2,1)S(1)} %add_convert_fusion.9.mine_1), channel_id=1, source_target_pairs={{0,1},{1,0},{2,3},{3,2},{4,5},{5,4},{6,7},{7,6},{8,9},{9,8},{10,11... | collective-permute-start | bytes 442376 | tf_op jit(solution)/shard_map/ppermute | solution.py:24
  129.7 6.1 %collective-permute-start.37 = (bf16[576,128]{1,0:T(8,128)(2,1)S(1)}, bf16[576,128]{1,0:T(8,128)(2,1)S(1)}, u32[]{:S(2)}, u32[]{:S(2)}) collective-permute-start(bf16[576,128]{1,0:T(8,128)(2,1)S(1)} %add_convert_fusion.11.mine_0), channel_id=1, source_target_pairs={{0,1},{1,0},{2,3},{3,2},{4,5},{5,4},{6,7},{7,6},{8,9},{9,8},{10,11... | collective-permute-start | bytes 442376 | tf_op jit(solution)/shard_map/ppermute | solution.py:24
  (21 other events, 228.7 us)

commit v8 on v7

--- a/solution.py
+++ b/solution.py
@@ -522,7 +522,7 @@
 
     def body(gn_own, gn_other, hidden, dy, gains, q, k, v, p, cosine, sine, *rest):
         mlp_refs, rest = rest[1 : n_mlp + 1], rest[n_mlp + 1 :]
-        ghid_out, halves_out, gctx, first_out, attn, held, attn_sems = rest
+        ghid_out, gj_out, attn, gctx, held, attn_sems = rest
         copies = place(shard_at(), mlp_pieces, mlp_refs, attn_layout(rows, width, attn), attn_sems)
         at = side_at()
         hat, inverse = standardize(hidden[...])
@@ -531,28 +531,14 @@
         held[...] = grad_hidden[pair]
         ghid_out[...] = held[pl.ds(pl.multiple_of(at * BLOCK, BLOCK), BLOCK), :]
         halves = jnp.where(at == 0, grad_hidden[pair, 0:half], grad_hidden[pair, half:])
-        halves_out[...] = halves.astype(BF)
+        gj_out[:, 3 * half :] = halves.astype(BF)
         grad_low = grad_hidden.astype(BF)
         for copy in copies:
             copy.wait()
         own_rows = pl.ds(pl.multiple_of(at * half, 128), half)
         gctx[...] = dot_cols(grad_low, attn[own_rows, :]).astype(BF)
         cos, sin = cosine[BLOCK : 3 * BLOCK, :], sine[BLOCK : 3 * BLOCK, :]
-        for part, grad in enumerate(pair_back(0, gctx, q, k, v, p, cos, sin)):
-            first_out[:, part * 128 : (part + 1) * 128] = grad
-
-    return body
-
-
-def back_kernel(width):
-    half = width // 2
-
-    def body(first, halves, gctx, q, k, v, p, cosine, sine, sent, gj_out):
-        gj_out[:, 3 * half :] = halves[...]
-        cos, sin = cosine[BLOCK : 3 * BLOCK, :], sine[BLOCK : 3 * BLOCK, :]
-        for part in range(3):
-            gj_out[:, part * half : part * half + 128] = first[:, part * 128 : (part + 1) * 128]
-        for i in range(1, half // 128):
+        for i in range(half // 128):
             for part, grad in enumerate(pair_back(i, gctx, q, k, v, p, cos, sin)):
                 col = part * half + i * 128
                 gj_out[:, col : col + 128] = grad
@@ -900,35 +886,25 @@
         weight_bytes,
     )
 
-    ghid, halves, gctx, gj_first = call(
+    ghid, gj = call(
         hidden_back_kernel(names, len(arrays), rows, width),
         (
             shaped((BLOCK, width), F32),
-            shaped((2 * BLOCK, half), BF),
-            shaped((3 * BLOCK, half), BF),
-            shaped((2 * BLOCK, 3 * 128), BF),
+            shaped((2 * BLOCK, 4 * half), BF),
         ),
         (gn, gn_other, hidden, dy, gains, q, k, v, p, cosine, sine),
         [sums[1]] + arrays,
         [
             pltpu.VMEM((width, width), BF),
+            pltpu.VMEM((3 * BLOCK, half), BF),
             pltpu.VMEM((2 * BLOCK, width), F32),
             pltpu.SemaphoreType.DMA((len(names),)),
         ],
         5_000_000_000,
         weight_bytes,
     )
-    mlp_sums = scatter_sums(sums, chip_bits, gctx)
+    mlp_sums = scatter_sums(sums, chip_bits, gj)
     mix_other = xor_send(mix_send, "replica", 1)
-    gj = call(
-        back_kernel(width),
-        shaped((2 * BLOCK, 4 * half), BF),
-        (gj_first, halves, gctx, q, k, v, p, cosine, sine),
-        [mlp_sums[2]],
-        [],
-        6_000_000_000,
-        weight_bytes,
-    )
     gj_other = xor_send(gj, "shard", 1)
     norm_keep, norm_send = call(
         norm_back_kernel(qkv_names, len(qkv_arrays), rows, width),

time: 137 us -> 147 us (1.073)
  waiting for transfers between devices: 62 us -> 73 us
  starting transfers between devices: 42.5 us -> 40.7 us
    ppermute x33, waiting for transfers between devices: 59.2 us -> 72.9 us  [xor_send(): return lax.ppermute(array, axis, [(i, i ^ bit) for i in range(count)])]
    ppermute x4, waiting for transfers between devices: 2.79 us -> 0.01 us  [core_send(): lax.ppermute(array, 'shard', [(i, i ^ bits[i & 1]) for i in range(count)])]
    ppermute x33, starting transfers between devices: 37.7 us -> 35.9 us  [xor_send(): return lax.ppermute(array, axis, [(i, i ^ bit) for i in range(count)])]
    pallas_call x14 -> x13, Pallas kernels: 26.3 us -> 26.4 us  [call(): pl.pallas_call(kernel, out_shape=out_shape, in_specs=specs, out_specs=jax...]
  transfers between devices with their start and end apart: 39 -> 39, of which waited for: 21 -> 20; matrix products, arithmetic and copies ran while one was open for 2% -> 2% of each run, Pallas kernels for 11% -> 12%
where the time goes in v8:
time: 147 us; the launch traced here: 146 us
  waiting for transfers between devices  73 us (50%)
  starting transfers between devices  40.7 us (28%)
  Pallas kernels  26.4 us (18%)
  other arithmetic  4.26 us (3%)
    ppermute x33, waiting for transfers between devices, xor_send(): return lax.ppermute(array, axis, [(i, i ^ bit) for i in range(count)])  72.9 us
    ppermute x33, starting transfers between devices, xor_send(): return lax.ppermute(array, axis, [(i, i ^ bit) for i in range(count)])  35.9 us
    pallas_call x13, Pallas kernels, call(): pl.pallas_call(kernel, out_shape=out_shape, in_specs=specs, out_specs=jax...  26.4 us
    ppermute x4, starting transfers between devices, core_send(): lax.ppermute(array, 'shard', [(i, i ^ bits[i & 1]) for i in range(count)])  3.45 us
  transfers between devices with their start and end apart: 39, of which 20 were waited for; matrix products, arithmetic and copies ran while one was open for 2% of the time, Pallas kernels for 12%

profile of v8, /device:TPU:0, one launch (start us, length us, event | category | flops | bytes accessed | tf_op | source)
XLA Modules:
  0.0 146.3 jit_solution(14866526136935227229)
XLA Ops:
  0.7 1.8 %shard_map.153.rest_4_.rest_0_ = bf16[96,1280]{1,0:T(8,128)(2,1)} custom-call(bf16[96,2304]{1,0:T(8,128)(2,1)} %weight.5, bf16[1,96]{1,0:T(2,128)(2,1)} %bitcast.17, bf16[1,96]{1,0:T(2,128)(2,1)} %bitcast.19), custom_call_target="tpu_custom_call" | custom-call | flops 1000000 | bytes 1000000 | tf_op jit(solution)/shard_map/pallas_call | solution.py:176
  2.5 3.0 %collective-permute-start.2 = (bf16[96,1280]{1,0:T(8,128)(2,1)}, bf16[96,1280]{1,0:T(8,128)(2,1)S(1)}, u32[]{:S(2)}, u32[]{:S(2)}) collective-permute-start(bf16[96,1280]{1,0:T(8,128)(2,1)} %shard_map.153.rest_4_.rest_0_), channel_id=1, source_target_pairs={{0,8},{4,12},{8,0},{12,4},{16,24},{20,28},{24,16},{28,20},{1,9},{5... | collective-permute-start | bytes 737288 | tf_op jit(solution)/shard_map/ppermute | solution.py:24
  5.5 1.5 %collective-permute-start.3 = (bf16[96,1280]{1,0:T(8,128)(2,1)}, bf16[96,1280]{1,0:T(8,128)(2,1)S(1)}, u32[]{:S(2)}, u32[]{:S(2)}) collective-permute-start(bf16[96,1280]{1,0:T(8,128)(2,1)} %shard_map.153.rest_4_.rest_0_), channel_id=1, source_target_pairs={{0,16},{4,20},{8,24},{12,28},{16,0},{20,4},{24,8},{28,12},{1,17},{... | collective-permute-start | bytes 737288 | tf_op jit(solution)/shard_map/ppermute | solution.py:24
  9.3 4.5 %collective-permute-start.1 = (bf16[144,768]{1,0:T(8,128)(2,1)S(1)}, bf16[144,768]{1,0:T(8,128)(2,1)S(1)}, u32[]{:S(2)}, u32[]{:S(2)}) collective-permute-start(bf16[144,768]{1,0:T(8,128)(2,1)S(1)} %pad_maximum_fusion.1), channel_id=1, source_target_pairs={{0,1},{1,0},{2,3},{3,2},{4,5},{5,4},{6,7},{7,6},{8,9},{9,8},{10,11... | collective-permute-start | bytes 663560 | tf_op jit(solution)/shard_map/ppermute | solution.py:24
  15.6 9.0 %collective-permute-done.1.partner = bf16[144,768]{1,0:T(8,128)(2,1)S(1)} collective-permute-done((bf16[144,768]{1,0:T(8,128)(2,1)S(1)}, bf16[144,768]{1,0:T(8,128)(2,1)S(1)}, u32[]{:S(2)}, u32[]{:S(2)}) %collective-permute-start.1) | collective-permute-done | bytes 221216 | tf_op jit(solution)/shard_map/ppermute | solution.py:24
  27.0 1.9 %collective-permute-start.6 = (bf16[144,768]{1,0:T(8,128)(2,1)S(1)}, bf16[144,768]{1,0:T(8,128)(2,1)S(1)}, u32[]{:S(2)}, u32[]{:S(2)}) collective-permute-start(bf16[144,768]{1,0:T(8,128)(2,1)S(1)} %collective-permute-done.near), channel_id=1, source_target_pairs={{0,1},{1,0},{2,3},{3,2},{4,5},{5,4},{6,7},{7,6},{8,9},{9,8},{10,11... | collective-permute-start | bytes 663560 | tf_op jit(solution)/shard_map/ppermute | solution.py:24
  29.6 6.0 %collective-permute-start.9 = (bf16[128,768]{1,0:T(8,128)(2,1)S(1)}, bf16[128,768]{1,0:T(8,128)(2,1)S(1)}, u32[]{:S(2)}, u32[]{:S(2)}) collective-permute-start(bf16[128,768]{1,0:T(8,128)(2,1)S(1)} %copy-done.4), channel_id=1, source_target_pairs={{0,1},{1,0},{2,3},{3,2},{4,5},{5,4},{6,7},{7,6},{8,9},{9,8},{10,11... | collective-permute-start | bytes 589832 | tf_op jit(solution)/shard_map/ppermute | solution.py:24
  35.6 1.6 %collective-permute-start.8 = (bf16[64,768]{1,0:T(8,128)(2,1)S(1)}, bf16[64,768]{1,0:T(8,128)(2,1)S(1)}, u32[]{:S(2)}, u32[]{:S(2)}) collective-permute-start(bf16[64,768]{1,0:T(8,128)(2,1)S(1)} %collective-permute-done.7.near), channel_id=1, source_target_pairs={{0,1},{1,0},{2,3},{3,2},{4,5},{5,4},{6,7},{7,6},{8,9},{9,8},{10,11... | collective-permute-start | bytes 294920 | tf_op jit(solution)/shard_map/ppermute | solution.py:24
  39.2 2.2 %collective-permute-done.10.rest_2_ = bf16[96,2816]{1,0:T(8,128)(2,1)S(1)} collective-permute-done((bf16[96,2816]{1,0:T(8,128)(2,1)S(1)}, bf16[96,2816]{1,0:T(8,128)(2,1)S(1)}, u32[]{:S(2)}, u32[]{:S(2)}) %collective-permute-start.10) | collective-permute-done | bytes 540704 | tf_op jit(solution)/shard_map/ppermute | solution.py:24
  41.5 2.9 %collective-permute-start.15 = (bf16[96,1408]{1,0:T(8,128)(2,1)S(1)}, bf16[96,1408]{1,0:T(8,128)(2,1)S(1)}, u32[]{:S(2)}, u32[]{:S(2)}) collective-permute-start(bf16[96,1408]{1,0:T(8,128)(2,1)S(1)} %slice.88.rest_2_), channel_id=1, source_target_pairs={{0,16},{4,20},{8,24},{12,28},{16,0},{20,4},{24,8},{28,12},{1,17},{... | collective-permute-start | bytes 811016 | tf_op jit(solution)/shard_map/ppermute | solution.py:24
  44.5 4.3 %shard_map.155 = (bf16[384,384]{1,0:T(8,128)(2,1)S(1)}, bf16[512,384]{1,0:T(8,128)(2,1)S(1)}, bf16[512,384]{1,0:T(8,128)(2,1)S(1)}, bf16[18,128,256]{2,1,0:T(8,1...) custom-call(bf16[512,768]{1,0:T(8,128)(2,1)S(1)} %get-tuple-element.76.tok, ...), custom_call_target="tpu_custom_call" | custom-call | flops 7000000000 | bytes 3538944 | tf_op jit(solution)/shard_map/pallas_call | solution.py:176
  52.2 3.3 %collective-permute-done.18.rest_7_ = bf16[96,1408]{1,0:T(8,128)(2,1)S(1)} collective-permute-done((bf16[96,1408]{1,0:T(8,128)(2,1)S(1)}, bf16[96,1408]{1,0:T(8,128)(2,1)S(1)}, u32[]{:S(2)}, u32[]{:S(2)}) %collective-permute-start.18) | collective-permute-done | bytes 270368 | tf_op jit(solution)/shard_map/ppermute | solution.py:24
  55.9 4.7 %collective-permute-done.13.ctx_other = bf16[384,384]{1,0:T(8,128)(2,1)S(1)} collective-permute-done((bf16[384,384]{1,0:T(8,128)(2,1)S(1)}, bf16[384,384]{1,0:T(8,128)(2,1)S(1)}, u32[]{:S(2)}, u32[]{:S(2)}) %collective-permute-start.13) | collective-permute-done | bytes 294944 | tf_op jit(solution)/shard_map/ppermute | solution.py:24
  60.6 5.2 %shard_map.157 = (f32[128,768]{1,0:T(8,128)S(1)}, bf16[128,768]{1,0:T(8,128)(2,1)S(1)}, bf16[256,2688]{1,0:T(8,128)(2,1)S(1)}, bf16[256,768]{1,0:T(8,128)(2,1)S(...) custom-call(bf16[512,768]{1,0:T(8,128)(2,1)S(1)} %get-tuple-element.76.tok, ...), custom_call_target="tpu_custom_call" | custom-call | flops 8000000000 | bytes 7077888 | tf_op jit(solution)/shard_map/pallas_call | solution.py:176
  66.8 3.1 %collective-permute-done.21.dy_other = bf16[384,768]{1,0:T(8,128)(2,1)S(1)} collective-permute-done((bf16[384,768]{1,0:T(8,128)(2,1)S(1)}, bf16[384,768]{1,0:T(8,128)(2,1)S(1)}, u32[]{:S(2)}, u32[]{:S(2)}) %collective-permute-start.21) | collective-permute-done | bytes 589856 | tf_op jit(solution)/shard_map/ppermute | solution.py:24
  72.0 10.2 %collective-permute-done.24.gn_other = bf16[384,768]{1,0:T(8,128)(2,1)S(1)} collective-permute-done((bf16[384,768]{1,0:T(8,128)(2,1)S(1)}, bf16[384,768]{1,0:T(8,128)(2,1)S(1)}, u32[]{:S(2)}, u32[]{:S(2)}) %collective-permute-start.24) | collective-permute-done | bytes 589856 | tf_op jit(solution)/shard_map/ppermute | solution.py:24
  82.2 4.8 %shard_map.159 = (f32[128,768]{1,0:T(8,128)S(1)}, bf16[256,1536]{1,0:T(8,128)(2,1)S(1)}) custom-call(bf16[384,768]{1,0:T(8,128)(2,1)S(1)} %get-tuple-element.105.gn_own, bf16[384,768]{1,0:T(8,128)(2,1)S(1)} %collective-permute-done.24.gn_other, f32[384,768]{1,0:T(8,128)S(1)} %get-tuple-element.106.hidden, bf16[384,768]{1,0:T(8,128)(2,1)S(1)} %shard_map.156.dy.dy_own, ...), custom_call_target="tpu_custom_call" | custom-call | flops 5000000000 | bytes 3538944 | tf_op jit(solution)/shard_map/pallas_call | solution.py:176
  87.1 2.3 %shard_map.160 = (f32[128,768]{1,0:T(8,128)S(1)}, bf16[128,768]{1,0:T(8,128)(2,1)S(1)}) custom-call(bf16[256,1536]{1,0:T(8,128)(2,1)S(1)} %get-tuple-element.111.gj.own, bf16[96,1280]{1,0:T(8,128)(2,1)S(1)} %copy-done.3, bf16[96,1280]{1,0:T(8,128)(2,1)S(1)} %collective-permute-done.2.rest_5_.rest_1_, ...), custom_call_target="tpu_custom_call" | custom-call | flops 3000000000 | bytes 3538944 | tf_op jit(solution)/shard_map/pallas_call | solution.py:176
  92.2 1.7 %collective-permute-start.26 = (bf16[128,768]{1,0:T(8,128)(2,1)S(1)}, bf16[128,768]{1,0:T(8,128)(2,1)S(1)}, u32[]{:S(2)}, u32[]{:S(2)}) collective-permute-start(bf16[128,768]{1,0:T(8,128)(2,1)S(1)} %get-tuple-element.113), channel_id=1, source_target_pairs={{0,1},{1,0},{2,3},{3,2},{4,5},{5,4},{6,7},{7,6},{8,9},{9,8},{10,11... | collective-permute-start | bytes 589832 | tf_op jit(solution)/shard_map/ppermute | solution.py:24
  94.6 5.1 %collective-permute-done.28.other = bf16[128,768]{1,0:T(8,128)(2,1)S(1)} collective-permute-done((bf16[128,768]{1,0:T(8,128)(2,1)S(1)}, bf16[128,768]{1,0:T(8,128)(2,1)S(1)}, u32[]{:S(2)}, u32[]{:S(2)}) %collective-permute-start.28) | collective-permute-done | bytes 196640 | tf_op jit(solution)/shard_map/ppermute | solution.py:24
  100.8 1.6 %collective-permute-done.26 = bf16[128,768]{1,0:T(8,128)(2,1)S(1)} collective-permute-done((bf16[128,768]{1,0:T(8,128)(2,1)S(1)}, bf16[128,768]{1,0:T(8,128)(2,1)S(1)}, u32[]{:S(2)}, u32[]{:S(2)}) %collective-permute-start.26) | collective-permute-done | bytes 196640 | tf_op jit(solution)/shard_map/ppermute | solution.py:24
  102.5 2.4 %collective-permute-start.33 = (bf16[720,128]{1,0:T(8,128)(2,1)S(1)}, bf16[720,128]{1,0:T(8,128)(2,1)S(1)}, u32[]{:S(2)}, u32[]{:S(2)}) collective-permute-start(bf16[720,128]{1,0:T(8,128)(2,1)S(1)} %get-tuple-element.138), channel_id=1, source_target_pairs={{0,2},{1,3},{2,0},{3,1},{4,6},{5,7},{6,4},{7,5},{8,10},{9,11},{10,... | collective-permute-start | bytes 552968 | tf_op jit(solution)/shard_map/ppermute | solution.py:24
  106.4 1.5 %collective-permute-start.30 = (bf16[1,1152,128]{2,1,0:T(8,128)(2,1)S(1)}, bf16[1,1152,128]{2,1,0:T(8,128)(2,1)S(1)}, u32[]{:S(2)}, u32[]{:S(2)}) collective-permute-start(bf16[1,1152,128]{2,1,0:T(8,128)(2,1)S(1)} %get-tuple-element.137), channel_id=1, source_target_pairs={{0,16},{4,12},{8,24},{12,4},{16,0},{20,28},{24,8},{28,20},{1,17},{... | collective-permute-start | bytes 884744 | tf_op jit(solution)/shard_map/ppermute | solution.py:33
  107.9 10.6 %collective-permute-done.33 = bf16[720,128]{1,0:T(8,128)(2,1)S(1)} collective-permute-done((bf16[720,128]{1,0:T(8,128)(2,1)S(1)}, bf16[720,128]{1,0:T(8,128)(2,1)S(1)}, u32[]{:S(2)}, u32[]{:S(2)}) %collective-permute-start.33) | collective-permute-done | bytes 184352 | tf_op jit(solution)/shard_map/ppermute | solution.py:24
  118.6 2.6 %collective-permute-done.32 = bf16[720,128]{1,0:T(8,128)(2,1)S(1)} collective-permute-done((bf16[720,128]{1,0:T(8,128)(2,1)S(1)}, bf16[720,128]{1,0:T(8,128)(2,1)S(1)}, u32[]{:S(2)}, u32[]{:S(2)}) %collective-permute-start.32) | collective-permute-done | bytes 184352 | tf_op jit(solution)/shard_map/ppermute | solution.py:24
  122.0 3.5 %collective-permute-start.36 = (bf16[576,128]{1,0:T(8,128)(2,1)S(1)}, bf16[576,128]{1,0:T(8,128)(2,1)S(1)}, u32[]{:S(2)}, u32[]{:S(2)}) collective-permute-start(bf16[576,128]{1,0:T(8,128)(2,1)S(1)} %get-tuple-element.140), channel_id=1, source_target_pairs={{0,2},{1,3},{2,0},{3,1},{4,6},{5,7},{6,4},{7,5},{8,10},{9,11},{10,... | collective-permute-start | bytes 442376 | tf_op jit(solution)/shard_map/ppermute | solution.py:24
  126.1 6.4 %collective-permute-done.34.other_0 = bf16[720,128]{1,0:T(8,128)(2,1)S(1)} collective-permute-done((bf16[720,128]{1,0:T(8,128)(2,1)S(1)}, bf16[720,128]{1,0:T(8,128)(2,1)S(1)}, u32[]{:S(2)}, u32[]{:S(2)}) %collective-permute-start.34) | collective-permute-done | bytes 184352 | tf_op jit(solution)/shard_map/ppermute | solution.py:24
  132.5 1.6 %shard_map.163 = (f32[96,2304]{1,0:T(8,128)}, f32[144,768]{1,0:T(8,128)}, f32[1,96]{1,0:T(1,128)}) custom-call(bf16[720,128]{1,0:T(8,128)(2,1)S(1)} %add_convert_fusion.7.mine_0, bf16[720,128]{1,0:T(8,128)(2,1)S(1)} %add_convert_fusion.5.mine_1, bf16[720,128]{1,0:T(8,128)(2,1)S(1)} %collective-permute-done.34.other_0, ...), custom_call_target="tpu_custom_call" | custom-call | flops 1000000 | bytes 4000000 | tf_op jit(solution)/shard_map/pallas_call | solution.py:176
  134.2 2.3 %collective-permute-done.36 = bf16[576,128]{1,0:T(8,128)(2,1)S(1)} collective-permute-done((bf16[576,128]{1,0:T(8,128)(2,1)S(1)}, bf16[576,128]{1,0:T(8,128)(2,1)S(1)}, u32[]{:S(2)}, u32[]{:S(2)}) %collective-permute-start.36) | collective-permute-done | bytes 147488 | tf_op jit(solution)/shard_map/ppermute | solution.py:24
  136.6 2.2 %collective-permute-done.31 = bf16[576,128]{1,0:T(8,128)(2,1)S(1)} collective-permute-done((bf16[576,128]{1,0:T(8,128)(2,1)S(1)}, bf16[576,128]{1,0:T(8,128)(2,1)S(1)}, u32[]{:S(2)}, u32[]{:S(2)}) %collective-permute-start.31) | collective-permute-done | bytes 147488 | tf_op jit(solution)/shard_map/ppermute | solution.py:24
  139.0 3.9 %collective-permute-done.38.other_1 = bf16[576,128]{1,0:T(8,128)(2,1)S(1)} collective-permute-done((bf16[576,128]{1,0:T(8,128)(2,1)S(1)}, bf16[576,128]{1,0:T(8,128)(2,1)S(1)}, u32[]{:S(2)}, u32[]{:S(2)}) %collective-permute-start.38) | collective-permute-done | bytes 147488 | tf_op jit(solution)/shard_map/ppermute | solution.py:24
  142.9 2.1 %collective-permute-done.37.other_0 = bf16[576,128]{1,0:T(8,128)(2,1)S(1)} collective-permute-done((bf16[576,128]{1,0:T(8,128)(2,1)S(1)}, bf16[576,128]{1,0:T(8,128)(2,1)S(1)}, u32[]{:S(2)}, u32[]{:S(2)}) %collective-permute-start.37) | collective-permute-done | bytes 147488 | tf_op jit(solution)/shard_map/ppermute | solution.py:24
  (106 shorter events, 25.5 us)
Async XLA Ops:
  2.5 11.3 %collective-permute-start.2 = (bf16[96,1280]{1,0:T(8,128)(2,1)}, bf16[96,1280]{1,0:T(8,128)(2,1)S(1)}, u32[]{:S(2)}, u32[]{:S(2)}) collective-permute-start(bf16[96,1280]{1,0:T(8,128)(2,1)} %shard_map.153.rest_4_.rest_0_), channel_id=1, source_target_pairs={{0,8},{4,12},{8,0},{12,4},{16,24},{20,28},{24,16},{28,20},{1,9},{5... | collective-permute-start | bytes 737288 | tf_op jit(solution)/shard_map/ppermute | solution.py:24
  5.5 8.3 %collective-permute-start.3 = (bf16[96,1280]{1,0:T(8,128)(2,1)}, bf16[96,1280]{1,0:T(8,128)(2,1)S(1)}, u32[]{:S(2)}, u32[]{:S(2)}) collective-permute-start(bf16[96,1280]{1,0:T(8,128)(2,1)} %shard_map.153.rest_4_.rest_0_), channel_id=1, source_target_pairs={{0,16},{4,20},{8,24},{12,28},{16,0},{20,4},{24,8},{28,12},{1,17},{... | collective-permute-start | bytes 737288 | tf_op jit(solution)/shard_map/ppermute | solution.py:24
  8.6 6.9 %collective-permute-start = (bf16[144,768]{1,0:T(8,128)(2,1)S(1)}, bf16[144,768]{1,0:T(8,128)(2,1)S(1)}, u32[]{:S(2)}, u32[]{:S(2)}) collective-permute-start(bf16[144,768]{1,0:T(8,128)(2,1)S(1)} %pad_maximum_fusion.1), channel_id=1, source_target_pairs={{1,2},{2,1},{3,4},{4,3},{5,6},{6,5},{7,8},{8,7},{9,10},{10,9},{11,... | collective-permute-start | bytes 663560 | tf_op jit(solution)/shard_map/ppermute | solution.py:754
  9.3 15.3 %collective-permute-start.1 = (bf16[144,768]{1,0:T(8,128)(2,1)S(1)}, bf16[144,768]{1,0:T(8,128)(2,1)S(1)}, u32[]{:S(2)}, u32[]{:S(2)}) collective-permute-start(bf16[144,768]{1,0:T(8,128)(2,1)S(1)} %pad_maximum_fusion.1), channel_id=1, source_target_pairs={{0,1},{1,0},{2,3},{3,2},{4,5},{5,4},{6,7},{7,6},{8,9},{9,8},{10,11... | collective-permute-start | bytes 663560 | tf_op jit(solution)/shard_map/ppermute | solution.py:24
  13.8 10.8 %collective-permute-start.4 = (bf16[96,640]{1,0:T(8,128)(2,1)S(1)}, bf16[96,640]{1,0:T(8,128)(2,1)S(1)}, u32[]{:S(2)}, u32[]{:S(2)}) collective-permute-start(bf16[96,640]{1,0:T(8,128)(2,1)S(1)} %slice.66), channel_id=1, source_target_pairs={{0,16},{4,20},{8,24},{12,28},{16,0},{20,4},{24,8},{28,12},{1,17},{... | collective-permute-start | bytes 368648 | tf_op jit(solution)/shard_map/ppermute | solution.py:24
  14.8 9.8 %collective-permute-start.5 = (bf16[96,640]{1,0:T(8,128)(2,1)S(1)}, bf16[96,640]{1,0:T(8,128)(2,1)S(1)}, u32[]{:S(2)}, u32[]{:S(2)}) collective-permute-start(bf16[96,640]{1,0:T(8,128)(2,1)S(1)} %slice.67), channel_id=1, source_target_pairs={{0,8},{4,12},{8,0},{12,4},{16,24},{20,28},{24,16},{28,20},{1,9},{5... | collective-permute-start | bytes 368648 | tf_op jit(solution)/shard_map/ppermute | solution.py:24
  25.7 18.8 %collective-permute-start.12 = (bf16[384,1280]{1,0:T(8,128)(2,1)}, bf16[384,1280]{1,0:T(8,128)(2,1)}, u32[]{:S(2)}, u32[]{:S(2)}) collective-permute-start(bf16[384,1280]{1,0:T(8,128)(2,1)} %maximum_maximum_fusion), channel_id=1, source_target_pairs={{0,4},{4,0},{8,12},{12,8},{16,20},{20,16},{24,28},{28,24},{1,5},{5... | collective-permute-start | bytes 2949128 | tf_op jit(solution)/shard_map/ppermute | solution.py:24
  25.8 15.6 %collective-permute-start.10 = (bf16[96,2816]{1,0:T(8,128)(2,1)S(1)}, bf16[96,2816]{1,0:T(8,128)(2,1)S(1)}, u32[]{:S(2)}, u32[]{:S(2)}) collective-permute-start(bf16[96,2816]{1,0:T(8,128)(2,1)S(1)} %shard_map.152.rest_1_), channel_id=1, source_target_pairs={{0,8},{4,12},{8,0},{12,4},{16,24},{20,28},{24,16},{28,20},{1,9},{5... | collective-permute-start | bytes 1622024 | tf_op jit(solution)/shard_map/ppermute | solution.py:24
  27.0 17.4 %collective-permute-start.11 = (bf16[96,2816]{1,0:T(8,128)(2,1)S(1)}, bf16[96,2816]{1,0:T(8,128)(2,1)S(1)}, u32[]{:S(2)}, u32[]{:S(2)}) collective-permute-start(bf16[96,2816]{1,0:T(8,128)(2,1)S(1)} %shard_map.152.rest_1_), channel_id=1, source_target_pairs={{0,16},{4,20},{8,24},{12,28},{16,0},{20,4},{24,8},{28,12},{1,17},{... | collective-permute-start | bytes 1622024 | tf_op jit(solution)/shard_map/ppermute | solution.py:24
  27.0 8.6 %collective-permute-start.6 = (bf16[144,768]{1,0:T(8,128)(2,1)S(1)}, bf16[144,768]{1,0:T(8,128)(2,1)S(1)}, u32[]{:S(2)}, u32[]{:S(2)}) collective-permute-start(bf16[144,768]{1,0:T(8,128)(2,1)S(1)} %collective-permute-done.near), channel_id=1, source_target_pairs={{0,1},{1,0},{2,3},{3,2},{4,5},{5,4},{6,7},{7,6},{8,9},{9,8},{10,11... | collective-permute-start | bytes 663560 | tf_op jit(solution)/shard_map/ppermute | solution.py:24
  29.6 14.9 %collective-permute-start.9 = (bf16[128,768]{1,0:T(8,128)(2,1)S(1)}, bf16[128,768]{1,0:T(8,128)(2,1)S(1)}, u32[]{:S(2)}, u32[]{:S(2)}) collective-permute-start(bf16[128,768]{1,0:T(8,128)(2,1)S(1)} %copy-done.4), channel_id=1, source_target_pairs={{0,1},{1,0},{2,3},{3,2},{4,5},{5,4},{6,7},{7,6},{8,9},{9,8},{10,11... | collective-permute-start | bytes 589832 | tf_op jit(solution)/shard_map/ppermute | solution.py:24
  35.6 8.9 %collective-permute-start.8 = (bf16[64,768]{1,0:T(8,128)(2,1)S(1)}, bf16[64,768]{1,0:T(8,128)(2,1)S(1)}, u32[]{:S(2)}, u32[]{:S(2)}) collective-permute-start(bf16[64,768]{1,0:T(8,128)(2,1)S(1)} %collective-permute-done.7.near), channel_id=1, source_target_pairs={{0,1},{1,0},{2,3},{3,2},{4,5},{5,4},{6,7},{7,6},{8,9},{9,8},{10,11... | collective-permute-start | bytes 294920 | tf_op jit(solution)/shard_map/ppermute | solution.py:24
  41.5 8.0 %collective-permute-start.15 = (bf16[96,1408]{1,0:T(8,128)(2,1)S(1)}, bf16[96,1408]{1,0:T(8,128)(2,1)S(1)}, u32[]{:S(2)}, u32[]{:S(2)}) collective-permute-start(bf16[96,1408]{1,0:T(8,128)(2,1)S(1)} %slice.88.rest_2_), channel_id=1, source_target_pairs={{0,16},{4,20},{8,24},{12,28},{16,0},{20,4},{24,8},{28,12},{1,17},{... | collective-permute-start | bytes 811016 | tf_op jit(solution)/shard_map/ppermute | solution.py:24
  44.4 6.5 %collective-permute-start.16 = (bf16[96,1408]{1,0:T(8,128)(2,1)S(1)}, bf16[96,1408]{1,0:T(8,128)(2,1)S(1)}, u32[]{:S(2)}, u32[]{:S(2)}) collective-permute-start(bf16[96,1408]{1,0:T(8,128)(2,1)S(1)} %slice.89.rest_3_), channel_id=1, source_target_pairs={{0,8},{4,12},{8,0},{12,4},{16,24},{20,28},{24,16},{28,20},{1,9},{5... | collective-permute-start | bytes 811016 | tf_op jit(solution)/shard_map/ppermute | solution.py:24
  51.0 9.6 %collective-permute-start.17 = (bf16[288,2816]{1,0:T(8,128)(2,1)S(1)}, bf16[288,2816]{1,0:T(8,128)(2,1)S(1)}, u32[]{:S(2)}, u32[]{:S(2)}) collective-permute-start(bf16[288,2816]{1,0:T(8,128)(2,1)S(1)} %pad_maximum_fusion), channel_id=1, source_target_pairs={{0,4},{4,0},{8,12},{12,8},{16,20},{20,16},{24,28},{28,24},{1,5},{5... | collective-permute-start | bytes 4866056 | tf_op jit(solution)/shard_map/ppermute | solution.py:24
  51.1 9.5 %collective-permute-start.14 = (bf16[256,768]{1,0:T(8,128)(2,1)S(1)}, bf16[256,768]{1,0:T(8,128)(2,1)S(1)}, u32[]{:S(2)}, u32[]{:S(2)}) collective-permute-start(bf16[256,768]{1,0:T(8,128)(2,1)S(1)} %get-tuple-element.94.normed_own), channel_id=1, source_target_pairs={{0,4},{4,0},{8,12},{12,8},{16,20},{20,16},{24,28},{28,24},{1,5},{5... | collective-permute-start | bytes 1179656 | tf_op jit(solution)/shard_map/ppermute | solution.py:24
  51.6 9.0 %collective-permute-start.13 = (bf16[384,384]{1,0:T(8,128)(2,1)S(1)}, bf16[384,384]{1,0:T(8,128)(2,1)S(1)}, u32[]{:S(2)}, u32[]{:S(2)}) collective-permute-start(bf16[384,384]{1,0:T(8,128)(2,1)S(1)} %get-tuple-element.89.ctx_own), channel_id=1, source_target_pairs={{0,1},{1,0},{2,3},{3,2},{4,5},{5,4},{6,7},{7,6},{8,9},{9,8},{10,11... | collective-permute-start | bytes 884744 | tf_op jit(solution)/shard_map/ppermute | solution.py:24
  66.5 15.7 %collective-permute-start.24 = (bf16[384,768]{1,0:T(8,128)(2,1)S(1)}, bf16[384,768]{1,0:T(8,128)(2,1)S(1)}, u32[]{:S(2)}, u32[]{:S(2)}) collective-permute-start(bf16[384,768]{1,0:T(8,128)(2,1)S(1)} %get-tuple-element.105.gn_own), channel_id=1, source_target_pairs={{0,1},{1,0},{2,3},{3,2},{4,5},{5,4},{6,7},{7,6},{8,9},{9,8},{10,11... | collective-permute-start | bytes 1769480 | tf_op jit(solution)/shard_map/ppermute | solution.py:24
  71.8 17.5 %collective-permute-start.23 = (bf16[2,1440,128]{2,1,0:T(8,128)(2,1)S(1)}, bf16[2,1440,128]{2,1,0:T(8,128)(2,1)S(1)}, u32[]{:S(2)}, u32[]{:S(2)}) collective-permute-start(bf16[2,1440,128]{2,1,0:T(8,128)(2,1)S(1)} %get-tuple-element.104), channel_id=1, source_target_pairs={{0,8},{4,20},{8,0},{12,28},{16,24},{20,4},{24,16},{28,12},{1,9},{5... | collective-permute-start | bytes 2211848 | tf_op jit(solution)/shard_map/ppermute | solution.py:33
  89.6 12.8 %collective-permute-start.25 = (bf16[1,1440,128]{2,1,0:T(8,128)(2,1)S(1)}, bf16[1,1440,128]{2,1,0:T(8,128)(2,1)S(1)}, u32[]{:S(2)}, u32[]{:S(2)}) collective-permute-start(bf16[1,1440,128]{2,1,0:T(8,128)(2,1)S(1)} %get-tuple-element.134), channel_id=1, source_target_pairs={{0,16},{4,12},{8,24},{12,4},{16,0},{20,28},{24,8},{28,20},{1,17},{... | collective-permute-start | bytes 1105928 | tf_op jit(solution)/shard_map/ppermute | solution.py:33
  91.8 7.9 %collective-permute-start.28 = (bf16[128,768]{1,0:T(8,128)(2,1)S(1)}, bf16[128,768]{1,0:T(8,128)(2,1)S(1)}, u32[]{:S(2)}, u32[]{:S(2)}) collective-permute-start(bf16[128,768]{1,0:T(8,128)(2,1)S(1)} %get-tuple-element.118), channel_id=1, source_target_pairs={{0,1},{1,0},{2,3},{3,2},{4,5},{5,4},{6,7},{7,6},{8,9},{9,8},{10,11... | collective-permute-start | bytes 589832 | tf_op jit(solution)/shard_map/ppermute | solution.py:24
  92.2 10.2 %collective-permute-start.26 = (bf16[128,768]{1,0:T(8,128)(2,1)S(1)}, bf16[128,768]{1,0:T(8,128)(2,1)S(1)}, u32[]{:S(2)}, u32[]{:S(2)}) collective-permute-start(bf16[128,768]{1,0:T(8,128)(2,1)S(1)} %get-tuple-element.113), channel_id=1, source_target_pairs={{0,1},{1,0},{2,3},{3,2},{4,5},{5,4},{6,7},{7,6},{8,9},{9,8},{10,11... | collective-permute-start | bytes 589832 | tf_op jit(solution)/shard_map/ppermute | solution.py:24
  93.9 12.3 %collective-permute-start.29 = (bf16[2,1152,128]{2,1,0:T(8,128)(2,1)S(1)}, bf16[2,1152,128]{2,1,0:T(8,128)(2,1)S(1)}, u32[]{:S(2)}, u32[]{:S(2)}) collective-permute-start(bf16[2,1152,128]{2,1,0:T(8,128)(2,1)S(1)} %get-tuple-element.120), channel_id=1, source_target_pairs={{0,8},{4,20},{8,0},{12,28},{16,24},{20,4},{24,16},{28,12},{1,9},{5... | collective-permute-start | bytes 1769480 | tf_op jit(solution)/shard_map/ppermute | solution.py:33
  102.5 15.9 %collective-permute-start.33 = (bf16[720,128]{1,0:T(8,128)(2,1)S(1)}, bf16[720,128]{1,0:T(8,128)(2,1)S(1)}, u32[]{:S(2)}, u32[]{:S(2)}) collective-permute-start(bf16[720,128]{1,0:T(8,128)(2,1)S(1)} %get-tuple-element.138), channel_id=1, source_target_pairs={{0,2},{1,3},{2,0},{3,1},{4,6},{5,7},{6,4},{7,5},{8,10},{9,11},{10,... | collective-permute-start | bytes 552968 | tf_op jit(solution)/shard_map/ppermute | solution.py:24
  104.9 16.3 %collective-permute-start.32 = (bf16[720,128]{1,0:T(8,128)(2,1)S(1)}, bf16[720,128]{1,0:T(8,128)(2,1)S(1)}, u32[]{:S(2)}, u32[]{:S(2)}) collective-permute-start(bf16[720,128]{1,0:T(8,128)(2,1)S(1)} %get-tuple-element.139), channel_id=1, source_target_pairs={{0,2},{1,3},{2,0},{3,1},{4,6},{5,7},{6,4},{7,5},{8,10},{9,11},{10,... | collective-permute-start | bytes 552968 | tf_op jit(solution)/shard_map/ppermute | solution.py:24
  106.4 15.6 %collective-permute-start.30 = (bf16[1,1152,128]{2,1,0:T(8,128)(2,1)S(1)}, bf16[1,1152,128]{2,1,0:T(8,128)(2,1)S(1)}, u32[]{:S(2)}, u32[]{:S(2)}) collective-permute-start(bf16[1,1152,128]{2,1,0:T(8,128)(2,1)S(1)} %get-tuple-element.137), channel_id=1, source_target_pairs={{0,16},{4,12},{8,24},{12,4},{16,0},{20,28},{24,8},{28,20},{1,17},{... | collective-permute-start | bytes 884744 | tf_op jit(solution)/shard_map/ppermute | solution.py:33
  118.5 7.7 %collective-permute-start.35 = (bf16[720,128]{1,0:T(8,128)(2,1)S(1)}, bf16[720,128]{1,0:T(8,128)(2,1)S(1)}, u32[]{:S(2)}, u32[]{:S(2)}) collective-permute-start(bf16[720,128]{1,0:T(8,128)(2,1)S(1)} %add_convert_fusion.5.mine_1), channel_id=1, source_target_pairs={{0,1},{1,0},{2,3},{3,2},{4,5},{5,4},{6,7},{7,6},{8,9},{9,8},{10,11... | collective-permute-start | bytes 552968 | tf_op jit(solution)/shard_map/ppermute | solution.py:24
  121.2 11.3 %collective-permute-start.34 = (bf16[720,128]{1,0:T(8,128)(2,1)S(1)}, bf16[720,128]{1,0:T(8,128)(2,1)S(1)}, u32[]{:S(2)}, u32[]{:S(2)}) collective-permute-start(bf16[720,128]{1,0:T(8,128)(2,1)S(1)} %add_convert_fusion.7.mine_0), channel_id=1, source_target_pairs={{0,1},{1,0},{2,3},{3,2},{4,5},{5,4},{6,7},{7,6},{8,9},{9,8},{10,11... | collective-permute-start | bytes 552968 | tf_op jit(solution)/shard_map/ppermute | solution.py:24
  122.0 14.5 %collective-permute-start.36 = (bf16[576,128]{1,0:T(8,128)(2,1)S(1)}, bf16[576,128]{1,0:T(8,128)(2,1)S(1)}, u32[]{:S(2)}, u32[]{:S(2)}) collective-permute-start(bf16[576,128]{1,0:T(8,128)(2,1)S(1)} %get-tuple-element.140), channel_id=1, source_target_pairs={{0,2},{1,3},{2,0},{3,1},{4,6},{5,7},{6,4},{7,5},{8,10},{9,11},{10,... | collective-permute-start | bytes 442376 | tf_op jit(solution)/shard_map/ppermute | solution.py:24
  125.6 13.3 %collective-permute-start.31 = (bf16[576,128]{1,0:T(8,128)(2,1)S(1)}, bf16[576,128]{1,0:T(8,128)(2,1)S(1)}, u32[]{:S(2)}, u32[]{:S(2)}) collective-permute-start(bf16[576,128]{1,0:T(8,128)(2,1)S(1)} %get-tuple-element.141), channel_id=1, source_target_pairs={{0,2},{1,3},{2,0},{3,1},{4,6},{5,7},{6,4},{7,5},{8,10},{9,11},{10,... | collective-permute-start | bytes 442376 | tf_op jit(solution)/shard_map/ppermute | solution.py:24
  136.5 6.3 %collective-permute-start.38 = (bf16[576,128]{1,0:T(8,128)(2,1)S(1)}, bf16[576,128]{1,0:T(8,128)(2,1)S(1)}, u32[]{:S(2)}, u32[]{:S(2)}) collective-permute-start(bf16[576,128]{1,0:T(8,128)(2,1)S(1)} %add_convert_fusion.9.mine_1), channel_id=1, source_target_pairs={{0,1},{1,0},{2,3},{3,2},{4,5},{5,4},{6,7},{7,6},{8,9},{9,8},{10,11... | collective-permute-start | bytes 442376 | tf_op jit(solution)/shard_map/ppermute | solution.py:24
  138.9 6.1 %collective-permute-start.37 = (bf16[576,128]{1,0:T(8,128)(2,1)S(1)}, bf16[576,128]{1,0:T(8,128)(2,1)S(1)}, u32[]{:S(2)}, u32[]{:S(2)}) collective-permute-start(bf16[576,128]{1,0:T(8,128)(2,1)S(1)} %add_convert_fusion.11.mine_0), channel_id=1, source_target_pairs={{0,1},{1,0},{2,3},{3,2},{4,5},{5,4},{6,7},{7,6},{8,9},{9,8},{10,11... | collective-permute-start | bytes 442376 | tf_op jit(solution)/shard_map/ppermute | solution.py:24
  (21 other events, 243.6 us)
